TPU v7x, 32 devices: a whole 2x2x4 slice. The times are simulated.
32 devices in a mesh: dp: 8 (over z, x), seq: 4 (over y, core).
Axes of the slice: x: 2, y: 2, z: 4, core: 2. Of those that a mesh axis runs over, the one named last changes fastest.
Arguments:
- stream: float32 [8, 2048, 1024], P('dp', 'seq'), may hold values from -6 to 6
- cotangent: float32 [8, 2048, 1024], P('dp', 'seq'), may hold values from -6 to 6
- positions: int32 [8, 2048], P('dp', 'seq'), may hold values from 0 to 2047
- mixing_weight: float32 [2, 1024, 3072], P(None, ('dp', 'seq')), may hold values from -0.1875 to 0.1875
- mixing_first: float32 [2, 1024, 3072], P(None, ('dp', 'seq')), may hold values from -0.0012207031 to 0.0012207031
- mixing_second: float32 [2, 1024, 3072], P(None, ('dp', 'seq')), may hold values from 3.9694434e-08 to 1.5877774e-07
- mixing_average: float32 [2, 1024, 3072], P(None, ('dp', 'seq')), may hold values from -0.00036621094 to 0.00036621094
- output_weight: float32 [2, 1024, 1024], P(None, ('dp', 'seq')), may hold values from -1.5 to 1.5
- output_first: float32 [2, 1024, 1024], P(None, ('dp', 'seq')), may hold values from -0.0012207031 to 0.0012207031
- output_second: float32 [2, 1024, 1024], P(None, ('dp', 'seq')), may hold values from 3.9694434e-08 to 1.5877774e-07
- output_average: float32 [2, 1024, 1024], P(None, ('dp', 'seq')), may hold values from -0.0029296875 to 0.0029296875
- expand_weight: float32 [2, 1024, 4096], P(None, ('dp', 'seq')), may hold values from -0.1875 to 0.1875
- expand_first: float32 [2, 1024, 4096], P(None, ('dp', 'seq')), may hold values from -0.0012207031 to 0.0012207031
- expand_second: float32 [2, 1024, 4096], P(None, ('dp', 'seq')), may hold values from 9.923609e-09 to 3.9694434e-08
- expand_average: float32 [2, 1024, 4096], P(None, ('dp', 'seq')), may hold values from -0.00036621094 to 0.00036621094
- shrink_weight: float32 [2, 4096, 1024], P(None, ('dp', 'seq')), may hold values from -0.09375 to 0.09375
- shrink_first: float32 [2, 4096, 1024], P(None, ('dp', 'seq')), may hold values from -0.0012207031 to 0.0012207031
- shrink_second: float32 [2, 4096, 1024], P(None, ('dp', 'seq')), may hold values from 3.9694434e-08 to 1.5877774e-07
- shrink_average: float32 [2, 4096, 1024], P(None, ('dp', 'seq')), may hold values from -0.00018310547 to 0.00018310547
- affine_weight: float32 [2, 13312], P(None, ('dp', 'seq')), may hold values from -0.3 to 1.5, as said below
- affine_first: float32 [2, 13312], P(None, ('dp', 'seq')), may hold values from -0.0048828125 to 0.0048828125
- affine_second: float32 [2, 13312], P(None, ('dp', 'seq')), may hold values from 6.3511095e-07 to 2.5404438e-06
- affine_average: float32 [2, 13312], P(None, ('dp', 'seq')), may hold values from -0.001 to 0.002
Outputs:
- result: float32 [8, 2048, 1024], P('dp', 'seq')
- stream_grad: float32 [8, 2048, 1024], P('dp', 'seq')
- gradient_norm: float32 [], replicated
- mixing_master: float32 [2, 1024, 3072], P(None, ('dp', 'seq'))
- mixing_moment: float32 [2, 1024, 3072], P(None, ('dp', 'seq'))
- mixing_square: float32 [2, 1024, 3072], P(None, ('dp', 'seq'))
- mixing_smooth: float32 [2, 1024, 3072], P(None, ('dp', 'seq'))
- output_master: float32 [2, 1024, 1024], P(None, ('dp', 'seq'))
- output_moment: float32 [2, 1024, 1024], P(None, ('dp', 'seq'))
- output_square: float32 [2, 1024, 1024], P(None, ('dp', 'seq'))
- output_smooth: float32 [2, 1024, 1024], P(None, ('dp', 'seq'))
- expand_master: float32 [2, 1024, 4096], P(None, ('dp', 'seq'))
- expand_moment: float32 [2, 1024, 4096], P(None, ('dp', 'seq'))
- expand_square: float32 [2, 1024, 4096], P(None, ('dp', 'seq'))
- expand_smooth: float32 [2, 1024, 4096], P(None, ('dp', 'seq'))
- shrink_master: float32 [2, 4096, 1024], P(None, ('dp', 'seq'))
- shrink_moment: float32 [2, 4096, 1024], P(None, ('dp', 'seq'))
- shrink_square: float32 [2, 4096, 1024], P(None, ('dp', 'seq'))
- shrink_smooth: float32 [2, 4096, 1024], P(None, ('dp', 'seq'))
- affine_master: float32 [2, 13312], P(None, ('dp', 'seq'))
- affine_moment: float32 [2, 13312], P(None, ('dp', 'seq'))
- affine_square: float32 [2, 13312], P(None, ('dp', 'seq'))
- affine_smooth: float32 [2, 13312], P(None, ('dp', 'seq'))
Inputs may be any that keep to these rules, and one draw needn't show every extreme that they name: `affine_weight`: the entries of the two norms' gains lie between 0.5 and 1.5, those of the biases between -0.3 and 0.3.
All inputs are finite; a program needn't handle non-finite values.
Results may differ from a plain program's by a relative error of at most 0.012.
Values may be sent and summed in bfloat16 or wider, within the bound.
No kernel may reach another device: no remote copies, remote signals or barrier semaphores. Data moves between devices by JAX's collectives and lax.ppermute only.
A program may use at most 384 MiB of HBM per device.

v0:
```python
from functools import partial
import math

import jax
import jax.numpy as jnp
from jax import lax
from jax.sharding import PartitionSpec as P

D = 1024
H = 16
HD = 64
ROT = 16
FF = 4096
LEN = 2048
LAYERS = 2
STEP = 3


NORM_EPS = 1e-05
CLIP_LIMIT = 1.0
BETA_FIRST = 0.5
BETA_SECOND = 0.5
ADAM_EPS = 1e-08
WEIGHT_DECAY = 0.01
EMA_DECAY = 0.999
SMALL_RATE = 0.1
MASK_VALUE = -1e30


def layer_norm(values, norm_gain, norm_shift):
    centre = values - jnp.mean(values, -1, keepdims=True)
    spread = jnp.mean(centre * centre, -1, keepdims=True)
    return centre * lax.rsqrt(spread + NORM_EPS) * norm_gain + norm_shift


def phases(positions, rotary):
    steps_half = jnp.arange(rotary // 2).astype(jnp.float32)
    frequency = 10000.0 ** (-2.0 * steps_half / rotary)
    angles = positions.astype(jnp.float32)[..., None] * frequency
    angles = jnp.concatenate([angles, angles], -1)
    return (jnp.cos(angles), jnp.sin(angles))


def rotate(values, cosine_table, sine_table, rotary):
    halfway = rotary // 2
    turning = values[..., :rotary]
    swapped = jnp.concatenate([-turning[..., halfway:], turning[..., :halfway]], -1)
    return jnp.concatenate(
        [turning * cosine_table + swapped * sine_table, values[..., rotary:]], -1
    )


def rotate_back(values, cosine_table, sine_table, rotary):
    halfway = rotary // 2
    turning = values[..., :rotary]
    sine_part = turning * sine_table
    swapped = jnp.concatenate([sine_part[..., halfway:], -sine_part[..., :halfway]], -1)
    return jnp.concatenate([turning * cosine_table + swapped, values[..., rotary:]], -1)


def split_affine(affine):
    bounds = [D, D, D, D, 3 * D, D, FF, D]
    pieces = []
    offset = 0
    for length in bounds:
        pieces.append(affine[offset : offset + length])
        offset = offset + length
    return pieces


def add_into(totals, part_value, position):
    current_part = lax.dynamic_index_in_dim(totals, position, 0, keepdims=False)
    return lax.dynamic_update_index_in_dim(totals, current_part + part_value, position, 0)


def attend(head_view):
    sequence_count, length = (head_view.shape[0], head_view.shape[1])
    block_rows = min(512, length)
    per_sequence = length // block_rows
    key_index = jnp.arange(length, dtype=jnp.int32)

    def one_block(block_index):
        sequence_pick = block_index // per_sequence
        start_row = block_index % per_sequence * block_rows
        sequence = lax.dynamic_index_in_dim(head_view, sequence_pick, 0, keepdims=False)
        query_block = lax.dynamic_slice_in_dim(sequence[:, 0], start_row, block_rows, 0)
        scores = jnp.einsum(
            "qhd,khd->hqk", query_block, sequence[:, 1], preferred_element_type=jnp.float32
        )
        row_index = start_row + jnp.arange(block_rows, dtype=jnp.int32)
        scores = jnp.where(key_index[None, :] <= row_index[:, None], scores, MASK_VALUE)
        highest = jnp.max(scores, -1, keepdims=True)
        exponent = jnp.exp(scores - highest)
        totals = jnp.sum(exponent, -1, keepdims=True)
        weights = (exponent / totals).astype(jnp.bfloat16)
        attended = jnp.einsum(
            "hqk,khd->qhd", weights, sequence[:, 2], preferred_element_type=jnp.float32
        )
        return (attended.astype(jnp.bfloat16), (highest + jnp.log(totals))[..., 0])

    attended, log_totals = lax.map(
        one_block, jnp.arange(sequence_count * per_sequence, dtype=jnp.int32)
    )
    return (
        attended.reshape(sequence_count, length, head_view.shape[3] * head_view.shape[4]),
        log_totals,
    )


def attend_back(head_view, log_totals, grad_heads):
    sequence_count, length = (head_view.shape[0], head_view.shape[1])
    block_rows = min(512, length)
    per_sequence = length // block_rows
    key_index = jnp.arange(length, dtype=jnp.int32)
    zero_state = jnp.zeros(
        (sequence_count, length, head_view.shape[3], head_view.shape[4]), jnp.float32
    )

    def one_block(carried, block_index):
        key_grad, value_grad = carried
        sequence_pick = block_index // per_sequence
        start_row = block_index % per_sequence * block_rows
        sequence = lax.dynamic_index_in_dim(head_view, sequence_pick, 0, keepdims=False)
        query_block = lax.dynamic_slice_in_dim(sequence[:, 0], start_row, block_rows, 0)
        grad_sequence = lax.dynamic_index_in_dim(grad_heads, sequence_pick, 0, keepdims=False)
        grad_block = lax.dynamic_slice_in_dim(grad_sequence, start_row, block_rows, 0)
        scores = jnp.einsum(
            "qhd,khd->hqk", query_block, sequence[:, 1], preferred_element_type=jnp.float32
        )
        row_index = start_row + jnp.arange(block_rows, dtype=jnp.int32)
        scores = jnp.where(key_index[None, :] <= row_index[:, None], scores, MASK_VALUE)
        softmax_out = jnp.exp(scores - log_totals[block_index][..., None])
        rounded = softmax_out.astype(jnp.bfloat16)
        value_part = jnp.einsum(
            "hqk,qhd->khd", rounded, grad_block, preferred_element_type=jnp.float32
        )
        prob_grad = jnp.einsum(
            "qhd,khd->hqk", grad_block, sequence[:, 2], preferred_element_type=jnp.float32
        )
        inner_sum = jnp.sum(softmax_out * prob_grad, -1, keepdims=True)
        score_grad = (softmax_out * (prob_grad - inner_sum)).astype(jnp.bfloat16)
        query_grad = jnp.einsum(
            "hqk,khd->qhd", score_grad, sequence[:, 1], preferred_element_type=jnp.float32
        )
        key_part = jnp.einsum(
            "hqk,qhd->khd", score_grad, query_block, preferred_element_type=jnp.float32
        )
        key_grad = add_into(key_grad, key_part, sequence_pick)
        value_grad = add_into(value_grad, value_part, sequence_pick)
        return ((key_grad, value_grad), query_grad.astype(jnp.bfloat16))

    (key_grad, value_grad), query_grads = lax.scan(
        one_block,
        (zero_state, zero_state),
        jnp.arange(sequence_count * per_sequence, dtype=jnp.int32),
    )
    query_grads = query_grads.reshape(zero_state.shape)
    return jnp.stack(
        [query_grads, key_grad.astype(jnp.bfloat16), value_grad.astype(jnp.bfloat16)], 2
    )


def reduce_grads(mixing_grad, output_grad, expand_grad, shrink_grad, affine_grad):
    return (
        lax.psum_scatter(mixing_grad, ("dp", "seq"), scatter_dimension=0, tiled=True),
        lax.psum_scatter(output_grad, ("dp", "seq"), scatter_dimension=0, tiled=True),
        lax.psum_scatter(expand_grad, ("dp", "seq"), scatter_dimension=0, tiled=True),
        lax.psum_scatter(shrink_grad, ("dp", "seq"), scatter_dimension=0, tiled=True),
        lax.psum_scatter(affine_grad, ("dp", "seq"), scatter_dimension=0, tiled=True),
    )


def adamw_update(
    weight, first_moment, second, average, gradient, clip_scale, step_rate, decay_rate
):
    clipped = gradient * clip_scale
    first_new = BETA_FIRST * first_moment + (1.0 - BETA_FIRST) * clipped
    second_new = BETA_SECOND * second + (1.0 - BETA_SECOND) * clipped * clipped
    first_hat = first_new / (1.0 - BETA_FIRST**STEP)
    second_hat = second_new / (1.0 - BETA_SECOND**STEP)
    weight_new = weight - step_rate * (
        first_hat / (jnp.sqrt(second_hat) + ADAM_EPS) + decay_rate * weight
    )
    average_new = EMA_DECAY * average + (1.0 - EMA_DECAY) * weight_new
    return (weight_new, first_new, second_new, average_new)


def local(
    stream,
    cotangent,
    positions,
    mixing_weight,
    mixing_first,
    mixing_second,
    mixing_average,
    output_weight,
    output_first,
    output_second,
    output_average,
    expand_weight,
    expand_first,
    expand_second,
    expand_average,
    shrink_weight,
    shrink_first,
    shrink_second,
    shrink_average,
    affine_weight,
    affine_first,
    affine_second,
    affine_average,
):
    position_parts = lax.axis_size("seq")
    sequence_count = stream.shape[0]
    part_rows = stream.shape[1]
    row_count = sequence_count * part_rows
    local_heads = H // position_parts
    head_width = local_heads * HD
    full_length = part_rows * position_parts
    query_scale = 1.0 / math.sqrt(HD)
    cosine_table, sine_table = phases(positions, ROT)
    cosine_table = cosine_table[:, :, None, :]
    sine_table = sine_table[:, :, None, :]
    current = stream.reshape(row_count, D)
    stored = []
    for layer_index in range(LAYERS):
        weights_now = (
            lax.all_gather(
                mixing_weight[layer_index].astype(jnp.bfloat16), ("dp", "seq"), axis=0, tiled=True
            ),
            lax.all_gather(
                output_weight[layer_index].astype(jnp.bfloat16), ("dp", "seq"), axis=0, tiled=True
            ),
            lax.all_gather(
                expand_weight[layer_index].astype(jnp.bfloat16), ("dp", "seq"), axis=0, tiled=True
            ),
            lax.all_gather(
                shrink_weight[layer_index].astype(jnp.bfloat16), ("dp", "seq"), axis=0, tiled=True
            ),
            lax.all_gather(
                affine_weight[layer_index].astype(jnp.bfloat16), ("dp", "seq"), axis=0, tiled=True
            ),
        )
        mixing, output, expand, shrink, affine = weights_now
        (
            gain_one,
            shift_one,
            gain_two,
            shift_two,
            mixing_bias,
            output_bias,
            expand_bias,
            shrink_bias,
        ) = split_affine(affine.astype(jnp.float32))
        normed_one = layer_norm(current, gain_one, shift_one).astype(jnp.bfloat16)
        mixed_rows = jnp.dot(normed_one, mixing, preferred_element_type=jnp.float32) + mixing_bias
        mixed_rows = mixed_rows.reshape(sequence_count, part_rows, 3, H, HD)
        query_rows = rotate(mixed_rows[:, :, 0], cosine_table, sine_table, ROT) * query_scale
        key_rows = rotate(mixed_rows[:, :, 1], cosine_table, sine_table, ROT)
        outgoing = jnp.stack([query_rows, key_rows, mixed_rows[:, :, 2]], 2).astype(jnp.bfloat16)
        outgoing = outgoing.reshape(sequence_count, part_rows, 3, position_parts, head_width)
        head_view = lax.all_to_all(outgoing, "seq", split_axis=3, concat_axis=1, tiled=True)
        head_view = head_view.reshape(sequence_count, full_length, 3, local_heads, HD)
        attended, log_totals = attend(head_view)
        returned = lax.all_to_all(
            attended.reshape(sequence_count, full_length, 1, head_width),
            "seq",
            split_axis=1,
            concat_axis=2,
            tiled=True,
        )
        attended_rows = returned.reshape(row_count, D)
        branch_one = (
            jnp.dot(attended_rows, output, preferred_element_type=jnp.float32) + output_bias
        )
        normed_two = layer_norm(current, gain_two, shift_two).astype(jnp.bfloat16)
        hidden = jnp.dot(normed_two, expand, preferred_element_type=jnp.float32) + expand_bias
        activated = jax.nn.gelu(hidden, approximate=False).astype(jnp.bfloat16)
        branch_two = jnp.dot(activated, shrink, preferred_element_type=jnp.float32) + shrink_bias
        stored.append(
            (
                current,
                normed_one,
                normed_two,
                head_view,
                log_totals,
                attended_rows,
                hidden,
                activated,
                weights_now,
            )
        )
        current = current + branch_one + branch_two
    result = current.reshape(sequence_count, part_rows, D)
    gradient = cotangent.reshape(row_count, D)
    reduced = [None] * LAYERS
    for layer_index in reversed(range(LAYERS)):
        (
            current,
            normed_one,
            normed_two,
            head_view,
            log_totals,
            attended_rows,
            hidden,
            activated,
            kept_weights,
        ) = stored[layer_index]
        weights_now = (
            lax.all_gather(
                mixing_weight[layer_index].astype(jnp.bfloat16), ("dp", "seq"), axis=0, tiled=True
            ),
            lax.all_gather(
                output_weight[layer_index].astype(jnp.bfloat16), ("dp", "seq"), axis=0, tiled=True
            ),
            lax.all_gather(
                expand_weight[layer_index].astype(jnp.bfloat16), ("dp", "seq"), axis=0, tiled=True
            ),
            lax.all_gather(
                shrink_weight[layer_index].astype(jnp.bfloat16), ("dp", "seq"), axis=0, tiled=True
            ),
            lax.all_gather(
                affine_weight[layer_index].astype(jnp.bfloat16), ("dp", "seq"), axis=0, tiled=True
            ),
        )
        mixing, output, expand, shrink, affine = weights_now
        gain_one, shift_one, gain_two, shift_two = split_affine(affine.astype(jnp.float32))[:4]
        grad_low = gradient.astype(jnp.bfloat16)
        shrink_grad = jnp.dot(activated.T, grad_low, preferred_element_type=jnp.float32)
        output_grad = jnp.dot(attended_rows.T, grad_low, preferred_element_type=jnp.float32)
        activated_grad = jnp.dot(grad_low, shrink.T, preferred_element_type=jnp.float32)
        unused_value, gelu_pull = jax.vjp(partial(jax.nn.gelu, approximate=False), hidden)
        hidden_grad = gelu_pull(activated_grad)[0]
        hidden_low = hidden_grad.astype(jnp.bfloat16)
        expand_grad = jnp.dot(normed_two.T, hidden_low, preferred_element_type=jnp.float32)
        normed_two_grad = jnp.dot(hidden_low, expand.T, preferred_element_type=jnp.float32)
        attended_grad = jnp.dot(grad_low, output.T, preferred_element_type=jnp.float32).astype(
            jnp.bfloat16
        )
        grad_heads = lax.all_to_all(
            attended_grad.reshape(sequence_count, part_rows, position_parts, head_width),
            "seq",
            split_axis=2,
            concat_axis=1,
            tiled=True,
        )
        grad_heads = grad_heads.reshape(sequence_count, full_length, local_heads, HD)
        head_grads = attend_back(head_view, log_totals, grad_heads)
        row_grads = lax.all_to_all(
            head_grads.reshape(sequence_count, full_length, 3, 1, head_width),
            "seq",
            split_axis=1,
            concat_axis=3,
            tiled=True,
        )
        row_grads = row_grads.reshape(sequence_count, part_rows, 3, H, HD).astype(jnp.float32)
        query_grad = rotate_back(row_grads[:, :, 0] * query_scale, cosine_table, sine_table, ROT)
        key_grad = rotate_back(row_grads[:, :, 1], cosine_table, sine_table, ROT)
        mixed_grad = jnp.stack([query_grad, key_grad, row_grads[:, :, 2]], 2).reshape(
            row_count, 3 * D
        )
        mixed_low = mixed_grad.astype(jnp.bfloat16)
        mixing_grad = jnp.dot(normed_one.T, mixed_low, preferred_element_type=jnp.float32)
        normed_one_grad = jnp.dot(mixed_low, mixing.T, preferred_element_type=jnp.float32)
        unused_one, pull_one = jax.vjp(layer_norm, current, gain_one, shift_one)
        input_one, gain_one_grad, shift_one_grad = pull_one(normed_one_grad)
        unused_two, pull_two = jax.vjp(layer_norm, current, gain_two, shift_two)
        input_two, gain_two_grad, shift_two_grad = pull_two(normed_two_grad)
        output_sum = jnp.sum(gradient, 0)
        affine_grad = jnp.concatenate(
            [
                gain_one_grad,
                shift_one_grad,
                gain_two_grad,
                shift_two_grad,
                jnp.sum(mixed_grad, 0),
                output_sum,
                jnp.sum(hidden_grad, 0),
                output_sum,
            ]
        )
        reduced[layer_index] = reduce_grads(
            mixing_grad, output_grad, expand_grad, shrink_grad, affine_grad
        )
        gradient = gradient + input_one + input_two
    stream_grad = gradient.reshape(sequence_count, part_rows, D)
    stacked = []
    local_squares = jnp.float32(0.0)
    for kind_index in range(5):
        kind_grad = jnp.stack([reduced[layer_index][kind_index] for layer_index in range(LAYERS)])
        stacked.append(kind_grad)
        local_squares = local_squares + jnp.sum(kind_grad * kind_grad)
    total_squares = lax.psum(local_squares, ("dp", "seq"))
    gradient_norm = jnp.sqrt(total_squares)
    clip_scale = jnp.minimum(1.0, CLIP_LIMIT / (gradient_norm + 1e-06))
    step_rates = (D ** (-0.5), (D * 32 // LEN) ** (-0.5), D ** (-0.5), FF ** (-0.5), SMALL_RATE)
    decays = (WEIGHT_DECAY, WEIGHT_DECAY, WEIGHT_DECAY, WEIGHT_DECAY, 0.0)
    states = (
        (mixing_weight, mixing_first, mixing_second, mixing_average),
        (output_weight, output_first, output_second, output_average),
        (expand_weight, expand_first, expand_second, expand_average),
        (shrink_weight, shrink_first, shrink_second, shrink_average),
        (affine_weight, affine_first, affine_second, affine_average),
    )
    updated = ()
    for kind_index in range(5):
        weight, first_moment, second, average = states[kind_index]
        updated = updated + adamw_update(
            weight,
            first_moment,
            second,
            average,
            stacked[kind_index],
            clip_scale,
            step_rates[kind_index],
            decays[kind_index],
        )
    return (result, stream_grad, gradient_norm) + updated


def solution(mesh):
    return jax.shard_map(
        local,
        mesh=mesh,
        in_specs=(
            P("dp", "seq", None),
            P("dp", "seq", None),
            P("dp", "seq"),
            P(None, ("dp", "seq"), None),
            P(None, ("dp", "seq"), None),
            P(None, ("dp", "seq"), None),
            P(None, ("dp", "seq"), None),
            P(None, ("dp", "seq"), None),
            P(None, ("dp", "seq"), None),
            P(None, ("dp", "seq"), None),
            P(None, ("dp", "seq"), None),
            P(None, ("dp", "seq"), None),
            P(None, ("dp", "seq"), None),
            P(None, ("dp", "seq"), None),
            P(None, ("dp", "seq"), None),
            P(None, ("dp", "seq"), None),
            P(None, ("dp", "seq"), None),
            P(None, ("dp", "seq"), None),
            P(None, ("dp", "seq"), None),
            P(None, ("dp", "seq")),
            P(None, ("dp", "seq")),
            P(None, ("dp", "seq")),
            P(None, ("dp", "seq")),
        ),
        out_specs=(
            P("dp", "seq", None),
            P("dp", "seq", None),
            P(),
            P(None, ("dp", "seq"), None),
            P(None, ("dp", "seq"), None),
            P(None, ("dp", "seq"), None),
            P(None, ("dp", "seq"), None),
            P(None, ("dp", "seq"), None),
            P(None, ("dp", "seq"), None),
            P(None, ("dp", "seq"), None),
            P(None, ("dp", "seq"), None),
            P(None, ("dp", "seq"), None),
            P(None, ("dp", "seq"), None),
            P(None, ("dp", "seq"), None),
            P(None, ("dp", "seq"), None),
            P(None, ("dp", "seq"), None),
            P(None, ("dp", "seq"), None),
            P(None, ("dp", "seq"), None),
            P(None, ("dp", "seq"), None),
            P(None, ("dp", "seq")),
            P(None, ("dp", "seq")),
            P(None, ("dp", "seq")),
            P(None, ("dp", "seq")),
        ),
        check_vma=False,
    )
```

profile of v0, /device:TPU:0, one launch (start us, length us, event | category | flops | bytes accessed | tf_op | source)
XLA Modules:
  0.0 2873.2 jit_solution(6960125846221919418)
XLA Ops:
  16.1 43.6 %all-reduce.5 = (bf16[13312]{0:T(1024)(128)(2,1)S(1)}, bf16[13312]{0:T(1024)(128)(2,1)}) all-reduce(bf16[13312]{0:T(1024)(128)(2,1)S(1)} %dynamic-update-slice, bf16[13312]{0:T(1024)(128)(2,1)S(1)} %dynamic-update-slice.1), channel_id=2, replica_groups=mesh['dp'=8,'seq'=4] {'dp','seq'}, use_global_device_ids=true, to_apply=%add | all-reduce | flops 26624 | bytes 106496
  61.7 22.4 all-gather.19.cloned.1.call-done
  112.4 32.8 %all-gather.29.cloned.1.call-done = bf16[1,1024,1024]{2,1,0:T(8,128)(2,1)} async-done(((bf16[1,32,1024]{2,1,0:T(8,128)(2,1)}), bf16[1,1024,1024]{2,1,0:T(8,128)(2,1)}) %all-gather.29.cloned.1.call-update) | async-done | bytes 2097168 | tf_op jit(solution)/shard_map/all_gather | solution.py:231
  168.6 62.7 %while.64 = (s32[]{:T(128)}, bf16[4,512,4,64]{1,3,2,0:T(8,128)(2,1)}, f32[4,4,512]{2,1,0:T(4,128)S(1)}, s32[4]{0:T(128)S(1)}, bf16[1,2048,3,4,64]{1,4,3,2,0:T(8,...) while((s32[]{:T(128)}, ...), condition=%wide.region_5.6_spmd.clone, body=%wide.region_2.5_spmd.clone.sunk | while | flops 1112668672 | bytes 59314476 | solution.py:101
  244.7 12.6 reduce.8
  290.4 27.7 multiply_convert_fusion.3
  318.2 48.9 %all-gather.25.cloned.1.call-done = bf16[1,4096,1024]{2,1,0:T(8,128)(2,1)} async-done(((bf16[1,128,1024]{2,1,0:T(8,128)(2,1)}), bf16[1,4096,1024]{2,1,0:T(8,128)(2,1)}) %all-gather.25.cloned.1.call-update) | async-done | bytes 8388624 | tf_op jit(solution)/shard_map/all_gather | solution.py:237
  379.2 59.4 %all-gather.27.cloned.1.call-done = bf16[1,1024,3072]{2,1,0:T(8,128)(2,1)} async-done(((bf16[1,32,3072]{2,1,0:T(8,128)(2,1)}), bf16[1,1024,3072]{2,1,0:T(8,128)(2,1)}) %all-gather.27.cloned.1.call-update) | async-done | bytes 6291472 | tf_op jit(solution)/shard_map/all_gather | solution.py:228
  467.2 67.9 %all-gather.31.cloned.1.call-done = bf16[1,1024,4096]{2,1,0:T(8,128)(2,1)} async-done(((bf16[1,32,4096]{2,1,0:T(8,128)(2,1)}), bf16[1,1024,4096]{2,1,0:T(8,128)(2,1)}) %all-gather.31.cloned.1.call-update) | async-done | bytes 8388624 | tf_op jit(solution)/shard_map/all_gather | solution.py:234
  535.1 28.0 multiply_convert_fusion.2
  573.1 63.4 %while.65 = (s32[]{:T(128)}, bf16[4,512,4,64]{1,3,2,0:T(8,128)(2,1)}, f32[4,4,512]{2,1,0:T(4,128)S(1)}, s32[4]{0:T(128)S(1)}, bf16[1,2048,3,4,64]{1,4,3,2,0:T(8,...) while((s32[]{:T(128)}, ...), condition=%wide.region_11.12_spmd.clone, body=%wide.region_8.11_spmd.clone.sunk | while | flops 1112668672 | bytes 59314476 | solution.py:101
  648.7 12.6 reduce.9
  673.3 211.5 %while.66 = (s32[]{:T(128)}, f32[1,2048,4,64]{1,3,2,0:T(8,128)}, f32[1,2048,4,64]{1,3,2,0:T(8,128)}, bf16[4,512,4,64]{1,3,2,0:T(8,128)(2,1)}, bf16[1,2048,3,4,64...) while((s32[]{:T(128)}, f32[1,2048,4,64]{1,3,2,0:T(8,128)}, ...), condition=%wide.region_14.15_spmd.clone, body=%wide.region_12.14_spmd.clone.sunk | while | flops 2736912896 | bytes 233108096 | solution.py:152
  694.6 12.1 multiply_reduce_fusion.19
  706.7 12.0 multiply_convert_fusion.6
  747.4 12.1 multiply_reduce_fusion.19
  759.4 12.0 multiply_convert_fusion.6
  800.1 12.1 multiply_reduce_fusion.19
  812.1 12.0 multiply_convert_fusion.6
  852.8 12.1 multiply_reduce_fusion.19
  864.9 12.0 multiply_convert_fusion.6
  900.8 14.7 fusion.236
  922.5 26.4 all-to-all-done.5
  994.7 14.3 all-to-all-done.6
  1017.7 214.0 %while.67 = (s32[]{:T(128)}, f32[1,2048,4,64]{1,3,2,0:T(8,128)}, f32[1,2048,4,64]{1,3,2,0:T(8,128)}, bf16[4,512,4,64]{1,3,2,0:T(8,128)(2,1)}, bf16[1,2048,3,4,64...) while((s32[]{:T(128)}, f32[1,2048,4,64]{1,3,2,0:T(8,128)}, ...), condition=%wide.region_21.22_spmd.clone, body=%wide.region_19.21_spmd.clone.sunk | while | flops 2736912896 | bytes 233107904 | solution.py:152
  1039.8 12.1 multiply_reduce_fusion.20
  1051.8 12.0 multiply_convert_fusion.7
  1093.2 12.1 multiply_reduce_fusion.20
  1105.2 12.0 multiply_convert_fusion.7
  1146.6 12.1 multiply_reduce_fusion.20
  1158.7 12.0 multiply_convert_fusion.7
  1200.0 12.1 multiply_reduce_fusion.20
  1212.1 12.0 multiply_convert_fusion.7
  1247.8 14.7 fusion.237
  1262.5 33.5 %all-to-all-done.7 = bf16[1,2048,3,1,256]{4,2,3,0,1:T(4,128)(2,1)} async-done(((bf16[1,2048,3,1,256]{4,2,3,0,1:T(4,128)(2,1)}), bf16[1,2048,3,1,256]{4,2,3,0,1:T(4,128)(2,1)}, u32[]{:S(2)}, u32[]{:S(2)}) %all-to-all-start.7) | async-done | bytes 3145760 | tf_op jit(solution)/shard_map/all_to_all | solution.py:349
  1342.8 11.0 fusion.208
  1366.1 13.4 fusion.163
  1380.2 13.3 fusion.160
  1432.9 20.3 all-reduce.8.cloned.1.call-done
  1455.4 142.2 %reduce-scatter.15.cloned.1.call-done = f32[32,1024]{1,0:T(8,128)} async-done(((f32[1024,1024]{1,0:T(8,128)}), f32[32,1024]{1,0:T(8,128)}) %reduce-scatter.15.cloned.1.call-update) | async-done | bytes 131088 | tf_op jit(solution)/shard_map/reduce_scatter | solution.py:166
  1597.5 139.2 %reduce-scatter.13.cloned.1.call-done = f32[32,1024]{1,0:T(8,128)} async-done(((f32[1024,1024]{1,0:T(8,128)}), f32[32,1024]{1,0:T(8,128)}) %reduce-scatter.13.cloned.1.call-update) | async-done | bytes 131088 | tf_op jit(solution)/shard_map/reduce_scatter | solution.py:166
  1738.4 155.9 %reduce-scatter.11.cloned.1.call-done = f32[32,3072]{1,0:T(8,128)} async-done(((f32[1024,3072]{1,0:T(8,128)}), f32[32,3072]{1,0:T(8,128)}) %reduce-scatter.11.cloned.1.call-update) | async-done | bytes 393232 | tf_op jit(solution)/shard_map/reduce_scatter | solution.py:165
  1894.2 161.5 %reduce-scatter.9.cloned.1.call-done = f32[32,3072]{1,0:T(8,128)} async-done(((f32[1024,3072]{1,0:T(8,128)}), f32[32,3072]{1,0:T(8,128)}) %reduce-scatter.9.cloned.1.call-update) | async-done | bytes 393232 | tf_op jit(solution)/shard_map/reduce_scatter | solution.py:165
  2059.0 181.1 %reduce-scatter.19.cloned.1.call-done = f32[32,4096]{1,0:T(8,128)} async-done(((f32[1024,4096]{1,0:T(8,128)}), f32[32,4096]{1,0:T(8,128)}) %reduce-scatter.19.cloned.1.call-update) | async-done | bytes 524304 | tf_op jit(solution)/shard_map/reduce_scatter | solution.py:167
  2240.1 186.7 %reduce-scatter.17.cloned.1.call-done = f32[32,4096]{1,0:T(8,128)} async-done(((f32[1024,4096]{1,0:T(8,128)}), f32[32,4096]{1,0:T(8,128)}) %reduce-scatter.17.cloned.1.call-update) | async-done | bytes 524304 | tf_op jit(solution)/shard_map/reduce_scatter | solution.py:167
  2429.5 184.0 %reduce-scatter.23.cloned.1.call-done = f32[128,1024]{1,0:T(8,128)} async-done(((f32[4096,1024]{1,0:T(8,128)}), f32[128,1024]{1,0:T(8,128)}) %reduce-scatter.23.cloned.1.call-update) | async-done | bytes 524304 | tf_op jit(solution)/shard_map/reduce_scatter | solution.py:168
  2613.6 186.7 %reduce-scatter.21.cloned.1.call-done = f32[128,1024]{1,0:T(8,128)} async-done(((f32[4096,1024]{1,0:T(8,128)}), f32[128,1024]{1,0:T(8,128)}) %reduce-scatter.21.cloned.1.call-update) | async-done | bytes 524304 | tf_op jit(solution)/shard_map/reduce_scatter | solution.py:168
  2807.8 42.0 %psum.7 = f32[]{:T(128)} all-reduce(f32[]{:T(128)S(6)} %add.574), channel_id=1, replica_groups=mesh['dp'=8,'seq'=4] {'dp','seq'}, use_global_device_ids=true, to_apply=%region_55.56 | all-reduce | flops 1 | bytes 8 | tf_op jit(solution)/shard_map/psum | solution.py:393
  (677 shorter events, 718.6 us)
Async XLA Ops:
  7.2 76.8 %all-gather.19.cloned.1.call-start = ((), (), s32[]{:S(2)}) async-start(), calls=%async_computation.24 | async-start | bytes 6488064 | tf_op jit(solution)/shard_map/all_gather | solution.py:228
  8.5 51.2 %copy-start.15 = (f32[1,512,1024]{2,1,0:T(8,128)S(1)}, f32[1,512,1024]{2,1,0:T(8,128)}, u32[]{:S(2)}) copy-start(f32[1,512,1024]{2,1,0:T(8,128)} %param.31) | copy-start | bytes 6291460
  9.3 135.9 %all-gather.29.cloned.1.call-start = ((), (), s32[]{:S(2)}) async-start(), calls=%async_computation.29 | async-start | bytes 2162688 | tf_op jit(solution)/shard_map/all_gather | solution.py:231
  11.0 274.8 %all-gather.21.cloned.1.call-start = ((), (), s32[]{:S(2)}) async-start(), calls=%async_computation.25 | async-start | bytes 2162688 | tf_op jit(solution)/shard_map/all_gather | solution.py:231
  11.8 278.6 %all-gather.23.cloned.1.call-start = ((), (), s32[]{:S(2)}) async-start(), calls=%async_computation.26 | async-start | bytes 8650752 | tf_op jit(solution)/shard_map/all_gather | solution.py:234
  14.0 353.1 %all-gather.25.cloned.1.call-start = ((), (), s32[]{:S(2)}) async-start(), calls=%async_computation.27 | async-start | bytes 8650752 | tf_op jit(solution)/shard_map/all_gather | solution.py:237
  14.9 423.7 %all-gather.27.cloned.1.call-start = ((), (), s32[]{:S(2)}) async-start(), calls=%async_computation.28 | async-start | bytes 6488064 | tf_op jit(solution)/shard_map/all_gather | solution.py:228
  59.7 32.6 %copy-start.61 = (f32[13312]{0:T(1024)}, f32[13312]{0:T(1024)S(1)}, u32[]{:S(2)}) copy-start(f32[13312]{0:T(1024)S(1)} %convert_element_type.337) | copy-start | bytes 159748
  60.1 43.8 %copy-start.53 = (f32[512,16]{0,1:T(8,128)}, f32[512,16]{0,1:T(8,128)S(1)}, u32[]{:S(2)}) copy-start(f32[512,16]{0,1:T(8,128)S(1)} %get-tuple-element.677) | copy-start | bytes 98308
  60.1 43.8 %copy-start.57 = (f32[512,16]{0,1:T(8,128)}, f32[512,16]{0,1:T(8,128)S(1)}, u32[]{:S(2)}) copy-start(f32[512,16]{0,1:T(8,128)S(1)} %get-tuple-element.678) | copy-start | bytes 98308
  60.1 32.2 %copy-start.68 = (f32[512]{0:T(512)}, f32[512]{0:T(512)S(1)}, u32[]{:S(2)}) copy-start(f32[512]{0:T(512)S(1)} %broadcast_multiply_fusion.2) | copy-start | bytes 6148
  61.0 31.3 %copy-start.94 = (f32[512]{0:T(512)}, f32[512]{0:T(512)S(1)}, u32[]{:S(2)}) copy-start(f32[512]{0:T(512)S(1)} %fusion.205) | copy-start | bytes 6148
  61.7 30.7 %copy-start.102 = (f32[1,1024]{1,0:T(1,128)}, f32[1,1024]{1,0:T(1,128)S(1)}, u32[]{:S(2)}) copy-start(f32[1,1024]{1,0:T(1,128)S(1)} %get-tuple-element.666) | copy-start | bytes 12292
  106.8 38.4 %copy-start.12 = (f32[1,512,1024]{2,1,0:T(8,128)S(1)}, f32[1,512,1024]{2,1,0:T(8,128)}, u32[]{:S(2)}) copy-start(f32[1,512,1024]{2,1,0:T(8,128)} %param.32) | copy-start | bytes 6291460
  106.8 45.5 %all-to-all-start = ((bf16[1,512,3,4,256]{1,4,2,0,3:T(8,128)(2,1)}), bf16[1,512,3,4,256]{1,4,2,0,3:T(8,128)(2,1)}, u32[]{:S(2)}, u32[]{:S(2)}) async-start(bf16[1,512,3,4,256]{1,4,2,0,3:T(8,128)(2,1)} %copy.134), calls=%async_computation | async-start | bytes 6291456 | tf_op jit(solution)/shard_map/all_to_all | solution.py:262
  111.7 423.4 %all-gather.31.cloned.1.call-start = ((), (), s32[]{:S(2)}) async-start(), calls=%async_computation.30 | async-start | bytes 8650752 | tf_op jit(solution)/shard_map/all_gather | solution.py:234
  152.4 108.4 %all-to-all-start.4 = ((bf16[1,512,4,256]{3,1,0,2:T(8,128)(2,1)}), bf16[1,512,4,256]{3,1,0,2:T(8,128)(2,1)}, u32[]{:S(2)}, u32[]{:S(2)}) async-start(bf16[1,512,4,256]{3,1,0,2:T(8,128)(2,1)} %copy.145), calls=%async_computation.4 | async-start | bytes 2097152 | tf_op jit(solution)/shard_map/all_to_all | solution.py:340
  260.8 21.2 all-to-all-start.1
  264.3 636.4 %all-gather.33.cloned.1.call-start = ((), (), s32[]{:S(2)}) async-start(), calls=%async_computation.31 | async-start | bytes 8650752 | tf_op jit(solution)/shard_map/all_gather | solution.py:237
  265.8 269.2 %copy-start.92 = (f32[1,4096]{1,0:T(1,128)}, f32[1,4096]{1,0:T(1,128)S(1)}, u32[]{:S(2)}) copy-start(f32[1,4096]{1,0:T(1,128)S(1)} %slice.475) | copy-start | bytes 49156
  268.8 169.8 %copy-start.85 = (f32[1,1024]{1,0:T(1,128)}, f32[1,1024]{1,0:T(1,128)S(1)}, u32[]{:S(2)}) copy-start(f32[1,1024]{1,0:T(1,128)S(1)} %get-tuple-element.661) | copy-start | bytes 12292
  268.8 169.8 %copy-start.108 = (f32[1,1024]{1,0:T(1,128)}, f32[1,1024]{1,0:T(1,128)S(1)}, u32[]{:S(2)}) copy-start(f32[1,1024]{1,0:T(1,128)S(1)} %get-tuple-element.660) | copy-start | bytes 12292
  268.8 266.3 %copy-start.82 = (f32[1,1024]{1,0:T(1,128)}, f32[1,1024]{1,0:T(1,128)S(1)}, u32[]{:S(2)}) copy-start(f32[1,1024]{1,0:T(1,128)S(1)} %get-tuple-element.659) | copy-start | bytes 12292
  268.8 266.3 %copy-start.106 = (f32[1,1024]{1,0:T(1,128)}, f32[1,1024]{1,0:T(1,128)S(1)}, u32[]{:S(2)}) copy-start(f32[1,1024]{1,0:T(1,128)S(1)} %get-tuple-element.658) | copy-start | bytes 12292
  285.8 32.4 %copy-start.28 = (bf16[1,512,4,1,256]{1,4,2,3,0:T(8,128)(2,1)}, bf16[1,512,4,1,256]{1,4,2,3,0:T(8,128)(2,1)S(1)}, u32[]{:S(2)}) copy-start(bf16[1,512,4,1,256]{1,4,2,3,0:T(8,128)(2,1)S(1)} %copy.138) | copy-start | bytes 3145732
  290.4 76.7 %copy-start.110 = (f32[1,1024]{1,0:T(1,128)S(1)}, f32[1,1024]{1,0:T(1,128)}, u32[]{:S(2)}) copy-start(f32[1,1024]{1,0:T(1,128)} %get-tuple-element.663) | copy-start | bytes 12292
  290.4 76.7 %copy-start.111 = (f32[1,1024]{1,0:T(1,128)S(1)}, f32[1,1024]{1,0:T(1,128)}, u32[]{:S(2)}) copy-start(f32[1,1024]{1,0:T(1,128)} %get-tuple-element.668) | copy-start | bytes 12292
  376.9 158.1 %copy-start.71 = (f32[512]{0:T(512)}, f32[512]{0:T(512)S(1)}, u32[]{:S(2)}) copy-start(f32[512]{0:T(512)S(1)} %broadcast_multiply_fusion.1) | copy-start | bytes 6148
  379.2 155.9 %copy-start.97 = (f32[512]{0:T(512)}, f32[512]{0:T(512)S(1)}, u32[]{:S(2)}) copy-start(f32[512]{0:T(512)S(1)} %fusion.206) | copy-start | bytes 6148
  463.3 99.8 %all-to-all-start.2 = ((bf16[1,512,3,4,256]{1,4,2,0,3:T(8,128)(2,1)}), bf16[1,512,3,4,256]{1,4,2,0,3:T(8,128)(2,1)S(1)}, u32[]{:S(2)}, u32[]{:S(2)}) async-start(bf16[1,512,3,4,256]{1,4,2,0,3:T(8,128)(2,1)} %copy.140), calls=%async_computation.2 | async-start | bytes 6291456 | tf_op jit(solution)/shard_map/all_to_all | solution.py:262
  664.8 230.9 %all-to-all-start.3 = ((bf16[4,2,65536]{2,1,0:T(2,128)(2,1)}), bf16[4,2,65536]{2,1,0:T(2,128)(2,1)}, u32[]{:S(2)}, u32[]{:S(2)}) async-start(bf16[4,2,65536]{2,1,0:T(2,128)(2,1)} %reshape.952), calls=%async_computation.3 | async-start | bytes 2097152 | tf_op jit(solution)/shard_map/all_to_all | solution.py:265
  895.7 53.2 %all-to-all-start.5 = ((bf16[1,2048,3,1,256]{4,2,3,0,1:T(4,128)(2,1)}), bf16[1,2048,3,1,256]{4,2,3,0,1:T(4,128)(2,1)}, u32[]{:S(2)}, u32[]{:S(2)}) async-start(bf16[1,2048,3,1,256]{4,2,3,0,1:T(4,128)(2,1)} %copy.148), calls=%async_computation.5 | async-start | bytes 8388608 | tf_op jit(solution)/shard_map/all_to_all | solution.py:349
  991.0 18.0 all-to-all-start.6
  1242.7 53.2 %all-to-all-start.7 = ((bf16[1,2048,3,1,256]{4,2,3,0,1:T(4,128)(2,1)}), bf16[1,2048,3,1,256]{4,2,3,0,1:T(4,128)(2,1)}, u32[]{:S(2)}, u32[]{:S(2)}) async-start(bf16[1,2048,3,1,256]{4,2,3,0,1:T(4,128)(2,1)} %copy.154), calls=%async_computation.7 | async-start | bytes 8388608 | tf_op jit(solution)/shard_map/all_to_all | solution.py:349
  1247.7 205.5 %all-reduce.8.cloned.1.call-start = ((), (), s32[]{:S(2)}) async-start(), calls=%async_computation.32 | async-start | bytes 212992
  1333.9 263.6 %reduce-scatter.15.cloned.1.call-start = ((), (), s32[]{:S(2)}) async-start(), calls=%async_computation.19 | async-start | bytes 4325376 | tf_op jit(solution)/shard_map/reduce_scatter | solution.py:166
  1337.2 399.5 %reduce-scatter.13.cloned.1.call-start = ((), (), s32[]{:S(2)}) async-start(), calls=%async_computation.18 | async-start | bytes 4325376 | tf_op jit(solution)/shard_map/reduce_scatter | solution.py:166
  1342.1 552.1 %reduce-scatter.11.cloned.1.call-start = ((), (), s32[]{:S(2)}) async-start(), calls=%async_computation.17 | async-start | bytes 12976128 | tf_op jit(solution)/shard_map/reduce_scatter | solution.py:165
  1353.9 701.9 %reduce-scatter.9.cloned.1.call-start = ((), (), s32[]{:S(2)}) async-start(), calls=%async_computation.16 | async-start | bytes 12976128 | tf_op jit(solution)/shard_map/reduce_scatter | solution.py:165
  1365.5 874.6 %reduce-scatter.19.cloned.1.call-start = ((), (), s32[]{:S(2)}) async-start(), calls=%async_computation.21 | async-start | bytes 17301504 | tf_op jit(solution)/shard_map/reduce_scatter | solution.py:167
  1379.5 1047.3 %reduce-scatter.17.cloned.1.call-start = ((), (), s32[]{:S(2)}) async-start(), calls=%async_computation.20 | async-start | bytes 17301504 | tf_op jit(solution)/shard_map/reduce_scatter | solution.py:167
  1393.6 1220.0 %reduce-scatter.23.cloned.1.call-start = ((), (), s32[]{:S(2)}) async-start(), calls=%async_computation.23 | async-start | bytes 17301504 | tf_op jit(solution)/shard_map/reduce_scatter | solution.py:168
  1404.0 1396.3 %reduce-scatter.21.cloned.1.call-start = ((), (), s32[]{:S(2)}) async-start(), calls=%async_computation.22 | async-start | bytes 17301504 | tf_op jit(solution)/shard_map/reduce_scatter | solution.py:168
  1432.3 1371.4 %copy-start.20 = (f32[512,1024]{1,0:T(8,128)S(1)}, f32[512,1024]{1,0:T(8,128)}, u32[]{:S(2)}) copy-start(f32[512,1024]{1,0:T(8,128)} %copy-done.19) | copy-start | bytes 6291460
  2803.7 46.8 %copy-start.89 = (f32[2,416]{1,0:T(2,128)S(1)}, f32[2,416]{1,0:T(2,128)}, u32[]{:S(2)}) copy-start(f32[2,416]{1,0:T(2,128)} %param.50) | copy-start | bytes 9988
  2803.7 48.1 %copy-start.52 = (f32[2,32,1024]{2,1,0:T(8,128)S(1)}, f32[2,32,1024]{2,1,0:T(8,128)}, u32[]{:S(2)}) copy-start(f32[2,32,1024]{2,1,0:T(8,128)} %param.38) | copy-start | bytes 786436
  2803.7 50.7 %copy-start.31 = (f32[2,32,3072]{2,1,0:T(8,128)S(1)}, f32[2,32,3072]{2,1,0:T(8,128)}, u32[]{:S(2)}) copy-start(f32[2,32,3072]{2,1,0:T(8,128)} %param.34) | copy-start | bytes 2359300
  2803.7 50.7 %copy-start.42 = (f32[32,3072]{1,0:T(8,128)S(1)}, f32[32,3072]{1,0:T(8,128)}, u32[]{:S(2)}) copy-start(f32[32,3072]{1,0:T(8,128)} %reduce-scatter.11.cloned.1.call-done) | copy-start | bytes 1179652
  (125 other events, 667.7 us)
Sparse Core Ops, SparseCore 0:
  11.5 72.4 all-gather.18
  87.5 57.7 all-gather.28
  148.7 55.2 all-gather.20
  207.3 79.6 all-gather.22
  290.3 76.7 all-gather.24
  370.4 68.1 all-gather.26
  442.1 92.9 all-gather.30
  538.5 75.6 all-gather.32
  1334.0 119.1 all-reduce.7
  1455.3 142.1 reduce-scatter.14
  1599.8 136.8 reduce-scatter.12
  1742.6 151.5 reduce-scatter.10
  1901.3 154.4 reduce-scatter.8
  2057.9 182.0 reduce-scatter.18
  2242.2 184.5 reduce-scatter.16
  2429.0 184.5 reduce-scatter.22
  2615.7 184.5 reduce-scatter.20
where the time goes:
time: 2880 us; the launch traced here: 2870 us
  waiting for transfers between devices  1680 us (58%)
  matrix products  537 us (19%)
  local copies, waits for them, and re-layouts  245 us (9%)
  other arithmetic  226 us (8%)
  blocking collectives  85.5 us (3%)
  loops' own time  44 us (2%)
  starting transfers between devices  35.8 us (1%)
    reduce_scatter x2, waiting for transfers between devices, reduce_grads(): lax.psum_scatter(shrink_grad, ('dp', 'seq'), scatter_dimension=0, tiled=T...  371 us
    reduce_scatter x2, waiting for transfers between devices, reduce_grads(): lax.psum_scatter(expand_grad, ('dp', 'seq'), scatter_dimension=0, tiled=T...  368 us
    reduce_scatter x2, waiting for transfers between devices, reduce_grads(): lax.psum_scatter(mixing_grad, ('dp', 'seq'), scatter_dimension=0, tiled=T...  317 us
    reduce_scatter x2, waiting for transfers between devices, reduce_grads(): lax.psum_scatter(output_grad, ('dp', 'seq'), scatter_dimension=0, tiled=T...  281 us
    dot_general x8, matrix products, one_block(): jnp.einsum('qhd,khd->hqk', grad_block, sequence[:, 2], preferred_element_...  96.5 us
    convert_element_type x8, other arithmetic, one_block(): score_grad = (softmax_out * (prob_grad - inner_sum)).astype(jnp.bfloat16)  95.7 us
    all_gather x2, waiting for transfers between devices, local(): lax.all_gather(mixing_weight[layer_index].astype(jnp.bfloat16), ('dp', 's...  81.8 us
    all_gather x2, waiting for transfers between devices, local(): lax.all_gather(expand_weight[layer_index].astype(jnp.bfloat16), ('dp', 's...  67.9 us
  transfers between devices with their start and end apart: 25, of which 19 were waited for; matrix products, arithmetic and copies ran while one was open for 23% of the time, Pallas kernels for 0%

commit v1 on v0

v1 whole, which is shorter than its diff:
```python
from functools import partial
import math

import jax
import jax.numpy as jnp
from jax import lax
from jax.experimental import pallas as pl
from jax.experimental.pallas import tpu as pltpu
from jax.sharding import PartitionSpec as P

D = 1024
H = 16
HD = 64
ROT = 16
FF = 4096
LEN = 2048
LAYERS = 2
STEP = 3

NORM_EPS = 1e-05
CLIP_LIMIT = 1.0
BETA_FIRST = 0.5
BETA_SECOND = 0.5
ADAM_EPS = 1e-08
WEIGHT_DECAY = 0.01
EMA_DECAY = 0.999
SMALL_RATE = 0.1
MASK_VALUE = -1e30
ROWS = 256
BLOCK = 512
QUERY_SCALE = 1.0 / math.sqrt(HD)
BF = jnp.bfloat16
F32 = jnp.float32
VMEM_LIMIT = 48 * 1024 * 1024


def dp_parts():
    size = lax.axis_size("dp")
    outer = 4 if size % 4 == 0 else size
    return outer, size // outer


def outer_ring(value):
    outer, inner = dp_parts()
    size = outer * inner
    return lax.ppermute(value, "dp", [(i, (i + inner) % size) for i in range(size)])


def inner_ring(value):
    outer, inner = dp_parts()
    moves = [
        (a * inner + b, a * inner + (b + 1) % inner) for a in range(outer) for b in range(inner)
    ]
    return lax.ppermute(value, "dp", moves)


def chip_ring(value):
    size = lax.axis_size("seq")
    return lax.ppermute(value, "seq", [(i, (i + 2) % size) for i in range(size)])


def core_swap(value):
    size = lax.axis_size("seq")
    return lax.ppermute(value, "seq", [(i, i ^ 1) for i in range(size)])


def put(total, piece, first, second):
    start = (first, second) + (0,) * (total.ndim - 2)
    return lax.dynamic_update_slice(total, piece[None, None], start)


def pick(total, first, second):
    sizes = (1, 1) + total.shape[2:]
    start = (first, second) + (0,) * (total.ndim - 2)
    return lax.dynamic_slice(total, start, sizes)[0, 0]


def dp_gather(value):
    outer, inner = dp_parts()
    me = lax.axis_index("dp")
    a, b = me // inner, me % inner
    total = jnp.zeros((outer, inner) + value.shape, value.dtype)
    piece = value
    for step in range(outer):
        passing = piece
        for turn in range(inner):
            total = put(total, passing, (a - step) % outer, (b - turn) % inner)
            if turn < inner - 1:
                passing = inner_ring(passing)
        if step < outer - 1:
            piece = outer_ring(piece)
    return total.reshape((outer * inner * value.shape[0],) + value.shape[1:])


def dp_scatter(value):
    outer, inner = dp_parts()
    me = lax.axis_index("dp")
    a, b = me // inner, me % inner
    rows = value.shape[0] // (outer * inner)
    value = value.reshape((outer, inner, rows) + value.shape[1:])

    def inner_sum(at):
        arrived = None
        for turn in range(1, inner):
            own = pick(value, at, (b - turn) % inner)
            if arrived is not None:
                own = (own.astype(F32) + arrived.astype(F32)).astype(BF)
            arrived = inner_ring(own)
        own = pick(value, at, b).astype(F32)
        return own if arrived is None else own + arrived.astype(F32)

    arrived = None
    for step in range(1, outer):
        part = inner_sum((a - step) % outer)
        if arrived is not None:
            part = part + arrived.astype(F32)
        arrived = outer_ring(part.astype(BF))
    part = inner_sum(a)
    return part if arrived is None else part + arrived.astype(F32)


def seq_gather(value):
    chips = lax.axis_size("seq") // 2
    me = lax.axis_index("seq")
    y, c = me // 2, me % 2
    total = jnp.zeros((chips, 2) + value.shape, value.dtype)
    piece = value
    for step in range(chips):
        at = (y - step) % chips
        total = put(total, piece, at, c)
        total = put(total, core_swap(piece), at, 1 - c)
        if step < chips - 1:
            piece = chip_ring(piece)
    return total.reshape((chips * 2 * value.shape[0],) + value.shape[1:])


def seq_scatter(value):
    chips = lax.axis_size("seq") // 2
    me = lax.axis_index("seq")
    y, c = me // 2, me % 2
    rows = value.shape[0] // (2 * chips)
    value = value.reshape((chips, 2, rows) + value.shape[1:])

    def core_sum(at):
        arrived = core_swap(pick(value, at, 1 - c))
        return pick(value, at, c).astype(F32) + arrived.astype(F32)

    arrived = None
    for step in range(1, chips):
        part = core_sum((y - step) % chips)
        if arrived is not None:
            part = part + arrived.astype(F32)
        arrived = chip_ring(part.astype(BF))
    part = core_sum(y)
    return part if arrived is None else part + arrived.astype(F32)


def seq_exchange(value):
    return lax.all_to_all(value, "seq", split_axis=0, concat_axis=0, tiled=True)


def head_masks(width, dtype):
    lane = lax.broadcasted_iota(jnp.int32, (1, width), 1) // HD
    return [(lane == h).astype(F32).astype(dtype) for h in range(width // HD)]


def swap_halves(values):
    width = values.shape[1]
    lane = lax.broadcasted_iota(jnp.int32, values.shape, 1) % HD
    return jnp.where(
        lane < ROT // 2,
        pltpu.roll(values, width - ROT // 2, 1),
        pltpu.roll(values, ROT // 2, 1),
    )


def widen(table, width):
    return jnp.concatenate([table] * (width // 128), axis=1) if width > 128 else table


def matmul(left, right):
    return lax.dot_general(left, right, (((1,), (0,)), ((), ())), preferred_element_type=F32)


def matmul_nt(left, right):
    return lax.dot_general(left, right, (((1,), (1,)), ((), ())), preferred_element_type=F32)


def matmul_tn(left, right):
    return lax.dot_general(left, right, (((0,), (0,)), ((), ())), preferred_element_type=F32)


def mix_kernel(x_ref, w_ref, c_ref, cos_ref, sin_ref, out_ref):
    width = w_ref.shape[1] // 3
    mixed = matmul(x_ref[...], w_ref[...]) + c_ref[...]
    cosine = widen(cos_ref[...], width)
    sine = widen(sin_ref[...], width)
    query = mixed[:, :width]
    key = mixed[:, width : 2 * width]
    query = (query * cosine + swap_halves(query) * sine) * QUERY_SCALE
    key = key * cosine + swap_halves(key) * sine
    out_ref[:, :width] = query.astype(BF)
    out_ref[:, width : 2 * width] = key.astype(BF)
    out_ref[:, 2 * width :] = mixed[:, 2 * width :].astype(BF)


def mix(x, weight, shift, cosine, sine):
    length, columns = x.shape[0], weight.shape[1]
    return pl.pallas_call(
        mix_kernel,
        grid=(length // ROWS,),
        in_specs=[
            pl.BlockSpec((ROWS, D), lambda i: (i, 0)),
            pl.BlockSpec((D, columns), lambda i: (0, 0)),
            pl.BlockSpec((1, columns), lambda i: (0, 0)),
            pl.BlockSpec((ROWS, 128), lambda i: (i, 0)),
            pl.BlockSpec((ROWS, 128), lambda i: (i, 0)),
        ],
        out_specs=pl.BlockSpec((ROWS, columns), lambda i: (i, 0)),
        out_shape=jax.ShapeDtypeStruct((length, columns), BF),
        compiler_params=pltpu.CompilerParams(vmem_limit_bytes=VMEM_LIMIT),
        cost_estimate=pl.CostEstimate(
            flops=2 * length * D * columns,
            bytes_accessed=2 * (length * D + D * columns + length * columns),
            transcendentals=0,
        ),
        name="mix",
    )(x, weight, shift, cosine, sine)


def attend_kernel(q_ref, k_ref, v_ref, o_ref, lse_ref, acc_ref, high_ref, sum_ref):
    block, width = q_ref.shape
    heads = width // HD
    i = pl.program_id(0)
    masks = head_masks(width, BF)
    query = q_ref[...]
    queries = [query * mask for mask in masks]
    acc_ref[...] = jnp.zeros(acc_ref.shape, F32)
    sum_ref[...] = jnp.zeros(sum_ref.shape, F32)
    high_ref[...] = jnp.full(high_ref.shape, MASK_VALUE, F32)

    def tile(j, diagonal):
        rows = pl.ds(pl.multiple_of(j * block, block), block)
        key = k_ref[rows, :]
        value = v_ref[rows, :]
        for h in range(heads):
            scores = matmul_nt(queries[h], key)
            if diagonal:
                row = lax.broadcasted_iota(jnp.int32, scores.shape, 0)
                column = lax.broadcasted_iota(jnp.int32, scores.shape, 1)
                scores = jnp.where(column <= row, scores, MASK_VALUE)
            old = high_ref[h]
            new = jnp.maximum(old, jnp.max(scores, 1, keepdims=True))
            weights = jnp.exp(scores - new[:, :1])
            shrink = jnp.exp(old - new)
            sum_ref[h] = sum_ref[h] * shrink + jnp.sum(weights, 1, keepdims=True)
            acc_ref[h] = acc_ref[h] * shrink[:, :1] + matmul(weights.astype(BF), value)
            high_ref[h] = new

    def step(j, carry):
        tile(j, False)
        return carry

    lax.fori_loop(0, i, step, 0)
    tile(i, True)
    lane = lax.broadcasted_iota(jnp.int32, (block, width), 1) // HD
    small_lane = lax.broadcasted_iota(jnp.int32, (block, 128), 1)
    total = jnp.zeros((block, width), F32)
    log_total = jnp.zeros((block, 128), F32)
    for h in range(heads):
        total = jnp.where(lane == h, acc_ref[h] / sum_ref[h][:, :1], total)
        log_total = jnp.where(small_lane == h, high_ref[h] + jnp.log(sum_ref[h]), log_total)
    o_ref[...] = total.astype(BF)
    lse_ref[...] = log_total


def attend(mixed):
    length, width = mixed.shape[0], mixed.shape[1] // 3
    heads = width // HD
    block = min(BLOCK, length)
    flops = 2 * length * length * width * 2
    return pl.pallas_call(
        attend_kernel,
        grid=(length // block,),
        in_specs=[
            pl.BlockSpec((block, width), lambda i: (i, 0)),
            pl.BlockSpec((length, width), lambda i: (0, 1)),
            pl.BlockSpec((length, width), lambda i: (0, 2)),
        ],
        out_specs=[
            pl.BlockSpec((block, width), lambda i: (i, 0)),
            pl.BlockSpec((block, 128), lambda i: (i, 0)),
        ],
        out_shape=[
            jax.ShapeDtypeStruct((length, width), BF),
            jax.ShapeDtypeStruct((length, 128), F32),
        ],
        scratch_shapes=[
            pltpu.VMEM((heads, block, width), F32),
            pltpu.VMEM((heads, block, 128), F32),
            pltpu.VMEM((heads, block, 128), F32),
        ],
        compiler_params=pltpu.CompilerParams(vmem_limit_bytes=VMEM_LIMIT),
        cost_estimate=pl.CostEstimate(
            flops=flops, bytes_accessed=8 * length * width, transcendentals=length * length * heads
        ),
        name="attend",
    )(mixed, mixed, mixed)


def attend_back_kernel(
    q_ref,
    k_ref,
    v_ref,
    do_ref,
    lse_ref,
    inner_ref,
    cos_ref,
    sin_ref,
    out_ref,
    total_ref,
    dq_ref,
    dk_ref,
    dv_ref,
):
    block, width = k_ref.shape
    length = q_ref.shape[0]
    heads = width // HD
    steps = length // block
    j = pl.program_id(0)
    masks = head_masks(width, BF)
    key = k_ref[...]
    value = v_ref[...]
    keys = [key * mask for mask in masks]

    @pl.when(j == 0)
    def _():
        dq_ref[...] = jnp.zeros(dq_ref.shape, F32)
        total_ref[...] = jnp.zeros(total_ref.shape, F32)

    dk_ref[...] = jnp.zeros(dk_ref.shape, F32)
    dv_ref[...] = jnp.zeros(dv_ref.shape, F32)

    def tile(i, diagonal):
        rows = pl.ds(pl.multiple_of(i * block, block), block)
        query = q_ref[rows, :]
        grad = do_ref[rows, :]
        log_total = lse_ref[:, rows]
        inner = inner_ref[:, rows]
        for h in range(heads):
            query_head = query * masks[h]
            grad_head = grad * masks[h]
            scores = matmul_nt(key, query_head) - log_total[h : h + 1, :]
            if diagonal:
                row = lax.broadcasted_iota(jnp.int32, scores.shape, 0)
                column = lax.broadcasted_iota(jnp.int32, scores.shape, 1)
                scores = jnp.where(row <= column, scores, MASK_VALUE)
            weights = jnp.exp(scores)
            dv_ref[...] += matmul(weights.astype(BF), grad_head)
            weight_grad = matmul_nt(value, grad_head)
            score_grad = (weights * (weight_grad - inner[h : h + 1, :])).astype(BF)
            dk_ref[...] += matmul(score_grad, query_head)
            dq_ref[rows, :] += matmul_tn(score_grad, keys[h])

    def step(i, carry):
        tile(i, False)
        return carry

    tile(j, True)
    lax.fori_loop(j + 1, steps, step, 0)

    own = pl.ds(pl.multiple_of(j * block, block), block)
    key_grad = dk_ref[...]
    cosine = widen(cos_ref[own, :], width)
    sine = widen(sin_ref[own, :], width)
    key_grad = key_grad * cosine - swap_halves(key_grad) * sine
    value_grad = dv_ref[...]
    out_ref[own, width : 2 * width] = key_grad.astype(BF)
    out_ref[own, 2 * width :] = value_grad.astype(BF)
    total_ref[:, width : 2 * width] += jnp.sum(key_grad, 0, keepdims=True)
    total_ref[:, 2 * width :] += jnp.sum(value_grad, 0, keepdims=True)
    query_grad = dq_ref[own, :] * QUERY_SCALE
    query_grad = query_grad * cosine - swap_halves(query_grad) * sine
    out_ref[own, :width] = query_grad.astype(BF)
    total_ref[:, :width] += jnp.sum(query_grad, 0, keepdims=True)


def attend_back(mixed, grads, log_total, inner, cosine, sine):
    length, width = mixed.shape[0], mixed.shape[1] // 3
    heads = width // HD
    block = min(BLOCK, length)
    flops = 2 * length * length * width * 5
    return pl.pallas_call(
        attend_back_kernel,
        grid=(length // block,),
        in_specs=[
            pl.BlockSpec((length, width), lambda j: (0, 0)),
            pl.BlockSpec((block, width), lambda j: (j, 1)),
            pl.BlockSpec((block, width), lambda j: (j, 2)),
            pl.BlockSpec((length, width), lambda j: (0, 0)),
            pl.BlockSpec((heads, length), lambda j: (0, 0)),
            pl.BlockSpec((heads, length), lambda j: (0, 0)),
            pl.BlockSpec((length, 128), lambda j: (0, 0)),
            pl.BlockSpec((length, 128), lambda j: (0, 0)),
        ],
        out_specs=[
            pl.BlockSpec((length, 3 * width), lambda j: (0, 0)),
            pl.BlockSpec((1, 3 * width), lambda j: (0, 0)),
        ],
        out_shape=[
            jax.ShapeDtypeStruct((length, 3 * width), BF),
            jax.ShapeDtypeStruct((1, 3 * width), F32),
        ],
        scratch_shapes=[
            pltpu.VMEM((length, width), F32),
            pltpu.VMEM((block, width), F32),
            pltpu.VMEM((block, width), F32),
        ],
        compiler_params=pltpu.CompilerParams(vmem_limit_bytes=VMEM_LIMIT),
        cost_estimate=pl.CostEstimate(
            flops=flops, bytes_accessed=16 * length * width, transcendentals=length * length * heads
        ),
        name="attend_back",
    )(mixed, mixed, mixed, grads, log_total, inner, cosine, sine)


def gelu_pair(values):
    size = jnp.abs(values) * (1.0 / math.sqrt(2.0))
    bell = jnp.exp(-size * size)
    turn = 1.0 / (1.0 + 0.3275911 * size)
    series = turn * (
        0.254829592
        + turn * (-0.284496736 + turn * (1.421413741 + turn * (-1.453152027 + turn * 1.061405429)))
    )
    tail = 0.5 * series * bell
    below = jnp.where(values < 0.0, tail, 1.0 - tail)
    slope = below + values * bell * (1.0 / math.sqrt(2.0 * math.pi))
    return values * below, slope


def feed_kernel(x_ref, wi_ref, ci_ref, wd_ref, o_ref, wo_ref, act_ref, slope_ref, out_ref):
    hidden = matmul(x_ref[...], wi_ref[...]) + ci_ref[...]
    activated, slope = gelu_pair(hidden)
    activated = activated.astype(BF)
    act_ref[...] = activated
    slope_ref[...] = slope.astype(BF)
    out = matmul(activated, wd_ref[...]) + matmul(o_ref[...], wo_ref[...])
    out_ref[...] = out.astype(BF)


def feed(x, expand, shift, shrink, attended, output):
    length, units, width = x.shape[0], expand.shape[1], attended.shape[1]
    return pl.pallas_call(
        feed_kernel,
        grid=(length // ROWS,),
        in_specs=[
            pl.BlockSpec((ROWS, D), lambda i: (i, 0)),
            pl.BlockSpec((D, units), lambda i: (0, 0)),
            pl.BlockSpec((1, units), lambda i: (0, 0)),
            pl.BlockSpec((units, D), lambda i: (0, 0)),
            pl.BlockSpec((ROWS, width), lambda i: (i, 0)),
            pl.BlockSpec((width, D), lambda i: (0, 0)),
        ],
        out_specs=[
            pl.BlockSpec((ROWS, units), lambda i: (i, 0)),
            pl.BlockSpec((ROWS, units), lambda i: (i, 0)),
            pl.BlockSpec((ROWS, D), lambda i: (i, 0)),
        ],
        out_shape=[
            jax.ShapeDtypeStruct((length, units), BF),
            jax.ShapeDtypeStruct((length, units), BF),
            jax.ShapeDtypeStruct((length, D), BF),
        ],
        compiler_params=pltpu.CompilerParams(vmem_limit_bytes=VMEM_LIMIT),
        cost_estimate=pl.CostEstimate(
            flops=2 * length * D * (2 * units + width),
            bytes_accessed=2 * (2 * D * units + 2 * length * D + 2 * length * units),
            transcendentals=length * units,
        ),
        name="feed",
    )(x, expand, shift, shrink, attended, output)


def rotary_tables(positions):
    steps_half = jnp.arange(ROT // 2).astype(F32)
    frequency = 10000.0 ** (-2.0 * steps_half / ROT)
    angles = positions.astype(F32)[:, None] * frequency
    cosine, sine = jnp.cos(angles), jnp.sin(angles)
    rest = jnp.zeros((positions.shape[0], HD - ROT), F32)
    cosine = jnp.concatenate([cosine, cosine, rest + 1.0] * 2, -1)
    sine = jnp.concatenate([-sine, sine, rest] * 2, -1)
    return cosine, sine


def split_affine(affine):
    bounds = [D, D, D, D, 3 * D, D, FF, D]
    pieces = []
    offset = 0
    for length in bounds:
        pieces.append(affine[offset : offset + length])
        offset = offset + length
    return pieces


def adamw_update(
    weight, first_moment, second, average, gradient, clip_scale, step_rate, decay_rate
):
    clipped = gradient * clip_scale
    first_new = BETA_FIRST * first_moment + (1.0 - BETA_FIRST) * clipped
    second_new = BETA_SECOND * second + (1.0 - BETA_SECOND) * clipped * clipped
    first_hat = first_new / (1.0 - BETA_FIRST**STEP)
    second_hat = second_new / (1.0 - BETA_SECOND**STEP)
    weight_new = weight - step_rate * (
        first_hat / (jnp.sqrt(second_hat) + ADAM_EPS) + decay_rate * weight
    )
    average_new = EMA_DECAY * average + (1.0 - EMA_DECAY) * weight_new
    return (weight_new, first_new, second_new, average_new)


def normalize(values):
    centre = values - jnp.mean(values, -1, keepdims=True)
    spread = jnp.mean(centre * centre, -1, keepdims=True)
    scale = lax.rsqrt(spread + NORM_EPS)
    return centre * scale, scale


def local(
    stream,
    cotangent,
    positions,
    mixing_weight,
    mixing_first,
    mixing_second,
    mixing_average,
    output_weight,
    output_first,
    output_second,
    output_average,
    expand_weight,
    expand_first,
    expand_second,
    expand_average,
    shrink_weight,
    shrink_first,
    shrink_second,
    shrink_average,
    affine_weight,
    affine_first,
    affine_second,
    affine_average,
):
    parts = lax.axis_size("seq")
    copies = lax.axis_size("dp")
    devices = parts * copies
    part = lax.axis_index("seq")
    width = D // parts
    units = FF // parts
    rows_d = D // devices
    rows_f = FF // devices
    rows = stream.shape[0] * stream.shape[1]
    small = affine_weight.shape[1]

    def part_of(vector, before):
        view = vector.reshape(before, parts, -1)
        return lax.dynamic_index_in_dim(view, part, 1, keepdims=False).reshape(-1)

    def spread_part(vector, before):
        view = jnp.zeros((before, parts, vector.shape[0] // before), F32)
        view = lax.dynamic_update_slice(view, vector.reshape(before, 1, -1), (0, part, 0))
        return view.reshape(-1)

    affine_low = affine_weight.astype(BF).reshape(1, LAYERS * small)
    affine_all = lax.all_to_all(
        jnp.broadcast_to(affine_low, (devices, LAYERS * small)),
        ("dp", "seq"),
        split_axis=0,
        concat_axis=0,
        tiled=True,
    )
    affine_all = affine_all.reshape(devices, LAYERS, small).transpose(1, 0, 2)
    affine_all = affine_all.reshape(LAYERS, devices * small).astype(F32)

    current = stream.reshape(rows, D)
    lane_positions = positions.reshape(rows // 128, 128)
    cosine, sine = rotary_tables(seq_gather(lane_positions).reshape(-1))
    gradient = cotangent.reshape(rows, D)

    def weights_of(layer):
        mixing = mixing_weight[layer].astype(BF).reshape(rows_d, 3, parts, width)
        mixing = mixing.transpose(2, 0, 1, 3).reshape(parts, rows_d, 3 * width)
        expand = expand_weight[layer].astype(BF).reshape(rows_d, copies, parts, rows_f)
        expand = expand.transpose(2, 0, 1, 3).reshape(parts, rows_d, units)
        both = seq_exchange(jnp.concatenate([mixing, expand], -1))
        both = both.reshape(parts * rows_d, 3 * width + units)
        mixing = dp_gather(both[:, : 3 * width])
        output = dp_gather(output_weight[layer].astype(BF))
        expand = dp_gather(both[:, 3 * width :])
        shrink = dp_gather(shrink_weight[layer].astype(BF))
        output = seq_exchange(output.reshape(parts, -1, D)).reshape(
            parts, copies // parts, rows_d, D
        )
        output = output.transpose(1, 0, 2, 3).reshape(width, D)
        return mixing, output, expand, shrink

    stored = []
    for layer in range(LAYERS):
        mixing, output, expand, shrink = weights_of(layer)
        (
            gain_one,
            shift_one,
            gain_two,
            shift_two,
            mixing_bias,
            output_bias,
            expand_bias,
            shrink_bias,
        ) = split_affine(affine_all[layer])
        mixing_scaled = (mixing.astype(F32) * gain_one[:, None]).astype(BF)
        expand_scaled = (expand.astype(F32) * gain_two[:, None]).astype(BF)
        mixing_shift = jnp.sum(mixing.astype(F32) * shift_one[:, None], 0)
        mixing_shift = mixing_shift + part_of(mixing_bias, 3)
        expand_shift = jnp.sum(expand.astype(F32) * shift_two[:, None], 0)
        expand_shift = expand_shift + part_of(expand_bias, copies)
        own_normed, scale = normalize(current)
        normed = seq_gather(own_normed.astype(BF))
        mixed = mix(normed, mixing_scaled, mixing_shift[None], cosine, sine)
        attended, log_total = attend(mixed)
        activated, slope, branch = feed(
            normed, expand_scaled, expand_shift[None], shrink, attended, output
        )
        stored.append(
            (
                own_normed,
                scale,
                normed,
                mixed,
                attended,
                log_total,
                activated,
                slope,
                mixing,
                mixing_scaled,
                output,
                expand,
                expand_scaled,
                shrink,
                (gain_one, shift_one, gain_two, shift_two),
            )
        )
        current = current + seq_scatter(branch) + output_bias + shrink_bias
    result = current.reshape(stream.shape)

    reduced = [None] * LAYERS
    for layer in reversed(range(LAYERS)):
        (
            own_normed,
            scale,
            normed,
            mixed,
            attended,
            log_total,
            activated,
            slope,
            mixing,
            mixing_scaled,
            output,
            expand,
            expand_scaled,
            shrink,
            (gain_one, shift_one, gain_two, shift_two),
        ) = stored[layer]
        heads = width // HD
        grads = seq_gather(gradient.astype(BF))
        attended_grad = matmul_nt(grads, output).astype(BF)
        hidden_grad = matmul_nt(grads, shrink) * slope.astype(F32)
        hidden_total = jnp.sum(hidden_grad, 0)
        hidden_low = hidden_grad.astype(BF)
        shrink_grad = dp_scatter(matmul_tn(activated, grads).astype(BF))
        output_grad = matmul_tn(attended, grads).astype(BF)
        output_grad = output_grad.reshape(copies // parts, parts, rows_d, D).transpose(1, 0, 2, 3)
        output_grad = seq_exchange(output_grad.reshape(parts, copies // parts * rows_d, D))
        output_grad = dp_scatter(output_grad.reshape(copies * rows_d, D))
        inner = attended_grad.astype(F32) * attended.astype(F32)
        inner = jnp.sum(inner.reshape(-1, heads, HD), -1).T
        mixed_low, mixed_total = attend_back(
            mixed, attended_grad, log_total[:, :heads].T, inner, cosine, sine
        )
        mixed_total = mixed_total[0]
        normed_grad = matmul_nt(hidden_low, expand_scaled) + matmul_nt(mixed_low, mixing_scaled)
        normed_grad = seq_scatter(normed_grad.astype(BF))
        expand_raw = matmul_tn(normed, hidden_low)
        mixing_raw = matmul_tn(normed, mixed_low)
        expand_grad = expand_raw * gain_two[:, None] + shift_two[:, None] * hidden_total
        mixing_grad = mixing_raw * gain_one[:, None] + shift_one[:, None] * mixed_total
        gain_two_grad = jnp.sum(expand_raw * expand.astype(F32), 1)
        gain_one_grad = jnp.sum(mixing_raw * mixing.astype(F32), 1)
        shift_two_grad = jnp.sum(expand.astype(F32) * hidden_total, 1)
        shift_one_grad = jnp.sum(mixing.astype(F32) * mixed_total, 1)
        expand_grad = dp_scatter(expand_grad.astype(BF))
        mixing_grad = dp_scatter(mixing_grad.astype(BF))
        both = jnp.concatenate([mixing_grad, expand_grad], -1).astype(BF)
        both = seq_exchange(both.reshape(parts, rows_d, 3 * width + units)).astype(F32)
        mixing_grad = both[..., : 3 * width].reshape(parts, rows_d, 3, width)
        mixing_grad = mixing_grad.transpose(1, 2, 0, 3).reshape(rows_d, 3 * D)
        expand_grad = both[..., 3 * width :].reshape(parts, rows_d, copies, rows_f)
        expand_grad = expand_grad.transpose(1, 2, 0, 3).reshape(rows_d, FF)
        output_sum = jnp.sum(gradient, 0)
        affine_grad = jnp.concatenate(
            [
                gain_one_grad,
                shift_one_grad,
                gain_two_grad,
                shift_two_grad,
                spread_part(mixed_total, 3),
                output_sum,
                spread_part(hidden_total, copies),
                output_sum,
            ]
        )
        affine_grad = lax.all_to_all(
            affine_grad.reshape(devices, small),
            ("dp", "seq"),
            split_axis=0,
            concat_axis=0,
            tiled=True,
        )
        affine_grad = jnp.sum(affine_grad, 0)
        reduced[layer] = (mixing_grad, output_grad, expand_grad, shrink_grad, affine_grad)
        projected = jnp.mean(normed_grad * own_normed, -1, keepdims=True)
        middle = jnp.mean(normed_grad, -1, keepdims=True)
        gradient = gradient + scale * (normed_grad - middle - own_normed * projected)
    stream_grad = gradient.reshape(stream.shape)

    stacked = []
    squares = jnp.float32(0.0)
    for kind in range(5):
        kind_grad = jnp.stack([reduced[layer][kind] for layer in range(LAYERS)])
        stacked.append(kind_grad)
        squares = squares + jnp.sum(kind_grad * kind_grad)
    squares = lax.all_to_all(
        jnp.broadcast_to(squares, (devices, 128)),
        ("dp", "seq"),
        split_axis=0,
        concat_axis=0,
        tiled=True,
    )
    gradient_norm = jnp.sqrt(jnp.sum(squares[:, 0]))
    clip_scale = jnp.minimum(1.0, CLIP_LIMIT / (gradient_norm + 1e-06))
    step_rates = (D ** (-0.5), (D * 32 // LEN) ** (-0.5), D ** (-0.5), FF ** (-0.5), SMALL_RATE)
    decays = (WEIGHT_DECAY, WEIGHT_DECAY, WEIGHT_DECAY, WEIGHT_DECAY, 0.0)
    states = (
        (mixing_weight, mixing_first, mixing_second, mixing_average),
        (output_weight, output_first, output_second, output_average),
        (expand_weight, expand_first, expand_second, expand_average),
        (shrink_weight, shrink_first, shrink_second, shrink_average),
        (affine_weight, affine_first, affine_second, affine_average),
    )
    updated = ()
    for kind in range(5):
        weight, first_moment, second, average = states[kind]
        updated = updated + adamw_update(
            weight,
            first_moment,
            second,
            average,
            stacked[kind],
            clip_scale,
            step_rates[kind],
            decays[kind],
        )
    return (result, stream_grad, gradient_norm) + updated


def solution(mesh):
    tokens = P("dp", "seq", None)
    matrix = P(None, ("dp", "seq"), None)
    vector = P(None, ("dp", "seq"))
    states = (matrix,) * 16 + (vector,) * 4
    return jax.shard_map(
        local,
        mesh=mesh,
        in_specs=(tokens, tokens, P("dp", "seq")) + states,
        out_specs=(tokens, tokens, P()) + states,
        check_vma=False,
    )
```

time: 2880 us -> 1110 us (0.39)
  waiting for transfers between devices: 1680 us -> 295 us
  matrix products: 537 us -> 123 us
  Pallas kernels: 0 us -> 230 us
  starting transfers between devices: 35.8 us -> 156 us
  other arithmetic: 226 us -> 107 us
  blocking collectives: 85.5 us -> 0 us
  local copies, waits for them, and re-layouts: 245 us -> 174 us
  loops' own time: 44 us -> 0 us
    reduce_scatter x8 -> x0, waiting for transfers between devices: 1340 us -> none  [the longest x2 371 us: reduce_grads(): lax.psum_scatter(shrink_grad, ('dp', 'seq'), scatter_dimension=0, tiled=T...]
    dot_general x80 -> x16, matrix products: 537 us -> 123 us  [the longest x8 66.5 us: matmul_nt(): lax.dot_general(left, right, (((1,), (1,)), ((), ())), preferred_element_...]
    ppermute x0 -> x139, waiting for transfers between devices: none -> 279 us  [the longest x48 131 us: outer_ring(): lax.ppermute(value, 'dp', [(i, (i + inner) % size) for i in range(size)])]
    all_gather x8 -> x0, waiting for transfers between devices: 231 us -> none  [the longest x2 81.8 us: local(): lax.all_gather(mixing_weight[layer_index].astype(jnp.bfloat16), ('dp', 's...]
    pallas_call x0 -> x8, Pallas kernels: none -> 230 us  [the longest x2 94.5 us: attend(): pl.pallas_call(attend_kernel, grid=(length // block,), in_specs=[pl.Block...]
    ppermute x0 -> x139, starting transfers between devices: none -> 109 us  [the longest x64 69.5 us: inner_ring(): return lax.ppermute(value, 'dp', moves)]
    convert_element_type x20 -> x36, other arithmetic: 108 us -> 34.4 us  [the longest x24 19.4 us: dp_scatter(): arrived = outer_ring(part.astype(BF))]
    all_to_all x8 -> x12, waiting for transfers between devices: 86.2 us -> 16.2 us  [the longest x8 13.2 us: seq_exchange(): return lax.all_to_all(value, 'seq', split_axis=0, concat_axis=0, tiled=True)]
  transfers between devices with their start and end apart: 25 -> 151, of which waited for: 19 -> 71; matrix products, arithmetic and copies ran while one was open for 23% -> 29% of each run, Pallas kernels for 0% -> 12%
where the time goes in v1:
time: 1110 us; the launch traced here: 1090 us
  waiting for transfers between devices  295 us (27%)
  Pallas kernels  230 us (21%)
  local copies, waits for them, and re-layouts  174 us (16%)
  starting transfers between devices  156 us (14%)
  matrix products  123 us (11%)
  other arithmetic  107 us (10%)
    ppermute x48, waiting for transfers between devices, outer_ring(): lax.ppermute(value, 'dp', [(i, (i + inner) % size) for i in range(size)])  131 us
    pallas_call x2, Pallas kernels, attend(): pl.pallas_call(attend_kernel, grid=(length // block,), in_specs=[pl.Block...  94.5 us
    ppermute x64, waiting for transfers between devices, inner_ring(): return lax.ppermute(value, 'dp', moves)  74.9 us
    pallas_call x2, Pallas kernels, attend_back(): pl.pallas_call(attend_back_kernel, grid=(length // block,), in_specs=[pl....  74.3 us
    ppermute x9, waiting for transfers between devices, chip_ring(): lax.ppermute(value, 'seq', [(i, (i + 2) % size) for i in range(size)])  72.2 us
    ppermute x64, starting transfers between devices, inner_ring(): return lax.ppermute(value, 'dp', moves)  69.5 us
    dot_general x8, matrix products, matmul_nt(): lax.dot_general(left, right, (((1,), (1,)), ((), ())), preferred_element_...  66.5 us
    dynamic_update_slice x80, local copies, waits for them, and re-layouts, put(): return lax.dynamic_update_slice(total, piece[None, None], start)  62 us
  transfers between devices with their start and end apart: 151, of which 71 were waited for; matrix products, arithmetic and copies ran while one was open for 29% of the time, Pallas kernels for 12%

profile of v1, /device:TPU:0, one launch (start us, length us, event | category | flops | bytes accessed | tf_op | source)
XLA Modules:
  0.0 1093.3 jit_solution(9739621849168123888)
XLA Ops:
  58.9 5.7 multiply_sine_fusion
  65.6 6.0 concatenate.37.cos_ref
  72.7 5.5 concatenate.38.sin_ref
  104.3 6.3 collective-permute-done.64
  119.7 5.4 collective-permute-done.32
  125.2 6.0 collective-permute-done.66
  166.4 6.6 collective-permute-done.49
  187.5 5.2 collective-permute-done.55
  195.0 5.9 collective-permute-done.41
  219.9 7.0 collective-permute-done.20
  233.6 7.0 collective-permute-done.57
  243.1 5.7 collective-permute-done.15
  250.4 7.5 collective-permute-done.52
  260.1 8.0 collective-permute-done.43
  271.5 4.8 collective-permute-done.6
  282.7 8.6 collective-permute-done.22
  299.6 4.8 collective-permute-done.23
  323.1 9.6 mix.2.q_ref.k_ref.v_ref
  334.7 47.3 %attend.2 = (bf16[2048,256]{1,0:T(8,128)(2,1)S(1)}, f32[2048,128]{1,0:T(8,128)S(1)}) custom-call(bf16[2048,768]{1,0:T(8,128)(2,1)S(1)} %copy-done.23, bf16[2048,768]{1,0:T(8,128)(2,1)S(1)} %copy-done.23, bf16[2048,768]{1,0:T(8,128)(2,1)S(1)} %copy-done.23), custom_call_target="tpu_custom_call" | custom-call | flops 4294967296 | bytes 4194304 | tf_op jit(solution)/shard_map/attend/pallas_call | solution.py:282
  382.0 20.9 %feed.2 = (bf16[2048,1024]{1,0:T(8,128)(2,1)}, bf16[2048,1024]{1,0:T(8,128)(2,1)}, bf16[2048,1024]{1,0:T(8,128)(2,1)}) custom-call(bf16[2048,1024]{1,0:T(8,128)(2,1)} %bitcast.5.x_ref, bf16[1024,1024]{1,0:T(8,128)(2,1)S(1)} %fusion.10.wi_ref, f32[1,1024]{1,0:T(1,128)S(1)} %fusion.110.ci_ref, bf16[1024,1024]{1,0:T(8,128)(2,1)S(1)} %bitcast.617, ...), custom_call_target="tpu_custom_call" | custom-call | flops 9663676416 | bytes 20971520 | tf_op jit(solution)/shard_map/feed/pallas_call | solution.py:453
  428.9 15.7 %collective-permute-done.36 = bf16[512,1024]{1,0:T(8,128)(2,1)S(1)} collective-permute-done((bf16[512,1024]{1,0:T(8,128)(2,1)S(1)}, bf16[512,1024]{1,0:T(8,128)(2,1)S(1)}, u32[]{:S(2)}, u32[]{:S(2)}) %collective-permute-start.36) | collective-permute-done | bytes 1048608 | tf_op jit(solution)/shard_map/ppermute | solution.py:59
  455.3 16.8 %collective-permute-done.38 = bf16[512,1024]{1,0:T(8,128)(2,1)} collective-permute-done((bf16[512,1024]{1,0:T(8,128)(2,1)}, bf16[512,1024]{1,0:T(8,128)(2,1)}, u32[]{:S(2)}, u32[]{:S(2)}) %collective-permute-start.38) | collective-permute-done | bytes 1048608 | tf_op jit(solution)/shard_map/ppermute | solution.py:59
  483.5 9.1 mix.3.q_ref.k_ref.v_ref
  494.5 47.3 %attend.3 = (bf16[2048,256]{1,0:T(8,128)(2,1)S(1)}, f32[2048,128]{1,0:T(8,128)S(1)}) custom-call(bf16[2048,768]{1,0:T(8,128)(2,1)S(1)} %copy-done.24, bf16[2048,768]{1,0:T(8,128)(2,1)S(1)} %copy-done.24, bf16[2048,768]{1,0:T(8,128)(2,1)S(1)} %copy-done.24), custom_call_target="tpu_custom_call" | custom-call | flops 4294967296 | bytes 4194304 | tf_op jit(solution)/shard_map/attend/pallas_call | solution.py:282
  551.8 5.2 convert_multiply_fusion.11
  563.3 37.3 %attend_back.2 = (bf16[2048,768]{1,0:T(8,128)(2,1)}, f32[1,768]{1,0:T(1,128)S(1)}) custom-call(bf16[2048,768]{1,0:T(8,128)(2,1)} %mix.3.q_ref.k_ref.v_ref, bf16[2048,768]{1,0:T(8,128)(2,1)} %mix.3.q_ref.k_ref.v_ref, bf16[2048,768]{1,0:T(8,128)(2,1)} %mix.3.q_ref.k_ref.v_ref, bf16[2048,256]{1,0:T(8,128)(2,1)S(1)} %copy-done.9, ...), custom_call_target="tpu_custom_call" | custom-call | flops 10737418240 | bytes 8388608 | tf_op jit(solution)/shard_map/attend_back/pallas_call | solution.py:393
  602.5 9.3 fusion.133
  611.8 5.4 fusion.15
  621.3 21.3 %feed.3 = (bf16[2048,1024]{1,0:T(8,128)(2,1)}, bf16[2048,1024]{1,0:T(8,128)(2,1)}, bf16[2048,1024]{1,0:T(8,128)(2,1)}) custom-call(bf16[2048,1024]{1,0:T(8,128)(2,1)} %bitcast.628, bf16[1024,1024]{1,0:T(8,128)(2,1)S(1)} %fusion.6.wi_ref, f32[1,1024]{1,0:T(1,128)S(1)} %fusion.112.ci_ref, bf16[1024,1024]{1,0:T(8,128)(2,1)} %bitcast.103.wd_ref, ...), custom_call_target="tpu_custom_call" | custom-call | flops 9663676416 | bytes 20971520 | tf_op jit(solution)/shard_map/feed/pallas_call | solution.py:453
  642.7 8.2 convolution_convert_fusion.2
  656.9 10.8 fusion
  669.7 11.0 %add_convert_fusion.1 = bf16[2048,1024]{1,0:T(8,128)(2,1)} fusion(f32[2048,1024]{1,0:T(8,128)} %fusion.133, bf16[1024,1024]{1,0:T(8,128)(2,1)S(1)} %fusion.6.wi_ref, f32[2048,1024]{1,0:T(8,128)} %get-tuple-element.168, bf16[2048,1024]{1,0:T(8,128)(2,1)S(1)} %copy-done.59), kind=kOutput, calls=%fused_computation.2 | convolution fusion | flops 4305453056 | bytes 27262976 | tf_op jit(solution)/shard_map/dot_general | solution.py:186
  680.7 9.5 fusion.7
  691.4 5.8 all-to-all-start.10
  726.4 5.3 collective-permute-done.122
  746.4 5.9 collective-permute-done.98
  771.8 18.3 %collective-permute-done.70 = bf16[512,1024]{1,0:T(8,128)(2,1)S(1)} collective-permute-done((bf16[512,1024]{1,0:T(8,128)(2,1)S(1)}, bf16[512,1024]{1,0:T(8,128)(2,1)S(1)}, u32[]{:S(2)}, u32[]{:S(2)}) %collective-permute-start.70) | collective-permute-done | bytes 1048608 | tf_op jit(solution)/shard_map/ppermute | solution.py:59
  812.7 10.6 collective-permute-done.78
  838.6 5.0 convert_multiply_fusion.10
  843.6 6.9 convolution_convert_fusion.3
  861.4 37.0 %attend_back.3 = (bf16[2048,768]{1,0:T(8,128)(2,1)}, f32[1,768]{1,0:T(1,128)S(1)}) custom-call(bf16[2048,768]{1,0:T(8,128)(2,1)} %mix.2.q_ref.k_ref.v_ref, bf16[2048,768]{1,0:T(8,128)(2,1)} %mix.2.q_ref.k_ref.v_ref, bf16[2048,768]{1,0:T(8,128)(2,1)} %mix.2.q_ref.k_ref.v_ref, bf16[2048,256]{1,0:T(8,128)(2,1)S(1)} %get-tuple-element.164.do_ref, ...), custom_call_target="tpu_custom_call" | custom-call | flops 10737418240 | bytes 8388608 | tf_op jit(solution)/shard_map/attend_back/pallas_call | solution.py:393
  900.4 8.0 fusion.134
  908.4 6.7 fusion.19
  918.1 6.6 fusion.2
  925.5 11.0 %fusion.11 = (f32[1024]{0:T(1024)S(1)}, bf16[1024,1024]{1,0:T(8,128)(2,1)}) fusion(bf16[4,2,128,1024]{3,2,1,0:T(8,128)(2,1)S(1)} %copy-done.34, f32[1024]{0:T(1024)S(1)} %get-tuple-element.165, f32[1024]{0:T(1024)S(1)} %bitcast.703, f32[1024]{0:T(1024)S(1)} %bitcast.705, bf16[2048,1024]{1,0:T(8,128)(2,1)} %bitcast.5.x_ref, ...), kind=kOutput, calls=%fused_computation.23 | convolution fusion | flops 4308597760 | bytes 20987904 | tf_op jit(solution)/shard_map/dot_general | solution.py:190
  942.1 10.7 add_convert_fusion
  994.4 5.1 collective-permute-done.112
  1078.4 7.2 collective-permute-done.82
  (875 shorter events, 544.0 us)
Async XLA Ops:
  0.7 54.1 %collective-permute-start.25 = (s32[4,128]{1,0:T(4,128)}, s32[4,128]{1,0:T(4,128)S(1)}, u32[]{:S(2)}, u32[]{:S(2)}) collective-permute-start(s32[4,128]{1,0:T(4,128)} %bitcast.757), channel_id=1, source_target_pairs={{0,2},{1,3},{2,0},{3,1},{4,6},{5,7},{6,4},{7,5},{8,10},{9,11},{10,... | collective-permute-start | bytes 6152 | tf_op jit(solution)/shard_map/ppermute | solution.py:59
  3.7 52.5 %collective-permute-start.24 = (s32[4,128]{1,0:T(4,128)}, s32[4,128]{1,0:T(4,128)S(1)}, u32[]{:S(2)}, u32[]{:S(2)}) collective-permute-start(s32[4,128]{1,0:T(4,128)} %bitcast.758), channel_id=1, source_target_pairs={{0,1},{1,0},{2,3},{3,2},{4,5},{5,4},{6,7},{7,6},{8,9},{9,8},{10,11... | collective-permute-start | bytes 6152 | tf_op jit(solution)/shard_map/ppermute | solution.py:64
  5.3 78.8 %collective-permute-start.62 = (bf16[32,1024]{1,0:T(8,128)(2,1)}, bf16[32,1024]{1,0:T(8,128)(2,1)S(1)}, u32[]{:S(2)}, u32[]{:S(2)}) collective-permute-start(bf16[32,1024]{1,0:T(8,128)(2,1)} %get-tuple-element.142), channel_id=1, source_target_pairs={{0,8},{4,12},{8,16},{12,20},{16,24},{20,28},{24,0},{28,4},{1,9},{5... | collective-permute-start | bytes 196616 | tf_op jit(solution)/shard_map/ppermute | solution.py:46
  6.9 71.9 %collective-permute-start.61 = (bf16[32,1024]{1,0:T(8,128)(2,1)}, bf16[32,1024]{1,0:T(8,128)(2,1)}, u32[]{:S(2)}, u32[]{:S(2)}) collective-permute-start(bf16[32,1024]{1,0:T(8,128)(2,1)} %get-tuple-element.142), channel_id=1, source_target_pairs={{0,4},{4,0},{8,12},{12,8},{16,20},{20,16},{24,28},{28,24},{1,5},{5... | collective-permute-start | bytes 196616 | tf_op jit(solution)/shard_map/ppermute | solution.py:54
  11.5 73.9 %all-to-all-start.1 = ((bf16[32,2,416]{2,1,0:T(2,128)(2,1)}), bf16[32,2,416]{2,1,0:T(2,128)(2,1)S(1)}, u32[]{:S(2)}, u32[]{:S(2)}) async-start(bf16[32,2,416]{2,1,0:T(2,128)(2,1)} %reshape.779), calls=%async_computation.1 | async-start | bytes 131072 | tf_op jit(solution)/shard_map/all_to_all | solution.py:573
  14.5 67.4 %collective-permute-start.28 = (bf16[32,1024]{1,0:T(8,128)(2,1)}, bf16[32,1024]{1,0:T(8,128)(2,1)}, u32[]{:S(2)}, u32[]{:S(2)}) collective-permute-start(bf16[32,1024]{1,0:T(8,128)(2,1)} %get-tuple-element.143), channel_id=1, source_target_pairs={{0,8},{4,12},{8,16},{12,20},{16,24},{20,28},{24,0},{28,4},{1,9},{5... | collective-permute-start | bytes 196616 | tf_op jit(solution)/shard_map/ppermute | solution.py:46
  57.4 81.0 %collective-permute-start.48 = (bf16[128,1024]{1,0:T(8,128)(2,1)}, bf16[128,1024]{1,0:T(8,128)(2,1)}, u32[]{:S(2)}, u32[]{:S(2)}) collective-permute-start(bf16[128,1024]{1,0:T(8,128)(2,1)} %get-tuple-element.128), channel_id=1, source_target_pairs={{0,8},{4,12},{8,16},{12,20},{16,24},{20,28},{24,0},{28,4},{1,9},{5... | collective-permute-start | bytes 786440 | tf_op jit(solution)/shard_map/ppermute | solution.py:46
  78.1 57.7 %collective-permute-start.47 = (bf16[128,1024]{1,0:T(8,128)(2,1)}, bf16[128,1024]{1,0:T(8,128)(2,1)}, u32[]{:S(2)}, u32[]{:S(2)}) collective-permute-start(bf16[128,1024]{1,0:T(8,128)(2,1)} %get-tuple-element.128), channel_id=1, source_target_pairs={{0,4},{4,0},{8,12},{12,8},{16,20},{20,16},{24,28},{28,24},{1,5},{5... | collective-permute-start | bytes 786440 | tf_op jit(solution)/shard_map/ppermute | solution.py:54
  78.8 55.5 %collective-permute-start.11 = (bf16[128,1024]{1,0:T(8,128)(2,1)}, bf16[128,1024]{1,0:T(8,128)(2,1)}, u32[]{:S(2)}, u32[]{:S(2)}) collective-permute-start(bf16[128,1024]{1,0:T(8,128)(2,1)} %get-tuple-element.129), channel_id=1, source_target_pairs={{0,8},{4,12},{8,16},{12,20},{16,24},{20,28},{24,0},{28,4},{1,9},{5... | collective-permute-start | bytes 786440 | tf_op jit(solution)/shard_map/ppermute | solution.py:46
  81.8 51.5 %collective-permute-start.10 = (bf16[128,1024]{1,0:T(8,128)(2,1)}, bf16[128,1024]{1,0:T(8,128)(2,1)}, u32[]{:S(2)}, u32[]{:S(2)}) collective-permute-start(bf16[128,1024]{1,0:T(8,128)(2,1)} %get-tuple-element.129), channel_id=1, source_target_pairs={{0,4},{4,0},{8,12},{12,8},{16,20},{20,16},{24,28},{28,24},{1,5},{5... | collective-permute-start | bytes 786440 | tf_op jit(solution)/shard_map/ppermute | solution.py:54
  85.4 57.3 %all-to-all-start.3 = ((bf16[4,32,1792]{2,1,0:T(8,128)(2,1)}), bf16[4,32,1792]{2,1,0:T(8,128)(2,1)S(1)}, u32[]{:S(2)}, u32[]{:S(2)}) async-start(bf16[4,32,1792]{2,1,0:T(8,128)(2,1)} %pad_maximum_fusion.2), calls=%async_computation.3 | async-start | bytes 917504 | tf_op jit(solution)/shard_map/all_to_all | solution.py:159
  131.2 277.2 %collective-permute-start.72 = (bf16[512,1024]{1,0:T(8,128)(2,1)}, bf16[512,1024]{1,0:T(8,128)(2,1)}, u32[]{:S(2)}, u32[]{:S(2)}) collective-permute-start(bf16[512,1024]{1,0:T(8,128)(2,1)} %get-tuple-element.102), channel_id=1, source_target_pairs={{0,2},{1,3},{2,0},{3,1},{4,6},{5,7},{6,4},{7,5},{8,10},{9,11},{10,... | collective-permute-start | bytes 3145736 | tf_op jit(solution)/shard_map/ppermute | solution.py:59
  133.3 275.7 %collective-permute-start.71 = (bf16[512,1024]{1,0:T(8,128)(2,1)}, bf16[512,1024]{1,0:T(8,128)(2,1)}, u32[]{:S(2)}, u32[]{:S(2)}) collective-permute-start(bf16[512,1024]{1,0:T(8,128)(2,1)} %get-tuple-element.102), channel_id=1, source_target_pairs={{0,1},{1,0},{2,3},{3,2},{4,5},{5,4},{6,7},{7,6},{8,9},{9,8},{10,11... | collective-permute-start | bytes 3145736 | tf_op jit(solution)/shard_map/ppermute | solution.py:64
  134.3 157.7 %collective-permute-start = (bf16[512,1024]{1,0:T(8,128)(2,1)}, bf16[512,1024]{1,0:T(8,128)(2,1)}, u32[]{:S(2)}, u32[]{:S(2)}) collective-permute-start(bf16[512,1024]{1,0:T(8,128)(2,1)} %fusion.39), channel_id=1, source_target_pairs={{0,1},{1,0},{2,3},{3,2},{4,5},{5,4},{6,7},{7,6},{8,9},{9,8},{10,11... | collective-permute-start | bytes 3145736 | tf_op jit(solution)/shard_map/ppermute | solution.py:64
  142.7 23.6 %collective-permute-start.13 = (bf16[128,1024]{1,0:T(8,128)(2,1)}, bf16[128,1024]{1,0:T(8,128)(2,1)S(1)}, u32[]{:S(2)}, u32[]{:S(2)}) collective-permute-start(bf16[128,1024]{1,0:T(8,128)(2,1)} %collective-permute-done.11), channel_id=1, source_target_pairs={{0,8},{4,12},{8,16},{12,20},{16,24},{20,28},{24,0},{28,4},{1,9},{5... | collective-permute-start | bytes 786440 | tf_op jit(solution)/shard_map/ppermute | solution.py:46
  155.0 46.7 %all-to-all-start.2 = ((bf16[4,64,1024]{2,1,0:T(8,128)(2,1)}), bf16[4,64,1024]{2,1,0:T(8,128)(2,1)}, u32[]{:S(2)}, u32[]{:S(2)}) async-start(bf16[4,64,1024]{2,1,0:T(8,128)(2,1)} %bitcast.689), calls=%async_computation.2 | async-start | bytes 1048576 | tf_op jit(solution)/shard_map/all_to_all | solution.py:159
  205.2 36.1 %collective-permute-start.14 = (bf16[128,1024]{1,0:T(8,128)(2,1)S(1)}, bf16[128,1024]{1,0:T(8,128)(2,1)}, u32[]{:S(2)}, u32[]{:S(2)}) collective-permute-start(bf16[128,1024]{1,0:T(8,128)(2,1)S(1)} %collective-permute-done.13), channel_id=1, source_target_pairs={{0,4},{4,0},{8,12},{12,8},{16,20},{20,16},{24,28},{28,24},{1,5},{5... | collective-permute-start | bytes 786440 | tf_op jit(solution)/shard_map/ppermute | solution.py:54
  268.9 25.9 %collective-permute-start.1 = (bf16[512,1024]{1,0:T(8,128)(2,1)S(1)}, bf16[512,1024]{1,0:T(8,128)(2,1)S(1)}, u32[]{:S(2)}, u32[]{:S(2)}) collective-permute-start(bf16[512,1024]{1,0:T(8,128)(2,1)S(1)} %copy-done.90), channel_id=1, source_target_pairs={{0,2},{1,3},{2,0},{3,1},{4,6},{5,7},{6,4},{7,5},{8,10},{9,11},{10,... | collective-permute-start | bytes 3145736 | tf_op jit(solution)/shard_map/ppermute | solution.py:59
  291.3 114.1 %collective-permute-start.59 = (bf16[128,768]{1,0:T(8,128)(2,1)S(1)}, bf16[128,768]{1,0:T(8,128)(2,1)S(1)}, u32[]{:S(2)}, u32[]{:S(2)}) collective-permute-start(bf16[128,768]{1,0:T(8,128)(2,1)S(1)} %collective-permute-done.57), channel_id=1, source_target_pairs={{0,8},{4,12},{8,16},{12,20},{16,24},{20,28},{24,0},{28,4},{1,9},{5... | collective-permute-start | bytes 589832 | tf_op jit(solution)/shard_map/ppermute | solution.py:46
  318.2 86.4 %collective-permute-start.58 = (bf16[128,768]{1,0:T(8,128)(2,1)S(1)}, bf16[128,768]{1,0:T(8,128)(2,1)S(1)}, u32[]{:S(2)}, u32[]{:S(2)}) collective-permute-start(bf16[128,768]{1,0:T(8,128)(2,1)S(1)} %collective-permute-done.57), channel_id=1, source_target_pairs={{0,4},{4,0},{8,12},{12,8},{16,20},{20,16},{24,28},{28,24},{1,5},{5... | collective-permute-start | bytes 589832 | tf_op jit(solution)/shard_map/ppermute | solution.py:54
  320.3 85.9 %collective-permute-start.53 = (bf16[128,1024]{1,0:T(8,128)(2,1)S(1)}, bf16[128,1024]{1,0:T(8,128)(2,1)S(1)}, u32[]{:S(2)}, u32[]{:S(2)}) collective-permute-start(bf16[128,1024]{1,0:T(8,128)(2,1)S(1)} %collective-permute-done.52), channel_id=1, source_target_pairs={{0,4},{4,0},{8,12},{12,8},{16,20},{20,16},{24,28},{28,24},{1,5},{5... | collective-permute-start | bytes 786440 | tf_op jit(solution)/shard_map/ppermute | solution.py:54
  409.0 63.1 %collective-permute-start.73 = (bf16[512,1024]{1,0:T(8,128)(2,1)}, bf16[512,1024]{1,0:T(8,128)(2,1)S(1)}, u32[]{:S(2)}, u32[]{:S(2)}) collective-permute-start(bf16[512,1024]{1,0:T(8,128)(2,1)} %collective-permute-done.72), channel_id=1, source_target_pairs={{0,1},{1,0},{2,3},{3,2},{4,5},{5,4},{6,7},{7,6},{8,9},{9,8},{10,11... | collective-permute-start | bytes 3145736 | tf_op jit(solution)/shard_map/ppermute | solution.py:64
  416.0 33.7 %collective-permute-start.46 = (bf16[128,1024]{1,0:T(8,128)(2,1)S(1)}, bf16[128,1024]{1,0:T(8,128)(2,1)S(1)}, u32[]{:S(2)}, u32[]{:S(2)}) collective-permute-start(bf16[128,1024]{1,0:T(8,128)(2,1)S(1)} %collective-permute-done.45), channel_id=1, source_target_pairs={{0,4},{4,0},{8,12},{12,8},{16,20},{20,16},{24,28},{28,24},{1,5},{5... | collective-permute-start | bytes 786440 | tf_op jit(solution)/shard_map/ppermute | solution.py:54
  419.6 25.1 %collective-permute-start.36 = (bf16[512,1024]{1,0:T(8,128)(2,1)S(1)}, bf16[512,1024]{1,0:T(8,128)(2,1)S(1)}, u32[]{:S(2)}, u32[]{:S(2)}) collective-permute-start(bf16[512,1024]{1,0:T(8,128)(2,1)S(1)} %fusion.30), channel_id=1, source_target_pairs={{0,2},{1,3},{2,0},{3,1},{4,6},{5,7},{6,4},{7,5},{8,10},{9,11},{10,... | collective-permute-start | bytes 3145736 | tf_op jit(solution)/shard_map/ppermute | solution.py:59
  448.0 24.1 %collective-permute-start.38 = (bf16[512,1024]{1,0:T(8,128)(2,1)}, bf16[512,1024]{1,0:T(8,128)(2,1)}, u32[]{:S(2)}, u32[]{:S(2)}) collective-permute-start(bf16[512,1024]{1,0:T(8,128)(2,1)} %get-tuple-element.82), channel_id=1, source_target_pairs={{0,2},{1,3},{2,0},{3,1},{4,6},{5,7},{6,4},{7,5},{8,10},{9,11},{10,... | collective-permute-start | bytes 3145736 | tf_op jit(solution)/shard_map/ppermute | solution.py:59
  619.3 89.5 %collective-permute-start.100 = (bf16[128,768]{1,0:T(8,128)(2,1)}, bf16[128,768]{1,0:T(8,128)(2,1)}, u32[]{:S(2)}, u32[]{:S(2)}) collective-permute-start(bf16[128,768]{1,0:T(8,128)(2,1)} %get-tuple-element.121), channel_id=1, source_target_pairs={{0,4},{4,0},{8,12},{12,8},{16,20},{20,16},{24,28},{28,24},{1,5},{5... | collective-permute-start | bytes 589832 | tf_op jit(solution)/shard_map/ppermute | solution.py:54
  620.7 101.3 %collective-permute-start.99 = (bf16[128,768]{1,0:T(8,128)(2,1)}, bf16[128,768]{1,0:T(8,128)(2,1)}, u32[]{:S(2)}, u32[]{:S(2)}) collective-permute-start(bf16[128,768]{1,0:T(8,128)(2,1)} %get-tuple-element.122), channel_id=1, source_target_pairs={{0,4},{4,0},{8,12},{12,8},{16,20},{20,16},{24,28},{28,24},{1,5},{5... | collective-permute-start | bytes 589832 | tf_op jit(solution)/shard_map/ppermute | solution.py:54
  651.9 59.0 %collective-permute-start.135 = (bf16[128,1024]{1,0:T(8,128)(2,1)}, bf16[128,1024]{1,0:T(8,128)(2,1)}, u32[]{:S(2)}, u32[]{:S(2)}) collective-permute-start(bf16[128,1024]{1,0:T(8,128)(2,1)} %get-tuple-element.108), channel_id=1, source_target_pairs={{0,4},{4,0},{8,12},{12,8},{16,20},{20,16},{24,28},{28,24},{1,5},{5... | collective-permute-start | bytes 786440 | tf_op jit(solution)/shard_map/ppermute | solution.py:54
  653.4 78.9 %collective-permute-start.134 = (bf16[128,1024]{1,0:T(8,128)(2,1)}, bf16[128,1024]{1,0:T(8,128)(2,1)S(1)}, u32[]{:S(2)}, u32[]{:S(2)}) collective-permute-start(bf16[128,1024]{1,0:T(8,128)(2,1)} %get-tuple-element.109), channel_id=1, source_target_pairs={{0,4},{4,0},{8,12},{12,8},{16,20},{20,16},{24,28},{28,24},{1,5},{5... | collective-permute-start | bytes 786440 | tf_op jit(solution)/shard_map/ppermute | solution.py:54
  708.7 25.0 %collective-permute-start.75 = (bf16[512,1024]{1,0:T(8,128)(2,1)}, bf16[512,1024]{1,0:T(8,128)(2,1)}, u32[]{:S(2)}, u32[]{:S(2)}) collective-permute-start(bf16[512,1024]{1,0:T(8,128)(2,1)} %get-tuple-element.92), channel_id=1, source_target_pairs={{0,1},{1,0},{2,3},{3,2},{4,5},{5,4},{6,7},{7,6},{8,9},{9,8},{10,11... | collective-permute-start | bytes 3145736 | tf_op jit(solution)/shard_map/ppermute | solution.py:64
  726.4 26.0 %collective-permute-start.69 = (bf16[512,1024]{1,0:T(8,128)(2,1)S(1)}, bf16[512,1024]{1,0:T(8,128)(2,1)S(1)}, u32[]{:S(2)}, u32[]{:S(2)}) collective-permute-start(bf16[512,1024]{1,0:T(8,128)(2,1)S(1)} %copy-done.85), channel_id=1, source_target_pairs={{0,1},{1,0},{2,3},{3,2},{4,5},{5,4},{6,7},{7,6},{8,9},{9,8},{10,11... | collective-permute-start | bytes 3145736 | tf_op jit(solution)/shard_map/ppermute | solution.py:64
  732.3 32.8 %collective-permute-start.74 = (bf16[512,1024]{1,0:T(8,128)(2,1)}, bf16[512,1024]{1,0:T(8,128)(2,1)S(1)}, u32[]{:S(2)}, u32[]{:S(2)}) collective-permute-start(bf16[512,1024]{1,0:T(8,128)(2,1)} %get-tuple-element.91), channel_id=1, source_target_pairs={{0,1},{1,0},{2,3},{3,2},{4,5},{5,4},{6,7},{7,6},{8,9},{9,8},{10,11... | collective-permute-start | bytes 3145736 | tf_op jit(solution)/shard_map/ppermute | solution.py:64
  743.3 26.1 %collective-permute-start.76 = (bf16[512,1024]{1,0:T(8,128)(2,1)S(1)}, bf16[512,1024]{1,0:T(8,128)(2,1)S(1)}, u32[]{:S(2)}, u32[]{:S(2)}) collective-permute-start(bf16[512,1024]{1,0:T(8,128)(2,1)S(1)} %fusion.22), channel_id=1, source_target_pairs={{0,2},{1,3},{2,0},{3,1},{4,6},{5,7},{6,4},{7,5},{8,10},{9,11},{10,... | collective-permute-start | bytes 3145736 | tf_op jit(solution)/shard_map/ppermute | solution.py:59
  759.8 30.2 %collective-permute-start.70 = (bf16[512,1024]{1,0:T(8,128)(2,1)S(1)}, bf16[512,1024]{1,0:T(8,128)(2,1)S(1)}, u32[]{:S(2)}, u32[]{:S(2)}) collective-permute-start(bf16[512,1024]{1,0:T(8,128)(2,1)S(1)} %fusion.24), channel_id=1, source_target_pairs={{0,2},{1,3},{2,0},{3,1},{4,6},{5,7},{6,4},{7,5},{8,10},{9,11},{10,... | collective-permute-start | bytes 3145736 | tf_op jit(solution)/shard_map/ppermute | solution.py:59
  762.6 34.5 %collective-permute-start.97 = (bf16[128,768]{1,0:T(8,128)(2,1)S(1)}, bf16[128,768]{1,0:T(8,128)(2,1)S(1)}, u32[]{:S(2)}, u32[]{:S(2)}) collective-permute-start(bf16[128,768]{1,0:T(8,128)(2,1)S(1)} %copy-done.110), channel_id=1, source_target_pairs={{0,4},{4,0},{8,12},{12,8},{16,20},{20,16},{24,28},{28,24},{1,5},{5... | collective-permute-start | bytes 589832 | tf_op jit(solution)/shard_map/ppermute | solution.py:54
  765.1 34.1 %collective-permute-start.133 = (bf16[128,1024]{1,0:T(8,128)(2,1)S(1)}, bf16[128,1024]{1,0:T(8,128)(2,1)S(1)}, u32[]{:S(2)}, u32[]{:S(2)}) collective-permute-start(bf16[128,1024]{1,0:T(8,128)(2,1)S(1)} %copy-done.104), channel_id=1, source_target_pairs={{0,4},{4,0},{8,12},{12,8},{16,20},{20,16},{24,28},{28,24},{1,5},{5... | collective-permute-start | bytes 786440 | tf_op jit(solution)/shard_map/ppermute | solution.py:54
  769.4 33.0 %collective-permute-start.104 = (bf16[128,1024]{1,0:T(8,128)(2,1)}, bf16[128,1024]{1,0:T(8,128)(2,1)S(1)}, u32[]{:S(2)}, u32[]{:S(2)}) collective-permute-start(bf16[128,1024]{1,0:T(8,128)(2,1)} %get-tuple-element.111), channel_id=1, source_target_pairs={{0,4},{4,0},{8,12},{12,8},{16,20},{20,16},{24,28},{28,24},{1,5},{5... | collective-permute-start | bytes 786440 | tf_op jit(solution)/shard_map/ppermute | solution.py:54
  771.7 29.1 %collective-permute-start.137 = (bf16[128,1024]{1,0:T(8,128)(2,1)S(1)}, bf16[128,1024]{1,0:T(8,128)(2,1)S(1)}, u32[]{:S(2)}, u32[]{:S(2)}) collective-permute-start(bf16[128,1024]{1,0:T(8,128)(2,1)S(1)} %fusion.46), channel_id=1, source_target_pairs={{0,8},{4,12},{8,16},{12,20},{16,24},{20,28},{24,0},{28,4},{1,9},{5... | collective-permute-start | bytes 786440 | tf_op jit(solution)/shard_map/ppermute | solution.py:46
  797.5 25.7 %collective-permute-start.78 = (bf16[512,1024]{1,0:T(8,128)(2,1)}, bf16[512,1024]{1,0:T(8,128)(2,1)}, u32[]{:S(2)}, u32[]{:S(2)}) collective-permute-start(bf16[512,1024]{1,0:T(8,128)(2,1)} %get-tuple-element.80), channel_id=1, source_target_pairs={{0,2},{1,3},{2,0},{3,1},{4,6},{5,7},{6,4},{7,5},{8,10},{9,11},{10,... | collective-permute-start | bytes 3145736 | tf_op jit(solution)/shard_map/ppermute | solution.py:59
  799.3 24.0 %collective-permute-start.132 = (bf16[128,1024]{1,0:T(8,128)(2,1)S(1)}, bf16[128,1024]{1,0:T(8,128)(2,1)S(1)}, u32[]{:S(2)}, u32[]{:S(2)}) collective-permute-start(bf16[128,1024]{1,0:T(8,128)(2,1)S(1)} %copy-done.103), channel_id=1, source_target_pairs={{0,4},{4,0},{8,12},{12,8},{16,20},{20,16},{24,28},{28,24},{1,5},{5... | collective-permute-start | bytes 786440 | tf_op jit(solution)/shard_map/ppermute | solution.py:54
  852.9 184.0 %collective-permute-start.125 = (bf16[128,1024]{1,0:T(8,128)(2,1)}, bf16[128,1024]{1,0:T(8,128)(2,1)}, u32[]{:S(2)}, u32[]{:S(2)}) collective-permute-start(bf16[128,1024]{1,0:T(8,128)(2,1)} %get-tuple-element.103), channel_id=1, source_target_pairs={{0,4},{4,0},{8,12},{12,8},{16,20},{20,16},{24,28},{28,24},{1,5},{5... | collective-permute-start | bytes 786440 | tf_op jit(solution)/shard_map/ppermute | solution.py:54
  854.3 111.8 %collective-permute-start.128 = (bf16[128,1024]{1,0:T(8,128)(2,1)}, bf16[128,1024]{1,0:T(8,128)(2,1)}, u32[]{:S(2)}, u32[]{:S(2)}) collective-permute-start(bf16[128,1024]{1,0:T(8,128)(2,1)} %get-tuple-element.104), channel_id=1, source_target_pairs={{0,4},{4,0},{8,12},{12,8},{16,20},{20,16},{24,28},{28,24},{1,5},{5... | collective-permute-start | bytes 786440 | tf_op jit(solution)/shard_map/ppermute | solution.py:54
  854.9 131.2 %collective-permute-start.127 = (bf16[128,1024]{1,0:T(8,128)(2,1)}, bf16[128,1024]{1,0:T(8,128)(2,1)}, u32[]{:S(2)}, u32[]{:S(2)}) collective-permute-start(bf16[128,1024]{1,0:T(8,128)(2,1)} %get-tuple-element.105), channel_id=1, source_target_pairs={{0,4},{4,0},{8,12},{12,8},{16,20},{20,16},{24,28},{28,24},{1,5},{5... | collective-permute-start | bytes 786440 | tf_op jit(solution)/shard_map/ppermute | solution.py:54
  916.1 45.7 %collective-permute-start.86 = (bf16[128,768]{1,0:T(8,128)(2,1)}, bf16[128,768]{1,0:T(8,128)(2,1)S(1)}, u32[]{:S(2)}, u32[]{:S(2)}) collective-permute-start(bf16[128,768]{1,0:T(8,128)(2,1)} %get-tuple-element.125), channel_id=1, source_target_pairs={{0,4},{4,0},{8,12},{12,8},{16,20},{20,16},{24,28},{28,24},{1,5},{5... | collective-permute-start | bytes 589832 | tf_op jit(solution)/shard_map/ppermute | solution.py:54
  916.7 60.6 %collective-permute-start.85 = (bf16[128,768]{1,0:T(8,128)(2,1)}, bf16[128,768]{1,0:T(8,128)(2,1)}, u32[]{:S(2)}, u32[]{:S(2)}) collective-permute-start(bf16[128,768]{1,0:T(8,128)(2,1)} %get-tuple-element.126), channel_id=1, source_target_pairs={{0,4},{4,0},{8,12},{12,8},{16,20},{20,16},{24,28},{28,24},{1,5},{5... | collective-permute-start | bytes 589832 | tf_op jit(solution)/shard_map/ppermute | solution.py:54
  987.5 24.0 %collective-permute-start.91 = (bf16[128,1024]{1,0:T(8,128)(2,1)}, bf16[128,1024]{1,0:T(8,128)(2,1)S(1)}, u32[]{:S(2)}, u32[]{:S(2)}) collective-permute-start(bf16[128,1024]{1,0:T(8,128)(2,1)} %get-tuple-element.118), channel_id=1, source_target_pairs={{0,4},{4,0},{8,12},{12,8},{16,20},{20,16},{24,28},{28,24},{1,5},{5... | collective-permute-start | bytes 786440 | tf_op jit(solution)/shard_map/ppermute | solution.py:54
  1023.3 55.2 %collective-permute-start.80 = (bf16[512,1024]{1,0:T(8,128)(2,1)}, bf16[512,1024]{1,0:T(8,128)(2,1)}, u32[]{:S(2)}, u32[]{:S(2)}) collective-permute-start(bf16[512,1024]{1,0:T(8,128)(2,1)} %get-tuple-element.89), channel_id=1, source_target_pairs={{0,1},{1,0},{2,3},{3,2},{4,5},{5,4},{6,7},{7,6},{8,9},{9,8},{10,11... | collective-permute-start | bytes 3145736 | tf_op jit(solution)/shard_map/ppermute | solution.py:64
  1059.9 25.8 %collective-permute-start.82 = (bf16[512,1024]{1,0:T(8,128)(2,1)}, bf16[512,1024]{1,0:T(8,128)(2,1)}, u32[]{:S(2)}, u32[]{:S(2)}) collective-permute-start(bf16[512,1024]{1,0:T(8,128)(2,1)} %fusion.20), channel_id=1, source_target_pairs={{0,2},{1,3},{2,0},{3,1},{4,6},{5,7},{6,4},{7,5},{8,10},{9,11},{10,... | collective-permute-start | bytes 3145736 | tf_op jit(solution)/shard_map/ppermute | solution.py:59
  (248 other events, 3164.5 us)

commit v2 on v1

v2 whole, which is shorter than its diff:
```python
from functools import partial
import math

import jax
import jax.numpy as jnp
from jax import lax
from jax.experimental import pallas as pl
from jax.experimental.pallas import tpu as pltpu
from jax.sharding import PartitionSpec as P

D = 1024
H = 16
HD = 64
ROT = 16
FF = 4096
LEN = 2048
LAYERS = 2
STEP = 3

NORM_EPS = 1e-05
CLIP_LIMIT = 1.0
BETA_FIRST = 0.5
BETA_SECOND = 0.5
ADAM_EPS = 1e-08
WEIGHT_DECAY = 0.01
EMA_DECAY = 0.999
SMALL_RATE = 0.1
MASK_VALUE = -1e30
ROWS = 256
BLOCK = 512
QUERY_SCALE = 1.0 / math.sqrt(HD)
BF = jnp.bfloat16
F32 = jnp.float32
VMEM_LIMIT = 48 * 1024 * 1024


def dp_parts():
    size = lax.axis_size("dp")
    outer = 4 if size % 4 == 0 else size
    return outer, size // outer


def outer_ring(value):
    outer, inner = dp_parts()
    size = outer * inner
    return lax.ppermute(value, "dp", [(i, (i + inner) % size) for i in range(size)])


def inner_ring(value):
    outer, inner = dp_parts()
    moves = [
        (a * inner + b, a * inner + (b + 1) % inner) for a in range(outer) for b in range(inner)
    ]
    return lax.ppermute(value, "dp", moves)


def chip_ring(value):
    size = lax.axis_size("seq")
    return lax.ppermute(value, "seq", [(i, (i + 2) % size) for i in range(size)])


def core_swap(value):
    size = lax.axis_size("seq")
    return lax.ppermute(value, "seq", [(i, i ^ 1) for i in range(size)])


def assemble_kernel(slots_ref, *refs):
    n = pl.program_id(0)
    for step, piece_ref in enumerate(refs[:-1]):

        @pl.when(n == step)
        def _(piece_ref=piece_ref):
            refs[-1][...] = piece_ref[...][None]


def assemble(pieces, slots):
    count, piece = len(pieces), pieces[0]
    total = pl.pallas_call(
        assemble_kernel,
        grid_spec=pltpu.PrefetchScalarGridSpec(
            num_scalar_prefetch=1,
            grid=(count,),
            in_specs=[pl.BlockSpec(memory_space=pltpu.VMEM)] * count,
            out_specs=pl.BlockSpec((1,) + piece.shape, lambda n, slots: (slots[n], 0, 0)),
        ),
        out_shape=jax.ShapeDtypeStruct((count,) + piece.shape, piece.dtype),
        compiler_params=pltpu.CompilerParams(vmem_limit_bytes=VMEM_LIMIT),
        cost_estimate=pl.CostEstimate(
            flops=0, bytes_accessed=4 * count * piece.size, transcendentals=0
        ),
        name="assemble",
    )(jnp.stack(slots).astype(jnp.int32), *pieces)
    return total.reshape((count * piece.shape[0],) + piece.shape[1:])


def pick(total, first, second):
    sizes = (1, 1) + total.shape[2:]
    start = (first, second) + (0,) * (total.ndim - 2)
    return lax.dynamic_slice(total, start, sizes)[0, 0]


class Gather:
    def __init__(self, value):
        self.pieces = [value]
        self.chains = []

    def forward(self):
        self.pieces.append(outer_ring(self.pieces[-1]))

    def cross(self):
        chain = [self.pieces[len(self.chains)]]
        for turn in range(1, dp_parts()[1]):
            chain.append(inner_ring(chain[-1]))
        self.chains.append(chain)

    def hold(self, *values):
        held = lax.optimization_barrier((values, self.pieces, self.chains))
        self.pieces, self.chains = held[1], held[2]
        return held[0]

    def done(self):
        outer, inner = dp_parts()
        me = lax.axis_index("dp")
        a, b = me // inner, me % inner
        pieces, slots = [], []
        for step, chain in enumerate(self.chains):
            for turn, piece in enumerate(chain):
                pieces.append(piece)
                slots.append((a - step) % outer * inner + (b - turn) % inner)
        return assemble(pieces, slots)


class Scatter:
    def __init__(self, *values):
        outer, inner = dp_parts()
        me = lax.axis_index("dp")
        self.a, self.b = me // inner, me % inner
        self.values = [
            value.reshape((outer, inner, -1) + value.shape[1:]) for value in values
        ]
        self.parts = []
        self.arrived = None
        self.steps = 0

    def own(self, at, turn):
        inner = dp_parts()[1]
        taken = [pick(value, at, (self.b - turn) % inner) for value in self.values]
        return taken[0] if len(taken) == 1 else jnp.concatenate(taken, -1)

    def cross(self):
        outer, inner = dp_parts()
        at = (self.a - len(self.parts) - 1) % outer
        arrived = None
        for turn in range(1, inner):
            own = self.own(at, turn)
            if arrived is not None:
                own = (own.astype(F32) + arrived.astype(F32)).astype(BF)
            arrived = inner_ring(own)
        self.parts.append((self.own(at, 0), arrived))

    def part(self):
        own, arrived = self.parts[self.steps]
        total = own.astype(F32)
        if arrived is not None:
            total = total + arrived.astype(F32)
        if self.arrived is not None:
            total = total + self.arrived.astype(F32)
        return total

    def forward(self):
        self.arrived = outer_ring(self.part().astype(BF))
        self.steps += 1

    def hold(self, *values):
        held = lax.optimization_barrier((values, self.values, self.parts, self.arrived))
        self.values, self.parts, self.arrived = held[1], held[2], held[3]
        return held[0]

    def done(self):
        return self.part()


def seq_gather(value):
    chips = lax.axis_size("seq") // 2
    me = lax.axis_index("seq")
    y, c = me // 2, me % 2
    pieces, slots = [], []
    piece = value
    for step in range(chips):
        at = (y - step) % chips
        pieces += [piece, core_swap(piece)]
        slots += [2 * at + c, 2 * at + 1 - c]
        if step < chips - 1:
            piece = chip_ring(piece)
    return assemble(pieces, slots)


class SeqScatter:
    def __init__(self, others, own):
        chips = lax.axis_size("seq") // 2
        self.core = lax.axis_index("seq") % 2
        rows = own.shape[0] // 2
        others = others.reshape((chips - 1, 2, rows) + own.shape[1:])
        self.values = [others[n] for n in range(chips - 1)]
        self.values.append(own.reshape((2, rows) + own.shape[1:]))
        self.sending = self.cores(0).astype(BF)

    def cores(self, n):
        value = self.values[n]
        kept = lax.dynamic_index_in_dim(value, self.core, 0, keepdims=False)
        passed = lax.dynamic_index_in_dim(value, 1 - self.core, 0, keepdims=False)
        return kept.astype(F32) + core_swap(passed).astype(F32)

    def hold(self, *values):
        held = lax.optimization_barrier((values, self.sending))
        self.sending = held[1]
        return held[0]

    def done(self):
        for n in range(1, len(self.values)):
            arrived = chip_ring(self.sending)
            total = self.cores(n) + arrived.astype(F32)
            self.sending = total.astype(BF)
        return total


def seq_exchange(value):
    return lax.all_to_all(value, "seq", split_axis=0, concat_axis=0, tiled=True)


def head_masks(width, dtype):
    lane = lax.broadcasted_iota(jnp.int32, (1, width), 1) // HD
    return [(lane == h).astype(F32).astype(dtype) for h in range(width // HD)]


def swap_halves(values):
    width = values.shape[1]
    lane = lax.broadcasted_iota(jnp.int32, values.shape, 1) % HD
    return jnp.where(
        lane < ROT // 2,
        pltpu.roll(values, width - ROT // 2, 1),
        pltpu.roll(values, ROT // 2, 1),
    )


def matmul(left, right):
    return lax.dot_general(left, right, (((1,), (0,)), ((), ())), preferred_element_type=F32)


def matmul_nt(left, right):
    return lax.dot_general(left, right, (((1,), (1,)), ((), ())), preferred_element_type=F32)


def matmul_tn(left, right):
    return lax.dot_general(left, right, (((0,), (0,)), ((), ())), preferred_element_type=F32)


def mix_kernel(x_ref, w_ref, c_ref, cos_ref, sin_ref, out_ref):
    mixed = matmul(x_ref[...], w_ref[...]) + c_ref[...]
    cosine, sine = cos_ref[...], sin_ref[...]
    for start in range(0, w_ref.shape[1], 3 * 128):
        query = mixed[:, start : start + 128]
        key = mixed[:, start + 128 : start + 256]
        query = (query * cosine + swap_halves(query) * sine) * QUERY_SCALE
        key = key * cosine + swap_halves(key) * sine
        out_ref[:, start : start + 128] = query.astype(BF)
        out_ref[:, start + 128 : start + 256] = key.astype(BF)
        out_ref[:, start + 256 : start + 384] = mixed[:, start + 256 : start + 384].astype(BF)


def mix(x, weight, shift, cosine, sine):
    length, columns = x.shape[0], weight.shape[1]
    return pl.pallas_call(
        mix_kernel,
        grid=(length // ROWS,),
        in_specs=[
            pl.BlockSpec((ROWS, D), lambda i: (i, 0)),
            pl.BlockSpec((D, columns), lambda i: (0, 0)),
            pl.BlockSpec((1, columns), lambda i: (0, 0)),
            pl.BlockSpec((ROWS, 128), lambda i: (i, 0)),
            pl.BlockSpec((ROWS, 128), lambda i: (i, 0)),
        ],
        out_specs=pl.BlockSpec((ROWS, columns), lambda i: (i, 0)),
        out_shape=jax.ShapeDtypeStruct((length, columns), BF),
        compiler_params=pltpu.CompilerParams(vmem_limit_bytes=VMEM_LIMIT),
        cost_estimate=pl.CostEstimate(
            flops=2 * length * D * columns,
            bytes_accessed=2 * (length * D + D * columns + length * columns),
            transcendentals=0,
        ),
        name="mix",
    )(x, weight, shift, cosine, sine)


def attend_kernel(q_ref, k_ref, v_ref, o_ref, lse_ref, acc_ref, turned_ref):
    block, width = q_ref.shape
    heads = width // HD
    i = pl.program_id(0)
    query = q_ref[...]
    queries = [query * mask for mask in head_masks(width, BF)]

    @pl.when(i == 0)
    def _():
        turned_ref[...] = v_ref[...].T

    acc_ref[...] = jnp.zeros(acc_ref.shape, F32)

    def tile(j, diagonal, carry):
        rows = pl.ds(pl.multiple_of(j * block, block), block)
        key = k_ref[rows, :]
        scores = [matmul_nt(key, queries[h]) for h in range(heads)]
        if diagonal:
            row = lax.broadcasted_iota(jnp.int32, (block, block), 0)
            column = lax.broadcasted_iota(jnp.int32, (block, block), 1)
            allowed = row <= column
            scores = [jnp.where(allowed, score, MASK_VALUE) for score in scores]
        highs = [
            jnp.maximum(carry[h][0], jnp.max(scores[h], 0, keepdims=True)) for h in range(heads)
        ]
        weights = [jnp.exp(scores[h] - highs[h]) for h in range(heads)]
        fades = [jnp.exp(carry[h][0] - highs[h]) for h in range(heads)]
        sums = [
            carry[h][1] * fades[h] + jnp.sum(weights[h], 0, keepdims=True) for h in range(heads)
        ]
        for h in range(heads):
            part = slice(h * HD, (h + 1) * HD)
            product = matmul(turned_ref[part, rows], weights[h].astype(BF))
            acc_ref[part, :] = acc_ref[part, :] * fades[h] + product
        return [(highs[h], sums[h]) for h in range(heads)]

    empty = (jnp.full((1, block), MASK_VALUE, F32), jnp.zeros((1, block), F32))
    carry = lax.fori_loop(0, i, lambda j, carry: tile(j, False, carry), [empty] * heads)
    carry = tile(i, True, carry)
    for h in range(heads):
        part = slice(h * HD, (h + 1) * HD)
        acc_ref[part, :] = acc_ref[part, :] / carry[h][1]
        lse_ref[h : h + 1, :] = carry[h][0] + jnp.log(carry[h][1])
    o_ref[...] = acc_ref[...].T.astype(BF)


def attend(mixed, half):
    length, width = mixed.shape[0], 128
    heads = width // HD
    block = min(BLOCK, length)
    return pl.pallas_call(
        attend_kernel,
        grid=(length // block,),
        in_specs=[
            pl.BlockSpec((block, width), lambda i: (i, 3 * half)),
            pl.BlockSpec((length, width), lambda i: (0, 3 * half + 1)),
            pl.BlockSpec((length, width), lambda i: (0, 3 * half + 2)),
        ],
        out_specs=[
            pl.BlockSpec((block, width), lambda i: (i, 0)),
            pl.BlockSpec((heads, block), lambda i: (0, i)),
        ],
        out_shape=[
            jax.ShapeDtypeStruct((length, width), BF),
            jax.ShapeDtypeStruct((heads, length), F32),
        ],
        scratch_shapes=[
            pltpu.VMEM((width, block), F32),
            pltpu.VMEM((width, length), BF),
        ],
        compiler_params=pltpu.CompilerParams(vmem_limit_bytes=VMEM_LIMIT),
        cost_estimate=pl.CostEstimate(
            flops=8 * length * length * width,
            bytes_accessed=8 * length * width,
            transcendentals=length * length * heads,
        ),
        name="attend",
    )(mixed, mixed, mixed)


def attend_back_kernel(
    q_ref,
    k_ref,
    v_ref,
    do_ref,
    o_ref,
    lse_ref,
    cos_ref,
    sin_ref,
    out_ref,
    total_ref,
    inner_ref,
    dq_ref,
    dk_ref,
    dv_ref,
):
    block, width = k_ref.shape
    length = q_ref.shape[0]
    heads = width // HD
    steps = length // block
    j = pl.program_id(0)
    masks = head_masks(width, BF)
    key = k_ref[...]
    value = v_ref[...]
    keys = [key * mask for mask in masks]
    values = [value * mask for mask in masks]

    @pl.when(j == 0)
    def _():
        dq_ref[...] = jnp.zeros(dq_ref.shape, F32)
        total_ref[...] = jnp.zeros(total_ref.shape, F32)
        product = do_ref[...].astype(F32) * o_ref[...].astype(F32)
        coarse = product.astype(BF)
        fine = (product - coarse.astype(F32)).astype(BF)
        row = lax.broadcasted_iota(jnp.int32, (8, width), 0)
        lane = lax.broadcasted_iota(jnp.int32, (8, width), 1) // HD
        chosen = (row == lane).astype(F32).astype(BF)
        inner_ref[...] = matmul_nt(chosen, coarse) + matmul_nt(chosen, fine)

    dk_ref[...] = jnp.zeros(dk_ref.shape, F32)
    dv_ref[...] = jnp.zeros(dv_ref.shape, F32)

    def tile(i, diagonal):
        rows = pl.ds(pl.multiple_of(i * block, block), block)
        query = q_ref[rows, :]
        grad = do_ref[rows, :]
        log_total = lse_ref[:, rows]
        inner = inner_ref[:, rows]
        scores = [matmul_nt(keys[h], query) for h in range(heads)]
        weight_grads = [matmul_nt(values[h], grad) for h in range(heads)]
        if diagonal:
            row = lax.broadcasted_iota(jnp.int32, (block, block), 0)
            column = lax.broadcasted_iota(jnp.int32, (block, block), 1)
            allowed = row <= column
            scores = [jnp.where(allowed, score, MASK_VALUE) for score in scores]
        weights = [jnp.exp(scores[h] - log_total[h : h + 1, :]) for h in range(heads)]
        low = [weight.astype(BF) for weight in weights]
        score_grads = [
            (weights[h] * (weight_grads[h] - inner[h : h + 1, :])).astype(BF)
            for h in range(heads)
        ]
        dv_ref[...] += matmul(
            jnp.concatenate(low, 1), jnp.concatenate([grad * mask for mask in masks], 0)
        )
        dk_ref[...] += matmul(
            jnp.concatenate(score_grads, 1),
            jnp.concatenate([query * mask for mask in masks], 0),
        )
        dq_ref[rows, :] += matmul_tn(
            jnp.concatenate(score_grads, 0), jnp.concatenate(keys, 0)
        )

    def step(i, carry):
        tile(i, False)
        return carry

    tile(j, True)
    lax.fori_loop(j + 1, steps, step, 0)

    own = pl.ds(pl.multiple_of(j * block, block), block)
    cosine = cos_ref[own, :]
    sine = sin_ref[own, :]
    key_grad = dk_ref[...]
    key_grad = key_grad * cosine - swap_halves(key_grad) * sine
    value_grad = dv_ref[...]
    query_grad = dq_ref[own, :] * QUERY_SCALE
    query_grad = query_grad * cosine - swap_halves(query_grad) * sine
    out_ref[:, :width] = query_grad.astype(BF)
    out_ref[:, width : 2 * width] = key_grad.astype(BF)
    out_ref[:, 2 * width :] = value_grad.astype(BF)
    total_ref[:, :width] += jnp.sum(query_grad, 0, keepdims=True)
    total_ref[:, width : 2 * width] += jnp.sum(key_grad, 0, keepdims=True)
    total_ref[:, 2 * width :] += jnp.sum(value_grad, 0, keepdims=True)


def attend_back(mixed, grads, attended, log_total, cosine, sine, half):
    length, width = mixed.shape[0], 128
    heads = width // HD
    block = min(BLOCK, length)
    return pl.pallas_call(
        attend_back_kernel,
        grid=(length // block,),
        in_specs=[
            pl.BlockSpec((length, width), lambda j: (0, 3 * half)),
            pl.BlockSpec((block, width), lambda j: (j, 3 * half + 1)),
            pl.BlockSpec((block, width), lambda j: (j, 3 * half + 2)),
            pl.BlockSpec((length, width), lambda j: (0, half)),
            pl.BlockSpec((length, width), lambda j: (0, 0)),
            pl.BlockSpec((heads, length), lambda j: (0, 0)),
            pl.BlockSpec((length, 128), lambda j: (0, 0)),
            pl.BlockSpec((length, 128), lambda j: (0, 0)),
        ],
        out_specs=[
            pl.BlockSpec((block, 3 * width), lambda j: (j, 0)),
            pl.BlockSpec((1, 3 * width), lambda j: (0, 0)),
        ],
        out_shape=[
            jax.ShapeDtypeStruct((length, 3 * width), BF),
            jax.ShapeDtypeStruct((1, 3 * width), F32),
        ],
        scratch_shapes=[
            pltpu.VMEM((8, length), F32),
            pltpu.VMEM((length, width), F32),
            pltpu.VMEM((block, width), F32),
            pltpu.VMEM((block, width), F32),
        ],
        compiler_params=pltpu.CompilerParams(vmem_limit_bytes=VMEM_LIMIT),
        cost_estimate=pl.CostEstimate(
            flops=20 * length * length * width,
            bytes_accessed=16 * length * width,
            transcendentals=length * length * heads,
        ),
        name="attend_back",
    )(mixed, mixed, mixed, grads, attended, log_total, cosine, sine)


def gelu_pair(values):
    size = jnp.abs(values) * (1.0 / math.sqrt(2.0))
    bell = jnp.exp(-size * size)
    turn = 1.0 / (1.0 + 0.3275911 * size)
    series = turn * (
        0.254829592
        + turn * (-0.284496736 + turn * (1.421413741 + turn * (-1.453152027 + turn * 1.061405429)))
    )
    tail = 0.5 * series * bell
    below = jnp.where(values < 0.0, tail, 1.0 - tail)
    slope = below + values * bell * (1.0 / math.sqrt(2.0 * math.pi))
    return values * below, slope


def chip_rows(own, length):
    chips = lax.axis_size("seq") // 2
    y = lax.axis_index("seq") // 2
    per = length // ROWS // chips
    if own:
        return per, lambda i, y_ref: y_ref[0] * per + i, y
    return (
        (chips - 1) * per,
        lambda i, y_ref: (y_ref[0] + chips - 1 - i // per) % chips * per + i % per,
        y,
    )


def feed_kernel(y_ref, x_ref, wi_ref, ci_ref, wd_ref, wo_ref, *refs):
    attended = refs[: wo_ref.shape[0] // 128]
    act_ref, slope_ref, out_ref = refs[-3:]
    hidden = matmul(x_ref[...], wi_ref[...]) + ci_ref[...]
    activated, slope = gelu_pair(hidden)
    activated = activated.astype(BF)
    act_ref[...] = activated
    slope_ref[...] = slope.astype(BF)
    out = matmul(activated, wd_ref[...])
    for half, o_ref in enumerate(attended):
        out = out + matmul(o_ref[...], wo_ref[half * 128 : (half + 1) * 128, :])
    out_ref[...] = out.astype(BF)


def feed(x, expand, shift, shrink, output, attended, own, kept=()):
    length, units, width = x.shape[0], expand.shape[1], output.shape[0]
    steps, row, y = chip_rows(own, length)

    def rows(columns):
        return pl.BlockSpec((ROWS, columns), lambda i, y_ref: (row(i, y_ref), 0))

    def whole(shape):
        return pl.BlockSpec(shape, lambda i, y_ref: (0, 0))

    first = 6 + len(attended)
    return pl.pallas_call(
        feed_kernel,
        grid_spec=pltpu.PrefetchScalarGridSpec(
            num_scalar_prefetch=1,
            grid=(steps,),
            in_specs=[rows(D), whole((D, units)), whole((1, units)), whole((units, D))]
            + [whole((width, D))]
            + [rows(128)] * len(attended)
            + [pl.BlockSpec(memory_space=pl.ANY)] * len(kept),
            out_specs=[
                rows(units),
                rows(units),
                pl.BlockSpec((ROWS, D), lambda i, y_ref: (i, 0)),
            ],
        ),
        out_shape=[
            jax.ShapeDtypeStruct((length, units), BF),
            jax.ShapeDtypeStruct((length, units), BF),
            jax.ShapeDtypeStruct((steps * ROWS, D), BF),
        ],
        input_output_aliases={first: 0, first + 1: 1} if kept else {},
        compiler_params=pltpu.CompilerParams(vmem_limit_bytes=VMEM_LIMIT),
        cost_estimate=pl.CostEstimate(
            flops=2 * steps * ROWS * D * (2 * units + width),
            bytes_accessed=2 * (2 * D * units + 2 * steps * ROWS * (D + units)),
            transcendentals=steps * ROWS * units,
        ),
        name="feed",
    )(y.reshape(1), x, expand, shift, shrink, output, *attended, *kept)


def norm_grad_kernel(y_ref, h_ref, wi_ref, wm_ref, *refs):
    out = matmul_nt(h_ref[...], wi_ref[...])
    for half, m_ref in enumerate(refs[:-1]):
        out = out + matmul_nt(m_ref[...], wm_ref[:, half * 384 : (half + 1) * 384])
    refs[-1][...] = out.astype(BF)


def norm_grad(hidden, expand, mixed, mixing, own):
    length, units, columns = hidden.shape[0], expand.shape[1], mixing.shape[1]
    steps, row, y = chip_rows(own, length)

    def rows(count):
        return pl.BlockSpec((ROWS, count), lambda i, y_ref: (row(i, y_ref), 0))

    def whole(shape):
        return pl.BlockSpec(shape, lambda i, y_ref: (0, 0))

    return pl.pallas_call(
        norm_grad_kernel,
        grid_spec=pltpu.PrefetchScalarGridSpec(
            num_scalar_prefetch=1,
            grid=(steps,),
            in_specs=[rows(units), whole((D, units)), whole((D, columns))]
            + [rows(384)] * len(mixed),
            out_specs=pl.BlockSpec((ROWS, D), lambda i, y_ref: (i, 0)),
        ),
        out_shape=jax.ShapeDtypeStruct((steps * ROWS, D), BF),
        compiler_params=pltpu.CompilerParams(vmem_limit_bytes=VMEM_LIMIT),
        cost_estimate=pl.CostEstimate(
            flops=2 * steps * ROWS * D * (units + columns),
            bytes_accessed=2 * (D + steps * ROWS) * (units + columns),
            transcendentals=0,
        ),
        name="norm_grad",
    )(y.reshape(1), hidden, expand, mixing, *mixed)


def home_spans(parts, copies, width, units):
    mixing, expand = [], []
    size = units // copies
    for p in range(parts):
        for half in range(width // 128):
            for kind in range(3):
                at = kind * parts * width + p * width + half * 128
                mixing.append((p, half * 384 + kind * 128, at, 128))
        for d in range(copies):
            expand.append((p, 3 * width + d * size, (d * parts + p) * size, size))
    return mixing, expand


def adam(grad, weight, first, second, average, rate, decay):
    first_new = BETA_FIRST * first + (1.0 - BETA_FIRST) * grad
    second_new = BETA_SECOND * second + (1.0 - BETA_SECOND) * grad * grad
    first_hat = first_new / (1.0 - BETA_FIRST**STEP)
    second_hat = second_new / (1.0 - BETA_SECOND**STEP)
    weight_new = weight - rate * (
        first_hat / (jnp.sqrt(second_hat) + ADAM_EPS) + decay * weight
    )
    return weight_new, first_new, second_new, EMA_DECAY * average + (1.0 - EMA_DECAY) * weight_new


def adam_kernel(spans, rates, clip_ref, exchanged_ref, output_ref, shrink_ref, *refs):
    clip = clip_ref[0]
    states, news = refs[:16], refs[16:]

    def step(kind, grad, columns):
        old = [ref[0, :, columns] for ref in states[4 * kind : 4 * kind + 4]]
        new = adam(grad.astype(F32) * clip, *old, rates[kind], WEIGHT_DECAY)
        for ref, value in zip(news[4 * kind : 4 * kind + 4], new):
            ref[0, :, columns] = value

    for kind, part in ((0, spans[0]), (2, spans[1])):
        for source, start, at, count in part:
            grad = exchanged_ref[0, source, :, start : start + count]
            step(kind, grad, slice(at, at + count))
    step(1, output_ref[0], slice(None))
    step(3, shrink_ref[0], slice(None))


def update(clip, exchanged, output, shrink, states, spans, rates):
    layers, parts, rows, columns = exchanged.shape
    chunk = 16 if rows % 16 == 0 else rows
    chunks = rows // chunk

    def block(array):
        size = array.shape[1] // chunks
        return pl.BlockSpec((1, size, array.shape[2]), lambda l, n: (l, n, 0))

    return pl.pallas_call(
        partial(adam_kernel, spans, rates),
        grid=(layers, chunks),
        in_specs=[
            pl.BlockSpec(memory_space=pltpu.SMEM),
            pl.BlockSpec((1, parts, chunk, columns), lambda l, n: (l, 0, n, 0)),
            block(output),
            block(shrink),
        ]
        + [block(state) for state in states],
        out_specs=[block(state) for state in states],
        out_shape=[jax.ShapeDtypeStruct(state.shape, F32) for state in states],
        compiler_params=pltpu.CompilerParams(vmem_limit_bytes=VMEM_LIMIT),
        name="update",
    )(clip, exchanged, output, shrink, *states)


def rotary_tables(positions):
    half = ROT // 2
    steps_half = jnp.arange(half).astype(F32)
    frequency = 10000.0 ** (-2.0 * steps_half / ROT)
    angles = positions.astype(F32)[None, :] * frequency[:, None]
    cosine = jnp.concatenate([jnp.cos(angles), jnp.ones_like(angles)], 0)
    entry = jnp.arange(128)[None, :] % HD
    index = jnp.arange(half)[:, None]
    turning = (entry < ROT) & (entry % half == index)
    still = (entry >= ROT) & (index == 0)
    sign = jnp.where(entry < half, -1.0, 1.0)
    spread_cosine = jnp.concatenate([turning, still], 0).astype(F32)
    spread_sine = turning.astype(F32) * sign

    def lay(table, spread):
        return lax.dot_general(
            table, spread, (((0,), (0,)), ((), ())), precision=lax.Precision.HIGHEST
        )

    return lay(cosine, spread_cosine), lay(jnp.sin(angles), spread_sine)


def split_affine(affine):
    bounds = [D, D, D, D, 3 * D, D, FF, D]
    pieces = []
    offset = 0
    for length in bounds:
        pieces.append(affine[offset : offset + length])
        offset = offset + length
    return pieces


def normalize(values):
    centre = values - jnp.mean(values, -1, keepdims=True)
    spread = jnp.mean(centre * centre, -1, keepdims=True)
    scale = lax.rsqrt(spread + NORM_EPS)
    return centre * scale, scale


def local(
    stream,
    cotangent,
    positions,
    mixing_weight,
    mixing_first,
    mixing_second,
    mixing_average,
    output_weight,
    output_first,
    output_second,
    output_average,
    expand_weight,
    expand_first,
    expand_second,
    expand_average,
    shrink_weight,
    shrink_first,
    shrink_second,
    shrink_average,
    affine_weight,
    affine_first,
    affine_second,
    affine_average,
):
    parts = lax.axis_size("seq")
    copies = lax.axis_size("dp")
    devices = parts * copies
    part = lax.axis_index("seq")
    width = D // parts
    units = FF // parts
    rows_d = D // devices
    rows_f = FF // devices
    rows = stream.shape[0] * stream.shape[1]
    small = affine_weight.shape[1]

    halves = width // 128
    outer = dp_parts()[0]

    def mixing_part(vector):
        view = vector.reshape(3, parts, halves, 128)
        view = lax.dynamic_index_in_dim(view, part, 1, keepdims=False)
        return view.transpose(1, 0, 2).reshape(-1)

    def expand_part(vector):
        view = vector.reshape(copies, parts, -1)
        return lax.dynamic_index_in_dim(view, part, 1, keepdims=False).reshape(-1)

    def spread_mixing(vector):
        view = jnp.zeros((3, parts, width), F32)
        vector = vector.reshape(halves, 3, 128).transpose(1, 0, 2).reshape(3, 1, width)
        return lax.dynamic_update_slice(view, vector, (0, part, 0)).reshape(-1)

    def spread_expand(vector):
        view = jnp.zeros((copies, parts, rows_f), F32)
        return lax.dynamic_update_slice(view, vector.reshape(copies, 1, rows_f), (0, part, 0)).reshape(-1)

    def arrange(mixing, expand):
        mixing = mixing.astype(BF).reshape(rows_d, 3, parts, halves, 128)
        mixing = mixing.transpose(2, 0, 3, 1, 4).reshape(parts, rows_d, 3 * width)
        expand = expand.astype(BF).reshape(rows_d, copies, parts, rows_f)
        expand = expand.transpose(2, 0, 1, 3).reshape(parts, rows_d, units)
        return [mixing, expand]

    def settle_output(gathered):
        gathered = gathered.reshape(parts, copies // parts * rows_d, D)
        output = seq_exchange(gathered).reshape(parts, copies // parts, rows_d, D)
        return output.transpose(1, 0, 2, 3).reshape(width, D)

    def scaled(weight, gain, shift, bias):
        wide = weight.astype(F32)
        return (wide * gain[:, None]).astype(BF), (jnp.sum(wide * shift[:, None], 0) + bias)[None]

    def shift_grads(raw, weight, total, gain, shift):
        wide = weight.astype(F32)
        return (
            (raw * gain[:, None] + shift[:, None] * total).astype(BF),
            jnp.sum(raw * wide, 1),
            jnp.sum(wide * total, 1),
        )

    def norm_back(gradient, normed_grad, own_normed, scale):
        projected = jnp.mean(normed_grad * own_normed, -1, keepdims=True)
        middle = jnp.mean(normed_grad, -1, keepdims=True)
        return gradient + scale * (normed_grad - middle - own_normed * projected)

    def outgoing_output(attended, grads):
        output_grad = jnp.concatenate([matmul_tn(out, grads).astype(BF) for out in attended], 0)
        output_grad = output_grad.reshape(copies // parts, parts, rows_d, D).transpose(1, 0, 2, 3)
        output_grad = seq_exchange(output_grad.reshape(parts, copies // parts * rows_d, D))
        return output_grad.reshape(-1, width)

    def affine_home(pieces):
        affine_grad = lax.all_to_all(
            jnp.concatenate(pieces).reshape(devices, small),
            ("dp", "seq"),
            split_axis=0,
            concat_axis=0,
            tiled=True,
        )
        return jnp.sum(affine_grad, 0)

    def sum_squares(*values):
        return sum(jnp.sum(value.astype(F32) * value.astype(F32)) for value in values)

    current = stream.reshape(rows, D)
    gradient = cotangent.reshape(rows, D)

    pair = jnp.stack([positions.reshape(-1) // 16, positions.reshape(-1) % 16]).astype(BF)
    pair = jnp.broadcast_to(pair.reshape(1, rows_d, -1), (parts, rows_d, 2 * rows // rows_d))
    both = jnp.concatenate(arrange(mixing_weight[0], expand_weight[0]) + [pair], -1)
    both = seq_exchange(both)
    pair = both[..., 3 * width + units :].astype(F32).reshape(parts, 2, rows)
    places = (pair[:, 0] * 16.0 + pair[:, 1]).reshape(-1)
    both = both.reshape(parts * rows_d, -1)
    near = Gather(
        jnp.concatenate(
            [both[:, : 3 * width], output_weight[0].astype(BF).reshape(-1, width)], -1
        )
    )
    affine_low, near.pieces = lax.optimization_barrier((affine_weight.astype(BF), near.pieces))
    affine_low = affine_low.reshape(1, LAYERS * small)
    affine_all = lax.all_to_all(
        jnp.broadcast_to(affine_low, (devices, LAYERS * small)),
        ("dp", "seq"),
        split_axis=0,
        concat_axis=0,
        tiled=True,
    )
    affine_all = affine_all.reshape(devices, LAYERS, small).transpose(1, 0, 2)
    affine_all = affine_all.reshape(LAYERS, devices * small).astype(F32)
    vectors = [split_affine(affine_all[layer]) for layer in range(LAYERS)]
    own_normed, scale = normalize(current)
    normed = seq_gather(own_normed.astype(BF))
    for step in range(outer - 1):
        near.forward()
        near.cross()
    expand_own, shrink_own, places = near.hold(
        both[:, 3 * width : 3 * width + units], shrink_weight[0], places
    )
    near.cross()
    far = Gather(
        jnp.concatenate([expand_own, shrink_own.astype(BF).reshape(-1, units)], -1)
    )
    far.forward()
    far.cross()
    cosine, sine = rotary_tables(places)
    gathered = near.done()
    mixing = gathered[:, : 3 * width]
    output = settle_output(gathered[:, 3 * width :].reshape(copies * rows_d, D))

    later = far.hold(
        *(weight[1] for weight in (mixing_weight, expand_weight, output_weight, shrink_weight))
    )
    later_both = seq_exchange(jnp.concatenate(arrange(later[0], later[1]), -1))
    later_both = later_both.reshape(parts * rows_d, -1)
    later_own = jnp.concatenate(
        [
            later_both[:, : 3 * width],
            later[2].astype(BF).reshape(-1, width),
            later_both[:, 3 * width :],
            later[3].astype(BF).reshape(-1, units),
        ],
        -1,
    )
    later_all = lax.all_gather(later_own, "dp", axis=0, tiled=True)

    gain_one, shift_one, gain_two, shift_two = vectors[0][:4]
    mixing_scaled, mixing_shift = scaled(mixing, gain_one, shift_one, mixing_part(vectors[0][4]))
    mixed = mix(normed, mixing_scaled, mixing_shift, cosine, sine)
    mixed, low_gradient = far.hold(mixed, gradient.astype(BF))
    grads = seq_gather(low_gradient)
    attended, logs = [], []
    for half in range(halves):
        if len(far.pieces) < outer:
            far.forward()
            far.cross()
        out, log_total = attend(mixed, half)
        mixed, out, log_total, grads = far.hold(mixed, out, log_total, grads)
        attended.append(out)
        logs.append(log_total)
    while len(far.pieces) < outer:
        far.forward()
    while len(far.chains) < outer:
        far.cross()
    gathered = far.done()
    expand, shrink = gathered[:, :units], gathered[:, units:].reshape(-1, D)
    expand_scaled, expand_shift = scaled(
        expand, gain_two, shift_two, expand_part(vectors[0][6])
    )
    weight_set = (normed, expand_scaled, expand_shift, shrink, output, attended)
    activated, slope, others = feed(*weight_set, False)
    activated, slope, own = feed(*weight_set, True, (activated, slope))
    stored = [(own_normed, scale, normed, mixed, attended, logs, activated, slope)]
    weights = [(mixing, mixing_scaled, output, expand, expand_scaled, shrink)]
    current = current + SeqScatter(others, own).done() + vectors[0][5] + vectors[0][7]

    own_normed, scale = normalize(current)
    normed = seq_gather(own_normed.astype(BF))
    mixing = later_all[:, : 3 * width]
    output = settle_output(later_all[:, 3 * width : 4 * width].reshape(copies * rows_d, D))
    expand = later_all[:, 4 * width : 4 * width + units]
    shrink = later_all[:, 4 * width + units :].reshape(-1, D)
    gain_one, shift_one, gain_two, shift_two = vectors[1][:4]
    mixing_scaled, mixing_shift = scaled(mixing, gain_one, shift_one, mixing_part(vectors[1][4]))
    expand_scaled, expand_shift = scaled(
        expand, gain_two, shift_two, expand_part(vectors[1][6])
    )
    mixed = mix(normed, mixing_scaled, mixing_shift, cosine, sine)
    attended, logs = [], []
    for half in range(halves):
        out, log_total = attend(mixed, half)
        attended.append(out)
        logs.append(log_total)
    weight_set = (normed, expand_scaled, expand_shift, shrink, output, attended)
    activated, slope, others = feed(*weight_set, False)
    activated, slope, own = feed(*weight_set, True, (activated, slope))
    result = current + SeqScatter(others, own).done() + vectors[1][5] + vectors[1][7]
    result = result.reshape(stream.shape)

    attended_grad = matmul_nt(grads, output).astype(BF)
    shrink_grad = matmul_tn(activated, grads).astype(BF).reshape(-1, units)
    output_grad = outgoing_output(attended, grads)
    later_first = lax.psum_scatter(
        jnp.concatenate([shrink_grad, output_grad], -1), "dp", scatter_dimension=0, tiled=True
    )
    hidden_grad = matmul_nt(grads, shrink) * slope.astype(F32)
    hidden_total = jnp.sum(hidden_grad, 0)
    hidden_low = hidden_grad.astype(BF)
    lows, totals = [], []
    for half in range(halves):
        low, total = attend_back(
            mixed, attended_grad, attended[half], logs[half], cosine, sine, half
        )
        lows.append(low)
        totals.append(total[0])
    mixed_total = jnp.concatenate(totals)
    output_sum = jnp.sum(gradient, 0)
    others = norm_grad(hidden_low, expand_scaled, lows, mixing_scaled, False)
    own = norm_grad(hidden_low, expand_scaled, lows, mixing_scaled, True)
    travel = SeqScatter(others, own)
    hidden_low, lows = travel.hold(hidden_low, lows)
    expand_raw = matmul_tn(normed, hidden_low)
    mixing_raw = jnp.concatenate([matmul_tn(normed, low) for low in lows], -1)
    expand_grad, gain_two_grad, shift_two_grad = shift_grads(
        expand_raw, expand, hidden_total, gain_two, shift_two
    )
    mixing_grad, gain_one_grad, shift_one_grad = shift_grads(
        mixing_raw, mixing, mixed_total, gain_one, shift_one
    )
    pieces = [gain_one_grad, shift_one_grad, gain_two_grad, shift_two_grad]
    pieces += [spread_mixing(mixed_total), output_sum, spread_expand(hidden_total), output_sum]
    normed_grad, expand_grad, mixing_grad, pieces = lax.optimization_barrier(
        (travel.done(), expand_grad, mixing_grad, pieces)
    )
    gradient = norm_back(gradient, normed_grad, own_normed, scale)
    low_gradient, expand_grad, mixing_grad, pieces = lax.optimization_barrier(
        (gradient.astype(BF), expand_grad, mixing_grad, pieces)
    )
    grads = seq_gather(low_gradient)
    later_second = lax.psum_scatter(
        jnp.concatenate([mixing_grad, expand_grad], -1), "dp", scatter_dimension=0, tiled=True
    )
    later_affine = affine_home(pieces)

    own_normed, scale, normed, mixed, attended, logs, activated, slope = stored[0]
    mixing, mixing_scaled, output, expand, expand_scaled, shrink = weights[0]
    gain_one, shift_one, gain_two, shift_two = vectors[0][:4]
    shrink_grad = matmul_tn(activated, grads).astype(BF).reshape(-1, units)
    hidden_grad = matmul_nt(grads, shrink) * slope.astype(F32)
    hidden_total = jnp.sum(hidden_grad, 0)
    hidden_low = hidden_grad.astype(BF)
    expand_raw = matmul_tn(normed, hidden_low)
    expand_grad, gain_two_grad, shift_two_grad = shift_grads(
        expand_raw, expand, hidden_total, gain_two, shift_two
    )
    attended_grad = matmul_nt(grads, output).astype(BF)
    far = Scatter(expand_grad, shrink_grad)
    (attended_grad,) = far.hold(attended_grad)
    far.cross()
    output_grad = outgoing_output(attended, grads)
    lows, totals = [], []
    for half in range(halves):
        low, total = attend_back(
            mixed, attended_grad, attended[half], logs[half], cosine, sine, half
        )
        mixed, low, total = far.hold(mixed, low, total)
        if len(far.parts) < outer:
            far.forward()
            far.cross()
        lows.append(low)
        totals.append(total[0])
    mixed_total = jnp.concatenate(totals)
    mixing_raw = jnp.concatenate([matmul_tn(normed, low) for low in lows], -1)
    mixing_grad, gain_one_grad, shift_one_grad = shift_grads(
        mixing_raw, mixing, mixed_total, gain_one, shift_one
    )
    mixing_grad, lows = far.hold(mixing_grad, lows)
    while len(far.parts) < outer:
        far.forward()
        far.cross()
    near = Scatter(mixing_grad, output_grad)
    near.cross()
    while far.steps < outer - 1:
        far.forward()
    others = norm_grad(hidden_low, expand_scaled, lows, mixing_scaled, False)
    own = norm_grad(hidden_low, expand_scaled, lows, mixing_scaled, True)
    travel = SeqScatter(others, own)
    for step in range(outer - 1):
        near.forward()
        near.cross()
    output_sum = jnp.sum(gradient, 0)
    pieces = [gain_one_grad, shift_one_grad, gain_two_grad, shift_two_grad]
    pieces += [spread_mixing(mixed_total), output_sum, spread_expand(hidden_total), output_sum]
    affine_grad = jnp.stack([affine_home(pieces), later_affine])
    gradient = norm_back(gradient, travel.done(), own_normed, scale)
    stream_grad = gradient.reshape(stream.shape)

    later_home = seq_exchange(later_second.reshape(parts, rows_d, -1))
    far_grad = far.done()
    near_grad = near.done()
    home = jnp.concatenate([near_grad[:, : 3 * width], far_grad[:, :units]], -1).astype(BF)
    home = seq_exchange(home.reshape(parts, rows_d, -1))
    squares = sum_squares(near_grad, far_grad, later_first, later_second, affine_grad)
    squares = lax.all_to_all(
        jnp.broadcast_to(squares, (devices, 128)),
        ("dp", "seq"),
        split_axis=0,
        concat_axis=0,
        tiled=True,
    )
    gradient_norm = jnp.sqrt(jnp.sum(squares[:, 0]))
    clip_scale = jnp.minimum(1.0, CLIP_LIMIT / (gradient_norm + 1e-06))
    exchanged = jnp.stack([home, later_home])
    output_grad = jnp.stack(
        [near_grad[:, 3 * width :].astype(BF), later_first[:, units:]]
    ).reshape(LAYERS, rows_d, D)
    shrink_grad = jnp.stack([far_grad[:, units:].astype(BF), later_first[:, :units]])
    shrink_grad = shrink_grad.reshape(LAYERS, rows_f, D)
    spans = home_spans(parts, copies, width, units)
    if rows_f % 128 or rows_d % 16:
        mixing_view = exchanged[..., : 3 * width].reshape(LAYERS, parts, rows_d, halves, 3, 128)
        mixing_view = mixing_view.transpose(0, 2, 4, 1, 3, 5).reshape(LAYERS, rows_d, 3 * D)
        expand_view = exchanged[..., 3 * width :].reshape(LAYERS, parts, rows_d, copies, rows_f)
        expand_view = expand_view.transpose(0, 2, 3, 1, 4).reshape(LAYERS, rows_d, FF)
        exchanged = jnp.concatenate([mixing_view, expand_view], -1)[:, None]
        spans = ([(0, 0, 0, 3 * D)], [(0, 3 * D, 0, FF)])
    states = (
        (mixing_weight, mixing_first, mixing_second, mixing_average)
        + (output_weight, output_first, output_second, output_average)
        + (expand_weight, expand_first, expand_second, expand_average)
        + (shrink_weight, shrink_first, shrink_second, shrink_average)
    )
    rates = (D ** (-0.5), (D * 32 // LEN) ** (-0.5), D ** (-0.5), FF ** (-0.5))
    updated = update(
        clip_scale.reshape(1), exchanged, output_grad, shrink_grad, states, spans, rates
    )
    affine_new = adam(
        affine_grad * clip_scale,
        affine_weight,
        affine_first,
        affine_second,
        affine_average,
        SMALL_RATE,
        0.0,
    )
    return (result, stream_grad, gradient_norm) + tuple(updated) + tuple(affine_new)


def solution(mesh):
    tokens = P("dp", "seq", None)
    matrix = P(None, ("dp", "seq"), None)
    vector = P(None, ("dp", "seq"))
    states = (matrix,) * 16 + (vector,) * 4
    return jax.shard_map(
        local,
        mesh=mesh,
        in_specs=(tokens, tokens, P("dp", "seq")) + states,
        out_specs=(tokens, tokens, P()) + states,
        check_vma=False,
    )
```

time: 1110 us -> 884 us (0.80)
  waiting for transfers between devices: 295 us -> 215 us
  local copies, waits for them, and re-layouts: 174 us -> 108 us
  matrix products: 123 us -> 73.7 us
  starting transfers between devices: 156 us -> 118 us
  Pallas kernels: 230 us -> 255 us
  other arithmetic: 107 us -> 84.3 us
  between operations: 8.5 us -> 21.6 us
    ppermute x48 -> x12, waiting for transfers between devices: 131 us -> 41.4 us  [outer_ring(): lax.ppermute(value, 'dp', [(i, (i + inner) % size) for i in range(size)])]
    pallas_call x2 -> x15, Pallas kernels: 42.2 us -> 118 us  [the longest x4 51.8 us: feed(): pl.pallas_call(feed_kernel, grid_spec=pltpu.PrefetchScalarGridSpec(num_sc...]
    dynamic_update_slice x84 -> x4, local copies, waits for them, and re-layouts: 62.2 us -> 0.59 us  [the longest x2 0.48 us: spread_expand(): lax.dynamic_update_slice(view, vector.reshape(copies, 1, rows_f), (0, par...]
    pallas_call x2 -> x4, Pallas kernels: 94.5 us -> 40.4 us  [attend(): pl.pallas_call(attend_kernel, grid=(length // block,), in_specs=[pl.Block...]
    ppermute x64 -> x16, waiting for transfers between devices: 74.9 us -> 22.3 us  [inner_ring(): return lax.ppermute(value, 'dp', moves)]
    ppermute x9 -> x8, waiting for transfers between devices: 72.2 us -> 124 us  [chip_ring(): lax.ppermute(value, 'seq', [(i, (i + 2) % size) for i in range(size)])]
    ppermute x64 -> x16, starting transfers between devices: 69.5 us -> 19.1 us  [inner_ring(): return lax.ppermute(value, 'dp', moves)]
    dot_general x8 -> x4, matrix products: 66.5 us -> 20.9 us  [matmul_nt(): lax.dot_general(left, right, (((1,), (1,)), ((), ())), preferred_element_...]
  transfers between devices with their start and end apart: 151 -> 67, of which waited for: 71 -> 26; matrix products, arithmetic and copies ran while one was open for 29% -> 25% of each run, Pallas kernels for 12% -> 25%
where the time goes in v2:
time: 884 us; the launch traced here: 875 us
  Pallas kernels  255 us (29%)
  waiting for transfers between devices  215 us (24%)
  starting transfers between devices  118 us (13%)
  local copies, waits for them, and re-layouts  108 us (12%)
  other arithmetic  84.3 us (10%)
  matrix products  73.7 us (8%)
  between operations  21.6 us (2%)
    ppermute x8, waiting for transfers between devices, chip_ring(): lax.ppermute(value, 'seq', [(i, (i + 2) % size) for i in range(size)])  124 us
    pallas_call x4, Pallas kernels, attend_back(): pl.pallas_call(attend_back_kernel, grid=(length // block,), in_specs=[pl....  78.5 us
    pallas_call x4, Pallas kernels, feed(): pl.pallas_call(feed_kernel, grid_spec=pltpu.PrefetchScalarGridSpec(num_sc...  51.8 us
    dot_general x12, matrix products, matmul_tn(): lax.dot_general(left, right, (((0,), (0,)), ((), ())), preferred_element_...  46.3 us
    ppermute x12, waiting for transfers between devices, outer_ring(): lax.ppermute(value, 'dp', [(i, (i + inner) % size) for i in range(size)])  41.4 us
    pallas_call x4, Pallas kernels, attend(): pl.pallas_call(attend_kernel, grid=(length // block,), in_specs=[pl.Block...  40.4 us
    unnamed x290, local copies, waits for them, and re-layouts  35.3 us
    all_to_all x8, starting transfers between devices, seq_exchange(): return lax.all_to_all(value, 'seq', split_axis=0, concat_axis=0, tiled=True)  33 us
  transfers between devices with their start and end apart: 67, of which 26 were waited for; matrix products, arithmetic and copies ran while one was open for 25% of the time, Pallas kernels for 25%

profile of v2, /device:TPU:0, one launch (start us, length us, event | category | flops | bytes accessed | tf_op | source)
XLA Modules:
  0.0 875.3 jit_solution(1706855260607327595)
XLA Ops:
  41.9 8.0 all-to-all-done.1
  73.2 7.4 collective-permute-done.10.refs_2_
  117.4 5.4 assemble.6
  122.9 9.3 %mix.2.q_ref.k_ref.v_ref = bf16[2048,768]{1,0:T(8,128)(2,1)} custom-call(bf16[2048,1024]{1,0:T(8,128)(2,1)} %bitcast.333, bf16[1024,768]{1,0:T(8,128)(2,1)S(1)} %get-tuple-element.357.w_ref.wm_ref, f32[1,768]{1,0:T(1,128)S(1)} %reshape_add_fusion.1.c_ref, f32[2048,128]{1,0:T(8,128)S(1)} %copy-done.29, f32[2048,128]{1,0:T(8,128)S(1)} %copy-done.25), custom_call_target="tpu_custom_call" | custom-call | flops 3221225472 | bytes 8912896 | tf_op jit(solution)/shard_map/mix/pallas_call | solution.py:273
  134.2 23.5 %collective-permute-done.13.refs_2_ = bf16[512,1024]{1,0:T(8,128)(2,1)S(1)} collective-permute-done((bf16[512,1024]{1,0:T(8,128)(2,1)S(1)}, bf16[512,1024]{1,0:T(8,128)(2,1)S(1)}, u32[]{:S(2)}, u32[]{:S(2)}) %collective-permute-start.13) | collective-permute-done | bytes 1048608 | tf_op jit(solution)/shard_map/ppermute | solution.py:59
  162.8 10.0 %attend.4 = (bf16[2048,128]{1,0:T(8,128)(2,1)S(1)}, f32[2,2048]{1,0:T(2,128)S(1)}) custom-call(bf16[2048,768]{1,0:T(8,128)(2,1)S(1)} %copy-done.60, bf16[2048,768]{1,0:T(8,128)(2,1)S(1)} %copy-done.60, bf16[2048,768]{1,0:T(8,128)(2,1)S(1)} %copy-done.60), custom_call_target="tpu_custom_call" | custom-call | flops 4294967296 | bytes 2097152 | tf_op jit(solution)/shard_map/attend/pallas_call | solution.py:345
  175.9 8.7 collective-permute-done.15.refs_4_
  185.5 11.6 %collective-permute-start.17 = (bf16[128,2048]{1,0:T(8,128)(2,1)}, bf16[128,2048]{1,0:T(8,128)(2,1)}, u32[]{:S(2)}, u32[]{:S(2)}) collective-permute-start(bf16[128,2048]{1,0:T(8,128)(2,1)} %collective-permute-done.15.refs_4_), channel_id=1, source_target_pairs={{0,8},{4,12},{8,16},{12,20},{16,24},{20,28},{24,0},{28,4},{1,9},{5... | collective-permute-start | bytes 1572872 | tf_op jit(solution)/shard_map/ppermute | solution.py:46
  206.1 10.0 %attend.5 = (bf16[2048,128]{1,0:T(8,128)(2,1)S(1)}, f32[2,2048]{1,0:T(2,128)S(1)}) custom-call(bf16[2048,768]{1,0:T(8,128)(2,1)S(1)} %copy-done.61, bf16[2048,768]{1,0:T(8,128)(2,1)S(1)} %copy-done.61, bf16[2048,768]{1,0:T(8,128)(2,1)S(1)} %copy-done.61), custom_call_target="tpu_custom_call" | custom-call | flops 4294967296 | bytes 2097152 | tf_op jit(solution)/shard_map/attend/pallas_call | solution.py:345
  222.4 9.6 %collective-permute-done.19.refs_7_ = bf16[128,2048]{1,0:T(8,128)(2,1)} collective-permute-done((bf16[128,2048]{1,0:T(8,128)(2,1)}, bf16[128,2048]{1,0:T(8,128)(2,1)}, u32[]{:S(2)}, u32[]{:S(2)}) %collective-permute-start.19) | collective-permute-done | bytes 524320 | tf_op jit(solution)/shard_map/ppermute | solution.py:54
  232.0 5.8 assemble.9
  241.9 13.2 %feed.4 = (bf16[2048,1024]{1,0:T(8,128)(2,1)}, bf16[2048,1024]{1,0:T(8,128)(2,1)}, bf16[1024,1024]{1,0:T(8,128)(2,1)S(1)}) custom-call(s32[1]{0:T(128)} %bitcast.1.y_ref, bf16[2048,1024]{1,0:T(8,128)(2,1)} %bitcast.334, bf16[1024,1024]{1,0:T(8,128)(2,1)S(1)} %get-tuple-element.334.wi_ref, f32[1,1024]{1,0:T(1,128)S(1)} %fusion.51.ci_ref, ...), custom_call_target="tpu_custom_call" | custom-call | flops 4831838208 | bytes 12582912 | tf_op jit(solution)/shard_map/feed/pallas_call | solution.py:563
  258.4 12.4 %feed.5 = (bf16[2048,1024]{1,0:T(8,128)(2,1)}, bf16[2048,1024]{1,0:T(8,128)(2,1)}, bf16[1024,1024]{1,0:T(8,128)(2,1)S(1)}) custom-call(s32[1]{0:T(128)} %bitcast.1.y_ref, bf16[2048,1024]{1,0:T(8,128)(2,1)} %bitcast.335, bf16[1024,1024]{1,0:T(8,128)(2,1)S(1)} %get-tuple-element.334.wi_ref, ...), custom_call_target="tpu_custom_call", output_to_operand_aliasing={{0}: (8, {}), {1}: (9, {})} | custom-call | flops 4831838208 | bytes 12582912 | tf_op jit(solution)/shard_map/feed/pallas_call | solution.py:563
  276.1 23.8 %collective-permute-done.22 = bf16[512,1024]{1,0:T(8,128)(2,1)S(1)} collective-permute-done((bf16[512,1024]{1,0:T(8,128)(2,1)S(1)}, bf16[512,1024]{1,0:T(8,128)(2,1)S(1)}, u32[]{:S(2)}, u32[]{:S(2)}) %collective-permute-start.22) | collective-permute-done | bytes 1048608 | tf_op jit(solution)/shard_map/ppermute | solution.py:59
  303.8 23.2 %collective-permute-done.24.refs_2_ = bf16[512,1024]{1,0:T(8,128)(2,1)S(1)} collective-permute-done((bf16[512,1024]{1,0:T(8,128)(2,1)S(1)}, bf16[512,1024]{1,0:T(8,128)(2,1)S(1)}, u32[]{:S(2)}, u32[]{:S(2)}) %collective-permute-start.24) | collective-permute-done | bytes 1048608 | tf_op jit(solution)/shard_map/ppermute | solution.py:59
  336.6 9.1 %mix.3.q_ref.k_ref.v_ref = bf16[2048,768]{1,0:T(8,128)(2,1)} custom-call(bf16[2048,1024]{1,0:T(8,128)(2,1)} %bitcast.339, bf16[1024,768]{1,0:T(8,128)(2,1)S(1)} %get-tuple-element.328.w_ref.wm_ref, f32[1,768]{1,0:T(1,128)S(1)} %reshape_add_fusion.c_ref, f32[2048,128]{1,0:T(8,128)S(1)} %copy-done.30, f32[2048,128]{1,0:T(8,128)S(1)} %copy-done.26), custom_call_target="tpu_custom_call" | custom-call | flops 3221225472 | bytes 8912896 | tf_op jit(solution)/shard_map/mix/pallas_call | solution.py:273
  348.7 10.4 %attend.6 = (bf16[2048,128]{1,0:T(8,128)(2,1)S(1)}, f32[2,2048]{1,0:T(2,128)S(1)}) custom-call(bf16[2048,768]{1,0:T(8,128)(2,1)S(1)} %copy-done.62, bf16[2048,768]{1,0:T(8,128)(2,1)S(1)} %copy-done.62, bf16[2048,768]{1,0:T(8,128)(2,1)S(1)} %copy-done.62), custom_call_target="tpu_custom_call" | custom-call | flops 4294967296 | bytes 2097152 | tf_op jit(solution)/shard_map/attend/pallas_call | solution.py:345
  359.2 10.0 %attend.7 = (bf16[2048,128]{1,0:T(8,128)(2,1)S(1)}, f32[2,2048]{1,0:T(2,128)S(1)}) custom-call(bf16[2048,768]{1,0:T(8,128)(2,1)S(1)} %copy-done.62, bf16[2048,768]{1,0:T(8,128)(2,1)S(1)} %copy-done.62, bf16[2048,768]{1,0:T(8,128)(2,1)S(1)} %copy-done.62), custom_call_target="tpu_custom_call" | custom-call | flops 4294967296 | bytes 2097152 | tf_op jit(solution)/shard_map/attend/pallas_call | solution.py:345
  382.7 7.2 fusion.67
  399.6 19.7 %attend_back.5 = (bf16[2048,384]{1,0:T(8,128)(2,1)S(1)}, f32[1,384]{1,0:T(1,128)S(1)}) custom-call(bf16[2048,768]{1,0:T(8,128)(2,1)} %mix.3.q_ref.k_ref.v_ref, bf16[2048,768]{1,0:T(8,128)(2,1)} %mix.3.q_ref.k_ref.v_ref, bf16[2048,768]{1,0:T(8,128)(2,1)} %mix.3.q_ref.k_ref.v_ref, bf16[2048,256]{1,0:T(8,128)(2,1)S(1)} %convolution_convert_fusion.1.do_ref, ...), custom_call_target="tpu_custom_call" | custom-call | flops 10737418240 | bytes 4194304 | tf_op jit(solution)/shard_map/attend_back/pallas_call | solution.py:474
  419.3 20.0 %attend_back.4 = (bf16[2048,384]{1,0:T(8,128)(2,1)S(1)}, f32[1,384]{1,0:T(1,128)S(1)}) custom-call(bf16[2048,768]{1,0:T(8,128)(2,1)} %mix.3.q_ref.k_ref.v_ref, bf16[2048,768]{1,0:T(8,128)(2,1)} %mix.3.q_ref.k_ref.v_ref, bf16[2048,768]{1,0:T(8,128)(2,1)} %mix.3.q_ref.k_ref.v_ref, bf16[2048,256]{1,0:T(8,128)(2,1)S(1)} %convolution_convert_fusion.1.do_ref, ...), custom_call_target="tpu_custom_call" | custom-call | flops 10737418240 | bytes 4194304 | tf_op jit(solution)/shard_map/attend_back/pallas_call | solution.py:474
  439.4 13.0 %feed.6 = (bf16[2048,1024]{1,0:T(8,128)(2,1)}, bf16[2048,1024]{1,0:T(8,128)(2,1)}, bf16[1024,1024]{1,0:T(8,128)(2,1)S(1)}) custom-call(s32[1]{0:T(128)} %bitcast.1.y_ref, bf16[2048,1024]{1,0:T(8,128)(2,1)} %bitcast.340, bf16[1024,1024]{1,0:T(8,128)(2,1)S(1)} %get-tuple-element.330.wi_ref, f32[1,1024]{1,0:T(1,128)S(1)} %fusion.53.ci_ref, ...), custom_call_target="tpu_custom_call" | custom-call | flops 4831838208 | bytes 12582912 | tf_op jit(solution)/shard_map/feed/pallas_call | solution.py:563
  452.4 13.2 %feed.7 = (bf16[2048,1024]{1,0:T(8,128)(2,1)}, bf16[2048,1024]{1,0:T(8,128)(2,1)}, bf16[1024,1024]{1,0:T(8,128)(2,1)S(1)}) custom-call(s32[1]{0:T(128)} %bitcast.1.y_ref, bf16[2048,1024]{1,0:T(8,128)(2,1)} %bitcast.341, bf16[1024,1024]{1,0:T(8,128)(2,1)S(1)} %get-tuple-element.330.wi_ref, ...), custom_call_target="tpu_custom_call", output_to_operand_aliasing={{0}: (8, {}), {1}: (9, {})} | custom-call | flops 4831838208 | bytes 12582912 | tf_op jit(solution)/shard_map/feed/pallas_call | solution.py:563
  467.0 8.6 fusion
  475.5 7.8 norm_grad.5
  483.3 7.8 norm_grad.4
  499.2 7.9 convolution_convert_fusion.2
  526.9 6.6 fusion.11
  533.5 30.0 %collective-permute-done.31 = bf16[512,1024]{1,0:T(8,128)(2,1)S(1)} collective-permute-done((bf16[512,1024]{1,0:T(8,128)(2,1)S(1)}, bf16[512,1024]{1,0:T(8,128)(2,1)S(1)}, u32[]{:S(2)}, u32[]{:S(2)}) %collective-permute-start.31) | collective-permute-done | bytes 1048608 | tf_op jit(solution)/shard_map/ppermute | solution.py:59
  573.5 23.1 %collective-permute-done.33.refs_2_ = bf16[512,1024]{1,0:T(8,128)(2,1)S(1)} collective-permute-done((bf16[512,1024]{1,0:T(8,128)(2,1)S(1)}, bf16[512,1024]{1,0:T(8,128)(2,1)S(1)}, u32[]{:S(2)}, u32[]{:S(2)}) %collective-permute-start.33) | collective-permute-done | bytes 1048608 | tf_op jit(solution)/shard_map/ppermute | solution.py:59
  597.4 14.5 %all-to-all-start.8 = ((f32[32,1,416]{2,1,0:T(1,128)}), f32[32,1,416]{2,1,0:T(1,128)S(1)}, u32[]{:S(2)}, u32[]{:S(2)}) async-start(f32[32,1,416]{2,1,0:T(1,128)} %all_to_all.55), calls=%async_computation.10 | async-start | bytes 131072 | tf_op jit(solution)/shard_map/all_to_all | solution.py:831
  631.9 4.8 convolution_convert_fusion.3
  636.7 5.4 fusion.2
  642.1 5.7 fusion.7
  656.9 19.4 %attend_back.6 = (bf16[2048,384]{1,0:T(8,128)(2,1)S(1)}, f32[1,384]{1,0:T(1,128)S(1)}) custom-call(bf16[2048,768]{1,0:T(8,128)(2,1)} %mix.2.q_ref.k_ref.v_ref, bf16[2048,768]{1,0:T(8,128)(2,1)} %mix.2.q_ref.k_ref.v_ref, bf16[2048,768]{1,0:T(8,128)(2,1)} %mix.2.q_ref.k_ref.v_ref, bf16[2048,256]{1,0:T(8,128)(2,1)S(1)} %copy-done.71, ...), custom_call_target="tpu_custom_call" | custom-call | flops 10737418240 | bytes 4194304 | tf_op jit(solution)/shard_map/attend_back/pallas_call | solution.py:474
  689.6 6.3 fusion.82
  695.9 19.4 %attend_back.7 = (bf16[2048,384]{1,0:T(8,128)(2,1)S(1)}, f32[1,384]{1,0:T(1,128)S(1)}) custom-call(bf16[2048,768]{1,0:T(8,128)(2,1)} %mix.2.q_ref.k_ref.v_ref, bf16[2048,768]{1,0:T(8,128)(2,1)} %mix.2.q_ref.k_ref.v_ref, bf16[2048,768]{1,0:T(8,128)(2,1)} %mix.2.q_ref.k_ref.v_ref, bf16[2048,256]{1,0:T(8,128)(2,1)S(1)} %copy-done.72, ...), custom_call_target="tpu_custom_call" | custom-call | flops 10737418240 | bytes 4194304 | tf_op jit(solution)/shard_map/attend_back/pallas_call | solution.py:474
  728.8 4.9 fusion.83
  741.7 5.8 all-to-all-start.7
  749.3 5.6 all-to-all-done.7
  763.9 7.9 norm_grad.7
  773.2 7.8 norm_grad.6
  787.5 5.8 collective-permute-done.47
  804.8 9.5 %collective-permute-done.49 = bf16[128,1024]{1,0:T(8,128)(2,1)S(1)} collective-permute-done((bf16[128,1024]{1,0:T(8,128)(2,1)S(1)}, bf16[128,1024]{1,0:T(8,128)(2,1)S(1)}, u32[]{:S(2)}, u32[]{:S(2)}) %collective-permute-start.49) | collective-permute-done | bytes 262176 | tf_op jit(solution)/shard_map/ppermute | solution.py:46
  828.7 5.7 all-to-all-start.9
  834.4 7.1 all-to-all-done.9
  845.7 5.4 add_bitcast_fusion
  858.2 9.0 %update.1 = (f32[2,32,3072]{2,1,0:T(8,128)}, f32[2,32,3072]{2,1,0:T(8,128)}, f32[2,32,3072]{2,1,0:T(8,128)}, f32[2,32,3072]{2,1,0:T(8,128)}, f32[2,32,1024]{2,1,...) custom-call(f32[1]{0:T(128)} %bitcast.144.clip_ref, ...), custom_call_target="tpu_custom_call" | custom-call | tf_op jit(solution)/shard_map/update/pallas_call | solution.py:682
  (617 shorter events, 327.5 us)
Async XLA Ops:
  18.5 52.6 %collective-permute-start.1 = (bf16[512,1024]{1,0:T(8,128)(2,1)S(1)}, bf16[512,1024]{1,0:T(8,128)(2,1)}, u32[]{:S(2)}, u32[]{:S(2)}) collective-permute-start(bf16[512,1024]{1,0:T(8,128)(2,1)S(1)} %fusion.37.refs_0_), channel_id=1, source_target_pairs={{0,2},{1,3},{2,0},{3,1},{4,6},{5,7},{6,4},{7,5},{8,10},{9,11},{10,... | collective-permute-start | bytes 3145736 | tf_op jit(solution)/shard_map/ppermute | solution.py:59
  31.3 25.2 %collective-permute-start.6 = (bf16[128,1024]{1,0:T(8,128)(2,1)S(1)}, bf16[128,1024]{1,0:T(8,128)(2,1)S(1)}, u32[]{:S(2)}, u32[]{:S(2)}) collective-permute-start(bf16[128,1024]{1,0:T(8,128)(2,1)S(1)} %pad_maximum_fusion.21.refs_0_), channel_id=1, source_target_pairs={{0,4},{4,0},{8,12},{12,8},{16,20},{20,16},{24,28},{28,24},{1,5},{5... | collective-permute-start | bytes 786440 | tf_op jit(solution)/shard_map/ppermute | solution.py:54
  57.2 60.2 %collective-permute-start = (bf16[512,1024]{1,0:T(8,128)(2,1)S(1)}, bf16[512,1024]{1,0:T(8,128)(2,1)}, u32[]{:S(2)}, u32[]{:S(2)}) collective-permute-start(bf16[512,1024]{1,0:T(8,128)(2,1)S(1)} %fusion.37.refs_0_), channel_id=1, source_target_pairs={{0,1},{1,0},{2,3},{3,2},{4,5},{5,4},{6,7},{7,6},{8,9},{9,8},{10,11... | collective-permute-start | bytes 3145736 | tf_op jit(solution)/shard_map/ppermute | solution.py:64
  65.3 15.3 %collective-permute-start.10 = (bf16[128,2048]{1,0:T(8,128)(2,1)S(1)}, bf16[128,2048]{1,0:T(8,128)(2,1)S(1)}, u32[]{:S(2)}, u32[]{:S(2)}) collective-permute-start(bf16[128,2048]{1,0:T(8,128)(2,1)S(1)} %pad_maximum_fusion.6.refs_0_), channel_id=1, source_target_pairs={{0,8},{4,12},{8,16},{12,20},{16,24},{20,28},{24,0},{28,4},{1,9},{5... | collective-permute-start | bytes 1572872 | tf_op jit(solution)/shard_map/ppermute | solution.py:46
  67.1 14.9 %collective-permute-start.11 = (bf16[128,2048]{1,0:T(8,128)(2,1)S(1)}, bf16[128,2048]{1,0:T(8,128)(2,1)S(1)}, u32[]{:S(2)}, u32[]{:S(2)}) collective-permute-start(bf16[128,2048]{1,0:T(8,128)(2,1)S(1)} %pad_maximum_fusion.6.refs_0_), channel_id=1, source_target_pairs={{0,4},{4,0},{8,12},{12,8},{16,20},{20,16},{24,28},{28,24},{1,5},{5... | collective-permute-start | bytes 1572872 | tf_op jit(solution)/shard_map/ppermute | solution.py:54
  71.1 46.3 %collective-permute-start.2 = (bf16[512,1024]{1,0:T(8,128)(2,1)}, bf16[512,1024]{1,0:T(8,128)(2,1)}, u32[]{:S(2)}, u32[]{:S(2)}) collective-permute-start(bf16[512,1024]{1,0:T(8,128)(2,1)} %collective-permute-done.1.refs_2_), channel_id=1, source_target_pairs={{0,1},{1,0},{2,3},{3,2},{4,5},{5,4},{6,7},{7,6},{8,9},{9,8},{10,11... | collective-permute-start | bytes 3145736 | tf_op jit(solution)/shard_map/ppermute | solution.py:64
  71.1 34.3 %collective-permute-start.9 = (bf16[128,1024]{1,0:T(8,128)(2,1)S(1)}, bf16[128,1024]{1,0:T(8,128)(2,1)}, u32[]{:S(2)}, u32[]{:S(2)}) collective-permute-start(bf16[128,1024]{1,0:T(8,128)(2,1)S(1)} %collective-permute-done.5.refs_6_), channel_id=1, source_target_pairs={{0,4},{4,0},{8,12},{12,8},{16,20},{20,16},{24,28},{28,24},{1,5},{5... | collective-permute-start | bytes 786440 | tf_op jit(solution)/shard_map/ppermute | solution.py:54
  94.5 18.3 %all-to-all-start.3 = ((bf16[4,32,1792]{2,1,0:T(8,128)(2,1)}), bf16[4,32,1792]{2,1,0:T(8,128)(2,1)}, u32[]{:S(2)}, u32[]{:S(2)}) async-start(bf16[4,32,1792]{2,1,0:T(8,128)(2,1)} %pad_maximum_fusion.19), calls=%async_computation.3 | async-start | bytes 917504 | tf_op jit(solution)/shard_map/all_to_all | solution.py:228
  98.7 235.7 %all-gather.2.cloned.1.call-start = ((), (), s32[]{:S(2)}) async-start(), calls=%async_computation.14 | async-start | bytes 7077888 | tf_op jit(solution)/shard_map/all_gather | solution.py:903
  132.2 25.5 %collective-permute-start.13 = (bf16[512,1024]{1,0:T(8,128)(2,1)S(1)}, bf16[512,1024]{1,0:T(8,128)(2,1)S(1)}, u32[]{:S(2)}, u32[]{:S(2)}) collective-permute-start(bf16[512,1024]{1,0:T(8,128)(2,1)S(1)} %copy-done.4), channel_id=1, source_target_pairs={{0,2},{1,3},{2,0},{3,1},{4,6},{5,7},{6,4},{7,5},{8,10},{9,11},{10,... | collective-permute-start | bytes 3145736 | tf_op jit(solution)/shard_map/ppermute | solution.py:59
  134.2 38.6 %collective-permute-start.12 = (bf16[512,1024]{1,0:T(8,128)(2,1)S(1)}, bf16[512,1024]{1,0:T(8,128)(2,1)S(1)}, u32[]{:S(2)}, u32[]{:S(2)}) collective-permute-start(bf16[512,1024]{1,0:T(8,128)(2,1)S(1)} %copy-done.4), channel_id=1, source_target_pairs={{0,1},{1,0},{2,3},{3,2},{4,5},{5,4},{6,7},{7,6},{8,9},{9,8},{10,11... | collective-permute-start | bytes 3145736 | tf_op jit(solution)/shard_map/ppermute | solution.py:64
  157.7 15.1 %collective-permute-start.14 = (bf16[512,1024]{1,0:T(8,128)(2,1)S(1)}, bf16[512,1024]{1,0:T(8,128)(2,1)S(1)}, u32[]{:S(2)}, u32[]{:S(2)}) collective-permute-start(bf16[512,1024]{1,0:T(8,128)(2,1)S(1)} %collective-permute-done.13.refs_2_), channel_id=1, source_target_pairs={{0,1},{1,0},{2,3},{3,2},{4,5},{5,4},{6,7},{7,6},{8,9},{9,8},{10,11... | collective-permute-start | bytes 3145736 | tf_op jit(solution)/shard_map/ppermute | solution.py:64
  157.7 26.9 %collective-permute-start.15 = (bf16[128,2048]{1,0:T(8,128)(2,1)S(1)}, bf16[128,2048]{1,0:T(8,128)(2,1)}, u32[]{:S(2)}, u32[]{:S(2)}) collective-permute-start(bf16[128,2048]{1,0:T(8,128)(2,1)S(1)} %copy-done.39), channel_id=1, source_target_pairs={{0,8},{4,12},{8,16},{12,20},{16,24},{20,28},{24,0},{28,4},{1,9},{5... | collective-permute-start | bytes 1572872 | tf_op jit(solution)/shard_map/ppermute | solution.py:46
  159.3 25.4 %collective-permute-start.16 = (bf16[128,2048]{1,0:T(8,128)(2,1)S(1)}, bf16[128,2048]{1,0:T(8,128)(2,1)S(1)}, u32[]{:S(2)}, u32[]{:S(2)}) collective-permute-start(bf16[128,2048]{1,0:T(8,128)(2,1)S(1)} %copy-done.39), channel_id=1, source_target_pairs={{0,4},{4,0},{8,12},{12,8},{16,20},{20,16},{24,28},{28,24},{1,5},{5... | collective-permute-start | bytes 1572872 | tf_op jit(solution)/shard_map/ppermute | solution.py:54
  185.5 33.7 %collective-permute-start.17 = (bf16[128,2048]{1,0:T(8,128)(2,1)}, bf16[128,2048]{1,0:T(8,128)(2,1)}, u32[]{:S(2)}, u32[]{:S(2)}) collective-permute-start(bf16[128,2048]{1,0:T(8,128)(2,1)} %collective-permute-done.15.refs_4_), channel_id=1, source_target_pairs={{0,8},{4,12},{8,16},{12,20},{16,24},{20,28},{24,0},{28,4},{1,9},{5... | collective-permute-start | bytes 1572872 | tf_op jit(solution)/shard_map/ppermute | solution.py:46
  197.1 22.1 %collective-permute-start.18 = (bf16[128,2048]{1,0:T(8,128)(2,1)}, bf16[128,2048]{1,0:T(8,128)(2,1)}, u32[]{:S(2)}, u32[]{:S(2)}) collective-permute-start(bf16[128,2048]{1,0:T(8,128)(2,1)} %collective-permute-done.15.refs_4_), channel_id=1, source_target_pairs={{0,4},{4,0},{8,12},{12,8},{16,20},{20,16},{24,28},{28,24},{1,5},{5... | collective-permute-start | bytes 1572872 | tf_op jit(solution)/shard_map/ppermute | solution.py:54
  199.9 21.4 %all-to-all-start.2 = ((bf16[4,64,1024]{2,1,0:T(8,128)(2,1)}), bf16[4,64,1024]{2,1,0:T(8,128)(2,1)}, u32[]{:S(2)}, u32[]{:S(2)}) async-start(bf16[4,64,1024]{2,1,0:T(8,128)(2,1)} %reshape_reshape.9), calls=%async_computation.2 | async-start | bytes 1048576 | tf_op jit(solution)/shard_map/all_to_all | solution.py:228
  274.1 25.9 %collective-permute-start.22 = (bf16[512,1024]{1,0:T(8,128)(2,1)S(1)}, bf16[512,1024]{1,0:T(8,128)(2,1)S(1)}, u32[]{:S(2)}, u32[]{:S(2)}) collective-permute-start(bf16[512,1024]{1,0:T(8,128)(2,1)S(1)} %fusion.30), channel_id=1, source_target_pairs={{0,2},{1,3},{2,0},{3,1},{4,6},{5,7},{6,4},{7,5},{8,10},{9,11},{10,... | collective-permute-start | bytes 3145736 | tf_op jit(solution)/shard_map/ppermute | solution.py:59
  302.1 25.0 %collective-permute-start.24 = (bf16[512,1024]{1,0:T(8,128)(2,1)S(1)}, bf16[512,1024]{1,0:T(8,128)(2,1)S(1)}, u32[]{:S(2)}, u32[]{:S(2)}) collective-permute-start(bf16[512,1024]{1,0:T(8,128)(2,1)S(1)} %fusion.36.refs_0_), channel_id=1, source_target_pairs={{0,2},{1,3},{2,0},{3,1},{4,6},{5,7},{6,4},{7,5},{8,10},{9,11},{10,... | collective-permute-start | bytes 3145736 | tf_op jit(solution)/shard_map/ppermute | solution.py:59
  303.8 23.3 %collective-permute-start.23 = (bf16[512,1024]{1,0:T(8,128)(2,1)S(1)}, bf16[512,1024]{1,0:T(8,128)(2,1)}, u32[]{:S(2)}, u32[]{:S(2)}) collective-permute-start(bf16[512,1024]{1,0:T(8,128)(2,1)S(1)} %fusion.36.refs_0_), channel_id=1, source_target_pairs={{0,1},{1,0},{2,3},{3,2},{4,5},{5,4},{6,7},{7,6},{8,9},{9,8},{10,11... | collective-permute-start | bytes 3145736 | tf_op jit(solution)/shard_map/ppermute | solution.py:64
  370.3 20.3 %all-to-all-start.4 = ((bf16[4,64,1024]{2,1,0:T(8,128)(2,1)}), bf16[4,64,1024]{2,1,0:T(8,128)(2,1)}, u32[]{:S(2)}, u32[]{:S(2)}) async-start(bf16[4,64,1024]{2,1,0:T(8,128)(2,1)} %reshape_reshape.10), calls=%async_computation.4 | async-start | bytes 1048576 | tf_op jit(solution)/shard_map/all_to_all | solution.py:228
  390.6 116.5 %all-to-all-start.6 = ((bf16[4,64,1024]{2,1,0:T(8,128)(2,1)}), bf16[4,64,1024]{2,1,0:T(8,128)(2,1)}, u32[]{:S(2)}, u32[]{:S(2)}) async-start(bf16[4,64,1024]{2,1,0:T(8,128)(2,1)} %bitcast.367), calls=%async_computation.6 | async-start | bytes 1048576 | tf_op jit(solution)/shard_map/all_to_all | solution.py:228
  394.8 321.8 %reduce-scatter.3.cloned.1.call-start = ((), (), s32[]{:S(2)}) async-start(), calls=%async_computation.15 | async-start | bytes 2949120 | tf_op jit(solution)/shard_map/reduce_scatter | solution.py:961
  492.1 21.1 %collective-permute-start.27 = (bf16[512,1024]{1,0:T(8,128)(2,1)}, bf16[512,1024]{1,0:T(8,128)(2,1)}, u32[]{:S(2)}, u32[]{:S(2)}) collective-permute-start(bf16[512,1024]{1,0:T(8,128)(2,1)} %dynamic-slice_bitcast_fusion.4), channel_id=1, source_target_pairs={{0,1},{1,0},{2,3},{3,2},{4,5},{5,4},{6,7},{7,6},{8,9},{9,8},{10,11... | collective-permute-start | bytes 3145736 | tf_op jit(solution)/shard_map/ppermute | solution.py:64
  495.2 22.2 %collective-permute-start.30 = (bf16[512,1024]{1,0:T(8,128)(2,1)}, bf16[512,1024]{1,0:T(8,128)(2,1)}, u32[]{:S(2)}, u32[]{:S(2)}) collective-permute-start(bf16[512,1024]{1,0:T(8,128)(2,1)} %dynamic-slice_bitcast_fusion.2), channel_id=1, source_target_pairs={{0,1},{1,0},{2,3},{3,2},{4,5},{5,4},{6,7},{7,6},{8,9},{9,8},{10,11... | collective-permute-start | bytes 3145736 | tf_op jit(solution)/shard_map/ppermute | solution.py:64
  497.6 35.9 %collective-permute-start.29 = (bf16[512,1024]{1,0:T(8,128)(2,1)}, bf16[512,1024]{1,0:T(8,128)(2,1)}, u32[]{:S(2)}, u32[]{:S(2)}) collective-permute-start(bf16[512,1024]{1,0:T(8,128)(2,1)} %dynamic-slice_bitcast_fusion.3), channel_id=1, source_target_pairs={{0,1},{1,0},{2,3},{3,2},{4,5},{5,4},{6,7},{7,6},{8,9},{9,8},{10,11... | collective-permute-start | bytes 3145736 | tf_op jit(solution)/shard_map/ppermute | solution.py:64
  499.1 66.8 %collective-permute-start.26 = (bf16[512,1024]{1,0:T(8,128)(2,1)}, bf16[512,1024]{1,0:T(8,128)(2,1)}, u32[]{:S(2)}, u32[]{:S(2)}) collective-permute-start(bf16[512,1024]{1,0:T(8,128)(2,1)} %dynamic-slice_bitcast_fusion.5), channel_id=1, source_target_pairs={{0,1},{1,0},{2,3},{3,2},{4,5},{5,4},{6,7},{7,6},{8,9},{9,8},{10,11... | collective-permute-start | bytes 3145736 | tf_op jit(solution)/shard_map/ppermute | solution.py:64
  515.4 50.6 %collective-permute-start.28 = (bf16[512,1024]{1,0:T(8,128)(2,1)S(1)}, bf16[512,1024]{1,0:T(8,128)(2,1)S(1)}, u32[]{:S(2)}, u32[]{:S(2)}) collective-permute-start(bf16[512,1024]{1,0:T(8,128)(2,1)S(1)} %fusion.24), channel_id=1, source_target_pairs={{0,2},{1,3},{2,0},{3,1},{4,6},{5,7},{6,4},{7,5},{8,10},{9,11},{10,... | collective-permute-start | bytes 3145736 | tf_op jit(solution)/shard_map/ppermute | solution.py:59
  524.1 39.3 %collective-permute-start.31 = (bf16[512,1024]{1,0:T(8,128)(2,1)S(1)}, bf16[512,1024]{1,0:T(8,128)(2,1)S(1)}, u32[]{:S(2)}, u32[]{:S(2)}) collective-permute-start(bf16[512,1024]{1,0:T(8,128)(2,1)S(1)} %fusion.22), channel_id=1, source_target_pairs={{0,2},{1,3},{2,0},{3,1},{4,6},{5,7},{6,4},{7,5},{8,10},{9,11},{10,... | collective-permute-start | bytes 3145736 | tf_op jit(solution)/shard_map/ppermute | solution.py:59
  571.8 24.8 %collective-permute-start.33 = (bf16[512,1024]{1,0:T(8,128)(2,1)S(1)}, bf16[512,1024]{1,0:T(8,128)(2,1)S(1)}, u32[]{:S(2)}, u32[]{:S(2)}) collective-permute-start(bf16[512,1024]{1,0:T(8,128)(2,1)S(1)} %convert_element_type.398.refs_0_), channel_id=1, source_target_pairs={{0,2},{1,3},{2,0},{3,1},{4,6},{5,7},{6,4},{7,5},{8,10},{9,11},{10,... | collective-permute-start | bytes 3145736 | tf_op jit(solution)/shard_map/ppermute | solution.py:59
  573.5 45.9 %collective-permute-start.32 = (bf16[512,1024]{1,0:T(8,128)(2,1)S(1)}, bf16[512,1024]{1,0:T(8,128)(2,1)}, u32[]{:S(2)}, u32[]{:S(2)}) collective-permute-start(bf16[512,1024]{1,0:T(8,128)(2,1)S(1)} %convert_element_type.398.refs_0_), channel_id=1, source_target_pairs={{0,1},{1,0},{2,3},{3,2},{4,5},{5,4},{6,7},{7,6},{8,9},{9,8},{10,11... | collective-permute-start | bytes 3145736 | tf_op jit(solution)/shard_map/ppermute | solution.py:64
  596.6 22.8 %collective-permute-start.34 = (bf16[512,1024]{1,0:T(8,128)(2,1)S(1)}, bf16[512,1024]{1,0:T(8,128)(2,1)}, u32[]{:S(2)}, u32[]{:S(2)}) collective-permute-start(bf16[512,1024]{1,0:T(8,128)(2,1)S(1)} %collective-permute-done.33.refs_2_), channel_id=1, source_target_pairs={{0,1},{1,0},{2,3},{3,2},{4,5},{5,4},{6,7},{7,6},{8,9},{9,8},{10,11... | collective-permute-start | bytes 3145736 | tf_op jit(solution)/shard_map/ppermute | solution.py:64
  597.4 21.9 %all-to-all-start.8 = ((f32[32,1,416]{2,1,0:T(1,128)}), f32[32,1,416]{2,1,0:T(1,128)S(1)}, u32[]{:S(2)}, u32[]{:S(2)}) async-start(f32[32,1,416]{2,1,0:T(1,128)} %all_to_all.55), calls=%async_computation.10 | async-start | bytes 131072 | tf_op jit(solution)/shard_map/all_to_all | solution.py:831
  611.9 212.9 %reduce-scatter.5.cloned.1.call-start = ((), (), s32[]{:S(2)}) async-start(), calls=%async_computation.16 | async-start | bytes 4128768 | tf_op jit(solution)/shard_map/reduce_scatter | solution.py:998
  649.6 32.8 %collective-permute-start.35 = (bf16[128,2048]{1,0:T(8,128)(2,1)}, bf16[128,2048]{1,0:T(8,128)(2,1)}, u32[]{:S(2)}, u32[]{:S(2)}) collective-permute-start(bf16[128,2048]{1,0:T(8,128)(2,1)} %pad_maximum_fusion.8), channel_id=1, source_target_pairs={{0,4},{4,0},{8,12},{12,8},{16,20},{20,16},{24,28},{28,24},{1,5},{5... | collective-permute-start | bytes 1572872 | tf_op jit(solution)/shard_map/ppermute | solution.py:54
  651.2 27.2 %all-to-all-start.5 = ((bf16[4,64,1024]{2,1,0:T(8,128)(2,1)}), bf16[4,64,1024]{2,1,0:T(8,128)(2,1)}, u32[]{:S(2)}, u32[]{:S(2)}) async-start(bf16[4,64,1024]{2,1,0:T(8,128)(2,1)} %bitcast.368), calls=%async_computation.5 | async-start | bytes 1048576 | tf_op jit(solution)/shard_map/all_to_all | solution.py:228
  684.4 37.0 %collective-permute-start.37 = (bf16[128,2048]{1,0:T(8,128)(2,1)}, bf16[128,2048]{1,0:T(8,128)(2,1)}, u32[]{:S(2)}, u32[]{:S(2)}) collective-permute-start(bf16[128,2048]{1,0:T(8,128)(2,1)} %add_convert_fusion.6), channel_id=1, source_target_pairs={{0,8},{4,12},{8,16},{12,20},{16,24},{20,28},{24,0},{28,4},{1,9},{5... | collective-permute-start | bytes 1572872 | tf_op jit(solution)/shard_map/ppermute | solution.py:46
  687.8 33.7 %collective-permute-start.36 = (bf16[128,2048]{1,0:T(8,128)(2,1)}, bf16[128,2048]{1,0:T(8,128)(2,1)}, u32[]{:S(2)}, u32[]{:S(2)}) collective-permute-start(bf16[128,2048]{1,0:T(8,128)(2,1)} %pad_maximum_fusion.10), channel_id=1, source_target_pairs={{0,4},{4,0},{8,12},{12,8},{16,20},{20,16},{24,28},{28,24},{1,5},{5... | collective-permute-start | bytes 1572872 | tf_op jit(solution)/shard_map/ppermute | solution.py:54
  723.8 32.6 %collective-permute-start.39 = (bf16[128,2048]{1,0:T(8,128)(2,1)}, bf16[128,2048]{1,0:T(8,128)(2,1)}, u32[]{:S(2)}, u32[]{:S(2)}) collective-permute-start(bf16[128,2048]{1,0:T(8,128)(2,1)} %add_convert_fusion.5), channel_id=1, source_target_pairs={{0,8},{4,12},{8,16},{12,20},{16,24},{20,28},{24,0},{28,4},{1,9},{5... | collective-permute-start | bytes 1572872 | tf_op jit(solution)/shard_map/ppermute | solution.py:46
  728.1 28.4 %collective-permute-start.38 = (bf16[128,2048]{1,0:T(8,128)(2,1)}, bf16[128,2048]{1,0:T(8,128)(2,1)}, u32[]{:S(2)}, u32[]{:S(2)}) collective-permute-start(bf16[128,2048]{1,0:T(8,128)(2,1)} %pad_maximum_fusion.12), channel_id=1, source_target_pairs={{0,4},{4,0},{8,12},{12,8},{16,20},{20,16},{24,28},{28,24},{1,5},{5... | collective-permute-start | bytes 1572872 | tf_op jit(solution)/shard_map/ppermute | solution.py:54
  758.7 35.2 %collective-permute-start.50 = (bf16[128,2048]{1,0:T(8,128)(2,1)S(1)}, bf16[128,2048]{1,0:T(8,128)(2,1)S(1)}, u32[]{:S(2)}, u32[]{:S(2)}) collective-permute-start(bf16[128,2048]{1,0:T(8,128)(2,1)S(1)} %pad_maximum_fusion.15), channel_id=1, source_target_pairs={{0,4},{4,0},{8,12},{12,8},{16,20},{20,16},{24,28},{28,24},{1,5},{5... | collective-permute-start | bytes 1572872 | tf_op jit(solution)/shard_map/ppermute | solution.py:54
  760.9 33.1 %collective-permute-start.51 = (bf16[128,2048]{1,0:T(8,128)(2,1)S(1)}, bf16[128,2048]{1,0:T(8,128)(2,1)S(1)}, u32[]{:S(2)}, u32[]{:S(2)}) collective-permute-start(bf16[128,2048]{1,0:T(8,128)(2,1)S(1)} %add_convert_fusion.4), channel_id=1, source_target_pairs={{0,8},{4,12},{8,16},{12,20},{16,24},{20,28},{24,0},{28,4},{1,9},{5... | collective-permute-start | bytes 1572872 | tf_op jit(solution)/shard_map/ppermute | solution.py:46
  761.7 24.7 %collective-permute-start.45 = (bf16[128,1024]{1,0:T(8,128)(2,1)S(1)}, bf16[128,1024]{1,0:T(8,128)(2,1)S(1)}, u32[]{:S(2)}, u32[]{:S(2)}) collective-permute-start(bf16[128,1024]{1,0:T(8,128)(2,1)S(1)} %pad_maximum_fusion.25), channel_id=1, source_target_pairs={{0,4},{4,0},{8,12},{12,8},{16,20},{20,16},{24,28},{28,24},{1,5},{5... | collective-permute-start | bytes 786440 | tf_op jit(solution)/shard_map/ppermute | solution.py:54
  763.2 20.7 %collective-permute-start.46 = (bf16[128,1024]{1,0:T(8,128)(2,1)S(1)}, bf16[128,1024]{1,0:T(8,128)(2,1)S(1)}, u32[]{:S(2)}, u32[]{:S(2)}) collective-permute-start(bf16[128,1024]{1,0:T(8,128)(2,1)S(1)} %pad_maximum_fusion.26), channel_id=1, source_target_pairs={{0,4},{4,0},{8,12},{12,8},{16,20},{20,16},{24,28},{28,24},{1,5},{5... | collective-permute-start | bytes 786440 | tf_op jit(solution)/shard_map/ppermute | solution.py:54
  773.1 21.8 %collective-permute-start.41 = (bf16[512,1024]{1,0:T(8,128)(2,1)S(1)}, bf16[512,1024]{1,0:T(8,128)(2,1)S(1)}, u32[]{:S(2)}, u32[]{:S(2)}) collective-permute-start(bf16[512,1024]{1,0:T(8,128)(2,1)S(1)} %dynamic-slice_bitcast_fusion), channel_id=1, source_target_pairs={{0,1},{1,0},{2,3},{3,2},{4,5},{5,4},{6,7},{7,6},{8,9},{9,8},{10,11... | collective-permute-start | bytes 3145736 | tf_op jit(solution)/shard_map/ppermute | solution.py:64
  786.4 18.4 %collective-permute-start.43 = (bf16[128,1024]{1,0:T(8,128)(2,1)S(1)}, bf16[128,1024]{1,0:T(8,128)(2,1)S(1)}, u32[]{:S(2)}, u32[]{:S(2)}) collective-permute-start(bf16[128,1024]{1,0:T(8,128)(2,1)S(1)} %pad_maximum_fusion.23), channel_id=1, source_target_pairs={{0,4},{4,0},{8,12},{12,8},{16,20},{20,16},{24,28},{28,24},{1,5},{5... | collective-permute-start | bytes 786440 | tf_op jit(solution)/shard_map/ppermute | solution.py:54
  793.9 27.5 %collective-permute-start.40 = (bf16[512,1024]{1,0:T(8,128)(2,1)}, bf16[512,1024]{1,0:T(8,128)(2,1)}, u32[]{:S(2)}, u32[]{:S(2)}) collective-permute-start(bf16[512,1024]{1,0:T(8,128)(2,1)} %dynamic-slice_bitcast_fusion.1), channel_id=1, source_target_pairs={{0,1},{1,0},{2,3},{3,2},{4,5},{5,4},{6,7},{7,6},{8,9},{9,8},{10,11... | collective-permute-start | bytes 3145736 | tf_op jit(solution)/shard_map/ppermute | solution.py:64
  796.3 25.8 %collective-permute-start.42 = (bf16[512,1024]{1,0:T(8,128)(2,1)}, bf16[512,1024]{1,0:T(8,128)(2,1)}, u32[]{:S(2)}, u32[]{:S(2)}) collective-permute-start(bf16[512,1024]{1,0:T(8,128)(2,1)} %fusion.20), channel_id=1, source_target_pairs={{0,2},{1,3},{2,0},{3,1},{4,6},{5,7},{6,4},{7,5},{8,10},{9,11},{10,... | collective-permute-start | bytes 3145736 | tf_op jit(solution)/shard_map/ppermute | solution.py:59
  (156 other events, 1815.8 us)
Sparse Core Ops, SparseCore 0:
  116.8 119.4 all-gather.1
  512.9 80.7 reduce-scatter.2
  616.4 98.1 reduce-scatter.4

commit v3 on v2

--- a/solution.py
+++ b/solution.py
@@ -32,6 +32,7 @@
 BF = jnp.bfloat16
 F32 = jnp.float32
 VMEM_LIMIT = 48 * 1024 * 1024
+LIGHT = pl.CostEstimate(flops=1000, bytes_accessed=1000, transcendentals=0)
 
 
 def dp_parts():
@@ -85,9 +86,7 @@
         ),
         out_shape=jax.ShapeDtypeStruct((count,) + piece.shape, piece.dtype),
         compiler_params=pltpu.CompilerParams(vmem_limit_bytes=VMEM_LIMIT),
-        cost_estimate=pl.CostEstimate(
-            flops=0, bytes_accessed=4 * count * piece.size, transcendentals=0
-        ),
+        cost_estimate=LIGHT,
         name="assemble",
     )(jnp.stack(slots).astype(jnp.int32), *pieces)
     return total.reshape((count * piece.shape[0],) + piece.shape[1:])
@@ -127,7 +126,7 @@
             for turn, piece in enumerate(chain):
                 pieces.append(piece)
                 slots.append((a - step) % outer * inner + (b - turn) % inner)
-        return assemble(pieces, slots)
+        return pieces, slots
 
 
 class Scatter:
@@ -180,33 +179,39 @@
         return self.part()
 
 
-def seq_gather(value):
-    chips = lax.axis_size("seq") // 2
-    me = lax.axis_index("seq")
-    y, c = me // 2, me % 2
-    pieces, slots = [], []
-    piece = value
-    for step in range(chips):
-        at = (y - step) % chips
-        pieces += [piece, core_swap(piece)]
-        slots += [2 * at + c, 2 * at + 1 - c]
-        if step < chips - 1:
-            piece = chip_ring(piece)
-    return assemble(pieces, slots)
+class SeqGather:
+    def __init__(self, value):
+        self.pieces = [value]
+        for step in range(1, lax.axis_size("seq") // 2):
+            self.pieces.append(chip_ring(self.pieces[-1]))
+
+    def hold(self, *values):
+        held = lax.optimization_barrier((values, self.pieces))
+        self.pieces = held[1]
+        return held[0]
+
+    def done(self):
+        chips = lax.axis_size("seq") // 2
+        me = lax.axis_index("seq")
+        y, c = me // 2, me % 2
+        pieces, slots = [], []
+        for step, piece in enumerate(self.pieces):
+            at = (y - step) % chips
+            pieces += [piece, core_swap(piece)]
+            slots += [2 * at + c, 2 * at + 1 - c]
+        return assemble(pieces, slots)
 
 
 class SeqScatter:
-    def __init__(self, others, own):
-        chips = lax.axis_size("seq") // 2
+    def __init__(self, others):
+        self.chips = lax.axis_size("seq") // 2
         self.core = lax.axis_index("seq") % 2
-        rows = own.shape[0] // 2
-        others = others.reshape((chips - 1, 2, rows) + own.shape[1:])
-        self.values = [others[n] for n in range(chips - 1)]
-        self.values.append(own.reshape((2, rows) + own.shape[1:]))
-        self.sending = self.cores(0).astype(BF)
-
-    def cores(self, n):
-        value = self.values[n]
+        rows = others.shape[0] // (2 * (self.chips - 1))
+        others = others.reshape((self.chips - 1, 2, rows) + others.shape[1:])
+        self.values = [others[n] for n in range(self.chips - 1)]
+        self.sending = self.cores(self.values[0]).astype(BF)
+
+    def cores(self, value):
         kept = lax.dynamic_index_in_dim(value, self.core, 0, keepdims=False)
         passed = lax.dynamic_index_in_dim(value, 1 - self.core, 0, keepdims=False)
         return kept.astype(F32) + core_swap(passed).astype(F32)
@@ -216,12 +221,22 @@
         self.sending = held[1]
         return held[0]
 
-    def done(self):
-        for n in range(1, len(self.values)):
+    def done(self, own, others=()):
+        own = own.reshape((2, own.shape[0] // 2) + own.shape[1:])
+        for value in self.values[1:] + [own]:
             arrived = chip_ring(self.sending)
-            total = self.cores(n) + arrived.astype(F32)
+            arrived, value, others = lax.optimization_barrier((arrived, value, others))
+            total = self.cores(value) + arrived.astype(F32)
             self.sending = total.astype(BF)
-        return total
+        return total, others
+
+
+def sum_exchange(value):
+    copies, parts = lax.axis_size("dp"), lax.axis_size("seq")
+    rows = value.shape[0] // (copies * parts)
+    value = value.reshape((copies * parts, rows) + value.shape[1:])
+    value = lax.all_to_all(value, ("dp", "seq"), split_axis=0, concat_axis=0, tiled=True)
+    return value.reshape((copies, parts) + value.shape[1:])
 
 
 def seq_exchange(value):
@@ -243,6 +258,14 @@
     )
 
 
+def as_column(row):
+    return jnp.broadcast_to(row, (128, row.shape[1])).T[:, :1]
+
+
+def as_row(column):
+    return jnp.broadcast_to(column, (column.shape[0], 128)).T[:1, :]
+
+
 def matmul(left, right):
     return lax.dot_general(left, right, (((1,), (0,)), ((), ())), preferred_element_type=F32)
 
@@ -255,10 +278,30 @@
     return lax.dot_general(left, right, (((0,), (0,)), ((), ())), preferred_element_type=F32)
 
 
-def mix_kernel(x_ref, w_ref, c_ref, cos_ref, sin_ref, out_ref):
-    mixed = matmul(x_ref[...], w_ref[...]) + c_ref[...]
+def mix_kernel(slots_ref, x_ref, gain_ref, low_ref, bias_ref, cos_ref, sin_ref, *refs):
+    out_ref, scaled_ref = refs[-3], refs[-2]
+    shift_ref = refs[-1]
+    columns = scaled_ref.shape[1]
+
+    @pl.when(pl.program_id(0) == 0)
+    def _():
+        if len(refs) == 4:
+            raw_ref = refs[0]
+        else:
+            pieces, raw_ref, rest_ref = refs[:-5], refs[-5], refs[-4]
+            for n, piece_ref in enumerate(pieces):
+                size = piece_ref.shape[0]
+                rows = pl.ds(pl.multiple_of(slots_ref[n] * size, size), size)
+                raw_ref[rows, :] = piece_ref[:, :columns]
+                rest_ref[rows, :] = piece_ref[:, columns:]
+        raw = raw_ref[...]
+        scaled_ref[...] = (raw.astype(F32) * as_column(gain_ref[...])).astype(BF)
+        low = jnp.broadcast_to(low_ref[...], (8, D)).astype(BF)
+        shift_ref[...] = matmul(low, raw) + bias_ref[...]
+
+    mixed = matmul(x_ref[...], scaled_ref[...]) + shift_ref[0:1, :]
     cosine, sine = cos_ref[...], sin_ref[...]
-    for start in range(0, w_ref.shape[1], 3 * 128):
+    for start in range(0, columns, 3 * 128):
         query = mixed[:, start : start + 128]
         key = mixed[:, start + 128 : start + 256]
         query = (query * cosine + swap_halves(query) * sine) * QUERY_SCALE
@@ -268,28 +311,47 @@
         out_ref[:, start + 256 : start + 384] = mixed[:, start + 256 : start + 384].astype(BF)
 
 
-def mix(x, weight, shift, cosine, sine):
-    length, columns = x.shape[0], weight.shape[1]
+def mix(x, weight, gain, low, bias, cosine, sine, slots=None):
+    length, columns = x.shape[0], bias.shape[0]
+
+    def whole(shape):
+        return pl.BlockSpec(shape, lambda i, slots_ref: (0, 0))
+
+    def rows(count):
+        return pl.BlockSpec((ROWS, count), lambda i, slots_ref: (i, 0))
+
+    out_specs = [rows(columns), whole((D, columns))]
+    out_shape = [
+        jax.ShapeDtypeStruct((length, columns), BF),
+        jax.ShapeDtypeStruct((D, columns), BF),
+    ]
+    if slots is None:
+        slots, weight_specs = jnp.zeros((1,), jnp.int32), [whole((D, columns))]
+    else:
+        slots = jnp.stack(slots).astype(jnp.int32)
+        weight_specs = [pl.BlockSpec(memory_space=pltpu.VMEM)] * len(weight)
+        rest = weight[0].shape[1] - columns
+        out_specs = [whole((D, columns)), whole((D, rest))] + out_specs
+        out_shape = [
+            jax.ShapeDtypeStruct((D, columns), BF),
+            jax.ShapeDtypeStruct((D, rest), BF),
+        ] + out_shape
     return pl.pallas_call(
         mix_kernel,
-        grid=(length // ROWS,),
-        in_specs=[
-            pl.BlockSpec((ROWS, D), lambda i: (i, 0)),
-            pl.BlockSpec((D, columns), lambda i: (0, 0)),
-            pl.BlockSpec((1, columns), lambda i: (0, 0)),
-            pl.BlockSpec((ROWS, 128), lambda i: (i, 0)),
-            pl.BlockSpec((ROWS, 128), lambda i: (i, 0)),
-        ],
-        out_specs=pl.BlockSpec((ROWS, columns), lambda i: (i, 0)),
-        out_shape=jax.ShapeDtypeStruct((length, columns), BF),
+        grid_spec=pltpu.PrefetchScalarGridSpec(
+            num_scalar_prefetch=1,
+            grid=(length // ROWS,),
+            in_specs=[rows(D), whole((1, D)), whole((1, D)), whole((1, columns))]
+            + [rows(128), rows(128)]
+            + weight_specs,
+            out_specs=out_specs,
+            scratch_shapes=[pltpu.VMEM((8, columns), F32)],
+        ),
+        out_shape=out_shape,
         compiler_params=pltpu.CompilerParams(vmem_limit_bytes=VMEM_LIMIT),
-        cost_estimate=pl.CostEstimate(
-            flops=2 * length * D * columns,
-            bytes_accessed=2 * (length * D + D * columns + length * columns),
-            transcendentals=0,
-        ),
+        cost_estimate=LIGHT,
         name="mix",
-    )(x, weight, shift, cosine, sine)
+    )(slots, x, gain[None], low[None], bias[None], cosine, sine, *weight)
 
 
 def attend_kernel(q_ref, k_ref, v_ref, o_ref, lse_ref, acc_ref, turned_ref):
@@ -363,11 +425,7 @@
             pltpu.VMEM((width, length), BF),
         ],
         compiler_params=pltpu.CompilerParams(vmem_limit_bytes=VMEM_LIMIT),
-        cost_estimate=pl.CostEstimate(
-            flops=8 * length * length * width,
-            bytes_accessed=8 * length * width,
-            transcendentals=length * length * heads,
-        ),
+        cost_estimate=LIGHT,
         name="attend",
     )(mixed, mixed, mixed)
 
@@ -499,11 +557,7 @@
             pltpu.VMEM((block, width), F32),
         ],
         compiler_params=pltpu.CompilerParams(vmem_limit_bytes=VMEM_LIMIT),
-        cost_estimate=pl.CostEstimate(
-            flops=20 * length * length * width,
-            bytes_accessed=16 * length * width,
-            transcendentals=length * length * heads,
-        ),
+        cost_estimate=LIGHT,
         name="attend_back",
     )(mixed, mixed, mixed, grads, attended, log_total, cosine, sine)
 
@@ -526,6 +580,8 @@
     chips = lax.axis_size("seq") // 2
     y = lax.axis_index("seq") // 2
     per = length // ROWS // chips
+    if own is None:
+        return length // ROWS, lambda i, y_ref: i, y
     if own:
         return per, lambda i, y_ref: y_ref[0] * per + i, y
     return (
@@ -535,60 +591,156 @@
     )
 
 
-def feed_kernel(y_ref, x_ref, wi_ref, ci_ref, wd_ref, wo_ref, *refs):
-    attended = refs[: wo_ref.shape[0] // 128]
-    act_ref, slope_ref, out_ref = refs[-3:]
-    hidden = matmul(x_ref[...], wi_ref[...]) + ci_ref[...]
+def feed_kernel(first, last, halves, count, y_ref, slots_ref, x_ref, *refs):
+    refs = list(refs)
+    if first:
+        gain_ref, low_ref, bias_ref = refs[:3]
+        del refs[:3]
+        if count:
+            pieces = refs[:count]
+            del refs[:count]
+        else:
+            raw_ref = refs.pop(0)
+    else:
+        scaled_ref, shift_ref = refs[:2]
+        del refs[:2]
+    if last:
+        out_ref = refs.pop()
+        if count:
+            shrink_ref = refs.pop()
+        else:
+            shrink_ref = refs.pop(0)
+        output_ref = refs.pop(0)
+        attended = refs[:halves]
+    if first:
+        if count:
+            raw_ref = refs.pop()
+        act_ref, slope_ref, scaled_ref, shift_ref = refs[-4:]
+        units = scaled_ref.shape[1]
+
+        @pl.when(pl.program_id(0) == 0)
+        def _():
+            if count:
+                for n, piece_ref in enumerate(pieces):
+                    size = piece_ref.shape[0]
+                    rows = pl.ds(pl.multiple_of(slots_ref[n] * size, size), size)
+                    raw_ref[rows, :] = piece_ref[:, :units]
+                    shrink_ref[rows, :] = piece_ref[:, units:]
+            raw = raw_ref[...]
+            scaled_ref[...] = (raw.astype(F32) * as_column(gain_ref[...])).astype(BF)
+            low = jnp.broadcast_to(low_ref[...], (8, D)).astype(BF)
+            shift_ref[...] = matmul(low, raw) + bias_ref[...]
+
+    else:
+        act_ref, slope_ref = refs[-2:]
+    hidden = matmul(x_ref[...], scaled_ref[...]) + shift_ref[0:1, :]
     activated, slope = gelu_pair(hidden)
     activated = activated.astype(BF)
     act_ref[...] = activated
     slope_ref[...] = slope.astype(BF)
-    out = matmul(activated, wd_ref[...])
-    for half, o_ref in enumerate(attended):
-        out = out + matmul(o_ref[...], wo_ref[half * 128 : (half + 1) * 128, :])
-    out_ref[...] = out.astype(BF)
-
-
-def feed(x, expand, shift, shrink, output, attended, own, kept=()):
-    length, units, width = x.shape[0], expand.shape[1], output.shape[0]
-    steps, row, y = chip_rows(own, length)
+    if last:
+        out = matmul(activated, shrink_ref[...])
+        for half, o_ref in enumerate(attended):
+            out = out + matmul(o_ref[...], output_ref[half * 128 : (half + 1) * 128, :])
+        out_ref[...] = out.astype(BF)
+
+
+def feed(rows_of, x, units, first=None, scaled=None, last=None, kept=(), slots=None):
+    length = x.shape[0]
+    steps, row, y = chip_rows(rows_of, length)
+
+    def rows(columns):
+        return pl.BlockSpec((ROWS, columns), lambda i, *_: (row(i, _[0]), 0))
+
+    def whole(shape, column=0):
+        return pl.BlockSpec(shape, lambda i, *_: (0, column))
+
+    specs, values, halves, count = [rows(D)], [x], 0, 0
+    out_specs = [rows(units), rows(units)]
+    out_shape = [jax.ShapeDtypeStruct((length, units), BF)] * 2
+    if first is not None:
+        gain, low, bias, weight = first
+        values += [gain[None], low[None], bias[None]]
+        specs += [whole((1, D)), whole((1, D)), whole((1, units))]
+        out_specs += [whole((D, units)), whole((8, units))]
+        out_shape += [
+            jax.ShapeDtypeStruct((D, units), BF),
+            jax.ShapeDtypeStruct((8, units), F32),
+        ]
+        if slots is not None:
+            count = len(weight)
+            values += weight
+            specs += [pl.BlockSpec(memory_space=pltpu.VMEM)] * count
+            out_specs += [whole((D, units))]
+            out_shape += [jax.ShapeDtypeStruct((D, units), BF)]
+        else:
+            values.append(weight[0])
+            specs.append(whole((D, units), weight[1]))
+    else:
+        values += list(scaled)
+        specs += [whole((D, units)), whole((8, units))]
+    if last is not None:
+        shrink, output, attended = last
+        halves = len(attended)
+        if count:
+            out_specs.append(whole((units, D)))
+            out_shape.append(jax.ShapeDtypeStruct((units, D), BF))
+        else:
+            values.append(shrink[0])
+            specs.append(whole((units, D), shrink[1]))
+        values += [output, *attended]
+        specs += [whole(output.shape)] + [rows(128)] * halves
+        out_specs.append(pl.BlockSpec((ROWS, D), lambda i, *_: (i, 0)))
+        out_shape.append(jax.ShapeDtypeStruct((steps * ROWS, D), BF))
+    aliases = {2 + len(values) + n: n for n in range(len(kept))}
+    values += list(kept)
+    specs += [pl.BlockSpec(memory_space=pl.ANY)] * len(kept)
+    slots = jnp.zeros((1,), jnp.int32) if slots is None else jnp.stack(slots).astype(jnp.int32)
+    return pl.pallas_call(
+        partial(feed_kernel, first is not None, last is not None, halves, count),
+        grid_spec=pltpu.PrefetchScalarGridSpec(
+            num_scalar_prefetch=2, grid=(steps,), in_specs=specs, out_specs=out_specs
+        ),
+        out_shape=out_shape,
+        input_output_aliases=aliases,
+        compiler_params=pltpu.CompilerParams(vmem_limit_bytes=VMEM_LIMIT),
+        cost_estimate=LIGHT,
+        name="feed",
+    )(y.reshape(1), slots, *values)
+
+
+def branch_kernel(y_ref, act_ref, shrink_ref, output_ref, *refs):
+    out = matmul(act_ref[...], shrink_ref[...])
+    for half, o_ref in enumerate(refs[:-1]):
+        out = out + matmul(o_ref[...], output_ref[half * 128 : (half + 1) * 128, :])
+    refs[-1][...] = out.astype(BF)
+
+
+def branch(rows_of, activated, shrink, output, attended):
+    length, units = activated.shape
+    steps, row, y = chip_rows(rows_of, length)
 
     def rows(columns):
         return pl.BlockSpec((ROWS, columns), lambda i, y_ref: (row(i, y_ref), 0))
 
-    def whole(shape):
-        return pl.BlockSpec(shape, lambda i, y_ref: (0, 0))
-
-    first = 6 + len(attended)
     return pl.pallas_call(
-        feed_kernel,
+        branch_kernel,
         grid_spec=pltpu.PrefetchScalarGridSpec(
             num_scalar_prefetch=1,
             grid=(steps,),
-            in_specs=[rows(D), whole((D, units)), whole((1, units)), whole((units, D))]
-            + [whole((width, D))]
-            + [rows(128)] * len(attended)
-            + [pl.BlockSpec(memory_space=pl.ANY)] * len(kept),
-            out_specs=[
+            in_specs=[
                 rows(units),
-                rows(units),
-                pl.BlockSpec((ROWS, D), lambda i, y_ref: (i, 0)),
-            ],
+                pl.BlockSpec((units, D), lambda i, y_ref: (0, shrink[1])),
+                pl.BlockSpec(output.shape, lambda i, y_ref: (0, 0)),
+            ]
+            + [rows(128)] * len(attended),
+            out_specs=pl.BlockSpec((ROWS, D), lambda i, y_ref: (i, 0)),
         ),
-        out_shape=[
-            jax.ShapeDtypeStruct((length, units), BF),
-            jax.ShapeDtypeStruct((length, units), BF),
-            jax.ShapeDtypeStruct((steps * ROWS, D), BF),
-        ],
-        input_output_aliases={first: 0, first + 1: 1} if kept else {},
+        out_shape=jax.ShapeDtypeStruct((steps * ROWS, D), BF),
         compiler_params=pltpu.CompilerParams(vmem_limit_bytes=VMEM_LIMIT),
-        cost_estimate=pl.CostEstimate(
-            flops=2 * steps * ROWS * D * (2 * units + width),
-            bytes_accessed=2 * (2 * D * units + 2 * steps * ROWS * (D + units)),
-            transcendentals=steps * ROWS * units,
-        ),
-        name="feed",
-    )(y.reshape(1), x, expand, shift, shrink, output, *attended, *kept)
+        cost_estimate=LIGHT,
+        name="branch",
+    )(y.reshape(1), activated, shrink[0], output, *attended)
 
 
 def norm_grad_kernel(y_ref, h_ref, wi_ref, wm_ref, *refs):
@@ -619,13 +771,148 @@
         ),
         out_shape=jax.ShapeDtypeStruct((steps * ROWS, D), BF),
         compiler_params=pltpu.CompilerParams(vmem_limit_bytes=VMEM_LIMIT),
-        cost_estimate=pl.CostEstimate(
-            flops=2 * steps * ROWS * D * (units + columns),
-            bytes_accessed=2 * (D + steps * ROWS) * (units + columns),
-            transcendentals=0,
-        ),
+        cost_estimate=LIGHT,
         name="norm_grad",
     )(y.reshape(1), hidden, expand, mixing, *mixed)
+
+
+def hidden_back_kernel(grad_ref, shrink_ref, slope_ref, output_ref, low_ref, total_ref, do_ref):
+    grads = grad_ref[...]
+    hidden = matmul_nt(grads, shrink_ref[...]) * slope_ref[...].astype(F32)
+    low_ref[...] = hidden.astype(BF)
+
+    @pl.when(pl.program_id(0) == 0)
+    def _():
+        total_ref[...] = jnp.zeros(total_ref.shape, F32)
+
+    total_ref[...] += jnp.sum(hidden, 0, keepdims=True)
+    do_ref[...] = matmul_nt(grads, output_ref[...]).astype(BF)
+
+
+def hidden_back(grads, shrink, slope, output):
+    length, units = slope.shape
+    width = output.shape[0]
+    array, column = shrink
+    return pl.pallas_call(
+        hidden_back_kernel,
+        grid=(length // BLOCK,),
+        in_specs=[
+            pl.BlockSpec((BLOCK, D), lambda i: (i, 0)),
+            pl.BlockSpec((units, D), lambda i: (0, column)),
+            pl.BlockSpec((BLOCK, units), lambda i: (i, 0)),
+            pl.BlockSpec((width, D), lambda i: (0, 0)),
+        ],
+        out_specs=[
+            pl.BlockSpec((BLOCK, units), lambda i: (i, 0)),
+            pl.BlockSpec((1, units), lambda i: (0, 0)),
+            pl.BlockSpec((BLOCK, width), lambda i: (i, 0)),
+        ],
+        out_shape=[
+            jax.ShapeDtypeStruct((length, units), BF),
+            jax.ShapeDtypeStruct((1, units), F32),
+            jax.ShapeDtypeStruct((length, width), BF),
+        ],
+        compiler_params=pltpu.CompilerParams(vmem_limit_bytes=VMEM_LIMIT),
+        cost_estimate=LIGHT,
+        name="hidden_back",
+    )(grads, array, slope, output)
+
+
+def product_kernel(x_ref, g_ref, out_ref):
+    out_ref[...] = matmul_tn(x_ref[...], g_ref[...]).astype(BF)
+
+
+def product(x, grads, block=BLOCK):
+    length, count = x.shape
+    block = min(block, count)
+    return pl.pallas_call(
+        product_kernel,
+        grid=(count // block,),
+        in_specs=[
+            pl.BlockSpec((length, block), lambda i: (0, i)),
+            pl.BlockSpec((length, D), lambda i: (0, 0)),
+        ],
+        out_specs=pl.BlockSpec((block, D), lambda i: (i, 0)),
+        out_shape=jax.ShapeDtypeStruct((count, D), BF),
+        compiler_params=pltpu.CompilerParams(vmem_limit_bytes=VMEM_LIMIT),
+        cost_estimate=LIGHT,
+        name="product",
+    )(x, grads)
+
+
+def weight_grad_kernel(x_ref, weight_ref, gain_ref, shift_ref, total_ref, *refs):
+    lows, (out_ref, gain_out_ref, shift_out_ref) = refs[:-3], refs[-3:]
+    gain, shift = as_column(gain_ref[...]), as_column(shift_ref[...])
+    x = x_ref[...]
+    start, gain_sum, shift_sum = 0, 0.0, 0.0
+    for low_ref in lows:
+        columns = slice(start, start + low_ref.shape[1])
+        start += low_ref.shape[1]
+        raw = matmul_tn(x, low_ref[...])
+        weight = weight_ref[:, columns].astype(F32)
+        total = total_ref[:, columns]
+        out_ref[:, columns] = (raw * gain + shift * total).astype(BF)
+        gain_sum = gain_sum + jnp.sum(raw * weight, 1, keepdims=True)
+        shift_sum = shift_sum + jnp.sum(weight * total, 1, keepdims=True)
+    gain_out_ref[...] = as_row(gain_sum)
+    shift_out_ref[...] = as_row(shift_sum)
+
+
+def weight_grad(x, lows, weight, gain, shift, total):
+    length, columns = x.shape[0], total.shape[1]
+    array, column = weight
+    row = pl.BlockSpec((1, ROWS), lambda i: (0, i))
+    return pl.pallas_call(
+        weight_grad_kernel,
+        grid=(D // ROWS,),
+        in_specs=[
+            pl.BlockSpec((length, ROWS), lambda i: (0, i)),
+            pl.BlockSpec((ROWS, columns), lambda i: (i, column)),
+            row,
+            row,
+            pl.BlockSpec((1, columns), lambda i: (0, 0)),
+        ]
+        + [pl.BlockSpec(low.shape, lambda i: (0, 0)) for low in lows],
+        out_specs=[pl.BlockSpec((ROWS, columns), lambda i: (i, 0)), row, row],
+        out_shape=[
+            jax.ShapeDtypeStruct((D, columns), BF),
+            jax.ShapeDtypeStruct((1, D), F32),
+            jax.ShapeDtypeStruct((1, D), F32),
+        ],
+        compiler_params=pltpu.CompilerParams(vmem_limit_bytes=VMEM_LIMIT),
+        cost_estimate=LIGHT,
+        name="weight_grad",
+    )(x, array, gain[None], shift[None], total, *lows)
+
+
+def pack_kernel(spans, mixing_ref, expand_ref, *refs):
+    out_ref = refs[-1]
+    for source_ref, part in ((mixing_ref, spans[0]), (expand_ref, spans[1])):
+        for p, start, at, count in part:
+            out_ref[p, :, start : start + count] = source_ref[0, :, at : at + count].astype(BF)
+    for pair_ref in refs[:-1]:
+        end = out_ref.shape[2] - pair_ref.shape[1]
+        for p in range(out_ref.shape[0]):
+            out_ref[p, :, end:] = pair_ref[...]
+
+
+def pack(mixing, expand, layer, spans, columns, pair=()):
+    parts, rows = lax.axis_size("seq"), mixing.shape[1]
+    columns = columns + sum(value.shape[1] for value in pair)
+    return pl.pallas_call(
+        partial(pack_kernel, spans),
+        grid=(1,),
+        in_specs=[
+            pl.BlockSpec((1,) + mixing.shape[1:], lambda i: (layer, 0, 0)),
+            pl.BlockSpec((1,) + expand.shape[1:], lambda i: (layer, 0, 0)),
+        ]
+        + [pl.BlockSpec(value.shape, lambda i: (0, 0)) for value in pair],
+        out_specs=pl.BlockSpec((parts, rows, columns), lambda i: (0, 0, 0)),
+        out_shape=jax.ShapeDtypeStruct((parts, rows, columns), BF),
+        compiler_params=pltpu.CompilerParams(vmem_limit_bytes=VMEM_LIMIT),
+        cost_estimate=LIGHT,
+        name="pack",
+    )(mixing, expand, *pair)
 
 
 def home_spans(parts, copies, width, units):
@@ -692,6 +979,7 @@
         out_specs=[block(state) for state in states],
         out_shape=[jax.ShapeDtypeStruct(state.shape, F32) for state in states],
         compiler_params=pltpu.CompilerParams(vmem_limit_bytes=VMEM_LIMIT),
+        cost_estimate=LIGHT,
         name="update",
     )(clip, exchanged, output, shrink, *states)
 
@@ -792,29 +1080,22 @@
         view = jnp.zeros((copies, parts, rows_f), F32)
         return lax.dynamic_update_slice(view, vector.reshape(copies, 1, rows_f), (0, part, 0)).reshape(-1)
 
-    def arrange(mixing, expand):
-        mixing = mixing.astype(BF).reshape(rows_d, 3, parts, halves, 128)
+    spans = home_spans(parts, copies, width, units)
+    aligned = rows_f % 128 == 0 and rows_d % 16 == 0
+
+    def arrange(layer, mixing, expand, pair=()):
+        if aligned:
+            return pack(mixing, expand, layer, spans, 3 * width + units, pair)
+        mixing = mixing[layer].astype(BF).reshape(rows_d, 3, parts, halves, 128)
         mixing = mixing.transpose(2, 0, 3, 1, 4).reshape(parts, rows_d, 3 * width)
-        expand = expand.astype(BF).reshape(rows_d, copies, parts, rows_f)
+        expand = expand[layer].astype(BF).reshape(rows_d, copies, parts, rows_f)
         expand = expand.transpose(2, 0, 1, 3).reshape(parts, rows_d, units)
-        return [mixing, expand]
-
-    def settle_output(gathered):
-        gathered = gathered.reshape(parts, copies // parts * rows_d, D)
-        output = seq_exchange(gathered).reshape(parts, copies // parts, rows_d, D)
+        pair = [jnp.broadcast_to(value, (parts,) + value.shape) for value in pair]
+        return jnp.concatenate([mixing, expand] + pair, -1)
+
+    def settle_output(exchanged):
+        output = exchanged.reshape(parts, copies // parts, rows_d, D)
         return output.transpose(1, 0, 2, 3).reshape(width, D)
-
-    def scaled(weight, gain, shift, bias):
-        wide = weight.astype(F32)
-        return (wide * gain[:, None]).astype(BF), (jnp.sum(wide * shift[:, None], 0) + bias)[None]
-
-    def shift_grads(raw, weight, total, gain, shift):
-        wide = weight.astype(F32)
-        return (
-            (raw * gain[:, None] + shift[:, None] * total).astype(BF),
-            jnp.sum(raw * wide, 1),
-            jnp.sum(wide * total, 1),
-        )
 
     def norm_back(gradient, normed_grad, own_normed, scale):
         projected = jnp.mean(normed_grad * own_normed, -1, keepdims=True)
@@ -822,31 +1103,34 @@
         return gradient + scale * (normed_grad - middle - own_normed * projected)
 
     def outgoing_output(attended, grads):
-        output_grad = jnp.concatenate([matmul_tn(out, grads).astype(BF) for out in attended], 0)
+        output_grad = jnp.concatenate([product(out, grads) for out in attended], 0)
         output_grad = output_grad.reshape(copies // parts, parts, rows_d, D).transpose(1, 0, 2, 3)
         output_grad = seq_exchange(output_grad.reshape(parts, copies // parts * rows_d, D))
         return output_grad.reshape(-1, width)
 
-    def affine_home(pieces):
-        affine_grad = lax.all_to_all(
-            jnp.concatenate(pieces).reshape(devices, small),
-            ("dp", "seq"),
-            split_axis=0,
-            concat_axis=0,
-            tiled=True,
-        )
-        return jnp.sum(affine_grad, 0)
+    def exchange_affine(pieces):
+        grads = jnp.concatenate(pieces).reshape(devices, 1, small)
+        return lax.all_to_all(grads, ("dp", "seq"), split_axis=0, concat_axis=0, tiled=True)
 
     def sum_squares(*values):
         return sum(jnp.sum(value.astype(F32) * value.astype(F32)) for value in values)
 
+    tie = lax.optimization_barrier
     current = stream.reshape(rows, D)
     gradient = cotangent.reshape(rows, D)
 
+    def view(array, column):
+        if units == D:
+            return array, column
+        return array[:, column * units : (column + 1) * units].reshape(-1, D), 0
+
     pair = jnp.stack([positions.reshape(-1) // 16, positions.reshape(-1) % 16]).astype(BF)
-    pair = jnp.broadcast_to(pair.reshape(1, rows_d, -1), (parts, rows_d, 2 * rows // rows_d))
-    both = jnp.concatenate(arrange(mixing_weight[0], expand_weight[0]) + [pair], -1)
+    pair = pair.reshape(rows_d, 2 * rows // rows_d)
+    both = arrange(0, mixing_weight, expand_weight, (pair,))
+    both, current = tie((both, current))
     both = seq_exchange(both)
+    own_normed, scale = normalize(current)
+    travel = SeqGather(own_normed.astype(BF))
     pair = both[..., 3 * width + units :].astype(F32).reshape(parts, 2, rows)
     places = (pair[:, 0] * 16.0 + pair[:, 1]).reshape(-1)
     both = both.reshape(parts * rows_d, -1)
@@ -855,8 +1139,11 @@
             [both[:, : 3 * width], output_weight[0].astype(BF).reshape(-1, width)], -1
         )
     )
-    affine_low, near.pieces = lax.optimization_barrier((affine_weight.astype(BF), near.pieces))
-    affine_low = affine_low.reshape(1, LAYERS * small)
+    places, affine_low, layer_mixing, layer_expand = near.hold(
+        places, affine_weight, mixing_weight, expand_weight
+    )
+    near.forward()
+    affine_low = affine_low.astype(BF).reshape(1, LAYERS * small)
     affine_all = lax.all_to_all(
         jnp.broadcast_to(affine_low, (devices, LAYERS * small)),
         ("dp", "seq"),
@@ -864,201 +1151,279 @@
         concat_axis=0,
         tiled=True,
     )
+    cosine, sine = rotary_tables(places)
+    later_both = arrange(1, layer_mixing, layer_expand)
+    cosine, sine, later_both, expand_own, shrink_own = near.hold(
+        cosine, sine, later_both, both[:, 3 * width : 3 * width + units], shrink_weight[0]
+    )
+    near.forward()
+    near.cross()
+    far_own = jnp.concatenate([expand_own, shrink_own.astype(BF).reshape(-1, units)], -1)
+    affine_all, far_own, near.pieces, near.chains, travel.pieces, later_both, low_gradient = tie(
+        (
+            affine_all,
+            far_own,
+            near.pieces,
+            near.chains,
+            travel.pieces,
+            later_both,
+            gradient,
+        )
+    )
+    normed = travel.done()
+    near.forward()
+    near.cross()
+    travel = SeqGather(low_gradient.astype(BF))
     affine_all = affine_all.reshape(devices, LAYERS, small).transpose(1, 0, 2)
     affine_all = affine_all.reshape(LAYERS, devices * small).astype(F32)
     vectors = [split_affine(affine_all[layer]) for layer in range(LAYERS)]
-    own_normed, scale = normalize(current)
-    normed = seq_gather(own_normed.astype(BF))
-    for step in range(outer - 1):
+    vectors, normed = near.hold(vectors, normed)
+    for step in range(3, outer - 1):
         near.forward()
         near.cross()
-    expand_own, shrink_own, places = near.hold(
-        both[:, 3 * width : 3 * width + units], shrink_weight[0], places
-    )
-    near.cross()
-    far = Gather(
-        jnp.concatenate([expand_own, shrink_own.astype(BF).reshape(-1, units)], -1)
-    )
+    while len(near.chains) < outer:
+        near.cross()
+    far = Gather(far_own)
+    far.pieces[0], near.pieces, near.chains = tie((far.pieces[0], near.pieces, near.chains))
     far.forward()
     far.cross()
-    cosine, sine = rotary_tables(places)
-    gathered = near.done()
-    mixing = gathered[:, : 3 * width]
-    output = settle_output(gathered[:, 3 * width :].reshape(copies * rows_d, D))
-
-    later = far.hold(
-        *(weight[1] for weight in (mixing_weight, expand_weight, output_weight, shrink_weight))
-    )
-    later_both = seq_exchange(jnp.concatenate(arrange(later[0], later[1]), -1))
+    pieces, slots = near.done()
+    later_both = seq_exchange(later_both)
+
+    gain_one, shift_one, gain_two, shift_two = vectors[0][:4]
+    mixing, output, mixed, mixing_scaled = mix(
+        normed, pieces, gain_one, shift_one, mixing_part(vectors[0][4]), cosine, sine, slots
+    )
+    mixed, output, later_both, later_shrink, later_output = far.hold(
+        mixed, output, later_both, shrink_weight[1], output_weight[1]
+    )
+    far.forward()
+    far.cross()
+    output = seq_exchange(output.reshape(parts, -1, D))
+
     later_both = later_both.reshape(parts * rows_d, -1)
     later_own = jnp.concatenate(
         [
+            later_both[:, 3 * width :],
+            later_shrink.astype(BF).reshape(-1, units),
             later_both[:, : 3 * width],
-            later[2].astype(BF).reshape(-1, width),
-            later_both[:, 3 * width :],
-            later[3].astype(BF).reshape(-1, units),
+            later_output.astype(BF).reshape(-1, width),
         ],
         -1,
     )
+    (later_own,) = travel.hold(later_own)
     later_all = lax.all_gather(later_own, "dp", axis=0, tiled=True)
-
-    gain_one, shift_one, gain_two, shift_two = vectors[0][:4]
-    mixing_scaled, mixing_shift = scaled(mixing, gain_one, shift_one, mixing_part(vectors[0][4]))
-    mixed = mix(normed, mixing_scaled, mixing_shift, cosine, sine)
-    mixed, low_gradient = far.hold(mixed, gradient.astype(BF))
-    grads = seq_gather(low_gradient)
-    attended, logs = [], []
-    for half in range(halves):
-        if len(far.pieces) < outer:
-            far.forward()
-            far.cross()
-        out, log_total = attend(mixed, half)
-        mixed, out, log_total, grads = far.hold(mixed, out, log_total, grads)
-        attended.append(out)
-        logs.append(log_total)
-    while len(far.pieces) < outer:
-        far.forward()
-    while len(far.chains) < outer:
-        far.cross()
-    gathered = far.done()
-    expand, shrink = gathered[:, :units], gathered[:, units:].reshape(-1, D)
-    expand_scaled, expand_shift = scaled(
-        expand, gain_two, shift_two, expand_part(vectors[0][6])
-    )
-    weight_set = (normed, expand_scaled, expand_shift, shrink, output, attended)
-    activated, slope, others = feed(*weight_set, False)
-    activated, slope, own = feed(*weight_set, True, (activated, slope))
-    stored = [(own_normed, scale, normed, mixed, attended, logs, activated, slope)]
-    weights = [(mixing, mixing_scaled, output, expand, expand_scaled, shrink)]
-    current = current + SeqScatter(others, own).done() + vectors[0][5] + vectors[0][7]
-
-    own_normed, scale = normalize(current)
-    normed = seq_gather(own_normed.astype(BF))
-    mixing = later_all[:, : 3 * width]
-    output = settle_output(later_all[:, 3 * width : 4 * width].reshape(copies * rows_d, D))
-    expand = later_all[:, 4 * width : 4 * width + units]
-    shrink = later_all[:, 4 * width + units :].reshape(-1, D)
-    gain_one, shift_one, gain_two, shift_two = vectors[1][:4]
-    mixing_scaled, mixing_shift = scaled(mixing, gain_one, shift_one, mixing_part(vectors[1][4]))
-    expand_scaled, expand_shift = scaled(
-        expand, gain_two, shift_two, expand_part(vectors[1][6])
-    )
-    mixed = mix(normed, mixing_scaled, mixing_shift, cosine, sine)
     attended, logs = [], []
     for half in range(halves):
         out, log_total = attend(mixed, half)
         attended.append(out)
         logs.append(log_total)
-    weight_set = (normed, expand_scaled, expand_shift, shrink, output, attended)
-    activated, slope, others = feed(*weight_set, False)
-    activated, slope, own = feed(*weight_set, True, (activated, slope))
-    result = current + SeqScatter(others, own).done() + vectors[1][5] + vectors[1][7]
-    result = result.reshape(stream.shape)
-
-    attended_grad = matmul_nt(grads, output).astype(BF)
-    shrink_grad = matmul_tn(activated, grads).astype(BF).reshape(-1, units)
+        if half == 0:
+            mixed, out, output = far.hold(mixed, out, output)
+            far.forward()
+            far.cross()
+    output = settle_output(output)
+    attended, logs = far.hold(attended, logs)
+    while len(far.pieces) < outer:
+        far.forward()
+    while len(far.chains) < outer:
+        far.cross()
+    grads = travel.done()
+    attended, logs, grads = far.hold(attended, logs, grads)
+    pieces, slots = far.done()
+    first = (gain_two, shift_two, expand_part(vectors[0][6]))
+    if units == D:
+        activated, slope, expand_scaled, expand_shift, expand, shrink, others = feed(
+            False,
+            normed,
+            units,
+            first=first + (pieces,),
+            last=(None, output, attended),
+            slots=slots,
+        )
+    else:
+        far_all = assemble(pieces, slots)
+        expand, shrink = far_all[:, :units], view(far_all, 1)[0]
+        activated, slope, expand_scaled, expand_shift, others = feed(
+            False,
+            normed,
+            units,
+            first=first + ((expand, 0),),
+            last=((shrink, 0), output, attended),
+        )
+    shrink = (shrink, 0)
+    travel = SeqScatter(others)
+    activated, slope = travel.hold(activated, slope)
+    activated, slope, own = feed(
+        True,
+        normed,
+        units,
+        scaled=(expand_scaled, expand_shift),
+        last=(shrink, output, attended),
+        kept=(activated, slope),
+    )
+    stored = [(own_normed, scale, normed, mixed, attended, logs, activated, slope)]
+    weights = [(mixing, mixing_scaled, output, expand, expand_scaled, shrink)]
+    current = current + travel.done(own)[0] + vectors[0][5] + vectors[0][7]
+
+    own_normed, scale = normalize(current)
+    travel = SeqGather(own_normed.astype(BF))
+    mixing = later_all[:, 2 * units : 2 * units + 3 * width]
+    later_output = later_all[:, 2 * units + 3 * width :].reshape(copies * rows_d, D)
+    mixing, later_output, later_all = travel.hold(mixing, later_output, later_all)
+    normed = travel.done()
+    expand, shrink = later_all, view(later_all, 1)
+    gain_one, shift_one, gain_two, shift_two = vectors[1][:4]
+    mixed, mixing_scaled = mix(
+        normed, [mixing], gain_one, shift_one, mixing_part(vectors[1][4]), cosine, sine
+    )
+    mixed, later_output = tie((mixed, later_output))
+    output = seq_exchange(later_output.reshape(parts, -1, D))
+    attended, logs = [], []
+    for half in range(halves):
+        out, log_total = attend(mixed, half)
+        attended.append(out)
+        logs.append(log_total)
+    activated, slope, expand_scaled, expand_shift = feed(
+        None,
+        normed,
+        units,
+        first=(gain_two, shift_two, expand_part(vectors[1][6]), (later_all, 0)),
+    )
+
+    grads, attended, logs, activated, output = tie((grads, attended, logs, activated, output))
+    output = settle_output(output)
     output_grad = outgoing_output(attended, grads)
-    later_first = lax.psum_scatter(
-        jnp.concatenate([shrink_grad, output_grad], -1), "dp", scatter_dimension=0, tiled=True
-    )
-    hidden_grad = matmul_nt(grads, shrink) * slope.astype(F32)
-    hidden_total = jnp.sum(hidden_grad, 0)
-    hidden_low = hidden_grad.astype(BF)
+    hidden_low, hidden_total, attended_grad = hidden_back(grads, shrink, slope, output)
+    shrink_grad = product(activated, grads).reshape(-1, units)
+    expand_grad, gain_two_grad, shift_two_grad = weight_grad(
+        normed, [hidden_low], (expand, 0), gain_two, shift_two, hidden_total
+    )
+    later_grad = jnp.concatenate([expand_grad, shrink_grad, output_grad], -1)
+    later_grad, attended_grad = tie((later_grad, attended_grad))
+    later_first = lax.psum_scatter(later_grad, "dp", scatter_dimension=0, tiled=True)
     lows, totals = [], []
     for half in range(halves):
         low, total = attend_back(
             mixed, attended_grad, attended[half], logs[half], cosine, sine, half
         )
         lows.append(low)
-        totals.append(total[0])
-    mixed_total = jnp.concatenate(totals)
-    output_sum = jnp.sum(gradient, 0)
+        totals.append(total)
+    mixed_total = jnp.concatenate(totals, -1)
     others = norm_grad(hidden_low, expand_scaled, lows, mixing_scaled, False)
+    travel = SeqScatter(others)
+    hidden_low, lows, activated = travel.hold(hidden_low, lows, activated)
     own = norm_grad(hidden_low, expand_scaled, lows, mixing_scaled, True)
-    travel = SeqScatter(others, own)
-    hidden_low, lows = travel.hold(hidden_low, lows)
-    expand_raw = matmul_tn(normed, hidden_low)
-    mixing_raw = jnp.concatenate([matmul_tn(normed, low) for low in lows], -1)
-    expand_grad, gain_two_grad, shift_two_grad = shift_grads(
-        expand_raw, expand, hidden_total, gain_two, shift_two
-    )
-    mixing_grad, gain_one_grad, shift_one_grad = shift_grads(
-        mixing_raw, mixing, mixed_total, gain_one, shift_one
-    )
-    pieces = [gain_one_grad, shift_one_grad, gain_two_grad, shift_two_grad]
-    pieces += [spread_mixing(mixed_total), output_sum, spread_expand(hidden_total), output_sum]
-    normed_grad, expand_grad, mixing_grad, pieces = lax.optimization_barrier(
-        (travel.done(), expand_grad, mixing_grad, pieces)
-    )
+    last = (shrink, output, attended)
+    result_others = branch(False, activated, *last)
+    result_own = branch(True, activated, *last)
+    normed_grad, (result_others, result_own) = travel.done(own, (result_others, result_own))
+    normed_grad, lows = tie((normed_grad, lows))
     gradient = norm_back(gradient, normed_grad, own_normed, scale)
-    low_gradient, expand_grad, mixing_grad, pieces = lax.optimization_barrier(
-        (gradient.astype(BF), expand_grad, mixing_grad, pieces)
-    )
-    grads = seq_gather(low_gradient)
-    later_second = lax.psum_scatter(
-        jnp.concatenate([mixing_grad, expand_grad], -1), "dp", scatter_dimension=0, tiled=True
-    )
-    later_affine = affine_home(pieces)
-
+    travel = SeqGather(gradient.astype(BF))
+    lows, own_piece = tie((lows, travel.pieces[0]))
+    mixing_grad, gain_one_grad, shift_one_grad = weight_grad(
+        normed, lows, (mixing, 0), gain_one, shift_one, mixed_total
+    )
+    (mixing_grad,) = travel.hold(mixing_grad)
+    grads = travel.done()
+    later_mixing = sum_exchange(mixing_grad)
+    output_sum = jnp.sum(cotangent.reshape(rows, D), 0)
+
+    def small_grads(*pieces):
+        gains, mixed_total, output_sum, hidden_total = pieces
+        pieces = [piece[0] for piece in gains]
+        pieces += [spread_mixing(mixed_total[0]), output_sum]
+        return pieces + [spread_expand(hidden_total[0]), output_sum]
+
+    gains = (gain_one_grad, shift_one_grad, gain_two_grad, shift_two_grad)
+    later_pieces = small_grads(gains, mixed_total, output_sum, hidden_total)
+
+    later_current, later_vectors = current, vectors[1]
+    current = stream.reshape(rows, D)
     own_normed, scale, normed, mixed, attended, logs, activated, slope = stored[0]
     mixing, mixing_scaled, output, expand, expand_scaled, shrink = weights[0]
     gain_one, shift_one, gain_two, shift_two = vectors[0][:4]
-    shrink_grad = matmul_tn(activated, grads).astype(BF).reshape(-1, units)
-    hidden_grad = matmul_nt(grads, shrink) * slope.astype(F32)
-    hidden_total = jnp.sum(hidden_grad, 0)
-    hidden_low = hidden_grad.astype(BF)
-    expand_raw = matmul_tn(normed, hidden_low)
-    expand_grad, gain_two_grad, shift_two_grad = shift_grads(
-        expand_raw, expand, hidden_total, gain_two, shift_two
-    )
-    attended_grad = matmul_nt(grads, output).astype(BF)
-    far = Scatter(expand_grad, shrink_grad)
-    (attended_grad,) = far.hold(attended_grad)
+    far = Scatter(product(activated, grads).reshape(-1, units))
+    (grads,) = far.hold(grads)
     far.cross()
+    hidden_low, hidden_total, attended_grad = hidden_back(grads, shrink, slope, output)
+    hidden_low, attended_grad, result_others, later_pieces = far.hold(
+        hidden_low, attended_grad, result_others, later_pieces
+    )
+    far.forward()
+    far.cross()
+    expand_grad, gain_two_grad, shift_two_grad = weight_grad(
+        normed, [hidden_low], (expand, 0), gain_two, shift_two, hidden_total
+    )
     output_grad = outgoing_output(attended, grads)
+    attended_grad, expand_grad, output_grad = far.hold(attended_grad, expand_grad, output_grad)
+    far_grad = lax.psum_scatter(
+        jnp.concatenate([expand_grad, output_grad], -1), "dp", scatter_dimension=0, tiled=True
+    )
+    travel = SeqScatter(result_others)
     lows, totals = [], []
     for half in range(halves):
+        if len(far.parts) < outer:
+            far.forward()
+            far.cross()
         low, total = attend_back(
             mixed, attended_grad, attended[half], logs[half], cosine, sine, half
         )
-        mixed, low, total = far.hold(mixed, low, total)
-        if len(far.parts) < outer:
-            far.forward()
-            far.cross()
+        mixed, low, total, later_mixing = far.hold(mixed, low, total, later_mixing)
+        if half == 0:
+            result, (mixed, low) = travel.done(result_own, (mixed, low))
+            exchanged = exchange_affine(later_pieces)
         lows.append(low)
-        totals.append(total[0])
-    mixed_total = jnp.concatenate(totals)
-    mixing_raw = jnp.concatenate([matmul_tn(normed, low) for low in lows], -1)
-    mixing_grad, gain_one_grad, shift_one_grad = shift_grads(
-        mixing_raw, mixing, mixed_total, gain_one, shift_one
-    )
-    mixing_grad, lows = far.hold(mixing_grad, lows)
+        totals.append(total)
+    exchanged, lows = tie((exchanged, lows))
+    later_affine = jnp.sum(exchanged, 0)
+    mixed_total = jnp.concatenate(totals, -1)
+    mixing_grad, gain_one_grad, shift_one_grad = weight_grad(
+        normed, lows, (mixing, 0), gain_one, shift_one, mixed_total
+    )
+    output_sum = jnp.sum(gradient, 0)
+    gains = (gain_one_grad, shift_one_grad, gain_two_grad, shift_two_grad)
+    pieces = small_grads(gains, mixed_total, output_sum, hidden_total)
+    pieces = jnp.concatenate(pieces).reshape(devices, small)
+    coarse = pieces.astype(BF)
+    fine = (pieces - coarse.astype(F32)).astype(BF)
+    pieces = jnp.concatenate([coarse, fine], -1)
+    extra = 128 * pl.cdiv(2 * small, 128 * rows_d)
+    pieces = jnp.pad(pieces, ((0, 0), (0, extra * rows_d - 2 * small)))
+    mixing_grad = jnp.concatenate([mixing_grad, pieces.reshape(D, extra)], -1)
+    mixing_grad, lows, result, later_first = tie((mixing_grad, lows, result, later_first))
+    mixing_grad = sum_exchange(mixing_grad)
+    result = later_current + result + later_vectors[5] + later_vectors[7]
+    result = result.reshape(stream.shape)
+    others = norm_grad(hidden_low, expand_scaled, lows, mixing_scaled, False)
+    travel = SeqScatter(others)
+    (lows,) = travel.hold(lows)
+    own = norm_grad(hidden_low, expand_scaled, lows, mixing_scaled, True)
     while len(far.parts) < outer:
         far.forward()
         far.cross()
-    near = Scatter(mixing_grad, output_grad)
-    near.cross()
     while far.steps < outer - 1:
         far.forward()
-    others = norm_grad(hidden_low, expand_scaled, lows, mixing_scaled, False)
-    own = norm_grad(hidden_low, expand_scaled, lows, mixing_scaled, True)
-    travel = SeqScatter(others, own)
-    for step in range(outer - 1):
-        near.forward()
-        near.cross()
-    output_sum = jnp.sum(gradient, 0)
-    pieces = [gain_one_grad, shift_one_grad, gain_two_grad, shift_two_grad]
-    pieces += [spread_mixing(mixed_total), output_sum, spread_expand(hidden_total), output_sum]
-    affine_grad = jnp.stack([affine_home(pieces), later_affine])
-    gradient = norm_back(gradient, travel.done(), own_normed, scale)
-    stream_grad = gradient.reshape(stream.shape)
-
-    later_home = seq_exchange(later_second.reshape(parts, rows_d, -1))
-    far_grad = far.done()
-    near_grad = near.done()
-    home = jnp.concatenate([near_grad[:, : 3 * width], far_grad[:, :units]], -1).astype(BF)
-    home = seq_exchange(home.reshape(parts, rows_d, -1))
-    squares = sum_squares(near_grad, far_grad, later_first, later_second, affine_grad)
+    shrink_grad = far.done()
+    later_mixing = jnp.sum(later_mixing.astype(F32), 0)
+    squares = sum_squares(shrink_grad, later_first, later_mixing, later_affine)
+    shrink_grad, later_mixing = shrink_grad.astype(BF), later_mixing.astype(BF)
+    normed_grad, (mixing_grad, squares, shrink_grad, later_mixing) = travel.done(
+        own, (mixing_grad, squares, shrink_grad, later_mixing)
+    )
+
+    home = jnp.stack([far_grad[:, :units], later_first[:, :units]], 1)
+    home = seq_exchange(home.reshape(parts, rows_d, 2, units))
+    output_grad = far_grad[:, units:]
+    pieces = mixing_grad[..., 3 * width :].reshape(devices, -1)[:, : 2 * small].astype(F32)
+    affine_grad = jnp.sum(pieces[:, :small] + pieces[:, small:], 0, keepdims=True)
+    mixing_grad = jnp.sum(mixing_grad[..., : 3 * width].astype(F32), 0)
+    squares = squares + sum_squares(mixing_grad, affine_grad, far_grad)
+    mixing_grad = mixing_grad.astype(BF)
+    affine_grad = jnp.stack([affine_grad[0], later_affine[0]])
+    squares, home = tie((squares, home))
+    expand_grad, later_expand = home[:, :, 0], home[:, :, 1]
     squares = lax.all_to_all(
         jnp.broadcast_to(squares, (devices, 128)),
         ("dp", "seq"),
@@ -1066,16 +1431,19 @@
         concat_axis=0,
         tiled=True,
     )
+    squares, normed_grad = tie((squares, normed_grad))
+    gradient = norm_back(gradient, normed_grad, own_normed, scale)
+    stream_grad = gradient.reshape(stream.shape)
     gradient_norm = jnp.sqrt(jnp.sum(squares[:, 0]))
     clip_scale = jnp.minimum(1.0, CLIP_LIMIT / (gradient_norm + 1e-06))
-    exchanged = jnp.stack([home, later_home])
-    output_grad = jnp.stack(
-        [near_grad[:, 3 * width :].astype(BF), later_first[:, units:]]
-    ).reshape(LAYERS, rows_d, D)
-    shrink_grad = jnp.stack([far_grad[:, units:].astype(BF), later_first[:, :units]])
+    output_grad = jnp.stack([output_grad, later_first[:, 2 * units :]])
+    output_grad = output_grad.reshape(LAYERS, rows_d, D)
+    shrink_grad = jnp.stack([shrink_grad, later_first[:, units : 2 * units]])
     shrink_grad = shrink_grad.reshape(LAYERS, rows_f, D)
-    spans = home_spans(parts, copies, width, units)
-    if rows_f % 128 or rows_d % 16:
+    mixing_grad = jnp.stack([mixing_grad, later_mixing])
+    expand_grad = jnp.stack([expand_grad, later_expand])
+    exchanged = jnp.concatenate([mixing_grad, expand_grad], -1)
+    if not aligned:
         mixing_view = exchanged[..., : 3 * width].reshape(LAYERS, parts, rows_d, halves, 3, 128)
         mixing_view = mixing_view.transpose(0, 2, 4, 1, 3, 5).reshape(LAYERS, rows_d, 3 * D)
         expand_view = exchanged[..., 3 * width :].reshape(LAYERS, parts, rows_d, copies, rows_f)

time: 884 us -> 780 us (0.88)
  waiting for transfers between devices: 215 us -> 118 us
  Pallas kernels: 255 us -> 333 us
  matrix products: 73.7 us -> 2.97 us
  starting transfers between devices: 118 us -> 92 us
  other arithmetic: 84.3 us -> 72 us
  blocking collectives: 0 us -> 11.9 us
    pallas_call x6 -> x21, Pallas kernels: 70.2 us -> 154 us  [the longest x3 44.3 us: feed(): pl.pallas_call(partial(feed_kernel, first is not None, last is not None,...]
    ppermute x8, waiting for transfers between devices: 124 us -> 45.6 us  [chip_ring(): lax.ppermute(value, 'seq', [(i, (i + 2) % size) for i in range(size)])]
    dot_general x16 -> x0, matrix products: 67.2 us -> none  [the longest x12 46.3 us: matmul_tn(): lax.dot_general(left, right, (((0,), (0,)), ((), ())), preferred_element_...]
    ppermute x12 -> x9, waiting for transfers between devices: 41.4 us -> 18.9 us  [outer_ring(): lax.ppermute(value, 'dp', [(i, (i + inner) % size) for i in range(size)])]
    unnamed x290 -> x268, local copies, waits for them, and re-layouts: 35.3 us -> 56.6 us
    ppermute x16, waiting for transfers between devices: 2.8 us -> 17.5 us  [core_swap(): return lax.ppermute(value, 'seq', [(i, i ^ 1) for i in range(size)])]
    reduce_sum x9 -> x5, other arithmetic: 17.9 us -> 5.26 us  [the longest x1 1.74 us: local(): output_sum = jnp.sum(cotangent.reshape(rows, D), 0)]
    all_to_all x0 -> x1, blocking collectives: none -> 11.9 us  [seq_exchange(): return lax.all_to_all(value, 'seq', split_axis=0, concat_axis=0, tiled=True)]
  transfers between devices with their start and end apart: 67 -> 59, of which waited for: 26 -> 25; matrix products, arithmetic and copies ran while one was open for 25% -> 15% of each run, Pallas kernels for 25% -> 34%
where the time goes in v3:
time: 780 us; the launch traced here: 768 us
  Pallas kernels  333 us (43%)
  waiting for transfers between devices  118 us (15%)
  local copies, waits for them, and re-layouts  115 us (15%)
  starting transfers between devices  92 us (12%)
  other arithmetic  72 us (9%)
  between operations  22.5 us (3%)
  blocking collectives  11.9 us (2%)
    pallas_call x4, Pallas kernels, attend_back(): pl.pallas_call(attend_back_kernel, grid=(length // block,), in_specs=[pl....  79.1 us
    unnamed x268, local copies, waits for them, and re-layouts  56.6 us
    ppermute x8, waiting for transfers between devices, chip_ring(): lax.ppermute(value, 'seq', [(i, (i + 2) % size) for i in range(size)])  45.6 us
    pallas_call x3, Pallas kernels, feed(): pl.pallas_call(partial(feed_kernel, first is not None, last is not None,...  44.3 us
    pallas_call x4, Pallas kernels, attend(): pl.pallas_call(attend_kernel, grid=(length // block,), in_specs=[pl.Block...  40 us
    pallas_call x4, Pallas kernels, weight_grad(): pl.pallas_call(weight_grad_kernel, grid=(D // ROWS,), in_specs=[pl.BlockS...  32.9 us
    pallas_call x4, Pallas kernels, norm_grad(): pl.pallas_call(norm_grad_kernel, grid_spec=pltpu.PrefetchScalarGridSpec(n...  31.8 us
    all_to_all x6, starting transfers between devices, seq_exchange(): return lax.all_to_all(value, 'seq', split_axis=0, concat_axis=0, tiled=True)  24.2 us
  transfers between devices with their start and end apart: 59, of which 25 were waited for; matrix products, arithmetic and copies ran while one was open for 15% of the time, Pallas kernels for 34%

profile of v3, /device:TPU:0, one launch (start us, length us, event | category | flops | bytes accessed | tf_op | source)
XLA Modules:
  0.0 767.5 jit_solution(7553437282477625850)
XLA Ops:
  11.2 4.2 all-to-all-start
  43.1 4.1 all-to-all-done.1
  58.6 5.2 assemble.4
  69.7 4.4 collective-permute-done.8.refs_5_
  80.4 4.1 all-to-all-start.2
  89.3 10.8 %mix.2 = (bf16[1024,768]{1,0:T(8,128)(2,1)}, bf16[1024,256]{1,0:T(8,128)(2,1)S(1)}, bf16[2048,768]{1,0:T(8,128)(2,1)}, bf16[1024,768]{1,0:T(8,128)(2,1)}) custom-call(s32[8]{0:T(128)S(1)} %stack.121.slots_ref, bf16[2048,1024]{1,0:T(8,128)(2,1)} %bitcast.253, f32[1,1024]{1,0:T(1,128)S(1)} %get-tuple-element.606, f32[1,1024]{1,0:T(1,128)S(1)} %get-tuple-element.605, ...), custom_call_target="tpu_custom_call" | custom-call | flops 1000 | bytes 1000 | tf_op jit(solution)/shard_map/mix/pallas_call | solution.py:339
  111.2 4.1 all-to-all-start.3
  115.4 10.0 %attend.4 = (bf16[2048,128]{1,0:T(8,128)(2,1)S(1)}, f32[2,2048]{1,0:T(2,128)S(1)}) custom-call(bf16[2048,768]{1,0:T(8,128)(2,1)S(1)} %copy-done, bf16[2048,768]{1,0:T(8,128)(2,1)S(1)} %copy-done, bf16[2048,768]{1,0:T(8,128)(2,1)S(1)} %copy-done), custom_call_target="tpu_custom_call" | custom-call | flops 1000 | bytes 1000 | tf_op jit(solution)/shard_map/attend/pallas_call | solution.py:407
  130.1 10.0 %attend.5 = (bf16[2048,128]{1,0:T(8,128)(2,1)S(1)}, f32[2,2048]{1,0:T(2,128)S(1)}) custom-call(bf16[2048,768]{1,0:T(8,128)(2,1)S(1)} %copy-done, bf16[2048,768]{1,0:T(8,128)(2,1)S(1)} %copy-done, bf16[2048,768]{1,0:T(8,128)(2,1)S(1)} %copy-done), custom_call_target="tpu_custom_call" | custom-call | flops 1000 | bytes 1000 | tf_op jit(solution)/shard_map/attend/pallas_call | solution.py:407
  140.9 16.3 %collective-permute-done.14.refs_9_ = bf16[128,2048]{1,0:T(8,128)(2,1)} collective-permute-done((bf16[128,2048]{1,0:T(8,128)(2,1)}, bf16[128,2048]{1,0:T(8,128)(2,1)}, u32[]{:S(2)}, u32[]{:S(2)}) %collective-permute-start.14) | collective-permute-done | bytes 524320 | tf_op jit(solution)/shard_map/ppermute | solution.py:47
  159.9 5.5 assemble.5
  165.4 9.2 %collective-permute-done.19.refs_10_ = bf16[128,2048]{1,0:T(8,128)(2,1)S(1)} collective-permute-done((bf16[128,2048]{1,0:T(8,128)(2,1)}, bf16[128,2048]{1,0:T(8,128)(2,1)S(1)}, u32[]{:S(2)}, u32[]{:S(2)}) %collective-permute-start.19) | collective-permute-done | bytes 524320 | tf_op jit(solution)/shard_map/ppermute | solution.py:55
  174.6 15.6 %feed.3 = (bf16[2048,1024]{1,0:T(8,128)(2,1)}, bf16[2048,1024]{1,0:T(8,128)(2,1)}, bf16[1024,1024]{1,0:T(8,128)(2,1)}, f32[8,1024]{1,0:T(8,128)S(1)}, bf16[1024,...) custom-call(s32[1]{0:T(128)} %bitcast.1.y_ref, s32[8]{0:T(128)S(1)} %stack.121.slots_ref, ...), custom_call_target="tpu_custom_call" | custom-call | flops 1000 | bytes 1000 | tf_op jit(solution)/shard_map/feed/pallas_call | solution.py:699
  199.4 12.5 %feed.4 = (bf16[2048,1024]{1,0:T(8,128)(2,1)}, bf16[2048,1024]{1,0:T(8,128)(2,1)}, bf16[1024,1024]{1,0:T(8,128)(2,1)S(1)}) custom-call(s32[1]{0:T(128)} %bitcast.1.y_ref, s32[1]{0:T(128)} %constant.381.clone.1.slots_ref, bf16[2048,1024]{1,0:T(8,128)(2,1)} %bitcast.255, ...), custom_call_target="tpu_custom_call", output_to_operand_aliasing={{0}: (9, {}), {1}: (10, {})} | custom-call | flops 1000 | bytes 1000 | tf_op jit(solution)/shard_map/feed/pallas_call | solution.py:699
  211.8 11.0 %collective-permute-done.21 = bf16[512,1024]{1,0:T(8,128)(2,1)S(1)} collective-permute-done((bf16[512,1024]{1,0:T(8,128)(2,1)S(1)}, bf16[512,1024]{1,0:T(8,128)(2,1)S(1)}, u32[]{:S(2)}, u32[]{:S(2)}) %collective-permute-start.21) | collective-permute-done | bytes 1048608 | tf_op jit(solution)/shard_map/ppermute | solution.py:60
  234.6 18.9 %collective-permute-done.23.refs_2_ = bf16[512,1024]{1,0:T(8,128)(2,1)} collective-permute-done((bf16[512,1024]{1,0:T(8,128)(2,1)}, bf16[512,1024]{1,0:T(8,128)(2,1)}, u32[]{:S(2)}, u32[]{:S(2)}) %collective-permute-start.23) | collective-permute-done | bytes 1048608 | tf_op jit(solution)/shard_map/ppermute | solution.py:60
  258.0 5.3 assemble.6
  263.3 9.8 %mix.3 = (bf16[2048,768]{1,0:T(8,128)(2,1)}, bf16[1024,768]{1,0:T(8,128)(2,1)S(1)}) custom-call(s32[1]{0:T(128)} %constant.381.clone.1.slots_ref, bf16[2048,1024]{1,0:T(8,128)(2,1)} %bitcast.258, f32[1,1024]{1,0:T(1,128)S(1)} %get-tuple-element.600, f32[1,1024]{1,0:T(1,128)S(1)} %get-tuple-element.599, f32[1,768]{1,0:T(1,128)S(1)} %broadcast_in_dim_reshape.14.bias_ref, ...), custom_call_target="tpu_custom_call" | custom-call | flops 1000 | bytes 1000 | tf_op jit(solution)/shard_map/mix/pallas_call | solution.py:339
  274.2 4.1 all-to-all-start.4
  281.0 10.0 %attend.6 = (bf16[2048,128]{1,0:T(8,128)(2,1)S(1)}, f32[2,2048]{1,0:T(2,128)S(1)}) custom-call(bf16[2048,768]{1,0:T(8,128)(2,1)S(1)} %copy-done.1, bf16[2048,768]{1,0:T(8,128)(2,1)S(1)} %copy-done.1, bf16[2048,768]{1,0:T(8,128)(2,1)S(1)} %copy-done.1), custom_call_target="tpu_custom_call" | custom-call | flops 1000 | bytes 1000 | tf_op jit(solution)/shard_map/attend/pallas_call | solution.py:407
  291.8 10.0 %attend.7 = (bf16[2048,128]{1,0:T(8,128)(2,1)S(1)}, f32[2,2048]{1,0:T(2,128)S(1)}) custom-call(bf16[2048,768]{1,0:T(8,128)(2,1)S(1)} %copy-done.1, bf16[2048,768]{1,0:T(8,128)(2,1)S(1)} %copy-done.1, bf16[2048,768]{1,0:T(8,128)(2,1)S(1)} %copy-done.1), custom_call_target="tpu_custom_call" | custom-call | flops 1000 | bytes 1000 | tf_op jit(solution)/shard_map/attend/pallas_call | solution.py:407
  302.6 16.3 %feed.5 = (bf16[2048,1024]{1,0:T(8,128)(2,1)}, bf16[2048,1024]{1,0:T(8,128)(2,1)}, bf16[1024,1024]{1,0:T(8,128)(2,1)S(1)}, f32[8,1024]{1,0:T(8,128)}) custom-call(s32[1]{0:T(128)} %bitcast.1.y_ref, s32[1]{0:T(128)} %constant.381.clone.1.slots_ref, bf16[2048,1024]{1,0:T(8,128)(2,1)} %bitcast.259, f32[1,1024]{1,0:T(1,128)S(1)} %get-tuple-element.598, ...), custom_call_target="tpu_custom_call" | custom-call | flops 1000 | bytes 1000 | tf_op jit(solution)/shard_map/feed/pallas_call | solution.py:699
  326.1 4.1 all-to-all-start.5
  330.3 7.8 %product.6 = bf16[1024,1024]{1,0:T(8,128)(2,1)S(1)} custom-call(bf16[2048,1024]{1,0:T(8,128)(2,1)} %get-tuple-element.439.x_ref.act_ref, bf16[2048,1024]{1,0:T(8,128)(2,1)} %bitcast.222), custom_call_target="tpu_custom_call" | custom-call | flops 1000 | bytes 1000 | tf_op jit(solution)/shard_map/product/pallas_call | solution.py:828
  340.5 12.0 %hidden_back.2 = (bf16[2048,1024]{1,0:T(8,128)(2,1)S(1)}, f32[1,1024]{1,0:T(1,128)S(1)}, bf16[2048,256]{1,0:T(8,128)(2,1)S(1)}) custom-call(bf16[2048,1024]{1,0:T(8,128)(2,1)} %bitcast.223, bf16[1024,3072]{1,0:T(8,128)(2,1)} %all-gather.2.cloned.1.call-done.refs_3_.shrink_ref.weight_ref, bf16[2048,1024]{1,0:T(8,128)(2,1)} %get-tuple-element.417.slope_ref, ...), custom_call_target="tpu_custom_call" | custom-call | flops 1000 | bytes 1000 | tf_op jit(solution)/shard_map/hidden_back/pallas_call | solution.py:796
  355.6 9.1 %weight_grad.4 = (bf16[1024,1024]{1,0:T(8,128)(2,1)S(1)}, f32[1,1024]{1,0:T(1,128)S(1)}, f32[1,1024]{1,0:T(1,128)S(1)}) custom-call(bf16[2048,1024]{1,0:T(8,128)(2,1)} %bitcast.260, bf16[1024,3072]{1,0:T(8,128)(2,1)} %all-gather.2.cloned.1.call-done.refs_3_.shrink_ref.weight_ref, f32[1,1024]{1,0:T(1,128)S(1)} %get-tuple-element.598, ...), custom_call_target="tpu_custom_call" | custom-call | flops 1000 | bytes 1000 | tf_op jit(solution)/shard_map/weight_grad/pallas_call | solution.py:865
  374.5 19.5 %attend_back.5 = (bf16[2048,384]{1,0:T(8,128)(2,1)S(1)}, f32[1,384]{1,0:T(1,128)S(1)}) custom-call(bf16[2048,768]{1,0:T(8,128)(2,1)} %get-tuple-element.404.q_ref.k_ref.v_ref, bf16[2048,768]{1,0:T(8,128)(2,1)} %get-tuple-element.404.q_ref.k_ref.v_ref, bf16[2048,768]{1,0:T(8,128)(2,1)} %get-tuple-element.404.q_ref.k_ref.v_ref, ...), custom_call_target="tpu_custom_call" | custom-call | flops 1000 | bytes 1000 | tf_op jit(solution)/shard_map/attend_back/pallas_call | solution.py:532
  394.1 20.4 %attend_back.4 = (bf16[2048,384]{1,0:T(8,128)(2,1)S(1)}, f32[1,384]{1,0:T(1,128)S(1)}) custom-call(bf16[2048,768]{1,0:T(8,128)(2,1)} %get-tuple-element.404.q_ref.k_ref.v_ref, bf16[2048,768]{1,0:T(8,128)(2,1)} %get-tuple-element.404.q_ref.k_ref.v_ref, bf16[2048,768]{1,0:T(8,128)(2,1)} %get-tuple-element.404.q_ref.k_ref.v_ref, ...), custom_call_target="tpu_custom_call" | custom-call | flops 1000 | bytes 1000 | tf_op jit(solution)/shard_map/attend_back/pallas_call | solution.py:532
  414.5 8.4 %norm_grad.4 = bf16[1024,1024]{1,0:T(8,128)(2,1)} custom-call(s32[1]{0:T(128)} %bitcast.1.y_ref, bf16[2048,1024]{1,0:T(8,128)(2,1)} %copy-done.8, bf16[1024,1024]{1,0:T(8,128)(2,1)} %copy-done.23, bf16[1024,768]{1,0:T(8,128)(2,1)S(1)} %copy-done.57, bf16[2048,384]{1,0:T(8,128)(2,1)S(1)} %get-tuple-element.445.refs_0_, ...), custom_call_target="tpu_custom_call" | custom-call | flops 1000 | bytes 1000 | tf_op jit(solution)/shard_map/norm_grad/pallas_call | solution.py:763
  433.6 5.8 branch.3
  440.8 6.0 branch.2
  448.1 7.8 %norm_grad.5 = bf16[1024,1024]{1,0:T(8,128)(2,1)} custom-call(s32[1]{0:T(128)} %bitcast.1.y_ref, bf16[2048,1024]{1,0:T(8,128)(2,1)} %copy-done.8, bf16[1024,1024]{1,0:T(8,128)(2,1)} %copy-done.23, bf16[1024,768]{1,0:T(8,128)(2,1)S(1)} %copy-done.58, bf16[2048,384]{1,0:T(8,128)(2,1)S(1)} %copy-done.17, bf16[2048,384]{1,0:T(8,128)(2,1)S(1)} %copy-done.15), custom_call_target="tpu_custom_call" | custom-call | flops 1000 | bytes 1000 | tf_op jit(solution)/shard_map/norm_grad/pallas_call | solution.py:763
  466.6 7.6 weight_grad.5
  475.4 15.7 %collective-permute-done.29.refs_2_ = bf16[512,1024]{1,0:T(8,128)(2,1)S(1)} collective-permute-done((bf16[512,1024]{1,0:T(8,128)(2,1)S(1)}, bf16[512,1024]{1,0:T(8,128)(2,1)S(1)}, u32[]{:S(2)}, u32[]{:S(2)}) %collective-permute-start.29) | collective-permute-done | bytes 1048608 | tf_op jit(solution)/shard_map/ppermute | solution.py:60
  498.6 8.0 %product.9 = bf16[1024,1024]{1,0:T(8,128)(2,1)S(1)} custom-call(bf16[2048,1024]{1,0:T(8,128)(2,1)} %get-tuple-element.450.x_ref, bf16[2048,1024]{1,0:T(8,128)(2,1)} %bitcast.218), custom_call_target="tpu_custom_call" | custom-call | flops 1000 | bytes 1000 | tf_op jit(solution)/shard_map/product/pallas_call | solution.py:828
  509.5 11.9 %all_to_all.68 = bf16[4,64,1024]{2,1,0:T(8,128)(2,1)} all-to-all(bf16[4,64,1024]{2,1,0:T(8,128)(2,1)S(1)} %bitcast.284), channel_id=1, replica_groups=mesh['dp'=8,'seq'=4] {'seq'}, dimensions={0} | all-to-all | bytes 1048576 | tf_op jit(solution)/shard_map/all_to_all | solution.py:243
  521.5 10.0 %all-to-all-start.7 = ((bf16[32,32,768]{2,1,0:T(8,128)(2,1)}), bf16[32,32,768]{2,1,0:T(8,128)(2,1)}, u32[]{:S(2)}, u32[]{:S(2)}) async-start(bf16[32,32,768]{2,1,0:T(8,128)(2,1)} %bitcast.242), calls=%async_computation.7 | async-start | bytes 3145728 | tf_op jit(solution)/shard_map/all_to_all | solution.py:238
  539.6 11.3 %hidden_back.3 = (bf16[2048,1024]{1,0:T(8,128)(2,1)}, f32[1,1024]{1,0:T(1,128)S(1)}, bf16[2048,256]{1,0:T(8,128)(2,1)S(1)}) custom-call(bf16[2048,1024]{1,0:T(8,128)(2,1)} %bitcast.219, bf16[1024,1024]{1,0:T(8,128)(2,1)S(1)} %copy-done.38, bf16[2048,1024]{1,0:T(8,128)(2,1)} %get-tuple-element.452.slope_ref, bf16[256,1024]{1,0:T(8,128)(2,1)S(1)} %bitcast.236), custom_call_target="tpu_custom_call" | custom-call | flops 1000 | bytes 1000 | tf_op jit(solution)/shard_map/hidden_back/pallas_call | solution.py:796
  560.1 8.6 %weight_grad.6 = (bf16[1024,1024]{1,0:T(8,128)(2,1)S(1)}, f32[1,1024]{1,0:T(1,128)S(1)}, f32[1,1024]{1,0:T(1,128)S(1)}) custom-call(bf16[2048,1024]{1,0:T(8,128)(2,1)} %bitcast.256, bf16[1024,1024]{1,0:T(8,128)(2,1)S(1)} %copy-done.69, f32[1,1024]{1,0:T(1,128)S(1)} %get-tuple-element.604, f32[1,1024]{1,0:T(1,128)S(1)} %get-tuple-element.603, ...), custom_call_target="tpu_custom_call" | custom-call | flops 1000 | bytes 1000 | tf_op jit(solution)/shard_map/weight_grad/pallas_call | solution.py:865
  585.4 19.6 %attend_back.6 = (bf16[2048,384]{1,0:T(8,128)(2,1)S(1)}, f32[1,384]{1,0:T(1,128)S(1)}) custom-call(bf16[2048,768]{1,0:T(8,128)(2,1)} %get-tuple-element.483.q_ref.k_ref.v_ref, bf16[2048,768]{1,0:T(8,128)(2,1)} %get-tuple-element.483.q_ref.k_ref.v_ref, bf16[2048,768]{1,0:T(8,128)(2,1)} %get-tuple-element.483.q_ref.k_ref.v_ref, ...), custom_call_target="tpu_custom_call" | custom-call | flops 1000 | bytes 1000 | tf_op jit(solution)/shard_map/attend_back/pallas_call | solution.py:532
  620.3 19.5 %attend_back.7 = (bf16[2048,384]{1,0:T(8,128)(2,1)S(1)}, f32[1,384]{1,0:T(1,128)S(1)}) custom-call(bf16[2048,768]{1,0:T(8,128)(2,1)} %get-tuple-element.483.q_ref.k_ref.v_ref, bf16[2048,768]{1,0:T(8,128)(2,1)} %get-tuple-element.483.q_ref.k_ref.v_ref, bf16[2048,768]{1,0:T(8,128)(2,1)} %get-tuple-element.483.q_ref.k_ref.v_ref, ...), custom_call_target="tpu_custom_call" | custom-call | flops 1000 | bytes 1000 | tf_op jit(solution)/shard_map/attend_back/pallas_call | solution.py:532
  644.2 7.6 weight_grad.7
  659.6 4.1 all-to-all-start.9
  665.1 7.9 %norm_grad.6 = bf16[1024,1024]{1,0:T(8,128)(2,1)} custom-call(s32[1]{0:T(128)} %bitcast.1.y_ref, bf16[2048,1024]{1,0:T(8,128)(2,1)} %get-tuple-element.464.refs_0_.h_ref, bf16[1024,1024]{1,0:T(8,128)(2,1)} %get-tuple-element.384.refs_0_.wi_ref, bf16[1024,768]{1,0:T(8,128)(2,1)S(1)} %copy-done.54, bf16[2048,384]{1,0:T(8,128)(2,1)S(1)} %copy-done.11, ...), custom_call_target="tpu_custom_call" | custom-call | flops 1000 | bytes 1000 | tf_op jit(solution)/shard_map/norm_grad/pallas_call | solution.py:763
  691.6 4.3 add_bitcast_fusion.1
  695.9 7.8 %norm_grad.7 = bf16[1024,1024]{1,0:T(8,128)(2,1)} custom-call(s32[1]{0:T(128)} %bitcast.1.y_ref, bf16[2048,1024]{1,0:T(8,128)(2,1)} %get-tuple-element.464.refs_0_.h_ref, bf16[1024,1024]{1,0:T(8,128)(2,1)} %get-tuple-element.384.refs_0_.wi_ref, bf16[1024,768]{1,0:T(8,128)(2,1)S(1)} %copy-done.55, bf16[2048,384]{1,0:T(8,128)(2,1)S(1)} %copy-done.11, ...), custom_call_target="tpu_custom_call" | custom-call | flops 1000 | bytes 1000 | tf_op jit(solution)/shard_map/norm_grad/pallas_call | solution.py:763
  709.3 8.0 %all-to-all-done.9 = bf16[32,32,896]{2,1,0:T(8,128)(2,1)} async-done(((bf16[32,32,896]{2,1,0:T(8,128)(2,1)}), bf16[32,32,896]{2,1,0:T(8,128)(2,1)}, u32[]{:S(2)}, u32[]{:S(2)}) %all-to-all-start.9) | async-done | bytes 1835040 | tf_op jit(solution)/shard_map/all_to_all | solution.py:238
  750.3 9.1 %update.1 = (f32[2,32,3072]{2,1,0:T(8,128)}, f32[2,32,3072]{2,1,0:T(8,128)}, f32[2,32,3072]{2,1,0:T(8,128)}, f32[2,32,3072]{2,1,0:T(8,128)}, f32[2,32,1024]{2,1,...) custom-call(f32[1]{0:T(128)} %bitcast.135.clip_ref, ...), custom_call_target="tpu_custom_call" | custom-call | flops 1000 | bytes 1000 | tf_op jit(solution)/shard_map/update/pallas_call | solution.py:969
  (539 shorter events, 281.6 us)
Async XLA Ops:
  11.2 13.4 %all-to-all-start = ((bf16[4,32,1824]{2,1,0:T(8,128)(2,1)}), bf16[4,32,1824]{2,1,0:T(8,128)(2,1)S(1)}, u32[]{:S(2)}, u32[]{:S(2)}) async-start(bf16[4,32,1824]{2,1,0:T(8,128)(2,1)} %pack.2), calls=%async_computation | async-start | bytes 983040 | tf_op jit(solution)/shard_map/all_to_all | solution.py:243
  17.3 32.8 %collective-permute-start.3 = (bf16[512,1024]{1,0:T(8,128)(2,1)}, bf16[512,1024]{1,0:T(8,128)(2,1)}, u32[]{:S(2)}, u32[]{:S(2)}) collective-permute-start(bf16[512,1024]{1,0:T(8,128)(2,1)} %fusion.11.refs_0_), channel_id=1, source_target_pairs={{0,2},{1,3},{2,0},{3,1},{4,6},{5,7},{6,4},{7,5},{8,10},{9,11},{10,... | collective-permute-start | bytes 3145736 | tf_op jit(solution)/shard_map/ppermute | solution.py:60
  25.4 14.3 %collective-permute-start = (bf16[128,1024]{1,0:T(8,128)(2,1)S(1)}, bf16[128,1024]{1,0:T(8,128)(2,1)S(1)}, u32[]{:S(2)}, u32[]{:S(2)}) collective-permute-start(bf16[128,1024]{1,0:T(8,128)(2,1)S(1)} %pad_maximum_fusion.9.refs_0_), channel_id=1, source_target_pairs={{0,8},{4,12},{8,16},{12,20},{16,24},{20,28},{24,0},{28,4},{1,9},{5... | collective-permute-start | bytes 786440 | tf_op jit(solution)/shard_map/ppermute | solution.py:47
  29.9 17.2 %all-to-all-start.1 = ((bf16[32,2,416]{2,1,0:T(2,128)(2,1)}), bf16[32,2,416]{2,1,0:T(2,128)(2,1)S(1)}, u32[]{:S(2)}, u32[]{:S(2)}) async-start(bf16[32,2,416]{2,1,0:T(2,128)(2,1)} %reshape.463), calls=%async_computation.1 | async-start | bytes 131072 | tf_op jit(solution)/shard_map/all_to_all | solution.py:1147
  39.7 10.3 %collective-permute-start.1 = (bf16[128,1024]{1,0:T(8,128)(2,1)S(1)}, bf16[128,1024]{1,0:T(8,128)(2,1)S(1)}, u32[]{:S(2)}, u32[]{:S(2)}) collective-permute-start(bf16[128,1024]{1,0:T(8,128)(2,1)S(1)} %collective-permute-done.refs_2_), channel_id=1, source_target_pairs={{0,8},{4,12},{8,16},{12,20},{16,24},{20,28},{24,0},{28,4},{1,9},{5... | collective-permute-start | bytes 786440 | tf_op jit(solution)/shard_map/ppermute | solution.py:47
  50.1 8.5 %collective-permute-start.4 = (bf16[512,1024]{1,0:T(8,128)(2,1)}, bf16[512,1024]{1,0:T(8,128)(2,1)}, u32[]{:S(2)}, u32[]{:S(2)}) collective-permute-start(bf16[512,1024]{1,0:T(8,128)(2,1)} %fusion.11.refs_0_), channel_id=1, source_target_pairs={{0,1},{1,0},{2,3},{3,2},{4,5},{5,4},{6,7},{7,6},{8,9},{9,8},{10,11... | collective-permute-start | bytes 3145736 | tf_op jit(solution)/shard_map/ppermute | solution.py:65
  54.7 10.1 %collective-permute-start.6 = (bf16[128,1024]{1,0:T(8,128)(2,1)S(1)}, bf16[128,1024]{1,0:T(8,128)(2,1)S(1)}, u32[]{:S(2)}, u32[]{:S(2)}) collective-permute-start(bf16[128,1024]{1,0:T(8,128)(2,1)S(1)} %collective-permute-done.1.refs_4_), channel_id=1, source_target_pairs={{0,8},{4,12},{8,16},{12,20},{16,24},{20,28},{24,0},{28,4},{1,9},{5... | collective-permute-start | bytes 786440 | tf_op jit(solution)/shard_map/ppermute | solution.py:47
  55.9 8.9 %collective-permute-start.7 = (bf16[128,1024]{1,0:T(8,128)(2,1)S(1)}, bf16[128,1024]{1,0:T(8,128)(2,1)S(1)}, u32[]{:S(2)}, u32[]{:S(2)}) collective-permute-start(bf16[128,1024]{1,0:T(8,128)(2,1)S(1)} %collective-permute-done.refs_2_), channel_id=1, source_target_pairs={{0,4},{4,0},{8,12},{12,8},{16,20},{20,16},{24,28},{28,24},{1,5},{5... | collective-permute-start | bytes 786440 | tf_op jit(solution)/shard_map/ppermute | solution.py:55
  64.8 9.3 %collective-permute-start.8 = (bf16[128,1024]{1,0:T(8,128)(2,1)S(1)}, bf16[128,1024]{1,0:T(8,128)(2,1)S(1)}, u32[]{:S(2)}, u32[]{:S(2)}) collective-permute-start(bf16[128,1024]{1,0:T(8,128)(2,1)S(1)} %collective-permute-done.1.refs_4_), channel_id=1, source_target_pairs={{0,4},{4,0},{8,12},{12,8},{16,20},{20,16},{24,28},{28,24},{1,5},{5... | collective-permute-start | bytes 786440 | tf_op jit(solution)/shard_map/ppermute | solution.py:55
  66.5 11.4 %collective-permute-start.9 = (bf16[128,1024]{1,0:T(8,128)(2,1)S(1)}, bf16[128,1024]{1,0:T(8,128)(2,1)S(1)}, u32[]{:S(2)}, u32[]{:S(2)}) collective-permute-start(bf16[128,1024]{1,0:T(8,128)(2,1)S(1)} %collective-permute-done.6.refs_6_), channel_id=1, source_target_pairs={{0,4},{4,0},{8,12},{12,8},{16,20},{20,16},{24,28},{28,24},{1,5},{5... | collective-permute-start | bytes 786440 | tf_op jit(solution)/shard_map/ppermute | solution.py:55
  68.0 38.5 %collective-permute-start.16 = (bf16[512,1024]{1,0:T(8,128)(2,1)}, bf16[512,1024]{1,0:T(8,128)(2,1)}, u32[]{:S(2)}, u32[]{:S(2)}) collective-permute-start(bf16[512,1024]{1,0:T(8,128)(2,1)} %convert_element_type.253.refs_0_), channel_id=1, source_target_pairs={{0,2},{1,3},{2,0},{3,1},{4,6},{5,7},{6,4},{7,5},{8,10},{9,11},{10,... | collective-permute-start | bytes 3145736 | tf_op jit(solution)/shard_map/ppermute | solution.py:60
  78.6 22.3 %collective-permute-start.10 = (bf16[128,2048]{1,0:T(8,128)(2,1)S(1)}, bf16[128,2048]{1,0:T(8,128)(2,1)}, u32[]{:S(2)}, u32[]{:S(2)}) collective-permute-start(bf16[128,2048]{1,0:T(8,128)(2,1)S(1)} %pad_maximum_fusion.4.refs_3_), channel_id=1, source_target_pairs={{0,8},{4,12},{8,16},{12,20},{16,24},{20,28},{24,0},{28,4},{1,9},{5... | collective-permute-start | bytes 1572872 | tf_op jit(solution)/shard_map/ppermute | solution.py:47
  79.5 21.5 %collective-permute-start.11 = (bf16[128,2048]{1,0:T(8,128)(2,1)S(1)}, bf16[128,2048]{1,0:T(8,128)(2,1)}, u32[]{:S(2)}, u32[]{:S(2)}) collective-permute-start(bf16[128,2048]{1,0:T(8,128)(2,1)S(1)} %pad_maximum_fusion.4.refs_3_), channel_id=1, source_target_pairs={{0,4},{4,0},{8,12},{12,8},{16,20},{20,16},{24,28},{28,24},{1,5},{5... | collective-permute-start | bytes 1572872 | tf_op jit(solution)/shard_map/ppermute | solution.py:55
  80.4 20.5 %all-to-all-start.2 = ((bf16[4,32,1792]{2,1,0:T(8,128)(2,1)}), bf16[4,32,1792]{2,1,0:T(8,128)(2,1)}, u32[]{:S(2)}, u32[]{:S(2)}) async-start(bf16[4,32,1792]{2,1,0:T(8,128)(2,1)} %pack.3), calls=%async_computation.2 | async-start | bytes 917504 | tf_op jit(solution)/shard_map/all_to_all | solution.py:243
  84.5 145.2 %all-gather.2.cloned.1.call-start = ((), (), s32[]{:S(2)}) async-start(), calls=%async_computation.14 | async-start | bytes 7077888 | tf_op jit(solution)/shard_map/all_gather | solution.py:1215
  106.6 19.6 %collective-permute-start.12 = (bf16[128,2048]{1,0:T(8,128)(2,1)}, bf16[128,2048]{1,0:T(8,128)(2,1)}, u32[]{:S(2)}, u32[]{:S(2)}) collective-permute-start(bf16[128,2048]{1,0:T(8,128)(2,1)} %collective-permute-done.10.refs_5_), channel_id=1, source_target_pairs={{0,8},{4,12},{8,16},{12,20},{16,24},{20,28},{24,0},{28,4},{1,9},{5... | collective-permute-start | bytes 1572872 | tf_op jit(solution)/shard_map/ppermute | solution.py:47
  108.0 18.6 %collective-permute-start.13 = (bf16[128,2048]{1,0:T(8,128)(2,1)}, bf16[128,2048]{1,0:T(8,128)(2,1)}, u32[]{:S(2)}, u32[]{:S(2)}) collective-permute-start(bf16[128,2048]{1,0:T(8,128)(2,1)} %collective-permute-done.10.refs_5_), channel_id=1, source_target_pairs={{0,4},{4,0},{8,12},{12,8},{16,20},{20,16},{24,28},{28,24},{1,5},{5... | collective-permute-start | bytes 1572872 | tf_op jit(solution)/shard_map/ppermute | solution.py:55
  111.2 15.0 %all-to-all-start.3 = ((bf16[4,64,1024]{2,1,0:T(8,128)(2,1)}), bf16[4,64,1024]{2,1,0:T(8,128)(2,1)}, u32[]{:S(2)}, u32[]{:S(2)}) async-start(bf16[4,64,1024]{2,1,0:T(8,128)(2,1)} %reshape.406), calls=%async_computation.3 | async-start | bytes 1048576 | tf_op jit(solution)/shard_map/all_to_all | solution.py:243
  126.6 30.7 %collective-permute-start.14 = (bf16[128,2048]{1,0:T(8,128)(2,1)}, bf16[128,2048]{1,0:T(8,128)(2,1)}, u32[]{:S(2)}, u32[]{:S(2)}) collective-permute-start(bf16[128,2048]{1,0:T(8,128)(2,1)} %collective-permute-done.12.refs_7_), channel_id=1, source_target_pairs={{0,8},{4,12},{8,16},{12,20},{16,24},{20,28},{24,0},{28,4},{1,9},{5... | collective-permute-start | bytes 1572872 | tf_op jit(solution)/shard_map/ppermute | solution.py:47
  127.9 29.3 %collective-permute-start.15 = (bf16[128,2048]{1,0:T(8,128)(2,1)}, bf16[128,2048]{1,0:T(8,128)(2,1)S(1)}, u32[]{:S(2)}, u32[]{:S(2)}) collective-permute-start(bf16[128,2048]{1,0:T(8,128)(2,1)} %collective-permute-done.12.refs_7_), channel_id=1, source_target_pairs={{0,4},{4,0},{8,12},{12,8},{16,20},{20,16},{24,28},{28,24},{1,5},{5... | collective-permute-start | bytes 1572872 | tf_op jit(solution)/shard_map/ppermute | solution.py:55
  129.6 30.3 %collective-permute-start.17 = (bf16[512,1024]{1,0:T(8,128)(2,1)}, bf16[512,1024]{1,0:T(8,128)(2,1)}, u32[]{:S(2)}, u32[]{:S(2)}) collective-permute-start(bf16[512,1024]{1,0:T(8,128)(2,1)} %convert_element_type.253.refs_0_), channel_id=1, source_target_pairs={{0,1},{1,0},{2,3},{3,2},{4,5},{5,4},{6,7},{7,6},{8,9},{9,8},{10,11... | collective-permute-start | bytes 3145736 | tf_op jit(solution)/shard_map/ppermute | solution.py:65
  129.6 30.3 %collective-permute-start.18 = (bf16[512,1024]{1,0:T(8,128)(2,1)}, bf16[512,1024]{1,0:T(8,128)(2,1)}, u32[]{:S(2)}, u32[]{:S(2)}) collective-permute-start(bf16[512,1024]{1,0:T(8,128)(2,1)} %collective-permute-done.16.refs_2_), channel_id=1, source_target_pairs={{0,1},{1,0},{2,3},{3,2},{4,5},{5,4},{6,7},{7,6},{8,9},{9,8},{10,11... | collective-permute-start | bytes 3145736 | tf_op jit(solution)/shard_map/ppermute | solution.py:65
  158.0 16.5 %collective-permute-start.19 = (bf16[128,2048]{1,0:T(8,128)(2,1)}, bf16[128,2048]{1,0:T(8,128)(2,1)S(1)}, u32[]{:S(2)}, u32[]{:S(2)}) collective-permute-start(bf16[128,2048]{1,0:T(8,128)(2,1)} %collective-permute-done.14.refs_9_), channel_id=1, source_target_pairs={{0,4},{4,0},{8,12},{12,8},{16,20},{20,16},{24,28},{28,24},{1,5},{5... | collective-permute-start | bytes 1572872 | tf_op jit(solution)/shard_map/ppermute | solution.py:55
  197.4 25.5 %collective-permute-start.21 = (bf16[512,1024]{1,0:T(8,128)(2,1)S(1)}, bf16[512,1024]{1,0:T(8,128)(2,1)S(1)}, u32[]{:S(2)}, u32[]{:S(2)}) collective-permute-start(bf16[512,1024]{1,0:T(8,128)(2,1)S(1)} %fusion.10), channel_id=1, source_target_pairs={{0,2},{1,3},{2,0},{3,1},{4,6},{5,7},{6,4},{7,5},{8,10},{9,11},{10,... | collective-permute-start | bytes 3145736 | tf_op jit(solution)/shard_map/ppermute | solution.py:60
  228.0 25.5 %collective-permute-start.23 = (bf16[512,1024]{1,0:T(8,128)(2,1)}, bf16[512,1024]{1,0:T(8,128)(2,1)}, u32[]{:S(2)}, u32[]{:S(2)}) collective-permute-start(bf16[512,1024]{1,0:T(8,128)(2,1)} %fusion.12.refs_0_), channel_id=1, source_target_pairs={{0,2},{1,3},{2,0},{3,1},{4,6},{5,7},{6,4},{7,5},{8,10},{9,11},{10,... | collective-permute-start | bytes 3145736 | tf_op jit(solution)/shard_map/ppermute | solution.py:60
  274.2 46.0 %all-to-all-start.4 = ((bf16[4,64,1024]{2,1,0:T(8,128)(2,1)}), bf16[4,64,1024]{2,1,0:T(8,128)(2,1)}, u32[]{:S(2)}, u32[]{:S(2)}) async-start(bf16[4,64,1024]{2,1,0:T(8,128)(2,1)} %bitcast.280), calls=%async_computation.4 | async-start | bytes 1048576 | tf_op jit(solution)/shard_map/all_to_all | solution.py:243
  326.1 39.9 %all-to-all-start.5 = ((bf16[4,64,1024]{2,1,0:T(8,128)(2,1)}), bf16[4,64,1024]{2,1,0:T(8,128)(2,1)}, u32[]{:S(2)}, u32[]{:S(2)}) async-start(bf16[4,64,1024]{2,1,0:T(8,128)(2,1)} %bitcast.281), calls=%async_computation.5 | async-start | bytes 1048576 | tf_op jit(solution)/shard_map/all_to_all | solution.py:243
  330.3 329.3 %reduce-scatter.3.cloned.1.call-start = ((), (), s32[]{:S(2)}) async-start(), calls=%async_computation.15 | async-start | bytes 5308416 | tf_op jit(solution)/shard_map/reduce_scatter | solution.py:1304
  428.5 27.5 %collective-permute-start.27 = (bf16[512,1024]{1,0:T(8,128)(2,1)}, bf16[512,1024]{1,0:T(8,128)(2,1)}, u32[]{:S(2)}, u32[]{:S(2)}) collective-permute-start(bf16[512,1024]{1,0:T(8,128)(2,1)} %fusion.5), channel_id=1, source_target_pairs={{0,2},{1,3},{2,0},{3,1},{4,6},{5,7},{6,4},{7,5},{8,10},{9,11},{10,... | collective-permute-start | bytes 3145736 | tf_op jit(solution)/shard_map/ppermute | solution.py:60
  465.9 25.2 %collective-permute-start.29 = (bf16[512,1024]{1,0:T(8,128)(2,1)S(1)}, bf16[512,1024]{1,0:T(8,128)(2,1)S(1)}, u32[]{:S(2)}, u32[]{:S(2)}) collective-permute-start(bf16[512,1024]{1,0:T(8,128)(2,1)S(1)} %convert_element_type.271.refs_0_), channel_id=1, source_target_pairs={{0,2},{1,3},{2,0},{3,1},{4,6},{5,7},{6,4},{7,5},{8,10},{9,11},{10,... | collective-permute-start | bytes 3145736 | tf_op jit(solution)/shard_map/ppermute | solution.py:60
  521.5 84.7 %all-to-all-start.7 = ((bf16[32,32,768]{2,1,0:T(8,128)(2,1)}), bf16[32,32,768]{2,1,0:T(8,128)(2,1)}, u32[]{:S(2)}, u32[]{:S(2)}) async-start(bf16[32,32,768]{2,1,0:T(8,128)(2,1)} %bitcast.242), calls=%async_computation.7 | async-start | bytes 3145728 | tf_op jit(solution)/shard_map/all_to_all | solution.py:238
  533.3 19.7 %collective-permute-start.32 = (bf16[128,1024]{1,0:T(8,128)(2,1)}, bf16[128,1024]{1,0:T(8,128)(2,1)}, u32[]{:S(2)}, u32[]{:S(2)}) collective-permute-start(bf16[128,1024]{1,0:T(8,128)(2,1)} %get-tuple-element.579), channel_id=1, source_target_pairs={{0,4},{4,0},{8,12},{12,8},{16,20},{20,16},{24,28},{28,24},{1,5},{5... | collective-permute-start | bytes 786440 | tf_op jit(solution)/shard_map/ppermute | solution.py:55
  554.8 17.3 %collective-permute-start.34 = (bf16[128,1024]{1,0:T(8,128)(2,1)}, bf16[128,1024]{1,0:T(8,128)(2,1)}, u32[]{:S(2)}, u32[]{:S(2)}) collective-permute-start(bf16[128,1024]{1,0:T(8,128)(2,1)} %add_convert_fusion.2), channel_id=1, source_target_pairs={{0,8},{4,12},{8,16},{12,20},{16,24},{20,28},{24,0},{28,4},{1,9},{5... | collective-permute-start | bytes 786440 | tf_op jit(solution)/shard_map/ppermute | solution.py:47
  557.6 21.5 %collective-permute-start.37 = (bf16[512,1024]{1,0:T(8,128)(2,1)}, bf16[512,1024]{1,0:T(8,128)(2,1)}, u32[]{:S(2)}, u32[]{:S(2)}) collective-permute-start(bf16[512,1024]{1,0:T(8,128)(2,1)} %dynamic-slice_bitcast_fusion.3), channel_id=1, source_target_pairs={{0,1},{1,0},{2,3},{3,2},{4,5},{5,4},{6,7},{7,6},{8,9},{9,8},{10,11... | collective-permute-start | bytes 3145736 | tf_op jit(solution)/shard_map/ppermute | solution.py:65
  559.5 12.7 %collective-permute-start.33 = (bf16[128,1024]{1,0:T(8,128)(2,1)}, bf16[128,1024]{1,0:T(8,128)(2,1)}, u32[]{:S(2)}, u32[]{:S(2)}) collective-permute-start(bf16[128,1024]{1,0:T(8,128)(2,1)} %get-tuple-element.577), channel_id=1, source_target_pairs={{0,4},{4,0},{8,12},{12,8},{16,20},{20,16},{24,28},{28,24},{1,5},{5... | collective-permute-start | bytes 786440 | tf_op jit(solution)/shard_map/ppermute | solution.py:55
  574.3 34.8 %collective-permute-start.36 = (bf16[128,1024]{1,0:T(8,128)(2,1)}, bf16[128,1024]{1,0:T(8,128)(2,1)}, u32[]{:S(2)}, u32[]{:S(2)}) collective-permute-start(bf16[128,1024]{1,0:T(8,128)(2,1)} %add_convert_fusion.1), channel_id=1, source_target_pairs={{0,8},{4,12},{8,16},{12,20},{16,24},{20,28},{24,0},{28,4},{1,9},{5... | collective-permute-start | bytes 786440 | tf_op jit(solution)/shard_map/ppermute | solution.py:47
  578.1 31.0 %collective-permute-start.35 = (bf16[128,1024]{1,0:T(8,128)(2,1)}, bf16[128,1024]{1,0:T(8,128)(2,1)}, u32[]{:S(2)}, u32[]{:S(2)}) collective-permute-start(bf16[128,1024]{1,0:T(8,128)(2,1)} %get-tuple-element.575), channel_id=1, source_target_pairs={{0,4},{4,0},{8,12},{12,8},{16,20},{20,16},{24,28},{28,24},{1,5},{5... | collective-permute-start | bytes 786440 | tf_op jit(solution)/shard_map/ppermute | solution.py:55
  581.7 37.3 %collective-permute-start.38 = (bf16[512,1024]{1,0:T(8,128)(2,1)}, bf16[512,1024]{1,0:T(8,128)(2,1)}, u32[]{:S(2)}, u32[]{:S(2)}) collective-permute-start(bf16[512,1024]{1,0:T(8,128)(2,1)} %fusion.3), channel_id=1, source_target_pairs={{0,2},{1,3},{2,0},{3,1},{4,6},{5,7},{6,4},{7,5},{8,10},{9,11},{10,... | collective-permute-start | bytes 3145736 | tf_op jit(solution)/shard_map/ppermute | solution.py:60
  606.1 35.9 %all-to-all-start.8 = ((f32[32,1,416]{2,1,0:T(1,128)}), f32[32,1,416]{2,1,0:T(1,128)S(1)}, u32[]{:S(2)}, u32[]{:S(2)}) async-start(f32[32,1,416]{2,1,0:T(1,128)} %reshape.435), calls=%async_computation.8 | async-start | bytes 131072 | tf_op jit(solution)/shard_map/all_to_all | solution.py:1113
  609.0 95.8 %reduce-scatter.5.cloned.1.call-start = ((), (), s32[]{:S(2)}) async-start(), calls=%async_computation.16 | async-start | bytes 2949120 | tf_op jit(solution)/shard_map/reduce_scatter | solution.py:1361
  611.2 29.8 %collective-permute-start.40 = (bf16[128,1024]{1,0:T(8,128)(2,1)}, bf16[128,1024]{1,0:T(8,128)(2,1)}, u32[]{:S(2)}, u32[]{:S(2)}) collective-permute-start(bf16[128,1024]{1,0:T(8,128)(2,1)} %add_convert_fusion), channel_id=1, source_target_pairs={{0,8},{4,12},{8,16},{12,20},{16,24},{20,28},{24,0},{28,4},{1,9},{5... | collective-permute-start | bytes 786440 | tf_op jit(solution)/shard_map/ppermute | solution.py:47
  614.8 26.2 %collective-permute-start.39 = (bf16[128,1024]{1,0:T(8,128)(2,1)}, bf16[128,1024]{1,0:T(8,128)(2,1)}, u32[]{:S(2)}, u32[]{:S(2)}) collective-permute-start(bf16[128,1024]{1,0:T(8,128)(2,1)} %get-tuple-element.573), channel_id=1, source_target_pairs={{0,4},{4,0},{8,12},{12,8},{16,20},{20,16},{24,28},{28,24},{1,5},{5... | collective-permute-start | bytes 786440 | tf_op jit(solution)/shard_map/ppermute | solution.py:55
  642.0 13.2 %collective-permute-start.41 = (bf16[512,1024]{1,0:T(8,128)(2,1)}, bf16[512,1024]{1,0:T(8,128)(2,1)}, u32[]{:S(2)}, u32[]{:S(2)}) collective-permute-start(bf16[512,1024]{1,0:T(8,128)(2,1)} %dynamic-slice_bitcast_fusion.2), channel_id=1, source_target_pairs={{0,1},{1,0},{2,3},{3,2},{4,5},{5,4},{6,7},{7,6},{8,9},{9,8},{10,11... | collective-permute-start | bytes 3145736 | tf_op jit(solution)/shard_map/ppermute | solution.py:65
  659.6 57.7 %all-to-all-start.9 = ((bf16[32,32,896]{2,1,0:T(8,128)(2,1)}), bf16[32,32,896]{2,1,0:T(8,128)(2,1)}, u32[]{:S(2)}, u32[]{:S(2)}) async-start(bf16[32,32,896]{2,1,0:T(8,128)(2,1)} %bitcast.277), calls=%async_computation.10 | async-start | bytes 3670016 | tf_op jit(solution)/shard_map/all_to_all | solution.py:238
  684.5 36.3 %collective-permute-start.43 = (bf16[512,1024]{1,0:T(8,128)(2,1)}, bf16[512,1024]{1,0:T(8,128)(2,1)}, u32[]{:S(2)}, u32[]{:S(2)}) collective-permute-start(bf16[512,1024]{1,0:T(8,128)(2,1)} %fusion.1), channel_id=1, source_target_pairs={{0,2},{1,3},{2,0},{3,1},{4,6},{5,7},{6,4},{7,5},{8,10},{9,11},{10,... | collective-permute-start | bytes 3145736 | tf_op jit(solution)/shard_map/ppermute | solution.py:60
  717.3 12.3 %all-to-all-start.10 = ((bf16[4,32,2,1024]{3,1,2,0:T(8,128)(2,1)}), bf16[4,32,2,1024]{3,1,2,0:T(8,128)(2,1)S(1)}, u32[]{:S(2)}, u32[]{:S(2)}) async-start(bf16[4,32,2,1024]{3,1,2,0:T(8,128)(2,1)} %pad_maximum_fusion.7), calls=%async_computation.12 | async-start | bytes 1048576 | tf_op jit(solution)/shard_map/all_to_all | solution.py:243
  724.8 10.2 %collective-permute-start.44 = (bf16[512,1024]{1,0:T(8,128)(2,1)S(1)}, bf16[512,1024]{1,0:T(8,128)(2,1)}, u32[]{:S(2)}, u32[]{:S(2)}) collective-permute-start(bf16[512,1024]{1,0:T(8,128)(2,1)S(1)} %dynamic-slice_bitcast_fusion), channel_id=1, source_target_pairs={{0,1},{1,0},{2,3},{3,2},{4,5},{5,4},{6,7},{7,6},{8,9},{9,8},{10,11... | collective-permute-start | bytes 3145736 | tf_op jit(solution)/shard_map/ppermute | solution.py:65
  730.2 10.8 %all-to-all-start.11 = ((f32[32,1,128]{2,1,0:T(1,128)}), f32[32,1,128]{2,1,0:T(1,128)S(1)}, u32[]{:S(2)}, u32[]{:S(2)}) async-start(f32[32,1,128]{2,1,0:T(1,128)} %broadcast_in_dim.82), calls=%async_computation.13 | async-start | bytes 32768 | tf_op jit(solution)/shard_map/all_to_all | solution.py:1427
  (135 other events, 837.6 us)
Sparse Core Ops, SparseCore 0:
  106.7 119.6 all-gather.1
  430.6 100.3 reduce-scatter.2
  619.1 85.6 reduce-scatter.4

commit v4 on v3

--- a/solution.py
+++ b/solution.py
@@ -31,7 +31,7 @@
 QUERY_SCALE = 1.0 / math.sqrt(HD)
 BF = jnp.bfloat16
 F32 = jnp.float32
-VMEM_LIMIT = 48 * 1024 * 1024
+VMEM_LIMIT = 60 * 1024 * 1024
 LIGHT = pl.CostEstimate(flops=1000, bytes_accessed=1000, transcendentals=0)
 
 
@@ -190,16 +190,19 @@
         self.pieces = held[1]
         return held[0]
 
-    def done(self):
+    def take(self, start, stop):
         chips = lax.axis_size("seq") // 2
         me = lax.axis_index("seq")
         y, c = me // 2, me % 2
         pieces, slots = [], []
-        for step, piece in enumerate(self.pieces):
+        for step in range(start, stop):
             at = (y - step) % chips
-            pieces += [piece, core_swap(piece)]
+            pieces += [self.pieces[step], core_swap(self.pieces[step])]
             slots += [2 * at + c, 2 * at + 1 - c]
-        return assemble(pieces, slots)
+        return pieces, slots
+
+    def done(self):
+        return assemble(*self.take(0, len(self.pieces)))
 
 
 class SeqScatter:
@@ -239,6 +242,30 @@
     return value.reshape((copies, parts) + value.shape[1:])
 
 
+def seq_swap(value):
+    size = lax.axis_size("seq")
+    chips = size // 2
+    me = lax.axis_index("seq")
+    y, c = me // 2, me % 2
+    value = value.reshape((chips, 2) + value.shape[1:])
+    kept = lax.dynamic_index_in_dim(value, c, 1, keepdims=False)
+    arrived = core_swap(lax.dynamic_index_in_dim(value, 1 - c, 1, keepdims=False))
+    pair = jnp.where(c == 0, jnp.stack([kept, arrived], 1), jnp.stack([arrived, kept], 1))
+    parts = []
+    for step in range(chips):
+        part = lax.dynamic_index_in_dim(pair, (y + step) % chips, 0, keepdims=False)
+        if step:
+            part = lax.ppermute(part, "seq", [(i, (i + 2 * step) % size) for i in range(size)])
+        parts.append(part)
+    if chips == 2:
+        total = jnp.where(y == 0, jnp.stack(parts), jnp.stack(parts[::-1]))
+    else:
+        total = jnp.zeros_like(pair)
+        for step, part in enumerate(parts):
+            total = lax.dynamic_update_index_in_dim(total, part, (y - step) % chips, 0)
+    return total.reshape((size,) + value.shape[2:])
+
+
 def seq_exchange(value):
     return lax.all_to_all(value, "seq", split_axis=0, concat_axis=0, tiled=True)
 
@@ -278,28 +305,39 @@
     return lax.dot_general(left, right, (((0,), (0,)), ((), ())), preferred_element_type=F32)
 
 
-def mix_kernel(slots_ref, x_ref, gain_ref, low_ref, bias_ref, cos_ref, sin_ref, *refs):
-    out_ref, scaled_ref = refs[-3], refs[-2]
-    shift_ref = refs[-1]
-    columns = scaled_ref.shape[1]
-
-    @pl.when(pl.program_id(0) == 0)
-    def _():
-        if len(refs) == 4:
-            raw_ref = refs[0]
-        else:
-            pieces, raw_ref, rest_ref = refs[:-5], refs[-5], refs[-4]
-            for n, piece_ref in enumerate(pieces):
+def mix_kernel(count, pieces, x_slots_ref, slots_ref, *refs):
+    refs = list(refs)
+    inputs = refs[:count]
+    del refs[:count]
+    cos_ref, sin_ref = refs[:2]
+    i = pl.program_id(0)
+    if pieces:
+        gain_ref, low_ref, bias_ref = refs[2:5]
+        normed_ref, out_ref, raw_ref, scaled_ref, shift_ref = refs[-5:]
+        columns = scaled_ref.shape[1]
+
+        @pl.when(i == 0)
+        def _():
+            for n, piece_ref in enumerate(refs[5 : 5 + pieces]):
                 size = piece_ref.shape[0]
                 rows = pl.ds(pl.multiple_of(slots_ref[n] * size, size), size)
-                raw_ref[rows, :] = piece_ref[:, :columns]
-                rest_ref[rows, :] = piece_ref[:, columns:]
-        raw = raw_ref[...]
-        scaled_ref[...] = (raw.astype(F32) * as_column(gain_ref[...])).astype(BF)
-        low = jnp.broadcast_to(low_ref[...], (8, D)).astype(BF)
-        shift_ref[...] = matmul(low, raw) + bias_ref[...]
-
-    mixed = matmul(x_ref[...], scaled_ref[...]) + shift_ref[0:1, :]
+                raw_ref[rows, :] = piece_ref[...]
+            raw = raw_ref[...]
+            scaled_ref[...] = (raw.astype(F32) * as_column(gain_ref[...])).astype(BF)
+            low = jnp.broadcast_to(low_ref[...], (8, D)).astype(BF)
+            shift_ref[...] = matmul(low, raw) + bias_ref[...]
+
+    else:
+        scaled_ref, shift_ref = refs[2:4]
+        normed_ref, out_ref = refs[-2:]
+        columns = scaled_ref.shape[1]
+    for n, x_ref in enumerate(inputs):
+
+        @pl.when(i == n)
+        def _(x_ref=x_ref):
+            normed_ref[...] = x_ref[...]
+
+    mixed = matmul(normed_ref[...], scaled_ref[...]) + shift_ref[0:1, :]
     cosine, sine = cos_ref[...], sin_ref[...]
     for start in range(0, columns, 3 * 128):
         query = mixed[:, start : start + 128]
@@ -311,47 +349,52 @@
         out_ref[:, start + 256 : start + 384] = mixed[:, start + 256 : start + 384].astype(BF)
 
 
-def mix(x, weight, gain, low, bias, cosine, sine, slots=None):
-    length, columns = x.shape[0], bias.shape[0]
+def mix(inputs, x_slots, cosine, sine, first=None, scaled=None, kept=()):
+    count, size, length = len(inputs), inputs[0].shape[0], cosine.shape[0]
+    columns = (first[2].shape[0] if scaled is None else scaled[0].shape[1])
 
     def whole(shape):
-        return pl.BlockSpec(shape, lambda i, slots_ref: (0, 0))
-
-    def rows(count):
-        return pl.BlockSpec((ROWS, count), lambda i, slots_ref: (i, 0))
-
-    out_specs = [rows(columns), whole((D, columns))]
+        return pl.BlockSpec(shape, lambda i, *_: (0, 0))
+
+    def rows(width):
+        return pl.BlockSpec((size, width), lambda i, *_: (_[0][i], 0))
+
+    held = pl.BlockSpec(memory_space=pltpu.VMEM)
+    values = [*inputs, cosine, sine]
+    specs = [held] * count + [rows(128), rows(128)]
+    out_specs = [rows(D), rows(columns)]
     out_shape = [
+        jax.ShapeDtypeStruct((length, D), BF),
         jax.ShapeDtypeStruct((length, columns), BF),
-        jax.ShapeDtypeStruct((D, columns), BF),
     ]
-    if slots is None:
-        slots, weight_specs = jnp.zeros((1,), jnp.int32), [whole((D, columns))]
+    pieces, slots = (), [jnp.int32(0)]
+    if first is not None:
+        gain, low, bias, pieces, slots = first
+        values += [gain[None], low[None], bias[None], *pieces]
+        specs += [whole((1, D)), whole((1, D)), whole((1, columns))] + [held] * len(pieces)
+        out_specs += [whole((D, columns)), whole((D, columns)), whole((8, columns))]
+        out_shape += [
+            jax.ShapeDtypeStruct((D, columns), BF),
+            jax.ShapeDtypeStruct((D, columns), BF),
+            jax.ShapeDtypeStruct((8, columns), F32),
+        ]
     else:
-        slots = jnp.stack(slots).astype(jnp.int32)
-        weight_specs = [pl.BlockSpec(memory_space=pltpu.VMEM)] * len(weight)
-        rest = weight[0].shape[1] - columns
-        out_specs = [whole((D, columns)), whole((D, rest))] + out_specs
-        out_shape = [
-            jax.ShapeDtypeStruct((D, columns), BF),
-            jax.ShapeDtypeStruct((D, rest), BF),
-        ] + out_shape
+        values += list(scaled)
+        specs += [whole((D, columns)), whole((8, columns))]
+    aliases = {2 + len(values) + n: n for n in range(len(kept))}
+    values += list(kept)
+    specs += [pl.BlockSpec(memory_space=pl.ANY)] * len(kept)
     return pl.pallas_call(
-        mix_kernel,
+        partial(mix_kernel, count, len(pieces)),
         grid_spec=pltpu.PrefetchScalarGridSpec(
-            num_scalar_prefetch=1,
-            grid=(length // ROWS,),
-            in_specs=[rows(D), whole((1, D)), whole((1, D)), whole((1, columns))]
-            + [rows(128), rows(128)]
-            + weight_specs,
-            out_specs=out_specs,
-            scratch_shapes=[pltpu.VMEM((8, columns), F32)],
+            num_scalar_prefetch=2, grid=(count,), in_specs=specs, out_specs=out_specs
         ),
         out_shape=out_shape,
+        input_output_aliases=aliases,
         compiler_params=pltpu.CompilerParams(vmem_limit_bytes=VMEM_LIMIT),
         cost_estimate=LIGHT,
         name="mix",
-    )(slots, x, gain[None], low[None], bias[None], cosine, sine, *weight)
+    )(jnp.stack(x_slots).astype(jnp.int32), jnp.stack(slots).astype(jnp.int32), *values)
 
 
 def attend_kernel(q_ref, k_ref, v_ref, o_ref, lse_ref, acc_ref, turned_ref):
@@ -822,9 +865,9 @@
     out_ref[...] = matmul_tn(x_ref[...], g_ref[...]).astype(BF)
 
 
-def product(x, grads, block=BLOCK):
+def product(x, grads, column=0, wide=D):
     length, count = x.shape
-    block = min(block, count)
+    block = min(BLOCK, count)
     return pl.pallas_call(
         product_kernel,
         grid=(count // block,),
@@ -832,16 +875,16 @@
             pl.BlockSpec((length, block), lambda i: (0, i)),
             pl.BlockSpec((length, D), lambda i: (0, 0)),
         ],
-        out_specs=pl.BlockSpec((block, D), lambda i: (i, 0)),
-        out_shape=jax.ShapeDtypeStruct((count, D), BF),
+        out_specs=pl.BlockSpec((block, D), lambda i: (i, column)),
+        out_shape=jax.ShapeDtypeStruct((count, wide), BF),
         compiler_params=pltpu.CompilerParams(vmem_limit_bytes=VMEM_LIMIT),
         cost_estimate=LIGHT,
         name="product",
     )(x, grads)
 
 
-def weight_grad_kernel(x_ref, weight_ref, gain_ref, shift_ref, total_ref, *refs):
-    lows, (out_ref, gain_out_ref, shift_out_ref) = refs[:-3], refs[-3:]
+def weight_grad_kernel(count, x_ref, weight_ref, gain_ref, shift_ref, total_ref, *refs):
+    lows, (out_ref, gain_out_ref, shift_out_ref) = refs[:count], refs[-3:]
     gain, shift = as_column(gain_ref[...]), as_column(shift_ref[...])
     x = x_ref[...]
     start, gain_sum, shift_sum = 0, 0.0, 0.0
@@ -858,12 +901,12 @@
     shift_out_ref[...] = as_row(shift_sum)
 
 
-def weight_grad(x, lows, weight, gain, shift, total):
+def weight_grad(x, lows, weight, gain, shift, total, kept=()):
     length, columns = x.shape[0], total.shape[1]
     array, column = weight
     row = pl.BlockSpec((1, ROWS), lambda i: (0, i))
     return pl.pallas_call(
-        weight_grad_kernel,
+        partial(weight_grad_kernel, len(lows)),
         grid=(D // ROWS,),
         in_specs=[
             pl.BlockSpec((length, ROWS), lambda i: (0, i)),
@@ -872,17 +915,19 @@
             row,
             pl.BlockSpec((1, columns), lambda i: (0, 0)),
         ]
-        + [pl.BlockSpec(low.shape, lambda i: (0, 0)) for low in lows],
+        + [pl.BlockSpec(low.shape, lambda i: (0, 0)) for low in lows]
+        + [pl.BlockSpec(memory_space=pl.ANY)] * len(kept),
         out_specs=[pl.BlockSpec((ROWS, columns), lambda i: (i, 0)), row, row],
         out_shape=[
-            jax.ShapeDtypeStruct((D, columns), BF),
+            jax.ShapeDtypeStruct((D, kept[0].shape[1] if kept else columns), BF),
             jax.ShapeDtypeStruct((1, D), F32),
             jax.ShapeDtypeStruct((1, D), F32),
         ],
+        input_output_aliases={5 + len(lows): 0} if kept else {},
         compiler_params=pltpu.CompilerParams(vmem_limit_bytes=VMEM_LIMIT),
         cost_estimate=LIGHT,
         name="weight_grad",
-    )(x, array, gain[None], shift[None], total, *lows)
+    )(x, array, gain[None], shift[None], total, *lows, *kept)
 
 
 def pack_kernel(spans, mixing_ref, expand_ref, *refs):
@@ -1105,17 +1150,29 @@
     def outgoing_output(attended, grads):
         output_grad = jnp.concatenate([product(out, grads) for out in attended], 0)
         output_grad = output_grad.reshape(copies // parts, parts, rows_d, D).transpose(1, 0, 2, 3)
-        output_grad = seq_exchange(output_grad.reshape(parts, copies // parts * rows_d, D))
-        return output_grad.reshape(-1, width)
-
-    def exchange_affine(pieces):
-        grads = jnp.concatenate(pieces).reshape(devices, 1, small)
-        return lax.all_to_all(grads, ("dp", "seq"), split_axis=0, concat_axis=0, tiled=True)
+        return seq_swap(output_grad.reshape(parts, copies // parts * rows_d, D))
+
+    def beside(grads, *pieces):
+        pieces = [jnp.concatenate(piece).reshape(devices, small) for piece in pieces]
+        pieces = jnp.concatenate(pieces, -1)
+        coarse = pieces.astype(BF)
+        fine = (pieces - coarse.astype(F32)).astype(BF)
+        pieces = jnp.concatenate([coarse, fine], -1)
+        extra = 128 * pl.cdiv(pieces.shape[1], 128 * rows_d)
+        pieces = jnp.pad(pieces, ((0, 0), (0, extra * rows_d - pieces.shape[1])))
+        return jnp.concatenate([grads, pieces.reshape(D, extra)], -1)
+
+    def apart(summed, columns, count):
+        pieces = summed[..., columns:].reshape(devices, -1).astype(F32)
+        size = count * small
+        pieces = jnp.sum(pieces[:, :size] + pieces[:, size : 2 * size], 0).reshape(count, small)
+        return jnp.sum(summed[..., :columns].astype(F32), 0), list(pieces)
 
     def sum_squares(*values):
         return sum(jnp.sum(value.astype(F32) * value.astype(F32)) for value in values)
 
     tie = lax.optimization_barrier
+    chips = parts // 2
     current = stream.reshape(rows, D)
     gradient = cotangent.reshape(rows, D)
 
@@ -1134,13 +1191,14 @@
     pair = both[..., 3 * width + units :].astype(F32).reshape(parts, 2, rows)
     places = (pair[:, 0] * 16.0 + pair[:, 1]).reshape(-1)
     both = both.reshape(parts * rows_d, -1)
-    near = Gather(
-        jnp.concatenate(
-            [both[:, : 3 * width], output_weight[0].astype(BF).reshape(-1, width)], -1
-        )
-    )
-    places, affine_low, layer_mixing, layer_expand = near.hold(
-        places, affine_weight, mixing_weight, expand_weight
+    near = Gather(both[:, : 3 * width])
+    places, affine_low, layer_mixing, layer_expand, first_output, later_output = near.hold(
+        places,
+        affine_weight,
+        mixing_weight,
+        expand_weight,
+        output_weight[0],
+        output_weight[1],
     )
     near.forward()
     affine_low = affine_low.astype(BF).reshape(1, LAYERS * small)
@@ -1151,33 +1209,33 @@
         concat_axis=0,
         tiled=True,
     )
+    outputs = jnp.concatenate(
+        [value.astype(BF).reshape(-1, width) for value in (first_output, later_output)], -1
+    )
+    outputs = lax.all_gather(outputs, "dp", axis=0, tiled=True)
     cosine, sine = rotary_tables(places)
     later_both = arrange(1, layer_mixing, layer_expand)
-    cosine, sine, later_both, expand_own, shrink_own = near.hold(
-        cosine, sine, later_both, both[:, 3 * width : 3 * width + units], shrink_weight[0]
+    cosine, sine, later_both, expand_own, shrink_own, low_gradient = near.hold(
+        cosine,
+        sine,
+        later_both,
+        both[:, 3 * width : 3 * width + units],
+        shrink_weight[0],
+        gradient.astype(BF),
     )
     near.forward()
     near.cross()
     far_own = jnp.concatenate([expand_own, shrink_own.astype(BF).reshape(-1, units)], -1)
-    affine_all, far_own, near.pieces, near.chains, travel.pieces, later_both, low_gradient = tie(
-        (
-            affine_all,
-            far_own,
-            near.pieces,
-            near.chains,
-            travel.pieces,
-            later_both,
-            gradient,
-        )
-    )
-    normed = travel.done()
+    affine_all, far_own, near.pieces, near.chains, travel.pieces = tie(
+        (affine_all, far_own, near.pieces, near.chains, travel.pieces)
+    )
+    inputs, x_slots = travel.take(0, chips)
     near.forward()
     near.cross()
-    travel = SeqGather(low_gradient.astype(BF))
     affine_all = affine_all.reshape(devices, LAYERS, small).transpose(1, 0, 2)
     affine_all = affine_all.reshape(LAYERS, devices * small).astype(F32)
     vectors = [split_affine(affine_all[layer]) for layer in range(LAYERS)]
-    vectors, normed = near.hold(vectors, normed)
+    vectors, inputs = near.hold(vectors, inputs)
     for step in range(3, outer - 1):
         near.forward()
         near.cross()
@@ -1188,48 +1246,54 @@
     far.forward()
     far.cross()
     pieces, slots = near.done()
-    later_both = seq_exchange(later_both)
 
     gain_one, shift_one, gain_two, shift_two = vectors[0][:4]
-    mixing, output, mixed, mixing_scaled = mix(
-        normed, pieces, gain_one, shift_one, mixing_part(vectors[0][4]), cosine, sine, slots
-    )
-    mixed, output, later_both, later_shrink, later_output = far.hold(
-        mixed, output, later_both, shrink_weight[1], output_weight[1]
+    normed, mixed, mixing, mixing_scaled, _ = mix(
+        inputs,
+        x_slots,
+        cosine,
+        sine,
+        first=(gain_one, shift_one, mixing_part(vectors[0][4]), pieces, slots),
+    )
+    mixed, later_both, later_shrink, outputs, low_gradient = far.hold(
+        mixed, later_both, shrink_weight[1], outputs, low_gradient
     )
     far.forward()
     far.cross()
-    output = seq_exchange(output.reshape(parts, -1, D))
-
-    later_both = later_both.reshape(parts * rows_d, -1)
-    later_own = jnp.concatenate(
-        [
-            later_both[:, 3 * width :],
-            later_shrink.astype(BF).reshape(-1, units),
-            later_both[:, : 3 * width],
-            later_output.astype(BF).reshape(-1, width),
-        ],
-        -1,
-    )
-    (later_own,) = travel.hold(later_own)
-    later_all = lax.all_gather(later_own, "dp", axis=0, tiled=True)
+    travel = SeqGather(low_gradient)
+    later_both = seq_exchange(later_both)
+    outputs = jnp.stack(
+        [outputs[:, layer * width : (layer + 1) * width].reshape(parts, -1, D) for layer in (0, 1)],
+        1,
+    )
     attended, logs = [], []
     for half in range(halves):
         out, log_total = attend(mixed, half)
         attended.append(out)
         logs.append(log_total)
         if half == 0:
-            mixed, out, output = far.hold(mixed, out, output)
+            mixed, out, later_both, outputs = far.hold(mixed, out, later_both, outputs)
             far.forward()
             far.cross()
-    output = settle_output(output)
-    attended, logs = far.hold(attended, logs)
+            outputs = seq_exchange(outputs)
+            later_both = later_both.reshape(parts * rows_d, -1)
+            later_far = jnp.concatenate(
+                [later_both[:, 3 * width :], later_shrink.astype(BF).reshape(-1, units)], -1
+            )
+            later_near = later_both[:, : 3 * width]
+    attended, logs, later_far, later_near, outputs, travel.pieces = far.hold(
+        attended, logs, later_far, later_near, outputs, travel.pieces
+    )
+    output, later_output = (settle_output(outputs[:, layer]) for layer in (0, 1))
+    later_all = lax.all_gather(later_far, "dp", axis=0, tiled=True)
     while len(far.pieces) < outer:
         far.forward()
     while len(far.chains) < outer:
         far.cross()
-    grads = travel.done()
-    attended, logs, grads = far.hold(attended, logs, grads)
+    attended, logs, later_near = far.hold(attended, logs, later_near)
+    near = Gather(later_near)
+    near.forward()
+    near.cross()
     pieces, slots = far.done()
     first = (gain_two, shift_two, expand_part(vectors[0][6]))
     if units == D:
@@ -1252,8 +1316,11 @@
             last=((shrink, 0), output, attended),
         )
     shrink = (shrink, 0)
-    travel = SeqScatter(others)
-    activated, slope = travel.hold(activated, slope)
+    (others,) = near.hold(others)
+    near.forward()
+    near.cross()
+    cotangents, travel = travel, SeqScatter(others)
+    activated, slope, cotangents.pieces = travel.hold(activated, slope, cotangents.pieces)
     activated, slope, own = feed(
         True,
         normed,
@@ -1262,28 +1329,50 @@
         last=(shrink, output, attended),
         kept=(activated, slope),
     )
+    (own,) = near.hold(own)
+    grads = cotangents.done()
+    for step in range(2, outer - 1):
+        near.forward()
+        near.cross()
     stored = [(own_normed, scale, normed, mixed, attended, logs, activated, slope)]
     weights = [(mixing, mixing_scaled, output, expand, expand_scaled, shrink)]
-    current = current + travel.done(own)[0] + vectors[0][5] + vectors[0][7]
+    total, (near.pieces, near.chains, grads) = travel.done(
+        own, (near.pieces, near.chains, grads)
+    )
+    while len(near.chains) < outer:
+        near.cross()
+    current = current + total + vectors[0][5] + vectors[0][7]
 
     own_normed, scale = normalize(current)
     travel = SeqGather(own_normed.astype(BF))
-    mixing = later_all[:, 2 * units : 2 * units + 3 * width]
-    later_output = later_all[:, 2 * units + 3 * width :].reshape(copies * rows_d, D)
-    mixing, later_output, later_all = travel.hold(mixing, later_output, later_all)
-    normed = travel.done()
-    expand, shrink = later_all, view(later_all, 1)
+    pieces, slots = near.done()
     gain_one, shift_one, gain_two, shift_two = vectors[1][:4]
-    mixed, mixing_scaled = mix(
-        normed, [mixing], gain_one, shift_one, mixing_part(vectors[1][4]), cosine, sine
-    )
-    mixed, later_output = tie((mixed, later_output))
-    output = seq_exchange(later_output.reshape(parts, -1, D))
+    inputs, x_slots = travel.take(0, 1)
+    normed, mixed, mixing, mixing_scaled, mixing_shift = mix(
+        inputs,
+        x_slots,
+        cosine,
+        sine,
+        first=(gain_one, shift_one, mixing_part(vectors[1][4]), pieces, slots),
+    )
+    normed, mixed = travel.hold(normed, mixed)
+    inputs, x_slots = travel.take(1, chips)
+    normed, mixed = mix(
+        inputs,
+        x_slots,
+        cosine,
+        sine,
+        scaled=(mixing_scaled, mixing_shift),
+        kept=(normed, mixed),
+    )
+    output = later_output
     attended, logs = [], []
     for half in range(halves):
         out, log_total = attend(mixed, half)
         attended.append(out)
         logs.append(log_total)
+    attended, logs, later_all = tie((attended, logs, later_all))
+    expand, shrink = later_all, view(later_all, 1)
     activated, slope, expand_scaled, expand_shift = feed(
         None,
         normed,
@@ -1291,15 +1380,23 @@
         first=(gain_two, shift_two, expand_part(vectors[1][6]), (later_all, 0)),
     )
 
-    grads, attended, logs, activated, output = tie((grads, attended, logs, activated, output))
-    output = settle_output(output)
+    grads, attended, logs, activated = tie((grads, attended, logs, activated))
     output_grad = outgoing_output(attended, grads)
     hidden_low, hidden_total, attended_grad = hidden_back(grads, shrink, slope, output)
-    shrink_grad = product(activated, grads).reshape(-1, units)
-    expand_grad, gain_two_grad, shift_two_grad = weight_grad(
-        normed, [hidden_low], (expand, 0), gain_two, shift_two, hidden_total
-    )
-    later_grad = jnp.concatenate([expand_grad, shrink_grad, output_grad], -1)
+    if units == D:
+        later_grad = product(activated, grads, 1, 2 * units + width)
+        later_grad, gain_two_grad, shift_two_grad = weight_grad(
+            normed, [hidden_low], (expand, 0), gain_two, shift_two, hidden_total, (later_grad,)
+        )
+        output_grad = output_grad.reshape(-1, width)
+        later_grad = lax.dynamic_update_slice(later_grad, output_grad, (0, 2 * units))
+    else:
+        shrink_grad = product(activated, grads).reshape(-1, units)
+        expand_grad, gain_two_grad, shift_two_grad = weight_grad(
+            normed, [hidden_low], (expand, 0), gain_two, shift_two, hidden_total
+        )
+        output_grad = output_grad.reshape(-1, width)
+        later_grad = jnp.concatenate([expand_grad, shrink_grad, output_grad], -1)
     later_grad, attended_grad = tie((later_grad, attended_grad))
     later_first = lax.psum_scatter(later_grad, "dp", scatter_dimension=0, tiled=True)
     lows, totals = [], []
@@ -1348,21 +1445,25 @@
     (grads,) = far.hold(grads)
     far.cross()
     hidden_low, hidden_total, attended_grad = hidden_back(grads, shrink, slope, output)
-    hidden_low, attended_grad, result_others, later_pieces = far.hold(
-        hidden_low, attended_grad, result_others, later_pieces
+    hidden_low, attended_grad, grads, result_others, later_pieces = far.hold(
+        hidden_low, attended_grad, grads, result_others, later_pieces
     )
     far.forward()
     far.cross()
+    output_grad = outgoing_output(attended, grads)
     expand_grad, gain_two_grad, shift_two_grad = weight_grad(
         normed, [hidden_low], (expand, 0), gain_two, shift_two, hidden_total
     )
-    output_grad = outgoing_output(attended, grads)
-    attended_grad, expand_grad, output_grad = far.hold(attended_grad, expand_grad, output_grad)
-    far_grad = lax.psum_scatter(
-        jnp.concatenate([expand_grad, output_grad], -1), "dp", scatter_dimension=0, tiled=True
+    attended_grad, expand_grad, output_grad, later_mixing = far.hold(
+        attended_grad, expand_grad, output_grad, later_mixing
+    )
+    far_grad = lax.psum_scatter(expand_grad, "dp", scatter_dimension=0, tiled=True)
+    output_grad = lax.all_to_all(
+        output_grad.reshape(copies, parts * rows_d, width), "dp", 0, 0, tiled=True
     )
     travel = SeqScatter(result_others)
-    lows, totals = [], []
+    lows, totals, mixing_grads, gain_grads, shift_grads = [], [], [], [], []
+    arrived = output_grad
     for half in range(halves):
         if len(far.parts) < outer:
             far.forward()
@@ -1370,30 +1471,44 @@
         low, total = attend_back(
             mixed, attended_grad, attended[half], logs[half], cosine, sine, half
         )
-        mixed, low, total, later_mixing = far.hold(mixed, low, total, later_mixing)
         if half == 0:
+            mixed, low, total, arrived, later_first = far.hold(
+                mixed, low, total, arrived, later_first
+            )
+        else:
+            mixed, low, total, arrived = far.hold(mixed, low, total, arrived)
+        if half == 0:
+            output_grad = arrived
             result, (mixed, low) = travel.done(result_own, (mixed, low))
-            exchanged = exchange_affine(later_pieces)
+        else:
+            mixing_grads[-1] = arrived
+        mixing_grad, gain_one_grad, shift_one_grad = weight_grad(
+            normed,
+            [low],
+            (mixing, half),
+            gain_one,
+            shift_one,
+            total,
+        )
         lows.append(low)
         totals.append(total)
-    exchanged, lows = tie((exchanged, lows))
-    later_affine = jnp.sum(exchanged, 0)
-    mixed_total = jnp.concatenate(totals, -1)
-    mixing_grad, gain_one_grad, shift_one_grad = weight_grad(
-        normed, lows, (mixing, 0), gain_one, shift_one, mixed_total
-    )
-    output_sum = jnp.sum(gradient, 0)
-    gains = (gain_one_grad, shift_one_grad, gain_two_grad, shift_two_grad)
-    pieces = small_grads(gains, mixed_total, output_sum, hidden_total)
-    pieces = jnp.concatenate(pieces).reshape(devices, small)
-    coarse = pieces.astype(BF)
-    fine = (pieces - coarse.astype(F32)).astype(BF)
-    pieces = jnp.concatenate([coarse, fine], -1)
-    extra = 128 * pl.cdiv(2 * small, 128 * rows_d)
-    pieces = jnp.pad(pieces, ((0, 0), (0, extra * rows_d - 2 * small)))
-    mixing_grad = jnp.concatenate([mixing_grad, pieces.reshape(D, extra)], -1)
-    mixing_grad, lows, result, later_first = tie((mixing_grad, lows, result, later_first))
-    mixing_grad = sum_exchange(mixing_grad)
+        gain_grads.append(gain_one_grad)
+        shift_grads.append(shift_one_grad)
+        pieces = [later_pieces] if half == 0 else []
+        if half == halves - 1:
+            output_sum = jnp.sum(gradient, 0)
+            gains = (sum(gain_grads), sum(shift_grads), gain_two_grad, shift_two_grad)
+            pieces.append(
+                small_grads(gains, jnp.concatenate(totals, -1), output_sum, hidden_total)
+            )
+        mixing_grad = beside(mixing_grad, *pieces) if pieces else mixing_grad
+        if half == halves - 1:
+            mixing_grad, far_grad = tie((mixing_grad, far_grad))
+            home = jnp.stack([far_grad, later_first[:, :units]], 1)
+            home = seq_swap(home.reshape(parts, rows_d, 2, units))
+        mixing_grad, lows, mixed, attended_grad = tie((mixing_grad, lows, mixed, attended_grad))
+        arrived = sum_exchange(mixing_grad)
+        mixing_grads.append(arrived)
     result = later_current + result + later_vectors[5] + later_vectors[7]
     result = result.reshape(stream.shape)
     others = norm_grad(hidden_low, expand_scaled, lows, mixing_scaled, False)
@@ -1407,23 +1522,26 @@
         far.forward()
     shrink_grad = far.done()
     later_mixing = jnp.sum(later_mixing.astype(F32), 0)
-    squares = sum_squares(shrink_grad, later_first, later_mixing, later_affine)
-    shrink_grad, later_mixing = shrink_grad.astype(BF), later_mixing.astype(BF)
-    normed_grad, (mixing_grad, squares, shrink_grad, later_mixing) = travel.done(
-        own, (mixing_grad, squares, shrink_grad, later_mixing)
-    )
-
-    home = jnp.stack([far_grad[:, :units], later_first[:, :units]], 1)
-    home = seq_exchange(home.reshape(parts, rows_d, 2, units))
-    output_grad = far_grad[:, units:]
-    pieces = mixing_grad[..., 3 * width :].reshape(devices, -1)[:, : 2 * small].astype(F32)
-    affine_grad = jnp.sum(pieces[:, :small] + pieces[:, small:], 0, keepdims=True)
-    mixing_grad = jnp.sum(mixing_grad[..., : 3 * width].astype(F32), 0)
-    squares = squares + sum_squares(mixing_grad, affine_grad, far_grad)
-    mixing_grad = mixing_grad.astype(BF)
-    affine_grad = jnp.stack([affine_grad[0], later_affine[0]])
-    squares, home = tie((squares, home))
+    output_grad = jnp.sum(output_grad.astype(F32), 0)
+    squares = sum_squares(shrink_grad, output_grad, later_first, later_mixing)
+    shrink_grad, later_mixing, output_grad = (
+        value.astype(BF) for value in (shrink_grad, later_mixing, output_grad)
+    )
+    others = (mixing_grads[-1], own, squares, shrink_grad, later_mixing, output_grad, home)
+    others = tie(others)
+    mixing_grads[-1], own, squares, shrink_grad, later_mixing, output_grad, home = others
+
+    affine, parts_of_mixing = [], []
+    for half in range(halves):
+        count = (half == 0) + (half == halves - 1)
+        summed, pieces = apart(mixing_grads[half], 3 * 128, count)
+        parts_of_mixing.append(summed)
+        affine += pieces
+    affine_grad = jnp.stack(affine[::-1])
+    squares = squares + sum_squares(*parts_of_mixing, affine_grad, far_grad)
+    mixing_grad = jnp.concatenate(parts_of_mixing, -1).astype(BF)
     expand_grad, later_expand = home[:, :, 0], home[:, :, 1]
+    squares, own = tie((squares, own))
     squares = lax.all_to_all(
         jnp.broadcast_to(squares, (devices, 128)),
         ("dp", "seq"),
@@ -1431,8 +1549,9 @@
         concat_axis=0,
         tiled=True,
     )
-    squares, normed_grad = tie((squares, normed_grad))
+    normed_grad = travel.done(own)[0]
     gradient = norm_back(gradient, normed_grad, own_normed, scale)
+    gradient, squares = tie((gradient, squares))
     stream_grad = gradient.reshape(stream.shape)
     gradient_norm = jnp.sqrt(jnp.sum(squares[:, 0]))
     clip_scale = jnp.minimum(1.0, CLIP_LIMIT / (gradient_norm + 1e-06))

time: 780 us -> 737 us (0.945)
  local copies, waits for them, and re-layouts: 115 us -> 51.6 us
  Pallas kernels: 333 us -> 377 us
  waiting for transfers between devices: 118 us -> 101 us
  blocking collectives: 11.9 us -> 0 us
    unnamed x268 -> x186, local copies, waits for them, and re-layouts: 56.6 us -> 8.31 us
    ppermute x8, waiting for transfers between devices: 45.6 us -> 26.1 us  [chip_ring(): lax.ppermute(value, 'seq', [(i, (i + 2) % size) for i in range(size)])]
    ppermute x12 -> x16, waiting for transfers between devices: 18.1 us -> 36.1 us  [inner_ring(): return lax.ppermute(value, 'dp', moves)]
    pallas_call x6 -> x8, Pallas kernels: 53.6 us -> 67.6 us  [the longest x5 42.5 us: weight_grad(): pl.pallas_call(partial(weight_grad_kernel, len(lows)), grid=(D // ROWS,),...]
    pallas_call x6, Pallas kernels: 18.7 us -> 32.5 us  [product(): pl.pallas_call(product_kernel, grid=(count // block,), in_specs=[pl.Block...]
    all_to_all x6 -> x3, starting transfers between devices: 24.2 us -> 11.7 us  [seq_exchange(): return lax.all_to_all(value, 'seq', split_axis=0, concat_axis=0, tiled=True)]
    all_to_all x1 -> x0, blocking collectives: 11.9 us -> none  [seq_exchange(): return lax.all_to_all(value, 'seq', split_axis=0, concat_axis=0, tiled=True)]
    ppermute x12 -> x16, starting transfers between devices: 13.5 us -> 21.9 us  [inner_ring(): return lax.ppermute(value, 'dp', moves)]
  transfers between devices with their start and end apart: 59 -> 71, of which waited for: 25 -> 26; matrix products, arithmetic and copies ran while one was open for 15% -> 16% of each run, Pallas kernels for 34% -> 40%
where the time goes in v4:
time: 737 us; the launch traced here: 727 us
  Pallas kernels  377 us (51%)
  waiting for transfers between devices  101 us (14%)
  starting transfers between devices  97 us (13%)
  other arithmetic  71.7 us (10%)
  local copies, waits for them, and re-layouts  51.6 us (7%)
  between operations  22.9 us (3%)
    pallas_call x4, Pallas kernels, attend_back(): pl.pallas_call(attend_back_kernel, grid=(length // block,), in_specs=[pl....  85.3 us
    pallas_call x3, Pallas kernels, feed(): pl.pallas_call(partial(feed_kernel, first is not None, last is not None,...  46.6 us
    pallas_call x4, Pallas kernels, attend(): pl.pallas_call(attend_kernel, grid=(length // block,), in_specs=[pl.Block...  46.3 us
    pallas_call x5, Pallas kernels, weight_grad(): pl.pallas_call(partial(weight_grad_kernel, len(lows)), grid=(D // ROWS,),...  42.5 us
    ppermute x16, waiting for transfers between devices, inner_ring(): return lax.ppermute(value, 'dp', moves)  36.1 us
    pallas_call x4, Pallas kernels, norm_grad(): pl.pallas_call(norm_grad_kernel, grid_spec=pltpu.PrefetchScalarGridSpec(n...  34.3 us
    pallas_call x6, Pallas kernels, product(): pl.pallas_call(product_kernel, grid=(count // block,), in_specs=[pl.Block...  32.5 us
    ppermute x8, waiting for transfers between devices, chip_ring(): lax.ppermute(value, 'seq', [(i, (i + 2) % size) for i in range(size)])  26.1 us
  transfers between devices with their start and end apart: 71, of which 26 were waited for; matrix products, arithmetic and copies ran while one was open for 16% of the time, Pallas kernels for 40%

profile of v4, /device:TPU:0, one launch (start us, length us, event | category | flops | bytes accessed | tf_op | source)
XLA Modules:
  0.0 726.8 jit_solution(17053934434575680417)
XLA Ops:
  10.8 4.2 all-to-all-start
  31.7 5.3 all-to-all-start.1
  52.0 4.8 collective-permute-done.2.refs_10_
  63.9 4.7 collective-permute-done.7.refs_12_
  72.6 4.4 collective-permute-done.8.refs_14_
  85.2 11.1 %mix.3 = (bf16[2048,1024]{1,0:T(8,128)(2,1)}, bf16[2048,768]{1,0:T(8,128)(2,1)}, bf16[1024,768]{1,0:T(8,128)(2,1)}, bf16[1024,768]{1,0:T(8,128)(2,1)}, f32[8,768]{1,0:T(8,128)}) custom-call(s32[4]{0:T(128)} %pad_add_fusion.x_slots_ref.slots_ref, s32[8]{0:T(128)} %stack.210.slots_ref, bf16[512,1024]{1,0:T(8,128)(2,1)} %copy-done.15, ...), custom_call_target="tpu_custom_call" | custom-call | flops 1000 | bytes 1000 | tf_op jit(solution)/shard_map/mix/pallas_call | solution.py:387
  97.5 3.9 all-to-all-start.2
  104.7 11.6 %attend.4 = (bf16[2048,128]{1,0:T(8,128)(2,1)}, f32[2,2048]{1,0:T(2,128)}) custom-call(bf16[2048,768]{1,0:T(8,128)(2,1)} %get-tuple-element.575.q_ref.k_ref.v_ref, bf16[2048,768]{1,0:T(8,128)(2,1)} %get-tuple-element.575.q_ref.k_ref.v_ref, bf16[2048,768]{1,0:T(8,128)(2,1)} %get-tuple-element.575.q_ref.k_ref.v_ref), custom_call_target="tpu_custom_call" | custom-call | flops 1000 | bytes 1000 | tf_op jit(solution)/shard_map/attend/pallas_call | solution.py:450
  123.9 11.6 %attend.5 = (bf16[2048,128]{1,0:T(8,128)(2,1)}, f32[2,2048]{1,0:T(2,128)}) custom-call(bf16[2048,768]{1,0:T(8,128)(2,1)} %get-tuple-element.575.q_ref.k_ref.v_ref, bf16[2048,768]{1,0:T(8,128)(2,1)} %get-tuple-element.575.q_ref.k_ref.v_ref, bf16[2048,768]{1,0:T(8,128)(2,1)} %get-tuple-element.575.q_ref.k_ref.v_ref), custom_call_target="tpu_custom_call" | custom-call | flops 1000 | bytes 1000 | tf_op jit(solution)/shard_map/attend/pallas_call | solution.py:450
  138.9 4.3 all-to-all-done.3
  144.8 15.4 %collective-permute-done.17.refs_10_ = bf16[128,2048]{1,0:T(8,128)(2,1)S(1)} collective-permute-done((bf16[128,2048]{1,0:T(8,128)(2,1)}, bf16[128,2048]{1,0:T(8,128)(2,1)S(1)}, u32[]{:S(2)}, u32[]{:S(2)}) %collective-permute-start.17) | collective-permute-done | bytes 524320 | tf_op jit(solution)/shard_map/ppermute | solution.py:55
  164.2 16.6 %feed.3 = (bf16[2048,1024]{1,0:T(8,128)(2,1)}, bf16[2048,1024]{1,0:T(8,128)(2,1)}, bf16[1024,1024]{1,0:T(8,128)(2,1)}, f32[8,1024]{1,0:T(8,128)}, bf16[1024,1024...) custom-call(s32[1]{0:T(128)} %bitcast.1.y_ref, s32[8]{0:T(128)} %stack.210.slots_ref, ...), custom_call_target="tpu_custom_call" | custom-call | flops 1000 | bytes 1000 | tf_op jit(solution)/shard_map/feed/pallas_call | solution.py:742
  192.6 13.4 %feed.4 = (bf16[2048,1024]{1,0:T(8,128)(2,1)}, bf16[2048,1024]{1,0:T(8,128)(2,1)}, bf16[1024,1024]{1,0:T(8,128)(2,1)}) custom-call(s32[1]{0:T(128)} %bitcast.1.y_ref, s32[1]{0:T(128)} %constant.480.clone.1.slots_ref, bf16[2048,1024]{1,0:T(8,128)(2,1)} %get-tuple-element.374.x_ref, ...), custom_call_target="tpu_custom_call", output_to_operand_aliasing={{0}: (9, {}), {1}: (10, {})} | custom-call | flops 1000 | bytes 1000 | tf_op jit(solution)/shard_map/feed/pallas_call | solution.py:742
  209.7 5.4 assemble.2
  225.0 3.8 collective-permute-start.30
  234.9 7.6 %mix.4 = (bf16[2048,1024]{1,0:T(8,128)(2,1)}, bf16[2048,768]{1,0:T(8,128)(2,1)}, bf16[1024,768]{1,0:T(8,128)(2,1)}, bf16[1024,768]{1,0:T(8,128)(2,1)}, f32[8,768]{1,0:T(8,128)}) custom-call(s32[2]{0:T(128)} %pad_add_fusion.2.x_slots_ref, s32[8]{0:T(128)} %stack.210.slots_ref, bf16[512,1024]{1,0:T(8,128)(2,1)} %copy-done.16, ...), custom_call_target="tpu_custom_call" | custom-call | flops 1000 | bytes 1000 | tf_op jit(solution)/shard_map/mix/pallas_call | solution.py:387
  242.6 6.4 collective-permute-done.31.refs_0_
  252.8 6.4 mix.5
  259.2 11.6 %attend.7 = (bf16[2048,128]{1,0:T(8,128)(2,1)}, f32[2,2048]{1,0:T(2,128)}) custom-call(bf16[2048,768]{1,0:T(8,128)(2,1)} %get-tuple-element.475.q_ref.k_ref.v_ref, bf16[2048,768]{1,0:T(8,128)(2,1)} %get-tuple-element.475.q_ref.k_ref.v_ref, bf16[2048,768]{1,0:T(8,128)(2,1)} %get-tuple-element.475.q_ref.k_ref.v_ref), custom_call_target="tpu_custom_call" | custom-call | flops 1000 | bytes 1000 | tf_op jit(solution)/shard_map/attend/pallas_call | solution.py:450
  270.8 11.6 %attend.6 = (bf16[2048,128]{1,0:T(8,128)(2,1)}, f32[2,2048]{1,0:T(2,128)}) custom-call(bf16[2048,768]{1,0:T(8,128)(2,1)} %get-tuple-element.475.q_ref.k_ref.v_ref, bf16[2048,768]{1,0:T(8,128)(2,1)} %get-tuple-element.475.q_ref.k_ref.v_ref, bf16[2048,768]{1,0:T(8,128)(2,1)} %get-tuple-element.475.q_ref.k_ref.v_ref), custom_call_target="tpu_custom_call" | custom-call | flops 1000 | bytes 1000 | tf_op jit(solution)/shard_map/attend/pallas_call | solution.py:450
  282.4 16.6 %feed.5 = (bf16[2048,1024]{1,0:T(8,128)(2,1)}, bf16[2048,1024]{1,0:T(8,128)(2,1)}, bf16[1024,1024]{1,0:T(8,128)(2,1)}, f32[8,1024]{1,0:T(8,128)}) custom-call(s32[1]{0:T(128)} %bitcast.1.y_ref, s32[1]{0:T(128)} %constant.480.clone.1.slots_ref, bf16[2048,1024]{1,0:T(8,128)(2,1)} %get-tuple-element.473.x_ref, f32[1,1024]{1,0:T(1,128)} %get-tuple-element.706, ...), custom_call_target="tpu_custom_call" | custom-call | flops 1000 | bytes 1000 | tf_op jit(solution)/shard_map/feed/pallas_call | solution.py:742
  312.0 8.6 %product.6.refs_1_ = bf16[1024,2304]{1,0:T(8,128)(2,1)} custom-call(bf16[2048,1024]{1,0:T(8,128)(2,1)} %get-tuple-element.512.x_ref.act_ref, bf16[2048,1024]{1,0:T(8,128)(2,1)} %bitcast.252), custom_call_target="tpu_custom_call" | custom-call | flops 1000 | bytes 1000 | tf_op jit(solution)/shard_map/product/pallas_call | solution.py:871
  320.6 12.3 %hidden_back.2 = (bf16[2048,1024]{1,0:T(8,128)(2,1)}, f32[1,1024]{1,0:T(1,128)}, bf16[2048,256]{1,0:T(8,128)(2,1)}) custom-call(bf16[2048,1024]{1,0:T(8,128)(2,1)} %bitcast.253, bf16[1024,2048]{1,0:T(8,128)(2,1)} %all-gather.5.cloned.1.call-done.refs_3_.shrink_ref.weight_ref, bf16[2048,1024]{1,0:T(8,128)(2,1)} %get-tuple-element.492.slope_ref, ...), custom_call_target="tpu_custom_call" | custom-call | flops 1000 | bytes 1000 | tf_op jit(solution)/shard_map/hidden_back/pallas_call | solution.py:839
  332.9 9.7 %weight_grad.5 = (bf16[1024,2304]{1,0:T(8,128)(2,1)}, f32[1,1024]{1,0:T(1,128)}, f32[1,1024]{1,0:T(1,128)}) custom-call(bf16[2048,1024]{1,0:T(8,128)(2,1)} %get-tuple-element.473.x_ref, bf16[1024,2048]{1,0:T(8,128)(2,1)} %all-gather.5.cloned.1.call-done.refs_3_.shrink_ref.weight_ref, f32[1,1024]{1,0:T(1,128)} %get-tuple-element.706, ...), custom_call_target="tpu_custom_call", output_to_operand_aliasing={{0}: (6, {})} | custom-call | flops 1000 | bytes 1000 | tf_op jit(solution)/shard_map/weight_grad/pallas_call | solution.py:908
  343.9 21.2 %attend_back.5 = (bf16[2048,384]{1,0:T(8,128)(2,1)}, f32[1,384]{1,0:T(1,128)}) custom-call(bf16[2048,768]{1,0:T(8,128)(2,1)} %get-tuple-element.475.q_ref.k_ref.v_ref, bf16[2048,768]{1,0:T(8,128)(2,1)} %get-tuple-element.475.q_ref.k_ref.v_ref, bf16[2048,768]{1,0:T(8,128)(2,1)} %get-tuple-element.475.q_ref.k_ref.v_ref, ...), custom_call_target="tpu_custom_call" | custom-call | flops 1000 | bytes 1000 | tf_op jit(solution)/shard_map/attend_back/pallas_call | solution.py:575
  365.1 21.6 %attend_back.4 = (bf16[2048,384]{1,0:T(8,128)(2,1)}, f32[1,384]{1,0:T(1,128)}) custom-call(bf16[2048,768]{1,0:T(8,128)(2,1)} %get-tuple-element.475.q_ref.k_ref.v_ref, bf16[2048,768]{1,0:T(8,128)(2,1)} %get-tuple-element.475.q_ref.k_ref.v_ref, bf16[2048,768]{1,0:T(8,128)(2,1)} %get-tuple-element.475.q_ref.k_ref.v_ref, ...), custom_call_target="tpu_custom_call" | custom-call | flops 1000 | bytes 1000 | tf_op jit(solution)/shard_map/attend_back/pallas_call | solution.py:575
  386.7 8.6 %norm_grad.4 = bf16[1024,1024]{1,0:T(8,128)(2,1)} custom-call(s32[1]{0:T(128)} %bitcast.1.y_ref, bf16[2048,1024]{1,0:T(8,128)(2,1)} %get-tuple-element.509.refs_0_.h_ref, bf16[1024,1024]{1,0:T(8,128)(2,1)} %get-tuple-element.507.wi_ref, bf16[1024,768]{1,0:T(8,128)(2,1)} %get-tuple-element.469.refs_4_.wm_ref, bf16[2048,384]{1,0:T(8,128)(2,1)} %get-tuple-element.518.refs_0_, ...), custom_call_target="tpu_custom_call" | custom-call | flops 1000 | bytes 1000 | tf_op jit(solution)/shard_map/norm_grad/pallas_call | solution.py:806
  401.9 7.0 branch.3
  408.9 7.1 branch.2
  416.0 8.6 %norm_grad.5 = bf16[1024,1024]{1,0:T(8,128)(2,1)} custom-call(s32[1]{0:T(128)} %bitcast.1.y_ref, bf16[2048,1024]{1,0:T(8,128)(2,1)} %get-tuple-element.509.refs_0_.h_ref, bf16[1024,1024]{1,0:T(8,128)(2,1)} %get-tuple-element.507.wi_ref, bf16[1024,768]{1,0:T(8,128)(2,1)} %get-tuple-element.469.refs_4_.wm_ref, bf16[2048,384]{1,0:T(8,128)(2,1)} %get-tuple-element.518.refs_0_, ...), custom_call_target="tpu_custom_call" | custom-call | flops 1000 | bytes 1000 | tf_op jit(solution)/shard_map/norm_grad/pallas_call | solution.py:806
  437.7 9.0 %weight_grad.6 = (bf16[1024,768]{1,0:T(8,128)(2,1)}, f32[1,1024]{1,0:T(1,128)}, f32[1,1024]{1,0:T(1,128)}) custom-call(bf16[2048,1024]{1,0:T(8,128)(2,1)} %get-tuple-element.473.x_ref, bf16[1024,768]{1,0:T(8,128)(2,1)} %get-tuple-element.474.weight_ref, f32[1,1024]{1,0:T(1,128)} %get-tuple-element.708, f32[1,1024]{1,0:T(1,128)} %get-tuple-element.707, ...), custom_call_target="tpu_custom_call" | custom-call | flops 1000 | bytes 1000 | tf_op jit(solution)/shard_map/weight_grad/pallas_call | solution.py:908
  446.8 15.2 %collective-permute-done.38.refs_2_ = bf16[512,1024]{1,0:T(8,128)(2,1)} collective-permute-done((bf16[512,1024]{1,0:T(8,128)(2,1)S(1)}, bf16[512,1024]{1,0:T(8,128)(2,1)}, u32[]{:S(2)}, u32[]{:S(2)}) %collective-permute-start.38) | collective-permute-done | bytes 1048608 | tf_op jit(solution)/shard_map/ppermute | solution.py:60
  462.5 9.8 %all-to-all-start.4 = ((bf16[32,32,768]{2,1,0:T(8,128)(2,1)}), bf16[32,32,768]{2,1,0:T(8,128)(2,1)}, u32[]{:S(2)}, u32[]{:S(2)}) async-start(bf16[32,32,768]{2,1,0:T(8,128)(2,1)} %bitcast.308), calls=%async_computation.4 | async-start | bytes 3145728 | tf_op jit(solution)/shard_map/all_to_all | solution.py:241
  472.3 5.5 assemble.3
  477.8 8.6 %product.9 = bf16[1024,1024]{1,0:T(8,128)(2,1)} custom-call(bf16[2048,1024]{1,0:T(8,128)(2,1)} %get-tuple-element.523.x_ref, bf16[2048,1024]{1,0:T(8,128)(2,1)} %bitcast.254), custom_call_target="tpu_custom_call" | custom-call | flops 1000 | bytes 1000 | tf_op jit(solution)/shard_map/product/pallas_call | solution.py:871
  489.6 12.3 %hidden_back.3 = (bf16[2048,1024]{1,0:T(8,128)(2,1)}, f32[1,1024]{1,0:T(1,128)}, bf16[2048,256]{1,0:T(8,128)(2,1)}) custom-call(bf16[2048,1024]{1,0:T(8,128)(2,1)} %bitcast.255, bf16[1024,1024]{1,0:T(8,128)(2,1)} %get-tuple-element.437.refs_2_.shrink_ref, bf16[2048,1024]{1,0:T(8,128)(2,1)} %get-tuple-element.525.slope_ref, bf16[256,1024]{1,0:T(8,128)(2,1)} %bitcast.286), custom_call_target="tpu_custom_call" | custom-call | flops 1000 | bytes 1000 | tf_op jit(solution)/shard_map/hidden_back/pallas_call | solution.py:839
  505.7 3.9 product.10
  517.5 10.0 %weight_grad.7 = (bf16[1024,1024]{1,0:T(8,128)(2,1)}, f32[1,1024]{1,0:T(1,128)}, f32[1,1024]{1,0:T(1,128)}) custom-call(bf16[2048,1024]{1,0:T(8,128)(2,1)} %get-tuple-element.374.x_ref, bf16[1024,1024]{1,0:T(8,128)(2,1)} %get-tuple-element.537.weight_ref, f32[1,1024]{1,0:T(1,128)} %get-tuple-element.712, f32[1,1024]{1,0:T(1,128)} %get-tuple-element.711, ...), custom_call_target="tpu_custom_call" | custom-call | flops 1000 | bytes 1000 | tf_op jit(solution)/shard_map/weight_grad/pallas_call | solution.py:908
  546.1 21.4 %attend_back.6 = (bf16[2048,384]{1,0:T(8,128)(2,1)}, f32[1,384]{1,0:T(1,128)}) custom-call(bf16[2048,768]{1,0:T(8,128)(2,1)} %get-tuple-element.575.q_ref.k_ref.v_ref, bf16[2048,768]{1,0:T(8,128)(2,1)} %get-tuple-element.575.q_ref.k_ref.v_ref, bf16[2048,768]{1,0:T(8,128)(2,1)} %get-tuple-element.575.q_ref.k_ref.v_ref, ...), custom_call_target="tpu_custom_call" | custom-call | flops 1000 | bytes 1000 | tf_op jit(solution)/shard_map/attend_back/pallas_call | solution.py:575
  567.5 6.8 weight_grad.8
  594.4 21.2 %attend_back.7 = (bf16[2048,384]{1,0:T(8,128)(2,1)}, f32[1,384]{1,0:T(1,128)}) custom-call(bf16[2048,768]{1,0:T(8,128)(2,1)} %get-tuple-element.575.q_ref.k_ref.v_ref, bf16[2048,768]{1,0:T(8,128)(2,1)} %get-tuple-element.575.q_ref.k_ref.v_ref, bf16[2048,768]{1,0:T(8,128)(2,1)} %get-tuple-element.575.q_ref.k_ref.v_ref, ...), custom_call_target="tpu_custom_call" | custom-call | flops 1000 | bytes 1000 | tf_op jit(solution)/shard_map/attend_back/pallas_call | solution.py:575
  617.5 7.0 weight_grad.9
  629.5 3.9 all-to-all-start.7
  633.4 8.6 %norm_grad.6 = bf16[1024,1024]{1,0:T(8,128)(2,1)} custom-call(s32[1]{0:T(128)} %bitcast.1.y_ref, bf16[2048,1024]{1,0:T(8,128)(2,1)} %get-tuple-element.539.refs_0_.h_ref, bf16[1024,1024]{1,0:T(8,128)(2,1)} %get-tuple-element.435.refs_0_.wi_ref, bf16[1024,768]{1,0:T(8,128)(2,1)} %get-tuple-element.599.wm_ref, bf16[2048,384]{1,0:T(8,128)(2,1)} %get-tuple-element.602.refs_0_, ...), custom_call_target="tpu_custom_call" | custom-call | flops 1000 | bytes 1000 | tf_op jit(solution)/shard_map/norm_grad/pallas_call | solution.py:806
  655.2 4.2 collective-permute-done.56
  661.3 8.5 %norm_grad.7 = bf16[1024,1024]{1,0:T(8,128)(2,1)} custom-call(s32[1]{0:T(128)} %bitcast.1.y_ref, bf16[2048,1024]{1,0:T(8,128)(2,1)} %get-tuple-element.539.refs_0_.h_ref, bf16[1024,1024]{1,0:T(8,128)(2,1)} %get-tuple-element.435.refs_0_.wi_ref, bf16[1024,768]{1,0:T(8,128)(2,1)} %get-tuple-element.599.wm_ref, bf16[2048,384]{1,0:T(8,128)(2,1)} %get-tuple-element.602.refs_0_, ...), custom_call_target="tpu_custom_call" | custom-call | flops 1000 | bytes 1000 | tf_op jit(solution)/shard_map/norm_grad/pallas_call | solution.py:806
  688.5 5.4 all-to-all-start.8
  708.3 10.4 %update.1 = (f32[2,32,3072]{2,1,0:T(8,128)}, f32[2,32,3072]{2,1,0:T(8,128)}, f32[2,32,3072]{2,1,0:T(8,128)}, f32[2,32,3072]{2,1,0:T(8,128)}, f32[2,32,1024]{2,1,...) custom-call(f32[1]{0:T(128)} %bitcast.149.clip_ref, ...), custom_call_target="tpu_custom_call" | custom-call | flops 1000 | bytes 1000 | tf_op jit(solution)/shard_map/update/pallas_call | solution.py:1014
  (497 shorter events, 246.9 us)
Async XLA Ops:
  10.8 14.2 %all-to-all-start = ((bf16[4,32,1824]{2,1,0:T(8,128)(2,1)}), bf16[4,32,1824]{2,1,0:T(8,128)(2,1)}, u32[]{:S(2)}, u32[]{:S(2)}) async-start(bf16[4,32,1824]{2,1,0:T(8,128)(2,1)} %pack.2), calls=%async_computation | async-start | bytes 983040 | tf_op jit(solution)/shard_map/all_to_all | solution.py:270
  15.0 81.2 %all-gather.3.cloned.1.call-start = ((), (), s32[]{:S(2)}) async-start(), calls=%async_computation.11 | async-start | bytes 1179648 | tf_op jit(solution)/shard_map/all_gather | solution.py:1215
  15.9 44.2 %collective-permute-start.3 = (bf16[512,1024]{1,0:T(8,128)(2,1)S(1)}, bf16[512,1024]{1,0:T(8,128)(2,1)}, u32[]{:S(2)}, u32[]{:S(2)}) collective-permute-start(bf16[512,1024]{1,0:T(8,128)(2,1)S(1)} %fusion.15.refs_0_), channel_id=1, source_target_pairs={{0,2},{1,3},{2,0},{3,1},{4,6},{5,7},{6,4},{7,5},{8,10},{9,11},{10,... | collective-permute-start | bytes 3145736 | tf_op jit(solution)/shard_map/ppermute | solution.py:60
  31.7 15.7 %all-to-all-start.1 = ((bf16[32,2,416]{2,1,0:T(2,128)(2,1)}), bf16[32,2,416]{2,1,0:T(2,128)(2,1)S(1)}, u32[]{:S(2)}, u32[]{:S(2)}) async-start(bf16[32,2,416]{2,1,0:T(2,128)(2,1)} %reshape.477), calls=%async_computation.1 | async-start | bytes 131072 | tf_op jit(solution)/shard_map/all_to_all | solution.py:1205
  37.0 13.4 %collective-permute-start = (bf16[128,768]{1,0:T(8,128)(2,1)}, bf16[128,768]{1,0:T(8,128)(2,1)}, u32[]{:S(2)}, u32[]{:S(2)}) collective-permute-start(bf16[128,768]{1,0:T(8,128)(2,1)} %slice.265.refs_9_), channel_id=1, source_target_pairs={{0,8},{4,12},{8,16},{12,20},{16,24},{20,28},{24,0},{28,4},{1,9},{5... | collective-permute-start | bytes 589832 | tf_op jit(solution)/shard_map/ppermute | solution.py:47
  80.1 16.1 %collective-permute-start.11 = (bf16[128,2048]{1,0:T(8,128)(2,1)S(1)}, bf16[128,2048]{1,0:T(8,128)(2,1)S(1)}, u32[]{:S(2)}, u32[]{:S(2)}) collective-permute-start(bf16[128,2048]{1,0:T(8,128)(2,1)S(1)} %pad_maximum_fusion.3.refs_3_), channel_id=1, source_target_pairs={{0,4},{4,0},{8,12},{12,8},{16,20},{20,16},{24,28},{28,24},{1,5},{5... | collective-permute-start | bytes 1572872 | tf_op jit(solution)/shard_map/ppermute | solution.py:55
  81.8 14.5 %collective-permute-start.10 = (bf16[128,2048]{1,0:T(8,128)(2,1)S(1)}, bf16[128,2048]{1,0:T(8,128)(2,1)}, u32[]{:S(2)}, u32[]{:S(2)}) collective-permute-start(bf16[128,2048]{1,0:T(8,128)(2,1)S(1)} %pad_maximum_fusion.3.refs_3_), channel_id=1, source_target_pairs={{0,8},{4,12},{8,16},{12,20},{16,24},{20,28},{24,0},{28,4},{1,9},{5... | collective-permute-start | bytes 1572872 | tf_op jit(solution)/shard_map/ppermute | solution.py:47
  96.3 21.8 %collective-permute-start.13 = (bf16[128,2048]{1,0:T(8,128)(2,1)}, bf16[128,2048]{1,0:T(8,128)(2,1)}, u32[]{:S(2)}, u32[]{:S(2)}) collective-permute-start(bf16[128,2048]{1,0:T(8,128)(2,1)} %collective-permute-done.10.refs_5_), channel_id=1, source_target_pairs={{0,4},{4,0},{8,12},{12,8},{16,20},{20,16},{24,28},{28,24},{1,5},{5... | collective-permute-start | bytes 1572872 | tf_op jit(solution)/shard_map/ppermute | solution.py:55
  96.6 21.4 %collective-permute-start.12 = (bf16[128,2048]{1,0:T(8,128)(2,1)}, bf16[128,2048]{1,0:T(8,128)(2,1)}, u32[]{:S(2)}, u32[]{:S(2)}) collective-permute-start(bf16[128,2048]{1,0:T(8,128)(2,1)} %collective-permute-done.10.refs_5_), channel_id=1, source_target_pairs={{0,8},{4,12},{8,16},{12,20},{16,24},{20,28},{24,0},{28,4},{1,9},{5... | collective-permute-start | bytes 1572872 | tf_op jit(solution)/shard_map/ppermute | solution.py:47
  97.5 20.6 %all-to-all-start.2 = ((bf16[4,32,1792]{2,1,0:T(8,128)(2,1)}), bf16[4,32,1792]{2,1,0:T(8,128)(2,1)S(1)}, u32[]{:S(2)}, u32[]{:S(2)}) async-start(bf16[4,32,1792]{2,1,0:T(8,128)(2,1)} %pack.3), calls=%async_computation.2 | async-start | bytes 917504 | tf_op jit(solution)/shard_map/all_to_all | solution.py:270
  101.4 37.5 %collective-permute-start.14 = (bf16[512,1024]{1,0:T(8,128)(2,1)S(1)}, bf16[512,1024]{1,0:T(8,128)(2,1)}, u32[]{:S(2)}, u32[]{:S(2)}) collective-permute-start(bf16[512,1024]{1,0:T(8,128)(2,1)S(1)} %get-tuple-element.450.refs_0_), channel_id=1, source_target_pairs={{0,2},{1,3},{2,0},{3,1},{4,6},{5,7},{6,4},{7,5},{8,10},{9,11},{10,... | collective-permute-start | bytes 3145736 | tf_op jit(solution)/shard_map/ppermute | solution.py:60
  118.0 25.2 %all-to-all-start.3 = ((bf16[4,2,64,1024]{3,2,1,0:T(8,128)(2,1)}), bf16[4,2,64,1024]{3,2,1,0:T(8,128)(2,1)S(1)}, u32[]{:S(2)}, u32[]{:S(2)}) async-start(bf16[4,2,64,1024]{3,2,1,0:T(8,128)(2,1)} %pad_maximum_fusion), calls=%async_computation.3 | async-start | bytes 2097152 | tf_op jit(solution)/shard_map/all_to_all | solution.py:270
  121.6 160.8 %all-gather.5.cloned.1.call-start = ((), (), s32[]{:S(2)}) async-start(), calls=%async_computation.12 | async-start | bytes 4718592 | tf_op jit(solution)/shard_map/all_gather | solution.py:1288
  121.6 15.4 %collective-permute-start.16 = (bf16[128,2048]{1,0:T(8,128)(2,1)}, bf16[128,2048]{1,0:T(8,128)(2,1)}, u32[]{:S(2)}, u32[]{:S(2)}) collective-permute-start(bf16[128,2048]{1,0:T(8,128)(2,1)} %collective-permute-done.12.refs_7_), channel_id=1, source_target_pairs={{0,4},{4,0},{8,12},{12,8},{16,20},{20,16},{24,28},{28,24},{1,5},{5... | collective-permute-start | bytes 1572872 | tf_op jit(solution)/shard_map/ppermute | solution.py:55
  122.6 16.3 %collective-permute-start.15 = (bf16[128,2048]{1,0:T(8,128)(2,1)}, bf16[128,2048]{1,0:T(8,128)(2,1)}, u32[]{:S(2)}, u32[]{:S(2)}) collective-permute-start(bf16[128,2048]{1,0:T(8,128)(2,1)} %collective-permute-done.12.refs_7_), channel_id=1, source_target_pairs={{0,8},{4,12},{8,16},{12,20},{16,24},{20,28},{24,0},{28,4},{1,9},{5... | collective-permute-start | bytes 1572872 | tf_op jit(solution)/shard_map/ppermute | solution.py:47
  143.2 17.0 %collective-permute-start.17 = (bf16[128,2048]{1,0:T(8,128)(2,1)}, bf16[128,2048]{1,0:T(8,128)(2,1)S(1)}, u32[]{:S(2)}, u32[]{:S(2)}) collective-permute-start(bf16[128,2048]{1,0:T(8,128)(2,1)} %collective-permute-done.15.refs_9_), channel_id=1, source_target_pairs={{0,4},{4,0},{8,12},{12,8},{16,20},{20,16},{24,28},{28,24},{1,5},{5... | collective-permute-start | bytes 1572872 | tf_op jit(solution)/shard_map/ppermute | solution.py:55
  144.7 422.8 %reduce-scatter.3.cloned.1.call-start = ((), (), s32[]{:S(2)}) async-start(), calls=%async_computation.13 | async-start | bytes 5308416 | tf_op jit(solution)/shard_map/reduce_scatter | solution.py:1401
  160.2 20.7 %collective-permute-start.19 = (bf16[128,768]{1,0:T(8,128)(2,1)}, bf16[128,768]{1,0:T(8,128)(2,1)S(1)}, u32[]{:S(2)}, u32[]{:S(2)}) collective-permute-start(bf16[128,768]{1,0:T(8,128)(2,1)} %slice.284.refs_7_), channel_id=1, source_target_pairs={{0,4},{4,0},{8,12},{12,8},{16,20},{20,16},{24,28},{28,24},{1,5},{5... | collective-permute-start | bytes 589832 | tf_op jit(solution)/shard_map/ppermute | solution.py:55
  161.6 19.3 %collective-permute-start.18 = (bf16[128,768]{1,0:T(8,128)(2,1)}, bf16[128,768]{1,0:T(8,128)(2,1)S(1)}, u32[]{:S(2)}, u32[]{:S(2)}) collective-permute-start(bf16[128,768]{1,0:T(8,128)(2,1)} %slice.284.refs_7_), channel_id=1, source_target_pairs={{0,8},{4,12},{8,16},{12,20},{16,24},{20,28},{24,0},{28,4},{1,9},{5... | collective-permute-start | bytes 589832 | tf_op jit(solution)/shard_map/ppermute | solution.py:47
  189.0 20.8 %collective-permute-start.26 = (bf16[512,1024]{1,0:T(8,128)(2,1)S(1)}, bf16[512,1024]{1,0:T(8,128)(2,1)}, u32[]{:S(2)}, u32[]{:S(2)}) collective-permute-start(bf16[512,1024]{1,0:T(8,128)(2,1)S(1)} %get-tuple-element.450.refs_0_), channel_id=1, source_target_pairs={{0,1},{1,0},{2,3},{3,2},{4,5},{5,4},{6,7},{7,6},{8,9},{9,8},{10,11... | collective-permute-start | bytes 3145736 | tf_op jit(solution)/shard_map/ppermute | solution.py:65
  189.1 20.6 %collective-permute-start.27 = (bf16[512,1024]{1,0:T(8,128)(2,1)}, bf16[512,1024]{1,0:T(8,128)(2,1)}, u32[]{:S(2)}, u32[]{:S(2)}) collective-permute-start(bf16[512,1024]{1,0:T(8,128)(2,1)} %collective-permute-done.14.refs_2_), channel_id=1, source_target_pairs={{0,1},{1,0},{2,3},{3,2},{4,5},{5,4},{6,7},{7,6},{8,9},{9,8},{10,11... | collective-permute-start | bytes 3145736 | tf_op jit(solution)/shard_map/ppermute | solution.py:65
  189.5 27.9 %collective-permute-start.21 = (bf16[512,1024]{1,0:T(8,128)(2,1)}, bf16[512,1024]{1,0:T(8,128)(2,1)}, u32[]{:S(2)}, u32[]{:S(2)}) collective-permute-start(bf16[512,1024]{1,0:T(8,128)(2,1)} %fusion.14), channel_id=1, source_target_pairs={{0,2},{1,3},{2,0},{3,1},{4,6},{5,7},{6,4},{7,5},{8,10},{9,11},{10,... | collective-permute-start | bytes 3145736 | tf_op jit(solution)/shard_map/ppermute | solution.py:60
  189.5 16.5 %collective-permute-start.23 = (bf16[128,768]{1,0:T(8,128)(2,1)S(1)}, bf16[128,768]{1,0:T(8,128)(2,1)S(1)}, u32[]{:S(2)}, u32[]{:S(2)}) collective-permute-start(bf16[128,768]{1,0:T(8,128)(2,1)S(1)} %collective-permute-done.18.refs_9_), channel_id=1, source_target_pairs={{0,4},{4,0},{8,12},{12,8},{16,20},{20,16},{24,28},{28,24},{1,5},{5... | collective-permute-start | bytes 589832 | tf_op jit(solution)/shard_map/ppermute | solution.py:55
  190.8 15.3 %collective-permute-start.22 = (bf16[128,768]{1,0:T(8,128)(2,1)S(1)}, bf16[128,768]{1,0:T(8,128)(2,1)S(1)}, u32[]{:S(2)}, u32[]{:S(2)}) collective-permute-start(bf16[128,768]{1,0:T(8,128)(2,1)S(1)} %collective-permute-done.18.refs_9_), channel_id=1, source_target_pairs={{0,8},{4,12},{8,16},{12,20},{16,24},{20,28},{24,0},{28,4},{1,9},{5... | collective-permute-start | bytes 589832 | tf_op jit(solution)/shard_map/ppermute | solution.py:47
  223.4 25.5 %collective-permute-start.31 = (bf16[512,1024]{1,0:T(8,128)(2,1)S(1)}, bf16[512,1024]{1,0:T(8,128)(2,1)}, u32[]{:S(2)}, u32[]{:S(2)}) collective-permute-start(bf16[512,1024]{1,0:T(8,128)(2,1)S(1)} %fusion.16.refs_0_), channel_id=1, source_target_pairs={{0,2},{1,3},{2,0},{3,1},{4,6},{5,7},{6,4},{7,5},{8,10},{9,11},{10,... | collective-permute-start | bytes 3145736 | tf_op jit(solution)/shard_map/ppermute | solution.py:60
  309.5 33.1 %collective-permute-start.34 = (bf16[2,64,1024]{2,1,0:T(8,128)(2,1)S(1)}, bf16[2,64,1024]{2,1,0:T(8,128)(2,1)S(1)}, u32[]{:S(2)}, u32[]{:S(2)}) collective-permute-start(bf16[2,64,1024]{2,1,0:T(8,128)(2,1)S(1)} %get-tuple-element.690), channel_id=1, source_target_pairs={{0,2},{1,3},{2,0},{3,1},{4,6},{5,7},{6,4},{7,5},{8,10},{9,11},{10,... | collective-permute-start | bytes 786440 | tf_op jit(solution)/shard_map/ppermute | solution.py:258
  401.4 25.4 %collective-permute-start.36 = (bf16[512,1024]{1,0:T(8,128)(2,1)S(1)}, bf16[512,1024]{1,0:T(8,128)(2,1)}, u32[]{:S(2)}, u32[]{:S(2)}) collective-permute-start(bf16[512,1024]{1,0:T(8,128)(2,1)S(1)} %fusion.9), channel_id=1, source_target_pairs={{0,2},{1,3},{2,0},{3,1},{4,6},{5,7},{6,4},{7,5},{8,10},{9,11},{10,... | collective-permute-start | bytes 3145736 | tf_op jit(solution)/shard_map/ppermute | solution.py:60
  436.5 25.5 %collective-permute-start.38 = (bf16[512,1024]{1,0:T(8,128)(2,1)S(1)}, bf16[512,1024]{1,0:T(8,128)(2,1)}, u32[]{:S(2)}, u32[]{:S(2)}) collective-permute-start(bf16[512,1024]{1,0:T(8,128)(2,1)S(1)} %convert_element_type.292.refs_0_), channel_id=1, source_target_pairs={{0,2},{1,3},{2,0},{3,1},{4,6},{5,7},{6,4},{7,5},{8,10},{9,11},{10,... | collective-permute-start | bytes 3145736 | tf_op jit(solution)/shard_map/ppermute | solution.py:60
  462.5 71.8 %all-to-all-start.4 = ((bf16[32,32,768]{2,1,0:T(8,128)(2,1)}), bf16[32,32,768]{2,1,0:T(8,128)(2,1)}, u32[]{:S(2)}, u32[]{:S(2)}) async-start(bf16[32,32,768]{2,1,0:T(8,128)(2,1)} %bitcast.308), calls=%async_computation.4 | async-start | bytes 3145728 | tf_op jit(solution)/shard_map/all_to_all | solution.py:241
  487.4 14.5 %collective-permute-start.41 = (bf16[128,1024]{1,0:T(8,128)(2,1)S(1)}, bf16[128,1024]{1,0:T(8,128)(2,1)S(1)}, u32[]{:S(2)}, u32[]{:S(2)}) collective-permute-start(bf16[128,1024]{1,0:T(8,128)(2,1)S(1)} %get-tuple-element.665), channel_id=1, source_target_pairs={{0,4},{4,0},{8,12},{12,8},{16,20},{20,16},{24,28},{28,24},{1,5},{5... | collective-permute-start | bytes 786440 | tf_op jit(solution)/shard_map/ppermute | solution.py:55
  512.3 16.3 %collective-permute-start.42 = (bf16[512,1024]{1,0:T(8,128)(2,1)}, bf16[512,1024]{1,0:T(8,128)(2,1)}, u32[]{:S(2)}, u32[]{:S(2)}) collective-permute-start(bf16[512,1024]{1,0:T(8,128)(2,1)} %dynamic-slice_bitcast_fusion.3), channel_id=1, source_target_pairs={{0,1},{1,0},{2,3},{3,2},{4,5},{5,4},{6,7},{7,6},{8,9},{9,8},{10,11... | collective-permute-start | bytes 3145736 | tf_op jit(solution)/shard_map/ppermute | solution.py:65
  512.8 14.7 %collective-permute-start.45 = (bf16[2,64,1024]{2,1,0:T(8,128)(2,1)S(1)}, bf16[2,64,1024]{2,1,0:T(8,128)(2,1)}, u32[]{:S(2)}, u32[]{:S(2)}) collective-permute-start(bf16[2,64,1024]{2,1,0:T(8,128)(2,1)S(1)} %get-tuple-element.686), channel_id=1, source_target_pairs={{0,2},{1,3},{2,0},{3,1},{4,6},{5,7},{6,4},{7,5},{8,10},{9,11},{10,... | collective-permute-start | bytes 786440 | tf_op jit(solution)/shard_map/ppermute | solution.py:258
  514.4 17.8 %collective-permute-start.47 = (bf16[128,1024]{1,0:T(8,128)(2,1)S(1)}, bf16[128,1024]{1,0:T(8,128)(2,1)S(1)}, u32[]{:S(2)}, u32[]{:S(2)}) collective-permute-start(bf16[128,1024]{1,0:T(8,128)(2,1)S(1)} %add_convert_fusion.2), channel_id=1, source_target_pairs={{0,8},{4,12},{8,16},{12,20},{16,24},{20,28},{24,0},{28,4},{1,9},{5... | collective-permute-start | bytes 786440 | tf_op jit(solution)/shard_map/ppermute | solution.py:47
  517.0 15.2 %collective-permute-start.46 = (bf16[128,1024]{1,0:T(8,128)(2,1)S(1)}, bf16[128,1024]{1,0:T(8,128)(2,1)}, u32[]{:S(2)}, u32[]{:S(2)}) collective-permute-start(bf16[128,1024]{1,0:T(8,128)(2,1)S(1)} %get-tuple-element.663), channel_id=1, source_target_pairs={{0,4},{4,0},{8,12},{12,8},{16,20},{20,16},{24,28},{28,24},{1,5},{5... | collective-permute-start | bytes 786440 | tf_op jit(solution)/shard_map/ppermute | solution.py:55
  531.6 36.0 %collective-permute-start.43 = (bf16[512,1024]{1,0:T(8,128)(2,1)}, bf16[512,1024]{1,0:T(8,128)(2,1)}, u32[]{:S(2)}, u32[]{:S(2)}) collective-permute-start(bf16[512,1024]{1,0:T(8,128)(2,1)} %fusion.7), channel_id=1, source_target_pairs={{0,2},{1,3},{2,0},{3,1},{4,6},{5,7},{6,4},{7,5},{8,10},{9,11},{10,... | collective-permute-start | bytes 3145736 | tf_op jit(solution)/shard_map/ppermute | solution.py:60
  535.4 32.1 %all-to-all-start.5 = ((bf16[8,128,256]{2,1,0:T(8,128)(2,1)}), bf16[8,128,256]{2,1,0:T(8,128)(2,1)S(1)}, u32[]{:S(2)}, u32[]{:S(2)}) async-start(bf16[8,128,256]{2,1,0:T(8,128)(2,1)} %reshape.442), calls=%async_computation.5 | async-start | bytes 1048576 | tf_op jit(solution)/shard_map/all_to_all | solution.py:1461
  538.9 90.6 %reduce-scatter.5.cloned.1.call-start = ((), (), s32[]{:S(2)}) async-start(), calls=%async_computation.14 | async-start | bytes 2359296 | tf_op jit(solution)/shard_map/reduce_scatter | solution.py:1460
  540.7 26.7 %collective-permute-start.49 = (bf16[128,1024]{1,0:T(8,128)(2,1)}, bf16[128,1024]{1,0:T(8,128)(2,1)}, u32[]{:S(2)}, u32[]{:S(2)}) collective-permute-start(bf16[128,1024]{1,0:T(8,128)(2,1)} %add_convert_fusion.1), channel_id=1, source_target_pairs={{0,8},{4,12},{8,16},{12,20},{16,24},{20,28},{24,0},{28,4},{1,9},{5... | collective-permute-start | bytes 786440 | tf_op jit(solution)/shard_map/ppermute | solution.py:47
  544.4 23.1 %collective-permute-start.48 = (bf16[128,1024]{1,0:T(8,128)(2,1)}, bf16[128,1024]{1,0:T(8,128)(2,1)}, u32[]{:S(2)}, u32[]{:S(2)}) collective-permute-start(bf16[128,1024]{1,0:T(8,128)(2,1)} %get-tuple-element.661), channel_id=1, source_target_pairs={{0,4},{4,0},{8,12},{12,8},{16,20},{20,16},{24,28},{28,24},{1,5},{5... | collective-permute-start | bytes 786440 | tf_op jit(solution)/shard_map/ppermute | solution.py:55
  576.6 40.9 %all-to-all-start.6 = ((bf16[32,32,512]{2,1,0:T(8,128)(2,1)}), bf16[32,32,512]{2,1,0:T(8,128)(2,1)S(1)}, u32[]{:S(2)}, u32[]{:S(2)}) async-start(bf16[32,32,512]{2,1,0:T(8,128)(2,1)} %bitcast.289), calls=%async_computation.7 | async-start | bytes 2097152 | tf_op jit(solution)/shard_map/all_to_all | solution.py:241
  585.3 32.1 %collective-permute-start.52 = (bf16[128,1024]{1,0:T(8,128)(2,1)}, bf16[128,1024]{1,0:T(8,128)(2,1)}, u32[]{:S(2)}, u32[]{:S(2)}) collective-permute-start(bf16[128,1024]{1,0:T(8,128)(2,1)} %add_convert_fusion), channel_id=1, source_target_pairs={{0,8},{4,12},{8,16},{12,20},{16,24},{20,28},{24,0},{28,4},{1,9},{5... | collective-permute-start | bytes 786440 | tf_op jit(solution)/shard_map/ppermute | solution.py:47
  588.8 28.6 %collective-permute-start.51 = (bf16[128,1024]{1,0:T(8,128)(2,1)S(1)}, bf16[128,1024]{1,0:T(8,128)(2,1)}, u32[]{:S(2)}, u32[]{:S(2)}) collective-permute-start(bf16[128,1024]{1,0:T(8,128)(2,1)S(1)} %get-tuple-element.659), channel_id=1, source_target_pairs={{0,4},{4,0},{8,12},{12,8},{16,20},{20,16},{24,28},{28,24},{1,5},{5... | collective-permute-start | bytes 786440 | tf_op jit(solution)/shard_map/ppermute | solution.py:55
  594.4 88.9 %collective-permute-start.50 = (bf16[512,1024]{1,0:T(8,128)(2,1)}, bf16[512,1024]{1,0:T(8,128)(2,1)}, u32[]{:S(2)}, u32[]{:S(2)}) collective-permute-start(bf16[512,1024]{1,0:T(8,128)(2,1)} %dynamic-slice_bitcast_fusion.2), channel_id=1, source_target_pairs={{0,1},{1,0},{2,3},{3,2},{4,5},{5,4},{6,7},{7,6},{8,9},{9,8},{10,11... | collective-permute-start | bytes 3145736 | tf_op jit(solution)/shard_map/ppermute | solution.py:65
  629.5 40.3 %all-to-all-start.7 = ((bf16[32,32,512]{2,1,0:T(8,128)(2,1)}), bf16[32,32,512]{2,1,0:T(8,128)(2,1)}, u32[]{:S(2)}, u32[]{:S(2)}) async-start(bf16[32,32,512]{2,1,0:T(8,128)(2,1)} %bitcast.290), calls=%async_computation.9 | async-start | bytes 2097152 | tf_op jit(solution)/shard_map/all_to_all | solution.py:241
  648.2 11.2 %collective-permute-start.56 = (bf16[2,32,2,1024]{3,1,0,2:T(8,128)(2,1)}, bf16[2,32,2,1024]{3,1,0,2:T(8,128)(2,1)}, u32[]{:S(2)}, u32[]{:S(2)}) collective-permute-start(bf16[2,32,2,1024]{3,1,0,2:T(8,128)(2,1)} %get-tuple-element.682), channel_id=1, source_target_pairs={{0,2},{1,3},{2,0},{3,1},{4,6},{5,7},{6,4},{7,5},{8,10},{9,11},{10,... | collective-permute-start | bytes 786440 | tf_op jit(solution)/shard_map/ppermute | solution.py:258
  651.2 29.7 %collective-permute-start.54 = (bf16[512,1024]{1,0:T(8,128)(2,1)}, bf16[512,1024]{1,0:T(8,128)(2,1)S(1)}, u32[]{:S(2)}, u32[]{:S(2)}) collective-permute-start(bf16[512,1024]{1,0:T(8,128)(2,1)} %fusion.1), channel_id=1, source_target_pairs={{0,2},{1,3},{2,0},{3,1},{4,6},{5,7},{6,4},{7,5},{8,10},{9,11},{10,... | collective-permute-start | bytes 3145736 | tf_op jit(solution)/shard_map/ppermute | solution.py:60
  683.3 17.2 %collective-permute-start.57 = (bf16[512,1024]{1,0:T(8,128)(2,1)}, bf16[512,1024]{1,0:T(8,128)(2,1)}, u32[]{:S(2)}, u32[]{:S(2)}) collective-permute-start(bf16[512,1024]{1,0:T(8,128)(2,1)} %dynamic-slice_bitcast_fusion), channel_id=1, source_target_pairs={{0,1},{1,0},{2,3},{3,2},{4,5},{5,4},{6,7},{7,6},{8,9},{9,8},{10,11... | collective-permute-start | bytes 3145736 | tf_op jit(solution)/shard_map/ppermute | solution.py:65
  688.5 17.8 %all-to-all-start.8 = ((f32[32,1,128]{2,1,0:T(1,128)}), f32[32,1,128]{2,1,0:T(1,128)S(1)}, u32[]{:S(2)}, u32[]{:S(2)}) async-start(f32[32,1,128]{2,1,0:T(1,128)} %broadcast_in_dim.42), calls=%async_computation.10 | async-start | bytes 32768 | tf_op jit(solution)/shard_map/all_to_all | solution.py:1545
  (106 other events, 956.9 us)
Sparse Core Ops, SparseCore 0:
  29.5 44.6 all-gather.2
  144.9 84.1 all-gather.4
  396.8 132.9 reduce-scatter.2
  546.0 77.4 reduce-scatter.4

commit v5 on v4

--- a/solution.py
+++ b/solution.py
@@ -92,12 +92,6 @@
     return total.reshape((count * piece.shape[0],) + piece.shape[1:])
 
 
-def pick(total, first, second):
-    sizes = (1, 1) + total.shape[2:]
-    start = (first, second) + (0,) * (total.ndim - 2)
-    return lax.dynamic_slice(total, start, sizes)[0, 0]
-
-
 class Gather:
     def __init__(self, value):
         self.pieces = [value]
@@ -129,56 +123,6 @@
         return pieces, slots
 
 
-class Scatter:
-    def __init__(self, *values):
-        outer, inner = dp_parts()
-        me = lax.axis_index("dp")
-        self.a, self.b = me // inner, me % inner
-        self.values = [
-            value.reshape((outer, inner, -1) + value.shape[1:]) for value in values
-        ]
-        self.parts = []
-        self.arrived = None
-        self.steps = 0
-
-    def own(self, at, turn):
-        inner = dp_parts()[1]
-        taken = [pick(value, at, (self.b - turn) % inner) for value in self.values]
-        return taken[0] if len(taken) == 1 else jnp.concatenate(taken, -1)
-
-    def cross(self):
-        outer, inner = dp_parts()
-        at = (self.a - len(self.parts) - 1) % outer
-        arrived = None
-        for turn in range(1, inner):
-            own = self.own(at, turn)
-            if arrived is not None:
-                own = (own.astype(F32) + arrived.astype(F32)).astype(BF)
-            arrived = inner_ring(own)
-        self.parts.append((self.own(at, 0), arrived))
-
-    def part(self):
-        own, arrived = self.parts[self.steps]
-        total = own.astype(F32)
-        if arrived is not None:
-            total = total + arrived.astype(F32)
-        if self.arrived is not None:
-            total = total + self.arrived.astype(F32)
-        return total
-
-    def forward(self):
-        self.arrived = outer_ring(self.part().astype(BF))
-        self.steps += 1
-
-    def hold(self, *values):
-        held = lax.optimization_barrier((values, self.values, self.parts, self.arrived))
-        self.values, self.parts, self.arrived = held[1], held[2], held[3]
-        return held[0]
-
-    def done(self):
-        return self.part()
-
-
 class SeqGather:
     def __init__(self, value):
         self.pieces = [value]
@@ -242,28 +186,33 @@
     return value.reshape((copies, parts) + value.shape[1:])
 
 
-def seq_swap(value):
-    size = lax.axis_size("seq")
-    chips = size // 2
-    me = lax.axis_index("seq")
-    y, c = me // 2, me % 2
-    value = value.reshape((chips, 2) + value.shape[1:])
-    kept = lax.dynamic_index_in_dim(value, c, 1, keepdims=False)
-    arrived = core_swap(lax.dynamic_index_in_dim(value, 1 - c, 1, keepdims=False))
-    pair = jnp.where(c == 0, jnp.stack([kept, arrived], 1), jnp.stack([arrived, kept], 1))
-    parts = []
-    for step in range(chips):
-        part = lax.dynamic_index_in_dim(pair, (y + step) % chips, 0, keepdims=False)
-        if step:
-            part = lax.ppermute(part, "seq", [(i, (i + 2 * step) % size) for i in range(size)])
-        parts.append(part)
-    if chips == 2:
-        total = jnp.where(y == 0, jnp.stack(parts), jnp.stack(parts[::-1]))
-    else:
-        total = jnp.zeros_like(pair)
-        for step, part in enumerate(parts):
-            total = lax.dynamic_update_index_in_dim(total, part, (y - step) % chips, 0)
-    return total.reshape((size,) + value.shape[2:])
+def flipped(values, index):
+    bit = 1
+    while bit < len(values):
+        chosen = (index & bit) > 0
+        values = [
+            jnp.where(chosen, values[n ^ bit], values[n]) for n in range(len(values))
+        ]
+        bit *= 2
+    return values
+
+
+class SeqSwap:
+    def __init__(self, value):
+        size = lax.axis_size("seq")
+        chunks = flipped([value[n] for n in range(size)], lax.axis_index("seq"))
+        self.value = [
+            lax.ppermute(chunk, "seq", [(i, i ^ n) for i in range(size)]) if n else chunk
+            for n, chunk in enumerate(chunks)
+        ]
+
+    def hold(self, *values):
+        held = lax.optimization_barrier((values, self.value))
+        self.value = held[1]
+        return held[0]
+
+    def done(self):
+        return jnp.stack(flipped(self.value, lax.axis_index("seq")))
 
 
 def seq_exchange(value):
@@ -515,17 +464,18 @@
     dk_ref[...] = jnp.zeros(dk_ref.shape, F32)
     dv_ref[...] = jnp.zeros(dv_ref.shape, F32)
 
-    def tile(i, diagonal):
-        rows = pl.ds(pl.multiple_of(i * block, block), block)
+    def tile(start, count, at, number, diagonal):
+        rows = pl.ds(pl.multiple_of(start, count), count)
+        part = slice(at, at + number)
         query = q_ref[rows, :]
         grad = do_ref[rows, :]
         log_total = lse_ref[:, rows]
         inner = inner_ref[:, rows]
-        scores = [matmul_nt(keys[h], query) for h in range(heads)]
-        weight_grads = [matmul_nt(values[h], grad) for h in range(heads)]
+        scores = [matmul_nt(keys[h][part, :], query) for h in range(heads)]
+        weight_grads = [matmul_nt(values[h][part, :], grad) for h in range(heads)]
         if diagonal:
-            row = lax.broadcasted_iota(jnp.int32, (block, block), 0)
-            column = lax.broadcasted_iota(jnp.int32, (block, block), 1)
+            row = lax.broadcasted_iota(jnp.int32, scores[0].shape, 0)
+            column = lax.broadcasted_iota(jnp.int32, scores[0].shape, 1)
             allowed = row <= column
             scores = [jnp.where(allowed, score, MASK_VALUE) for score in scores]
         weights = [jnp.exp(scores[h] - log_total[h : h + 1, :]) for h in range(heads)]
@@ -534,22 +484,25 @@
             (weights[h] * (weight_grads[h] - inner[h : h + 1, :])).astype(BF)
             for h in range(heads)
         ]
-        dv_ref[...] += matmul(
+        dv_ref[part, :] += matmul(
             jnp.concatenate(low, 1), jnp.concatenate([grad * mask for mask in masks], 0)
         )
-        dk_ref[...] += matmul(
+        dk_ref[part, :] += matmul(
             jnp.concatenate(score_grads, 1),
             jnp.concatenate([query * mask for mask in masks], 0),
         )
         dq_ref[rows, :] += matmul_tn(
-            jnp.concatenate(score_grads, 0), jnp.concatenate(keys, 0)
+            jnp.concatenate(score_grads, 0),
+            jnp.concatenate([keys[h][part, :] for h in range(heads)], 0),
         )
 
     def step(i, carry):
-        tile(i, False)
+        tile(i * block, block, 0, block, False)
         return carry
 
-    tile(j, True)
+    part_size = block // 2
+    tile(j * block, block, 0, part_size, True)
+    tile(j * block + part_size, part_size, part_size, part_size, True)
     lax.fori_loop(j + 1, steps, step, 0)
 
     own = pl.ds(pl.multiple_of(j * block, block), block)
@@ -619,12 +572,12 @@
     return values * below, slope
 
 
-def chip_rows(own, length):
+def chip_rows(own, length, size=ROWS):
     chips = lax.axis_size("seq") // 2
     y = lax.axis_index("seq") // 2
-    per = length // ROWS // chips
+    per = length // size // chips
     if own is None:
-        return length // ROWS, lambda i, y_ref: i, y
+        return length // size, lambda i, y_ref: i, y
     if own:
         return per, lambda i, y_ref: y_ref[0] * per + i, y
     return (
@@ -676,24 +629,28 @@
 
     else:
         act_ref, slope_ref = refs[-2:]
-    hidden = matmul(x_ref[...], scaled_ref[...]) + shift_ref[0:1, :]
-    activated, slope = gelu_pair(hidden)
-    activated = activated.astype(BF)
-    act_ref[...] = activated
-    slope_ref[...] = slope.astype(BF)
+    size = x_ref.shape[0] // 4
+    spans = [slice(n * size, (n + 1) * size) for n in range(4)]
+    hidden = [matmul(x_ref[span, :], scaled_ref[...]) + shift_ref[0:1, :] for span in spans]
+    for n, span in enumerate(spans):
+        activated, slope = gelu_pair(hidden[n])
+        act_ref[span, :] = activated.astype(BF)
+        slope_ref[span, :] = slope.astype(BF)
     if last:
-        out = matmul(activated, shrink_ref[...])
-        for half, o_ref in enumerate(attended):
-            out = out + matmul(o_ref[...], output_ref[half * 128 : (half + 1) * 128, :])
-        out_ref[...] = out.astype(BF)
+        for span in spans:
+            out = matmul(act_ref[span, :], shrink_ref[...])
+            for half, o_ref in enumerate(attended):
+                weight = output_ref[half * 128 : (half + 1) * 128, :]
+                out = out + matmul(o_ref[span, :], weight)
+            out_ref[span, :] = out.astype(BF)
 
 
 def feed(rows_of, x, units, first=None, scaled=None, last=None, kept=(), slots=None):
     length = x.shape[0]
-    steps, row, y = chip_rows(rows_of, length)
+    steps, row, y = chip_rows(rows_of, length, BLOCK)
 
     def rows(columns):
-        return pl.BlockSpec((ROWS, columns), lambda i, *_: (row(i, _[0]), 0))
+        return pl.BlockSpec((BLOCK, columns), lambda i, *_: (row(i, _[0]), 0))
 
     def whole(shape, column=0):
         return pl.BlockSpec(shape, lambda i, *_: (0, column))
@@ -733,8 +690,8 @@
             specs.append(whole((units, D), shrink[1]))
         values += [output, *attended]
         specs += [whole(output.shape)] + [rows(128)] * halves
-        out_specs.append(pl.BlockSpec((ROWS, D), lambda i, *_: (i, 0)))
-        out_shape.append(jax.ShapeDtypeStruct((steps * ROWS, D), BF))
+        out_specs.append(pl.BlockSpec((BLOCK, D), lambda i, *_: (i, 0)))
+        out_shape.append(jax.ShapeDtypeStruct((steps * BLOCK, D), BF))
     aliases = {2 + len(values) + n: n for n in range(len(kept))}
     values += list(kept)
     specs += [pl.BlockSpec(memory_space=pl.ANY)] * len(kept)
@@ -819,68 +776,26 @@
     )(y.reshape(1), hidden, expand, mixing, *mixed)
 
 
-def hidden_back_kernel(grad_ref, shrink_ref, slope_ref, output_ref, low_ref, total_ref, do_ref):
-    grads = grad_ref[...]
-    hidden = matmul_nt(grads, shrink_ref[...]) * slope_ref[...].astype(F32)
-    low_ref[...] = hidden.astype(BF)
-
-    @pl.when(pl.program_id(0) == 0)
-    def _():
-        total_ref[...] = jnp.zeros(total_ref.shape, F32)
-
-    total_ref[...] += jnp.sum(hidden, 0, keepdims=True)
-    do_ref[...] = matmul_nt(grads, output_ref[...]).astype(BF)
-
-
-def hidden_back(grads, shrink, slope, output):
-    length, units = slope.shape
-    width = output.shape[0]
-    array, column = shrink
-    return pl.pallas_call(
-        hidden_back_kernel,
-        grid=(length // BLOCK,),
-        in_specs=[
-            pl.BlockSpec((BLOCK, D), lambda i: (i, 0)),
-            pl.BlockSpec((units, D), lambda i: (0, column)),
-            pl.BlockSpec((BLOCK, units), lambda i: (i, 0)),
-            pl.BlockSpec((width, D), lambda i: (0, 0)),
-        ],
-        out_specs=[
-            pl.BlockSpec((BLOCK, units), lambda i: (i, 0)),
-            pl.BlockSpec((1, units), lambda i: (0, 0)),
-            pl.BlockSpec((BLOCK, width), lambda i: (i, 0)),
-        ],
-        out_shape=[
-            jax.ShapeDtypeStruct((length, units), BF),
-            jax.ShapeDtypeStruct((1, units), F32),
-            jax.ShapeDtypeStruct((length, width), BF),
-        ],
-        compiler_params=pltpu.CompilerParams(vmem_limit_bytes=VMEM_LIMIT),
-        cost_estimate=LIGHT,
-        name="hidden_back",
-    )(grads, array, slope, output)
-
-
-def product_kernel(x_ref, g_ref, out_ref):
-    out_ref[...] = matmul_tn(x_ref[...], g_ref[...]).astype(BF)
-
-
-def product(x, grads, column=0, wide=D):
-    length, count = x.shape
-    block = min(BLOCK, count)
+def product_kernel(g_ref, *refs):
+    for half, x_ref in enumerate(refs[:-1]):
+        product = matmul_tn(x_ref[...], g_ref[...])
+        refs[-1][half * 128 : (half + 1) * 128, :] = product.astype(BF)
+
+
+def product(inputs, grads):
+    rows = 128 * len(inputs)
+    block = D // 2
     return pl.pallas_call(
         product_kernel,
-        grid=(count // block,),
-        in_specs=[
-            pl.BlockSpec((length, block), lambda i: (0, i)),
-            pl.BlockSpec((length, D), lambda i: (0, 0)),
-        ],
-        out_specs=pl.BlockSpec((block, D), lambda i: (i, column)),
-        out_shape=jax.ShapeDtypeStruct((count, wide), BF),
+        grid=(D // block,),
+        in_specs=[pl.BlockSpec((grads.shape[0], block), lambda i: (0, i))]
+        + [pl.BlockSpec(x.shape, lambda i: (0, 0)) for x in inputs],
+        out_specs=pl.BlockSpec((rows, block), lambda i: (0, i)),
+        out_shape=jax.ShapeDtypeStruct((rows, D), BF),
         compiler_params=pltpu.CompilerParams(vmem_limit_bytes=VMEM_LIMIT),
         cost_estimate=LIGHT,
         name="product",
-    )(x, grads)
+    )(grads, *inputs)
 
 
 def weight_grad_kernel(count, x_ref, weight_ref, gain_ref, shift_ref, total_ref, *refs):
@@ -901,9 +816,10 @@
     shift_out_ref[...] = as_row(shift_sum)
 
 
-def weight_grad(x, lows, weight, gain, shift, total, kept=()):
+def weight_grad(x, lows, weight, gain, shift, total, wide=None):
     length, columns = x.shape[0], total.shape[1]
     array, column = weight
+    wide = wide or (0, columns)
     row = pl.BlockSpec((1, ROWS), lambda i: (0, i))
     return pl.pallas_call(
         partial(weight_grad_kernel, len(lows)),
@@ -915,49 +831,159 @@
             row,
             pl.BlockSpec((1, columns), lambda i: (0, 0)),
         ]
-        + [pl.BlockSpec(low.shape, lambda i: (0, 0)) for low in lows]
-        + [pl.BlockSpec(memory_space=pl.ANY)] * len(kept),
-        out_specs=[pl.BlockSpec((ROWS, columns), lambda i: (i, 0)), row, row],
+        + [pl.BlockSpec(low.shape, lambda i: (0, 0)) for low in lows],
+        out_specs=[pl.BlockSpec((ROWS, columns), lambda i: (i, wide[0])), row, row],
         out_shape=[
-            jax.ShapeDtypeStruct((D, kept[0].shape[1] if kept else columns), BF),
+            jax.ShapeDtypeStruct((D, wide[1]), BF),
             jax.ShapeDtypeStruct((1, D), F32),
             jax.ShapeDtypeStruct((1, D), F32),
         ],
-        input_output_aliases={5 + len(lows): 0} if kept else {},
         compiler_params=pltpu.CompilerParams(vmem_limit_bytes=VMEM_LIMIT),
         cost_estimate=LIGHT,
         name="weight_grad",
-    )(x, array, gain[None], shift[None], total, *lows, *kept)
-
-
-def pack_kernel(spans, mixing_ref, expand_ref, *refs):
-    out_ref = refs[-1]
-    for source_ref, part in ((mixing_ref, spans[0]), (expand_ref, spans[1])):
+    )(x, array, gain[None], shift[None], total, *lows)
+
+
+def pack_kernel(spans, split, mixing_ref, expand_ref, *refs):
+    outs = refs[-2:] if split else (refs[-1], refs[-1])
+    shift = split or 0
+    for source_ref, part, out_ref, back in (
+        (mixing_ref, spans[0], outs[0], 0),
+        (expand_ref, spans[1], outs[1], shift),
+    ):
         for p, start, at, count in part:
-            out_ref[p, :, start : start + count] = source_ref[0, :, at : at + count].astype(BF)
-    for pair_ref in refs[:-1]:
-        end = out_ref.shape[2] - pair_ref.shape[1]
-        for p in range(out_ref.shape[0]):
-            out_ref[p, :, end:] = pair_ref[...]
-
-
-def pack(mixing, expand, layer, spans, columns, pair=()):
+            columns = slice(start - back, start - back + count)
+            out_ref[p, :, columns] = source_ref[0, :, at : at + count].astype(BF)
+    for pair_ref in refs[: -2 if split else -1]:
+        end = outs[1].shape[2] - pair_ref.shape[1]
+        for p in range(outs[1].shape[0]):
+            outs[1][p, :, end:] = pair_ref[...]
+
+
+def pack(mixing, expand, layer, spans, columns, pair=(), split=0):
     parts, rows = lax.axis_size("seq"), mixing.shape[1]
     columns = columns + sum(value.shape[1] for value in pair)
-    return pl.pallas_call(
-        partial(pack_kernel, spans),
+    widths = [split, columns - split] if split else [columns]
+    made = pl.pallas_call(
+        partial(pack_kernel, spans, split),
         grid=(1,),
         in_specs=[
             pl.BlockSpec((1,) + mixing.shape[1:], lambda i: (layer, 0, 0)),
             pl.BlockSpec((1,) + expand.shape[1:], lambda i: (layer, 0, 0)),
         ]
         + [pl.BlockSpec(value.shape, lambda i: (0, 0)) for value in pair],
-        out_specs=pl.BlockSpec((parts, rows, columns), lambda i: (0, 0, 0)),
-        out_shape=jax.ShapeDtypeStruct((parts, rows, columns), BF),
+        out_specs=[pl.BlockSpec((parts, rows, w), lambda i: (0, 0, 0)) for w in widths],
+        out_shape=[jax.ShapeDtypeStruct((parts, rows, w), BF) for w in widths],
         compiler_params=pltpu.CompilerParams(vmem_limit_bytes=VMEM_LIMIT),
         cost_estimate=LIGHT,
         name="pack",
     )(mixing, expand, *pair)
+    return made if split else made[0]
+
+
+def feed_back_kernel(joined, kept, *refs):
+    grad_ref, shrink_ref, slope_ref, act_ref, x_ref, output_ref = refs[:6]
+    weight_ref, gain_ref, shift_ref = refs[6:9]
+    low_ref, total_ref, do_ref, gain_out_ref, shift_out_ref = refs[kept : kept + 5]
+    outs = refs[kept + 5 : -2]
+    expand_ref, shrink_acc_ref = refs[-2:]
+    i = pl.program_id(0)
+
+    @pl.when(i == 0)
+    def _():
+        total_ref[...] = jnp.zeros(total_ref.shape, F32)
+        expand_ref[...] = jnp.zeros(expand_ref.shape, F32)
+        shrink_acc_ref[...] = jnp.zeros(shrink_acc_ref.shape, F32)
+
+    grads = grad_ref[...]
+    hidden = matmul_nt(grads, shrink_ref[...]) * slope_ref[...].astype(F32)
+    low = hidden.astype(BF)
+    low_ref[...] = low
+    total_ref[...] += jnp.sum(hidden, 0, keepdims=True)
+    shrink_acc_ref[...] += matmul_tn(act_ref[...], grads)
+    do_ref[...] = matmul_nt(grads, output_ref[...]).astype(BF)
+    expand_ref[...] += matmul_tn(x_ref[...], low)
+
+    @pl.when(i == pl.num_programs(0) - 1)
+    def _():
+        gain, shift, total = as_column(gain_ref[...]), as_column(shift_ref[...]), total_ref[...]
+        units = total.shape[1]
+        raw = expand_ref[...]
+        weight = weight_ref[...].astype(F32)
+        outs[0][:, :units] = (raw * gain + shift * total).astype(BF)
+        if joined:
+            outs[0][:, units:] = shrink_acc_ref[...].astype(BF)
+        else:
+            outs[1][...] = shrink_acc_ref[...].astype(BF)
+        gain_out_ref[...] = as_row(jnp.sum(raw * weight, 1, keepdims=True))
+        shift_out_ref[...] = as_row(jnp.sum(weight * total, 1, keepdims=True))
+
+
+def feed_back(grads, shrink, slope, activated, x, output, weight, gain, shift, kept=()):
+    length, units = slope.shape
+    width, joined = output.shape[0], units == D
+
+    def rows(count):
+        return pl.BlockSpec((BLOCK, count), lambda i: (i, 0))
+
+    def whole(shape, column=0):
+        return pl.BlockSpec(shape, lambda i: (0, column))
+
+    out_specs = [rows(units), whole((1, units)), rows(width), whole((1, D)), whole((1, D))]
+    out_shape = [
+        jax.ShapeDtypeStruct((length, units), BF),
+        jax.ShapeDtypeStruct((1, units), F32),
+        jax.ShapeDtypeStruct((length, width), BF),
+        jax.ShapeDtypeStruct((1, D), F32),
+        jax.ShapeDtypeStruct((1, D), F32),
+    ]
+    if joined:
+        out_specs.append(whole((D, 2 * units)))
+        wide = kept[0].shape[1] if kept else 2 * units + width
+        out_shape.append(jax.ShapeDtypeStruct((D, wide), BF))
+    else:
+        out_specs += [whole((D, units)), whole((units, D))]
+        out_shape += [
+            jax.ShapeDtypeStruct((D, units), BF),
+            jax.ShapeDtypeStruct((units, D), BF),
+        ]
+    return pl.pallas_call(
+        partial(feed_back_kernel, joined, 9 + len(kept)),
+        grid=(length // BLOCK,),
+        in_specs=[
+            rows(D),
+            whole((units, D), shrink[1]),
+            rows(units),
+            rows(units),
+            rows(D),
+            whole((width, D)),
+            whole((D, units), weight[1]),
+            whole((1, D)),
+            whole((1, D)),
+        ]
+        + [pl.BlockSpec(memory_space=pl.ANY)] * len(kept),
+        out_specs=out_specs,
+        out_shape=out_shape,
+        input_output_aliases={9: 5} if kept else {},
+        scratch_shapes=[
+            pltpu.VMEM((D, units), F32),
+            pltpu.VMEM((units, D), F32),
+        ],
+        compiler_params=pltpu.CompilerParams(vmem_limit_bytes=VMEM_LIMIT),
+        cost_estimate=LIGHT,
+        name="feed_back",
+    )(
+        grads,
+        shrink[0],
+        slope,
+        activated,
+        x,
+        output,
+        weight[0],
+        gain[None],
+        shift[None],
+        *kept,
+    )
 
 
 def home_spans(parts, copies, width, units):
@@ -984,7 +1010,7 @@
     return weight_new, first_new, second_new, EMA_DECAY * average + (1.0 - EMA_DECAY) * weight_new
 
 
-def adam_kernel(spans, rates, clip_ref, exchanged_ref, output_ref, shrink_ref, *refs):
+def adam_kernel(spans, rates, clip_ref, mixing_ref, expand_ref, output_ref, shrink_ref, *refs):
     clip = clip_ref[0]
     states, news = refs[:16], refs[16:]
 
@@ -994,16 +1020,17 @@
         for ref, value in zip(news[4 * kind : 4 * kind + 4], new):
             ref[0, :, columns] = value
 
-    for kind, part in ((0, spans[0]), (2, spans[1])):
+    for kind, part, grad_ref in ((0, spans[0], mixing_ref), (2, spans[1], expand_ref)):
+        back = part[0][1]
         for source, start, at, count in part:
-            grad = exchanged_ref[0, source, :, start : start + count]
+            grad = grad_ref[0, source, :, start - back : start - back + count]
             step(kind, grad, slice(at, at + count))
     step(1, output_ref[0], slice(None))
     step(3, shrink_ref[0], slice(None))
 
 
-def update(clip, exchanged, output, shrink, states, spans, rates):
-    layers, parts, rows, columns = exchanged.shape
+def update(clip, mixing, expand, output, shrink, states, spans, rates):
+    layers, parts, rows = mixing.shape[:3]
     chunk = 16 if rows % 16 == 0 else rows
     chunks = rows // chunk
 
@@ -1016,7 +1043,8 @@
         grid=(layers, chunks),
         in_specs=[
             pl.BlockSpec(memory_space=pltpu.SMEM),
-            pl.BlockSpec((1, parts, chunk, columns), lambda l, n: (l, 0, n, 0)),
+            pl.BlockSpec((1, parts, chunk, mixing.shape[3]), lambda l, n: (l, 0, n, 0)),
+            pl.BlockSpec((1, parts, chunk, expand.shape[3]), lambda l, n: (l, 0, n, 0)),
             block(output),
             block(shrink),
         ]
@@ -1026,7 +1054,7 @@
         compiler_params=pltpu.CompilerParams(vmem_limit_bytes=VMEM_LIMIT),
         cost_estimate=LIGHT,
         name="update",
-    )(clip, exchanged, output, shrink, *states)
+    )(clip, mixing, expand, output, shrink, *states)
 
 
 def rotary_tables(positions):
@@ -1128,14 +1156,18 @@
     spans = home_spans(parts, copies, width, units)
     aligned = rows_f % 128 == 0 and rows_d % 16 == 0
 
-    def arrange(layer, mixing, expand, pair=()):
+    def arrange(layer, mixing, expand, pair=(), split=False):
         if aligned:
-            return pack(mixing, expand, layer, spans, 3 * width + units, pair)
+            return pack(
+                mixing, expand, layer, spans, 3 * width + units, pair, 3 * width * split
+            )
         mixing = mixing[layer].astype(BF).reshape(rows_d, 3, parts, halves, 128)
         mixing = mixing.transpose(2, 0, 3, 1, 4).reshape(parts, rows_d, 3 * width)
         expand = expand[layer].astype(BF).reshape(rows_d, copies, parts, rows_f)
         expand = expand.transpose(2, 0, 1, 3).reshape(parts, rows_d, units)
         pair = [jnp.broadcast_to(value, (parts,) + value.shape) for value in pair]
+        if split:
+            return mixing, jnp.concatenate([expand] + pair, -1)
         return jnp.concatenate([mixing, expand] + pair, -1)
 
     def settle_output(exchanged):
@@ -1146,11 +1178,6 @@
         projected = jnp.mean(normed_grad * own_normed, -1, keepdims=True)
         middle = jnp.mean(normed_grad, -1, keepdims=True)
         return gradient + scale * (normed_grad - middle - own_normed * projected)
-
-    def outgoing_output(attended, grads):
-        output_grad = jnp.concatenate([product(out, grads) for out in attended], 0)
-        output_grad = output_grad.reshape(copies // parts, parts, rows_d, D).transpose(1, 0, 2, 3)
-        return seq_swap(output_grad.reshape(parts, copies // parts * rows_d, D))
 
     def beside(grads, *pieces):
         pieces = [jnp.concatenate(piece).reshape(devices, small) for piece in pieces]
@@ -1201,6 +1228,23 @@
         output_weight[1],
     )
     near.forward()
+    outputs = jnp.concatenate(
+        [value.astype(BF).reshape(-1, width) for value in (first_output, later_output)], -1
+    )
+    outputs = lax.all_gather(outputs, "dp", axis=0, tiled=True)
+    cosine, sine = rotary_tables(places)
+    later_both = arrange(1, layer_mixing, layer_expand)
+    affine_low, cosine, sine, later_both, expand_own, shrink_own, low_gradient = near.hold(
+        affine_low,
+        cosine,
+        sine,
+        later_both,
+        both[:, 3 * width : 3 * width + units],
+        shrink_weight[0],
+        gradient.astype(BF),
+    )
+    near.forward()
+    near.cross()
     affine_low = affine_low.astype(BF).reshape(1, LAYERS * small)
     affine_all = lax.all_to_all(
         jnp.broadcast_to(affine_low, (devices, LAYERS * small)),
@@ -1209,22 +1253,6 @@
         concat_axis=0,
         tiled=True,
     )
-    outputs = jnp.concatenate(
-        [value.astype(BF).reshape(-1, width) for value in (first_output, later_output)], -1
-    )
-    outputs = lax.all_gather(outputs, "dp", axis=0, tiled=True)
-    cosine, sine = rotary_tables(places)
-    later_both = arrange(1, layer_mixing, layer_expand)
-    cosine, sine, later_both, expand_own, shrink_own, low_gradient = near.hold(
-        cosine,
-        sine,
-        later_both,
-        both[:, 3 * width : 3 * width + units],
-        shrink_weight[0],
-        gradient.astype(BF),
-    )
-    near.forward()
-    near.cross()
     far_own = jnp.concatenate([expand_own, shrink_own.astype(BF).reshape(-1, units)], -1)
     affine_all, far_own, near.pieces, near.chains, travel.pieces = tie(
         (affine_all, far_own, near.pieces, near.chains, travel.pieces)
@@ -1290,7 +1318,7 @@
         far.forward()
     while len(far.chains) < outer:
         far.cross()
-    attended, logs, later_near = far.hold(attended, logs, later_near)
+    attended, logs, later_near, grads = far.hold(attended, logs, later_near, travel.done())
     near = Gather(later_near)
     near.forward()
     near.cross()
@@ -1319,8 +1347,8 @@
     (others,) = near.hold(others)
     near.forward()
     near.cross()
-    cotangents, travel = travel, SeqScatter(others)
-    activated, slope, cotangents.pieces = travel.hold(activated, slope, cotangents.pieces)
+    travel = SeqScatter(others)
+    activated, slope = travel.hold(activated, slope)
     activated, slope, own = feed(
         True,
         normed,
@@ -1330,15 +1358,12 @@
         kept=(activated, slope),
     )
     (own,) = near.hold(own)
-    grads = cotangents.done()
     for step in range(2, outer - 1):
         near.forward()
         near.cross()
     stored = [(own_normed, scale, normed, mixed, attended, logs, activated, slope)]
     weights = [(mixing, mixing_scaled, output, expand, expand_scaled, shrink)]
-    total, (near.pieces, near.chains, grads) = travel.done(
-        own, (near.pieces, near.chains, grads)
-    )
+    total, (near.pieces, near.chains) = travel.done(own, (near.pieces, near.chains))
     while len(near.chains) < outer:
         near.cross()
     current = current + total + vectors[0][5] + vectors[0][7]
@@ -1381,22 +1406,35 @@
     )
 
     grads, attended, logs, activated = tie((grads, attended, logs, activated))
-    output_grad = outgoing_output(attended, grads)
-    hidden_low, hidden_total, attended_grad = hidden_back(grads, shrink, slope, output)
-    if units == D:
-        later_grad = product(activated, grads, 1, 2 * units + width)
-        later_grad, gain_two_grad, shift_two_grad = weight_grad(
-            normed, [hidden_low], (expand, 0), gain_two, shift_two, hidden_total, (later_grad,)
+
+    def feed_grads(gain, shift, kept=()):
+        output_grad, low_grads = tie((product(attended, grads), grads))
+        output_grad = output_grad.reshape(copies // parts, parts, rows_d, D).transpose(1, 0, 2, 3)
+        swap = SeqSwap(output_grad.reshape(parts, copies // parts * rows_d, D))
+        made = feed_back(
+            low_grads,
+            shrink,
+            slope,
+            activated,
+            normed,
+            output,
+            (expand, 0),
+            gain,
+            shift,
+            kept if units == D else (),
         )
-        output_grad = output_grad.reshape(-1, width)
-        later_grad = lax.dynamic_update_slice(later_grad, output_grad, (0, 2 * units))
-    else:
-        shrink_grad = product(activated, grads).reshape(-1, units)
-        expand_grad, gain_two_grad, shift_two_grad = weight_grad(
-            normed, [hidden_low], (expand, 0), gain_two, shift_two, hidden_total
-        )
-        output_grad = output_grad.reshape(-1, width)
-        later_grad = jnp.concatenate([expand_grad, shrink_grad, output_grad], -1)
+        made = swap.hold(*made)
+        low, total, attended_grad, gain_grad, shift_grad = made[:5]
+        output_grad = swap.done().reshape(-1, width)
+        if units == D:
+            joined = lax.dynamic_update_slice(made[5], output_grad, (0, 2 * units))
+        else:
+            joined = [made[5], made[6].reshape(-1, units), output_grad, *kept]
+            joined = jnp.concatenate(joined, -1)
+        return low, total, attended_grad, gain_grad, shift_grad, joined
+
+    made = feed_grads(gain_two, shift_two)
+    hidden_low, hidden_total, attended_grad, gain_two_grad, shift_two_grad, later_grad = made
     later_grad, attended_grad = tie((later_grad, attended_grad))
     later_first = lax.psum_scatter(later_grad, "dp", scatter_dimension=0, tiled=True)
     lows, totals = [], []
@@ -1419,12 +1457,12 @@
     gradient = norm_back(gradient, normed_grad, own_normed, scale)
     travel = SeqGather(gradient.astype(BF))
     lows, own_piece = tie((lows, travel.pieces[0]))
-    mixing_grad, gain_one_grad, shift_one_grad = weight_grad(
-        normed, lows, (mixing, 0), gain_one, shift_one, mixed_total
-    )
-    (mixing_grad,) = travel.hold(mixing_grad)
+    wide = (3, 2 * units + 4 * width) if units == D else None
+    later_mixing, gain_one_grad, shift_one_grad = weight_grad(
+        normed, lows, (mixing, 0), gain_one, shift_one, mixed_total, wide
+    )
+    (later_mixing,) = travel.hold(later_mixing)
     grads = travel.done()
-    later_mixing = sum_exchange(mixing_grad)
     output_sum = jnp.sum(cotangent.reshape(rows, D), 0)
 
     def small_grads(*pieces):
@@ -1441,47 +1479,23 @@
     own_normed, scale, normed, mixed, attended, logs, activated, slope = stored[0]
     mixing, mixing_scaled, output, expand, expand_scaled, shrink = weights[0]
     gain_one, shift_one, gain_two, shift_two = vectors[0][:4]
-    far = Scatter(product(activated, grads).reshape(-1, units))
-    (grads,) = far.hold(grads)
-    far.cross()
-    hidden_low, hidden_total, attended_grad = hidden_back(grads, shrink, slope, output)
-    hidden_low, attended_grad, grads, result_others, later_pieces = far.hold(
-        hidden_low, attended_grad, grads, result_others, later_pieces
-    )
-    far.forward()
-    far.cross()
-    output_grad = outgoing_output(attended, grads)
-    expand_grad, gain_two_grad, shift_two_grad = weight_grad(
-        normed, [hidden_low], (expand, 0), gain_two, shift_two, hidden_total
-    )
-    attended_grad, expand_grad, output_grad, later_mixing = far.hold(
-        attended_grad, expand_grad, output_grad, later_mixing
-    )
-    far_grad = lax.psum_scatter(expand_grad, "dp", scatter_dimension=0, tiled=True)
-    output_grad = lax.all_to_all(
-        output_grad.reshape(copies, parts * rows_d, width), "dp", 0, 0, tiled=True
-    )
+    made = feed_grads(gain_two, shift_two, (later_mixing,))
+    hidden_low, hidden_total, attended_grad, gain_two_grad, shift_two_grad, far_grad = made
+    far_grad, attended_grad, result_others, later_pieces = tie(
+        (far_grad, attended_grad, result_others, later_pieces)
+    )
+    far_grad = lax.psum_scatter(far_grad, "dp", scatter_dimension=0, tiled=True)
     travel = SeqScatter(result_others)
     lows, totals, mixing_grads, gain_grads, shift_grads = [], [], [], [], []
-    arrived = output_grad
     for half in range(halves):
-        if len(far.parts) < outer:
-            far.forward()
-            far.cross()
         low, total = attend_back(
             mixed, attended_grad, attended[half], logs[half], cosine, sine, half
         )
         if half == 0:
-            mixed, low, total, arrived, later_first = far.hold(
-                mixed, low, total, arrived, later_first
-            )
+            mixed, low, later_first = tie((mixed, low, later_first))
+            later_home = SeqSwap(later_first[:, :units].reshape(parts, rows_d, units))
         else:
-            mixed, low, total, arrived = far.hold(mixed, low, total, arrived)
-        if half == 0:
-            output_grad = arrived
-            result, (mixed, low) = travel.done(result_own, (mixed, low))
-        else:
-            mixing_grads[-1] = arrived
+            mixed, low = later_home.hold(mixed, low)
         mixing_grad, gain_one_grad, shift_one_grad = weight_grad(
             normed,
             [low],
@@ -1502,35 +1516,24 @@
                 small_grads(gains, jnp.concatenate(totals, -1), output_sum, hidden_total)
             )
         mixing_grad = beside(mixing_grad, *pieces) if pieces else mixing_grad
-        if half == halves - 1:
-            mixing_grad, far_grad = tie((mixing_grad, far_grad))
-            home = jnp.stack([far_grad, later_first[:, :units]], 1)
-            home = seq_swap(home.reshape(parts, rows_d, 2, units))
-        mixing_grad, lows, mixed, attended_grad = tie((mixing_grad, lows, mixed, attended_grad))
-        arrived = sum_exchange(mixing_grad)
-        mixing_grads.append(arrived)
+        if half == 0:
+            result, (mixing_grad,) = travel.done(result_own, (mixing_grad,))
+        mixing_grad, lows, mixed, attended_grad, mixing_grads = tie(
+            (mixing_grad, lows, mixed, attended_grad, mixing_grads)
+        )
+        mixing_grads.append(sum_exchange(mixing_grad))
     result = later_current + result + later_vectors[5] + later_vectors[7]
     result = result.reshape(stream.shape)
     others = norm_grad(hidden_low, expand_scaled, lows, mixing_scaled, False)
     travel = SeqScatter(others)
     (lows,) = travel.hold(lows)
     own = norm_grad(hidden_low, expand_scaled, lows, mixing_scaled, True)
-    while len(far.parts) < outer:
-        far.forward()
-        far.cross()
-    while far.steps < outer - 1:
-        far.forward()
-    shrink_grad = far.done()
-    later_mixing = jnp.sum(later_mixing.astype(F32), 0)
-    output_grad = jnp.sum(output_grad.astype(F32), 0)
-    squares = sum_squares(shrink_grad, output_grad, later_first, later_mixing)
-    shrink_grad, later_mixing, output_grad = (
-        value.astype(BF) for value in (shrink_grad, later_mixing, output_grad)
-    )
-    others = (mixing_grads[-1], own, squares, shrink_grad, later_mixing, output_grad, home)
-    others = tie(others)
-    mixing_grads[-1], own, squares, shrink_grad, later_mixing, output_grad, home = others
-
+    normed_grad = travel.done(own)[0]
+    gradient = norm_back(gradient, normed_grad, own_normed, scale)
+    squares = sum_squares(later_first)
+    mixing_grads[-1], gradient, result, squares = tie(
+        (mixing_grads[-1], gradient, result, squares)
+    )
     affine, parts_of_mixing = [], []
     for half in range(halves):
         count = (half == 0) + (half == halves - 1)
@@ -1538,10 +1541,12 @@
         parts_of_mixing.append(summed)
         affine += pieces
     affine_grad = jnp.stack(affine[::-1])
-    squares = squares + sum_squares(*parts_of_mixing, affine_grad, far_grad)
+    squares = squares + sum_squares(*parts_of_mixing, affine_grad)
     mixing_grad = jnp.concatenate(parts_of_mixing, -1).astype(BF)
-    expand_grad, later_expand = home[:, :, 0], home[:, :, 1]
-    squares, own = tie((squares, own))
+    far_grad, squares, mixing_grad = tie((far_grad, squares, mixing_grad))
+    stream_grad = gradient.reshape(stream.shape)
+
+    squares = squares + sum_squares(far_grad)
     squares = lax.all_to_all(
         jnp.broadcast_to(squares, (devices, 128)),
         ("dp", "seq"),
@@ -1549,26 +1554,27 @@
         concat_axis=0,
         tiled=True,
     )
-    normed_grad = travel.done(own)[0]
-    gradient = norm_back(gradient, normed_grad, own_normed, scale)
-    gradient, squares = tie((gradient, squares))
-    stream_grad = gradient.reshape(stream.shape)
+    home = jnp.concatenate([far_grad[:, :units], far_grad[:, 2 * units + width :]], -1)
+    home = SeqSwap(home.reshape(parts, rows_d, units + 3 * width))
+    output_grad = jnp.stack(
+        [far_grad[:, 2 * units : 2 * units + width], later_first[:, 2 * units :]]
+    ).reshape(LAYERS, rows_d, D)
+    shrink_grad = jnp.stack(
+        [far_grad[:, units : 2 * units], later_first[:, units : 2 * units]]
+    ).reshape(LAYERS, rows_f, D)
+    squares, output_grad, shrink_grad = home.hold(squares, output_grad, shrink_grad)
+    home = home.done()
+    expand_grad = jnp.stack([home[..., :units], later_home.done()])
+    later_mixing = home[..., units:]
     gradient_norm = jnp.sqrt(jnp.sum(squares[:, 0]))
     clip_scale = jnp.minimum(1.0, CLIP_LIMIT / (gradient_norm + 1e-06))
-    output_grad = jnp.stack([output_grad, later_first[:, 2 * units :]])
-    output_grad = output_grad.reshape(LAYERS, rows_d, D)
-    shrink_grad = jnp.stack([shrink_grad, later_first[:, units : 2 * units]])
-    shrink_grad = shrink_grad.reshape(LAYERS, rows_f, D)
     mixing_grad = jnp.stack([mixing_grad, later_mixing])
-    expand_grad = jnp.stack([expand_grad, later_expand])
-    exchanged = jnp.concatenate([mixing_grad, expand_grad], -1)
     if not aligned:
-        mixing_view = exchanged[..., : 3 * width].reshape(LAYERS, parts, rows_d, halves, 3, 128)
-        mixing_view = mixing_view.transpose(0, 2, 4, 1, 3, 5).reshape(LAYERS, rows_d, 3 * D)
-        expand_view = exchanged[..., 3 * width :].reshape(LAYERS, parts, rows_d, copies, rows_f)
-        expand_view = expand_view.transpose(0, 2, 3, 1, 4).reshape(LAYERS, rows_d, FF)
-        exchanged = jnp.concatenate([mixing_view, expand_view], -1)[:, None]
-        spans = ([(0, 0, 0, 3 * D)], [(0, 3 * D, 0, FF)])
+        mixing_grad = mixing_grad.reshape(LAYERS, parts, rows_d, halves, 3, 128)
+        mixing_grad = mixing_grad.transpose(0, 2, 4, 1, 3, 5).reshape(LAYERS, 1, rows_d, 3 * D)
+        expand_grad = expand_grad.reshape(LAYERS, parts, rows_d, copies, rows_f)
+        expand_grad = expand_grad.transpose(0, 2, 3, 1, 4).reshape(LAYERS, 1, rows_d, FF)
+        spans = ([(0, 0, 0, 3 * D)], [(0, 0, 0, FF)])
     states = (
         (mixing_weight, mixing_first, mixing_second, mixing_average)
         + (output_weight, output_first, output_second, output_average)
@@ -1577,7 +1583,7 @@
     )
     rates = (D ** (-0.5), (D * 32 // LEN) ** (-0.5), D ** (-0.5), FF ** (-0.5))
     updated = update(
-        clip_scale.reshape(1), exchanged, output_grad, shrink_grad, states, spans, rates
+        clip_scale.reshape(1), mixing_grad, expand_grad, output_grad, shrink_grad, states, spans, rates
     )
     affine_new = adam(
         affine_grad * clip_scale,

time: 737 us -> 712 us (0.966)
  waiting for transfers between devices: 101 us -> 140 us
  Pallas kernels: 377 us -> 351 us
  other arithmetic: 71.7 us -> 54.3 us
  starting transfers between devices: 97 us -> 85.1 us
    pallas_call x5 -> x3, Pallas kernels: 42.5 us -> 23 us  [weight_grad(): pl.pallas_call(partial(weight_grad_kernel, len(lows)), grid=(D // ROWS,),...]
    all_to_all x3 -> x2, waiting for transfers between devices: 2.07 us -> 19.6 us  [sum_exchange(): lax.all_to_all(value, ('dp', 'seq'), split_axis=0, concat_axis=0, tiled=T...]
    ppermute x16 -> x12, waiting for transfers between devices: 36.1 us -> 18.6 us  [inner_ring(): return lax.ppermute(value, 'dp', moves)]
    ppermute x8, waiting for transfers between devices: 26.1 us -> 39.2 us  [chip_ring(): lax.ppermute(value, 'seq', [(i, (i + 2) % size) for i in range(size)])]
    ppermute x12 -> x9, waiting for transfers between devices: 12 us -> 23.6 us  [outer_ring(): lax.ppermute(value, 'dp', [(i, (i + inner) % size) for i in range(size)])]
    all_to_all x3 -> x2, starting transfers between devices: 17.4 us -> 6.51 us  [sum_exchange(): lax.all_to_all(value, ('dp', 'seq'), split_axis=0, concat_axis=0, tiled=T...]
    ppermute x12 -> x9, starting transfers between devices: 14.9 us -> 25.5 us  [outer_ring(): lax.ppermute(value, 'dp', [(i, (i + inner) % size) for i in range(size)])]
    ppermute x16 -> x12, starting transfers between devices: 21.9 us -> 12.8 us  [inner_ring(): return lax.ppermute(value, 'dp', moves)]
  transfers between devices with their start and end apart: 71 -> 68, of which waited for: 26 -> 29; matrix products, arithmetic and copies ran while one was open for 16% -> 12% of each run, Pallas kernels for 40% -> 46%
where the time goes in v5:
time: 712 us; the launch traced here: 702 us
  Pallas kernels  351 us (49%)
  waiting for transfers between devices  140 us (20%)
  starting transfers between devices  85.1 us (12%)
  other arithmetic  54.3 us (8%)
  local copies, waits for them, and re-layouts  46.3 us (7%)
  between operations  20.9 us (3%)
    pallas_call x4, Pallas kernels, attend_back(): pl.pallas_call(attend_back_kernel, grid=(length // block,), in_specs=[pl....  80.5 us
    pallas_call x2, Pallas kernels, feed_back(): pl.pallas_call(partial(feed_back_kernel, joined, 9 + len(kept)), grid=(le...  49.8 us
    pallas_call x4, Pallas kernels, attend(): pl.pallas_call(attend_kernel, grid=(length // block,), in_specs=[pl.Block...  46.3 us
    pallas_call x3, Pallas kernels, feed(): pl.pallas_call(partial(feed_kernel, first is not None, last is not None,...  44.1 us
    ppermute x8, waiting for transfers between devices, chip_ring(): lax.ppermute(value, 'seq', [(i, (i + 2) % size) for i in range(size)])  39.2 us
    pallas_call x4, Pallas kernels, norm_grad(): pl.pallas_call(norm_grad_kernel, grid_spec=pltpu.PrefetchScalarGridSpec(n...  34.9 us
    ppermute x9, starting transfers between devices, outer_ring(): lax.ppermute(value, 'dp', [(i, (i + inner) % size) for i in range(size)])  25.5 us
    pallas_call x3, Pallas kernels, mix(): pl.pallas_call(partial(mix_kernel, count, len(pieces)), grid_spec=pltpu.P...  25.2 us
  transfers between devices with their start and end apart: 68, of which 29 were waited for; matrix products, arithmetic and copies ran while one was open for 12% of the time, Pallas kernels for 46%

profile of v5, /device:TPU:0, one launch (start us, length us, event | category | flops | bytes accessed | tf_op | source)
XLA Modules:
  0.0 702.4 jit_solution(12636304431285013111)
XLA Ops:
  10.8 4.2 all-to-all-start
  41.0 3.9 all-to-all-start.1
  48.3 4.4 all-to-all-done.1
  60.2 9.9 %collective-permute-done.6.refs_15_ = bf16[128,768]{1,0:T(8,128)(2,1)S(1)} collective-permute-done((bf16[128,768]{1,0:T(8,128)(2,1)}, bf16[128,768]{1,0:T(8,128)(2,1)S(1)}, u32[]{:S(2)}, u32[]{:S(2)}) %collective-permute-start.6) | collective-permute-done | bytes 196640 | tf_op jit(solution)/shard_map/ppermute | solution.py:47
  72.2 6.0 collective-permute-done.8.refs_14_
  84.9 11.1 %mix.3 = (bf16[2048,1024]{1,0:T(8,128)(2,1)}, bf16[2048,768]{1,0:T(8,128)(2,1)}, bf16[1024,768]{1,0:T(8,128)(2,1)}, bf16[1024,768]{1,0:T(8,128)(2,1)}, f32[8,768]{1,0:T(8,128)}) custom-call(s32[4]{0:T(128)} %pad_add_fusion.x_slots_ref.slots_ref, s32[8]{0:T(128)} %stack.201.slots_ref, bf16[512,1024]{1,0:T(8,128)(2,1)} %copy-done.16, ...), custom_call_target="tpu_custom_call" | custom-call | flops 1000 | bytes 1000 | tf_op jit(solution)/shard_map/mix/pallas_call | solution.py:336
  97.2 3.7 all-to-all-start.2
  104.3 11.6 %attend.4 = (bf16[2048,128]{1,0:T(8,128)(2,1)}, f32[2,2048]{1,0:T(2,128)}) custom-call(bf16[2048,768]{1,0:T(8,128)(2,1)} %get-tuple-element.580.q_ref.k_ref.v_ref, bf16[2048,768]{1,0:T(8,128)(2,1)} %get-tuple-element.580.q_ref.k_ref.v_ref, bf16[2048,768]{1,0:T(8,128)(2,1)} %get-tuple-element.580.q_ref.k_ref.v_ref), custom_call_target="tpu_custom_call" | custom-call | flops 1000 | bytes 1000 | tf_op jit(solution)/shard_map/attend/pallas_call | solution.py:399
  124.1 11.6 %attend.5 = (bf16[2048,128]{1,0:T(8,128)(2,1)}, f32[2,2048]{1,0:T(2,128)}) custom-call(bf16[2048,768]{1,0:T(8,128)(2,1)} %get-tuple-element.580.q_ref.k_ref.v_ref, bf16[2048,768]{1,0:T(8,128)(2,1)} %get-tuple-element.580.q_ref.k_ref.v_ref, bf16[2048,768]{1,0:T(8,128)(2,1)} %get-tuple-element.580.q_ref.k_ref.v_ref), custom_call_target="tpu_custom_call" | custom-call | flops 1000 | bytes 1000 | tf_op jit(solution)/shard_map/attend/pallas_call | solution.py:399
  137.8 5.0 all-to-all-done.3
  147.8 5.4 assemble.2
  153.2 6.6 collective-permute-done.19.refs_10_
  165.1 16.4 %feed.3 = (bf16[2048,1024]{1,0:T(8,128)(2,1)}, bf16[2048,1024]{1,0:T(8,128)(2,1)}, bf16[1024,1024]{1,0:T(8,128)(2,1)}, f32[8,1024]{1,0:T(8,128)}, bf16[1024,1024...) custom-call(s32[1]{0:T(128)} %bitcast.41.y_ref, s32[8]{0:T(128)} %stack.201.slots_ref, ...), custom_call_target="tpu_custom_call" | custom-call | flops 1000 | bytes 1000 | tf_op jit(solution)/shard_map/feed/pallas_call | solution.py:699
  189.4 15.7 %collective-permute-start.24 = (bf16[128,768]{1,0:T(8,128)(2,1)S(1)}, bf16[128,768]{1,0:T(8,128)(2,1)S(1)}, u32[]{:S(2)}, u32[]{:S(2)}) collective-permute-start(bf16[128,768]{1,0:T(8,128)(2,1)S(1)} %collective-permute-done.20.refs_9_), channel_id=1, source_target_pairs={{0,8},{4,12},{8,16},{12,20},{16,24},{20,28},{24,0},{28,4},{1,9},{5... | collective-permute-start | bytes 589832 | tf_op jit(solution)/shard_map/ppermute | solution.py:47
  205.3 13.0 %feed.4 = (bf16[2048,1024]{1,0:T(8,128)(2,1)}, bf16[2048,1024]{1,0:T(8,128)(2,1)}, bf16[1024,1024]{1,0:T(8,128)(2,1)}) custom-call(s32[1]{0:T(128)} %bitcast.41.y_ref, s32[1]{0:T(128)} %constant.382.clone.1.slots_ref, bf16[2048,1024]{1,0:T(8,128)(2,1)} %get-tuple-element.378.x_ref.refs_4_, ...), custom_call_target="tpu_custom_call", output_to_operand_aliasing={{0}: (9, {}), {1}: (10, {})} | custom-call | flops 1000 | bytes 1000 | tf_op jit(solution)/shard_map/feed/pallas_call | solution.py:699
  220.3 10.0 %collective-permute-done.26.refs_13_ = bf16[128,768]{1,0:T(8,128)(2,1)S(1)} collective-permute-done((bf16[128,768]{1,0:T(8,128)(2,1)S(1)}, bf16[128,768]{1,0:T(8,128)(2,1)S(1)}, u32[]{:S(2)}, u32[]{:S(2)}) %collective-permute-start.26) | collective-permute-done | bytes 196640 | tf_op jit(solution)/shard_map/ppermute | solution.py:47
  246.0 7.7 %mix.4 = (bf16[2048,1024]{1,0:T(8,128)(2,1)}, bf16[2048,768]{1,0:T(8,128)(2,1)}, bf16[1024,768]{1,0:T(8,128)(2,1)}, bf16[1024,768]{1,0:T(8,128)(2,1)}, f32[8,768]{1,0:T(8,128)}) custom-call(s32[2]{0:T(128)} %pad_add_fusion.2.x_slots_ref, s32[8]{0:T(128)} %stack.201.slots_ref, bf16[512,1024]{1,0:T(8,128)(2,1)} %copy-done.17, ...), custom_call_target="tpu_custom_call" | custom-call | flops 1000 | bytes 1000 | tf_op jit(solution)/shard_map/mix/pallas_call | solution.py:336
  253.7 9.2 %collective-permute-done.31.refs_0_ = bf16[512,1024]{1,0:T(8,128)(2,1)} collective-permute-done((bf16[512,1024]{1,0:T(8,128)(2,1)S(1)}, bf16[512,1024]{1,0:T(8,128)(2,1)}, u32[]{:S(2)}, u32[]{:S(2)}) %collective-permute-start.31) | collective-permute-done | bytes 1048608 | tf_op jit(solution)/shard_map/ppermute | solution.py:60
  266.7 6.4 mix.5
  273.1 11.6 %attend.6 = (bf16[2048,128]{1,0:T(8,128)(2,1)}, f32[2,2048]{1,0:T(2,128)}) custom-call(bf16[2048,768]{1,0:T(8,128)(2,1)} %get-tuple-element.478.q_ref.k_ref.v_ref, bf16[2048,768]{1,0:T(8,128)(2,1)} %get-tuple-element.478.q_ref.k_ref.v_ref, bf16[2048,768]{1,0:T(8,128)(2,1)} %get-tuple-element.478.q_ref.k_ref.v_ref), custom_call_target="tpu_custom_call" | custom-call | flops 1000 | bytes 1000 | tf_op jit(solution)/shard_map/attend/pallas_call | solution.py:399
  284.7 11.6 %attend.7 = (bf16[2048,128]{1,0:T(8,128)(2,1)}, f32[2,2048]{1,0:T(2,128)}) custom-call(bf16[2048,768]{1,0:T(8,128)(2,1)} %get-tuple-element.478.q_ref.k_ref.v_ref, bf16[2048,768]{1,0:T(8,128)(2,1)} %get-tuple-element.478.q_ref.k_ref.v_ref, bf16[2048,768]{1,0:T(8,128)(2,1)} %get-tuple-element.478.q_ref.k_ref.v_ref), custom_call_target="tpu_custom_call" | custom-call | flops 1000 | bytes 1000 | tf_op jit(solution)/shard_map/attend/pallas_call | solution.py:399
  296.3 14.7 %feed.5 = (bf16[2048,1024]{1,0:T(8,128)(2,1)}, bf16[2048,1024]{1,0:T(8,128)(2,1)}, bf16[1024,1024]{1,0:T(8,128)(2,1)}, f32[8,1024]{1,0:T(8,128)}) custom-call(s32[1]{0:T(128)} %bitcast.41.y_ref, s32[1]{0:T(128)} %constant.382.clone.1.slots_ref, bf16[2048,1024]{1,0:T(8,128)(2,1)} %get-tuple-element.476.x_ref.refs_4_, f32[1,1024]{1,0:T(1,128)} %get-tuple-element.720, ...), custom_call_target="tpu_custom_call" | custom-call | flops 1000 | bytes 1000 | tf_op jit(solution)/shard_map/feed/pallas_call | solution.py:699
  311.0 4.1 product.2
  319.0 25.0 %feed_back.2 = (bf16[2048,1024]{1,0:T(8,128)(2,1)}, f32[1,1024]{1,0:T(1,128)}, bf16[2048,256]{1,0:T(8,128)(2,1)}, f32[1,1024]{1,0:T(1,128)}, f32[1,1024]{1,0:T(1,128)}, /*index=5*/bf16[1024,2304]{1,0:T(8,128)(2,1)}) custom-call(bf16[2048,1024]{1,0:T(8,128)(2,1)} %bitcast.253, ...), custom_call_target="tpu_custom_call" | custom-call | flops 1000 | bytes 1000 | tf_op jit(solution)/shard_map/feed_back/pallas_call | solution.py:950
  345.5 20.4 %attend_back.4 = (bf16[2048,384]{1,0:T(8,128)(2,1)}, f32[1,384]{1,0:T(1,128)}) custom-call(bf16[2048,768]{1,0:T(8,128)(2,1)} %get-tuple-element.478.q_ref.k_ref.v_ref, bf16[2048,768]{1,0:T(8,128)(2,1)} %get-tuple-element.478.q_ref.k_ref.v_ref, bf16[2048,768]{1,0:T(8,128)(2,1)} %get-tuple-element.478.q_ref.k_ref.v_ref, ...), custom_call_target="tpu_custom_call" | custom-call | flops 1000 | bytes 1000 | tf_op jit(solution)/shard_map/attend_back/pallas_call | solution.py:528
  365.9 20.0 %attend_back.5 = (bf16[2048,384]{1,0:T(8,128)(2,1)}, f32[1,384]{1,0:T(1,128)}) custom-call(bf16[2048,768]{1,0:T(8,128)(2,1)} %get-tuple-element.478.q_ref.k_ref.v_ref, bf16[2048,768]{1,0:T(8,128)(2,1)} %get-tuple-element.478.q_ref.k_ref.v_ref, bf16[2048,768]{1,0:T(8,128)(2,1)} %get-tuple-element.478.q_ref.k_ref.v_ref, ...), custom_call_target="tpu_custom_call" | custom-call | flops 1000 | bytes 1000 | tf_op jit(solution)/shard_map/attend_back/pallas_call | solution.py:528
  385.9 8.7 %norm_grad.4 = bf16[1024,1024]{1,0:T(8,128)(2,1)} custom-call(s32[1]{0:T(128)} %bitcast.41.y_ref, bf16[2048,1024]{1,0:T(8,128)(2,1)} %get-tuple-element.523.h_ref, bf16[1024,1024]{1,0:T(8,128)(2,1)} %get-tuple-element.521.wi_ref, bf16[1024,768]{1,0:T(8,128)(2,1)} %get-tuple-element.472.refs_4_.wm_ref, bf16[2048,384]{1,0:T(8,128)(2,1)} %get-tuple-element.532.refs_0_, ...), custom_call_target="tpu_custom_call" | custom-call | flops 1000 | bytes 1000 | tf_op jit(solution)/shard_map/norm_grad/pallas_call | solution.py:763
  400.4 7.0 branch.2
  407.4 7.0 branch.3
  414.4 9.1 %norm_grad.5 = bf16[1024,1024]{1,0:T(8,128)(2,1)} custom-call(s32[1]{0:T(128)} %bitcast.41.y_ref, bf16[2048,1024]{1,0:T(8,128)(2,1)} %get-tuple-element.523.h_ref, bf16[1024,1024]{1,0:T(8,128)(2,1)} %get-tuple-element.521.wi_ref, bf16[1024,768]{1,0:T(8,128)(2,1)} %get-tuple-element.472.refs_4_.wm_ref, bf16[2048,384]{1,0:T(8,128)(2,1)} %get-tuple-element.532.refs_0_, ...), custom_call_target="tpu_custom_call" | custom-call | flops 1000 | bytes 1000 | tf_op jit(solution)/shard_map/norm_grad/pallas_call | solution.py:763
  436.3 9.1 %weight_grad.3 = (bf16[1024,3072]{1,0:T(8,128)(2,1)}, f32[1,1024]{1,0:T(1,128)}, f32[1,1024]{1,0:T(1,128)}) custom-call(bf16[2048,1024]{1,0:T(8,128)(2,1)} %get-tuple-element.476.x_ref.refs_4_, bf16[1024,768]{1,0:T(8,128)(2,1)} %get-tuple-element.477.weight_ref, f32[1,1024]{1,0:T(1,128)} %get-tuple-element.722, f32[1,1024]{1,0:T(1,128)} %get-tuple-element.721, ...), custom_call_target="tpu_custom_call" | custom-call | flops 1000 | bytes 1000 | tf_op jit(solution)/shard_map/weight_grad/pallas_call | solution.py:824
  445.4 14.6 %collective-permute-done.39.refs_2_ = bf16[512,1024]{1,0:T(8,128)(2,1)} collective-permute-done((bf16[512,1024]{1,0:T(8,128)(2,1)S(1)}, bf16[512,1024]{1,0:T(8,128)(2,1)}, u32[]{:S(2)}, u32[]{:S(2)}) %collective-permute-start.39) | collective-permute-done | bytes 1048608 | tf_op jit(solution)/shard_map/ppermute | solution.py:60
  460.5 3.6 collective-permute-done.40.refs_1_
  465.1 5.4 assemble.3
  470.5 4.1 product.3
  477.9 24.8 %feed_back.3 = (bf16[2048,1024]{1,0:T(8,128)(2,1)}, f32[1,1024]{1,0:T(1,128)}, bf16[2048,256]{1,0:T(8,128)(2,1)}, f32[1,1024]{1,0:T(1,128)}, f32[1,1024]{1,0:T(1,128)}, /*index=5*/bf16[1024,3072]{1,0:T(8,128)(2,1)}) custom-call(bf16[2048,1024]{1,0:T(8,128)(2,1)} %bitcast.251, ...), custom_call_target="tpu_custom_call", output_to_operand_aliasing={{5}: (9, {})} | custom-call | flops 1000 | bytes 1000 | tf_op jit(solution)/shard_map/feed_back/pallas_call | solution.py:950
  509.8 20.0 %attend_back.6 = (bf16[2048,384]{1,0:T(8,128)(2,1)}, f32[1,384]{1,0:T(1,128)}) custom-call(bf16[2048,768]{1,0:T(8,128)(2,1)} %get-tuple-element.580.q_ref.k_ref.v_ref, bf16[2048,768]{1,0:T(8,128)(2,1)} %get-tuple-element.580.q_ref.k_ref.v_ref, bf16[2048,768]{1,0:T(8,128)(2,1)} %get-tuple-element.580.q_ref.k_ref.v_ref, ...), custom_call_target="tpu_custom_call" | custom-call | flops 1000 | bytes 1000 | tf_op jit(solution)/shard_map/attend_back/pallas_call | solution.py:528
  530.8 6.8 weight_grad.4
  546.4 20.0 %attend_back.7 = (bf16[2048,384]{1,0:T(8,128)(2,1)}, f32[1,384]{1,0:T(1,128)}) custom-call(bf16[2048,768]{1,0:T(8,128)(2,1)} %get-tuple-element.580.q_ref.k_ref.v_ref, bf16[2048,768]{1,0:T(8,128)(2,1)} %get-tuple-element.580.q_ref.k_ref.v_ref, bf16[2048,768]{1,0:T(8,128)(2,1)} %get-tuple-element.580.q_ref.k_ref.v_ref, ...), custom_call_target="tpu_custom_call" | custom-call | flops 1000 | bytes 1000 | tf_op jit(solution)/shard_map/attend_back/pallas_call | solution.py:528
  567.3 7.1 %weight_grad.5 = (bf16[1024,384]{1,0:T(8,128)(2,1)}, f32[1,1024]{1,0:T(1,128)}, f32[1,1024]{1,0:T(1,128)}) custom-call(bf16[2048,1024]{1,0:T(8,128)(2,1)} %get-tuple-element.378.x_ref.refs_4_, bf16[1024,768]{1,0:T(8,128)(2,1)} %get-tuple-element.379.weight_ref, f32[1,1024]{1,0:T(1,128)} %get-tuple-element.728, f32[1,1024]{1,0:T(1,128)} %get-tuple-element.727, ...), custom_call_target="tpu_custom_call" | custom-call | flops 1000 | bytes 1000 | tf_op jit(solution)/shard_map/weight_grad/pallas_call | solution.py:824
  579.2 4.9 all-to-all-done.4
  584.1 8.6 %norm_grad.6 = bf16[1024,1024]{1,0:T(8,128)(2,1)} custom-call(s32[1]{0:T(128)} %bitcast.41.y_ref, bf16[2048,1024]{1,0:T(8,128)(2,1)} %get-tuple-element.600.h_ref, bf16[1024,1024]{1,0:T(8,128)(2,1)} %get-tuple-element.440.refs_0_.wi_ref, bf16[1024,768]{1,0:T(8,128)(2,1)} %get-tuple-element.601.wm_ref, bf16[2048,384]{1,0:T(8,128)(2,1)} %get-tuple-element.603.refs_0_, ...), custom_call_target="tpu_custom_call" | custom-call | flops 1000 | bytes 1000 | tf_op jit(solution)/shard_map/norm_grad/pallas_call | solution.py:763
  604.6 3.6 all-to-all-start.5
  608.3 8.6 %norm_grad.7 = bf16[1024,1024]{1,0:T(8,128)(2,1)} custom-call(s32[1]{0:T(128)} %bitcast.41.y_ref, bf16[2048,1024]{1,0:T(8,128)(2,1)} %get-tuple-element.600.h_ref, bf16[1024,1024]{1,0:T(8,128)(2,1)} %get-tuple-element.440.refs_0_.wi_ref, bf16[1024,768]{1,0:T(8,128)(2,1)} %get-tuple-element.601.wm_ref, bf16[2048,384]{1,0:T(8,128)(2,1)} %get-tuple-element.603.refs_0_, ...), custom_call_target="tpu_custom_call" | custom-call | flops 1000 | bytes 1000 | tf_op jit(solution)/shard_map/norm_grad/pallas_call | solution.py:763
  616.8 13.9 %collective-permute-done.51 = bf16[512,1024]{1,0:T(8,128)(2,1)} collective-permute-done((bf16[512,1024]{1,0:T(8,128)(2,1)}, bf16[512,1024]{1,0:T(8,128)(2,1)}, u32[]{:S(2)}, u32[]{:S(2)}) %collective-permute-start.51) | collective-permute-done | bytes 1048608 | tf_op jit(solution)/shard_map/ppermute | solution.py:60
  632.2 3.8 fusion.4
  643.4 14.7 %all-to-all-done.5 = bf16[32,32,512]{2,1,0:T(8,128)(2,1)} async-done(((bf16[32,32,512]{2,1,0:T(8,128)(2,1)}), bf16[32,32,512]{2,1,0:T(8,128)(2,1)}, u32[]{:S(2)}, u32[]{:S(2)}) %all-to-all-start.5) | async-done | bytes 1048608 | tf_op jit(solution)/shard_map/all_to_all | solution.py:185
  683.9 10.5 %update.1 = (f32[2,32,3072]{2,1,0:T(8,128)}, f32[2,32,3072]{2,1,0:T(8,128)}, f32[2,32,3072]{2,1,0:T(8,128)}, f32[2,32,3072]{2,1,0:T(8,128)}, f32[2,32,1024]{2,1,...) custom-call(f32[1]{0:T(128)} %bitcast.140.clip_ref, ...), custom_call_target="tpu_custom_call" | custom-call | flops 1000 | bytes 1000 | tf_op jit(solution)/shard_map/update/pallas_call | solution.py:1041
  (474 shorter events, 196.7 us)
Async XLA Ops:
  10.8 14.2 %all-to-all-start = ((bf16[4,32,1824]{2,1,0:T(8,128)(2,1)}), bf16[4,32,1824]{2,1,0:T(8,128)(2,1)}, u32[]{:S(2)}, u32[]{:S(2)}) async-start(bf16[4,32,1824]{2,1,0:T(8,128)(2,1)} %pack.2), calls=%async_computation | async-start | bytes 983040 | tf_op jit(solution)/shard_map/all_to_all | solution.py:219
  15.0 81.0 %all-gather.3.cloned.1.call-start = ((), (), s32[]{:S(2)}) async-start(), calls=%async_computation.9 | async-start | bytes 1179648 | tf_op jit(solution)/shard_map/all_gather | solution.py:1234
  15.9 40.1 %collective-permute-start.3 = (bf16[512,1024]{1,0:T(8,128)(2,1)S(1)}, bf16[512,1024]{1,0:T(8,128)(2,1)}, u32[]{:S(2)}, u32[]{:S(2)}) collective-permute-start(bf16[512,1024]{1,0:T(8,128)(2,1)S(1)} %fusion.15.refs_0_), channel_id=1, source_target_pairs={{0,2},{1,3},{2,0},{3,1},{4,6},{5,7},{6,4},{7,5},{8,10},{9,11},{10,... | collective-permute-start | bytes 3145736 | tf_op jit(solution)/shard_map/ppermute | solution.py:60
  28.4 10.2 %collective-permute-start = (bf16[128,768]{1,0:T(8,128)(2,1)}, bf16[128,768]{1,0:T(8,128)(2,1)}, u32[]{:S(2)}, u32[]{:S(2)}) collective-permute-start(bf16[128,768]{1,0:T(8,128)(2,1)} %slice.362.refs_9_), channel_id=1, source_target_pairs={{0,8},{4,12},{8,16},{12,20},{16,24},{20,28},{24,0},{28,4},{1,9},{5... | collective-permute-start | bytes 589832 | tf_op jit(solution)/shard_map/ppermute | solution.py:47
  41.0 11.6 %all-to-all-start.1 = ((bf16[32,2,416]{2,1,0:T(2,128)(2,1)}), bf16[32,2,416]{2,1,0:T(2,128)(2,1)S(1)}, u32[]{:S(2)}, u32[]{:S(2)}) async-start(bf16[32,2,416]{2,1,0:T(2,128)(2,1)} %reshape.488), calls=%async_computation.1 | async-start | bytes 131072 | tf_op jit(solution)/shard_map/all_to_all | solution.py:1249
  44.9 11.0 %collective-permute-start.1 = (bf16[128,768]{1,0:T(8,128)(2,1)}, bf16[128,768]{1,0:T(8,128)(2,1)}, u32[]{:S(2)}, u32[]{:S(2)}) collective-permute-start(bf16[128,768]{1,0:T(8,128)(2,1)} %collective-permute-done.refs_11_), channel_id=1, source_target_pairs={{0,8},{4,12},{8,16},{12,20},{16,24},{20,28},{24,0},{28,4},{1,9},{5... | collective-permute-start | bytes 589832 | tf_op jit(solution)/shard_map/ppermute | solution.py:47
  57.0 13.1 %collective-permute-start.4 = (bf16[512,1024]{1,0:T(8,128)(2,1)S(1)}, bf16[512,1024]{1,0:T(8,128)(2,1)S(1)}, u32[]{:S(2)}, u32[]{:S(2)}) collective-permute-start(bf16[512,1024]{1,0:T(8,128)(2,1)S(1)} %fusion.15.refs_0_), channel_id=1, source_target_pairs={{0,1},{1,0},{2,3},{3,2},{4,5},{5,4},{6,7},{7,6},{8,9},{9,8},{10,11... | collective-permute-start | bytes 3145736 | tf_op jit(solution)/shard_map/ppermute | solution.py:65
  57.0 13.1 %collective-permute-start.5 = (bf16[512,1024]{1,0:T(8,128)(2,1)}, bf16[512,1024]{1,0:T(8,128)(2,1)S(1)}, u32[]{:S(2)}, u32[]{:S(2)}) collective-permute-start(bf16[512,1024]{1,0:T(8,128)(2,1)} %collective-permute-done.3.refs_2_), channel_id=1, source_target_pairs={{0,1},{1,0},{2,3},{3,2},{4,5},{5,4},{6,7},{7,6},{8,9},{9,8},{10,11... | collective-permute-start | bytes 3145736 | tf_op jit(solution)/shard_map/ppermute | solution.py:65
  57.5 12.6 %collective-permute-start.6 = (bf16[128,768]{1,0:T(8,128)(2,1)}, bf16[128,768]{1,0:T(8,128)(2,1)S(1)}, u32[]{:S(2)}, u32[]{:S(2)}) collective-permute-start(bf16[128,768]{1,0:T(8,128)(2,1)} %collective-permute-done.1.refs_13_), channel_id=1, source_target_pairs={{0,8},{4,12},{8,16},{12,20},{16,24},{20,28},{24,0},{28,4},{1,9},{5... | collective-permute-start | bytes 589832 | tf_op jit(solution)/shard_map/ppermute | solution.py:47
  57.5 12.6 %collective-permute-start.7 = (bf16[128,768]{1,0:T(8,128)(2,1)}, bf16[128,768]{1,0:T(8,128)(2,1)S(1)}, u32[]{:S(2)}, u32[]{:S(2)}) collective-permute-start(bf16[128,768]{1,0:T(8,128)(2,1)} %collective-permute-done.refs_11_), channel_id=1, source_target_pairs={{0,4},{4,0},{8,12},{12,8},{16,20},{20,16},{24,28},{28,24},{1,5},{5... | collective-permute-start | bytes 589832 | tf_op jit(solution)/shard_map/ppermute | solution.py:55
  81.1 14.9 %collective-permute-start.10 = (bf16[128,2048]{1,0:T(8,128)(2,1)S(1)}, bf16[128,2048]{1,0:T(8,128)(2,1)}, u32[]{:S(2)}, u32[]{:S(2)}) collective-permute-start(bf16[128,2048]{1,0:T(8,128)(2,1)S(1)} %pad_maximum_fusion.3.refs_3_), channel_id=1, source_target_pairs={{0,8},{4,12},{8,16},{12,20},{16,24},{20,28},{24,0},{28,4},{1,9},{5... | collective-permute-start | bytes 1572872 | tf_op jit(solution)/shard_map/ppermute | solution.py:47
  81.2 14.9 %collective-permute-start.11 = (bf16[128,2048]{1,0:T(8,128)(2,1)S(1)}, bf16[128,2048]{1,0:T(8,128)(2,1)S(1)}, u32[]{:S(2)}, u32[]{:S(2)}) collective-permute-start(bf16[128,2048]{1,0:T(8,128)(2,1)S(1)} %pad_maximum_fusion.3.refs_3_), channel_id=1, source_target_pairs={{0,4},{4,0},{8,12},{12,8},{16,20},{20,16},{24,28},{28,24},{1,5},{5... | collective-permute-start | bytes 1572872 | tf_op jit(solution)/shard_map/ppermute | solution.py:55
  96.0 21.6 %collective-permute-start.12 = (bf16[128,2048]{1,0:T(8,128)(2,1)}, bf16[128,2048]{1,0:T(8,128)(2,1)}, u32[]{:S(2)}, u32[]{:S(2)}) collective-permute-start(bf16[128,2048]{1,0:T(8,128)(2,1)} %collective-permute-done.10.refs_5_), channel_id=1, source_target_pairs={{0,8},{4,12},{8,16},{12,20},{16,24},{20,28},{24,0},{28,4},{1,9},{5... | collective-permute-start | bytes 1572872 | tf_op jit(solution)/shard_map/ppermute | solution.py:47
  96.6 21.0 %collective-permute-start.13 = (bf16[128,2048]{1,0:T(8,128)(2,1)}, bf16[128,2048]{1,0:T(8,128)(2,1)}, u32[]{:S(2)}, u32[]{:S(2)}) collective-permute-start(bf16[128,2048]{1,0:T(8,128)(2,1)} %collective-permute-done.10.refs_5_), channel_id=1, source_target_pairs={{0,4},{4,0},{8,12},{12,8},{16,20},{20,16},{24,28},{28,24},{1,5},{5... | collective-permute-start | bytes 1572872 | tf_op jit(solution)/shard_map/ppermute | solution.py:55
  97.2 20.4 %all-to-all-start.2 = ((bf16[4,32,1792]{2,1,0:T(8,128)(2,1)}), bf16[4,32,1792]{2,1,0:T(8,128)(2,1)S(1)}, u32[]{:S(2)}, u32[]{:S(2)}) async-start(bf16[4,32,1792]{2,1,0:T(8,128)(2,1)} %pack.3), calls=%async_computation.2 | async-start | bytes 917504 | tf_op jit(solution)/shard_map/all_to_all | solution.py:219
  101.0 36.8 %collective-permute-start.14 = (bf16[512,1024]{1,0:T(8,128)(2,1)S(1)}, bf16[512,1024]{1,0:T(8,128)(2,1)}, u32[]{:S(2)}, u32[]{:S(2)}) collective-permute-start(bf16[512,1024]{1,0:T(8,128)(2,1)S(1)} %get-tuple-element.414.refs_0_), channel_id=1, source_target_pairs={{0,2},{1,3},{2,0},{3,1},{4,6},{5,7},{6,4},{7,5},{8,10},{9,11},{10,... | collective-permute-start | bytes 3145736 | tf_op jit(solution)/shard_map/ppermute | solution.py:60
  117.6 25.2 %all-to-all-start.3 = ((bf16[4,2,64,1024]{3,2,1,0:T(8,128)(2,1)}), bf16[4,2,64,1024]{3,2,1,0:T(8,128)(2,1)S(1)}, u32[]{:S(2)}, u32[]{:S(2)}) async-start(bf16[4,2,64,1024]{3,2,1,0:T(8,128)(2,1)} %pad_maximum_fusion), calls=%async_computation.3 | async-start | bytes 2097152 | tf_op jit(solution)/shard_map/all_to_all | solution.py:219
  121.1 175.2 %all-gather.5.cloned.1.call-start = ((), (), s32[]{:S(2)}) async-start(), calls=%async_computation.10 | async-start | bytes 4718592 | tf_op jit(solution)/shard_map/all_gather | solution.py:1316
  121.2 16.6 %collective-permute-start.15 = (bf16[128,2048]{1,0:T(8,128)(2,1)}, bf16[128,2048]{1,0:T(8,128)(2,1)}, u32[]{:S(2)}, u32[]{:S(2)}) collective-permute-start(bf16[128,2048]{1,0:T(8,128)(2,1)} %collective-permute-done.12.refs_7_), channel_id=1, source_target_pairs={{0,8},{4,12},{8,16},{12,20},{16,24},{20,28},{24,0},{28,4},{1,9},{5... | collective-permute-start | bytes 1572872 | tf_op jit(solution)/shard_map/ppermute | solution.py:47
  123.4 14.3 %collective-permute-start.16 = (bf16[128,2048]{1,0:T(8,128)(2,1)}, bf16[128,2048]{1,0:T(8,128)(2,1)}, u32[]{:S(2)}, u32[]{:S(2)}) collective-permute-start(bf16[128,2048]{1,0:T(8,128)(2,1)} %collective-permute-done.12.refs_7_), channel_id=1, source_target_pairs={{0,4},{4,0},{8,12},{12,8},{16,20},{20,16},{24,28},{28,24},{1,5},{5... | collective-permute-start | bytes 1572872 | tf_op jit(solution)/shard_map/ppermute | solution.py:55
  143.3 16.5 %collective-permute-start.19 = (bf16[128,2048]{1,0:T(8,128)(2,1)}, bf16[128,2048]{1,0:T(8,128)(2,1)}, u32[]{:S(2)}, u32[]{:S(2)}) collective-permute-start(bf16[128,2048]{1,0:T(8,128)(2,1)} %collective-permute-done.15.refs_9_), channel_id=1, source_target_pairs={{0,4},{4,0},{8,12},{12,8},{16,20},{20,16},{24,28},{28,24},{1,5},{5... | collective-permute-start | bytes 1572872 | tf_op jit(solution)/shard_map/ppermute | solution.py:55
  145.3 385.5 %reduce-scatter.3.cloned.1.call-start = ((), (), s32[]{:S(2)}) async-start(), calls=%async_computation.11 | async-start | bytes 5308416 | tf_op jit(solution)/shard_map/reduce_scatter | solution.py:1439
  159.8 21.7 %collective-permute-start.20 = (bf16[128,768]{1,0:T(8,128)(2,1)S(1)}, bf16[128,768]{1,0:T(8,128)(2,1)S(1)}, u32[]{:S(2)}, u32[]{:S(2)}) collective-permute-start(bf16[128,768]{1,0:T(8,128)(2,1)S(1)} %copy-done.30), channel_id=1, source_target_pairs={{0,8},{4,12},{8,16},{12,20},{16,24},{20,28},{24,0},{28,4},{1,9},{5... | collective-permute-start | bytes 589832 | tf_op jit(solution)/shard_map/ppermute | solution.py:47
  162.7 18.8 %collective-permute-start.21 = (bf16[128,768]{1,0:T(8,128)(2,1)S(1)}, bf16[128,768]{1,0:T(8,128)(2,1)S(1)}, u32[]{:S(2)}, u32[]{:S(2)}) collective-permute-start(bf16[128,768]{1,0:T(8,128)(2,1)S(1)} %copy-done.30), channel_id=1, source_target_pairs={{0,4},{4,0},{8,12},{12,8},{16,20},{20,16},{24,28},{28,24},{1,5},{5... | collective-permute-start | bytes 589832 | tf_op jit(solution)/shard_map/ppermute | solution.py:55
  189.4 41.0 %collective-permute-start.23 = (bf16[512,1024]{1,0:T(8,128)(2,1)}, bf16[512,1024]{1,0:T(8,128)(2,1)S(1)}, u32[]{:S(2)}, u32[]{:S(2)}) collective-permute-start(bf16[512,1024]{1,0:T(8,128)(2,1)} %fusion.14), channel_id=1, source_target_pairs={{0,2},{1,3},{2,0},{3,1},{4,6},{5,7},{6,4},{7,5},{8,10},{9,11},{10,... | collective-permute-start | bytes 3145736 | tf_op jit(solution)/shard_map/ppermute | solution.py:60
  189.4 28.9 %collective-permute-start.24 = (bf16[128,768]{1,0:T(8,128)(2,1)S(1)}, bf16[128,768]{1,0:T(8,128)(2,1)S(1)}, u32[]{:S(2)}, u32[]{:S(2)}) collective-permute-start(bf16[128,768]{1,0:T(8,128)(2,1)S(1)} %collective-permute-done.20.refs_9_), channel_id=1, source_target_pairs={{0,8},{4,12},{8,16},{12,20},{16,24},{20,28},{24,0},{28,4},{1,9},{5... | collective-permute-start | bytes 589832 | tf_op jit(solution)/shard_map/ppermute | solution.py:47
  205.0 13.2 %collective-permute-start.25 = (bf16[128,768]{1,0:T(8,128)(2,1)S(1)}, bf16[128,768]{1,0:T(8,128)(2,1)S(1)}, u32[]{:S(2)}, u32[]{:S(2)}) collective-permute-start(bf16[128,768]{1,0:T(8,128)(2,1)S(1)} %collective-permute-done.20.refs_9_), channel_id=1, source_target_pairs={{0,4},{4,0},{8,12},{12,8},{16,20},{20,16},{24,28},{28,24},{1,5},{5... | collective-permute-start | bytes 589832 | tf_op jit(solution)/shard_map/ppermute | solution.py:55
  218.3 12.0 %collective-permute-start.26 = (bf16[128,768]{1,0:T(8,128)(2,1)S(1)}, bf16[128,768]{1,0:T(8,128)(2,1)S(1)}, u32[]{:S(2)}, u32[]{:S(2)}) collective-permute-start(bf16[128,768]{1,0:T(8,128)(2,1)S(1)} %collective-permute-done.24.refs_11_), channel_id=1, source_target_pairs={{0,8},{4,12},{8,16},{12,20},{16,24},{20,28},{24,0},{28,4},{1,9},{5... | collective-permute-start | bytes 589832 | tf_op jit(solution)/shard_map/ppermute | solution.py:47
  218.4 11.9 %collective-permute-start.27 = (bf16[128,768]{1,0:T(8,128)(2,1)S(1)}, bf16[128,768]{1,0:T(8,128)(2,1)S(1)}, u32[]{:S(2)}, u32[]{:S(2)}) collective-permute-start(bf16[128,768]{1,0:T(8,128)(2,1)S(1)} %collective-permute-done.24.refs_11_), channel_id=1, source_target_pairs={{0,4},{4,0},{8,12},{12,8},{16,20},{20,16},{24,28},{28,24},{1,5},{5... | collective-permute-start | bytes 589832 | tf_op jit(solution)/shard_map/ppermute | solution.py:55
  237.4 25.5 %collective-permute-start.31 = (bf16[512,1024]{1,0:T(8,128)(2,1)S(1)}, bf16[512,1024]{1,0:T(8,128)(2,1)}, u32[]{:S(2)}, u32[]{:S(2)}) collective-permute-start(bf16[512,1024]{1,0:T(8,128)(2,1)S(1)} %fusion.16.refs_0_), channel_id=1, source_target_pairs={{0,2},{1,3},{2,0},{3,1},{4,6},{5,7},{6,4},{7,5},{8,10},{9,11},{10,... | collective-permute-start | bytes 3145736 | tf_op jit(solution)/shard_map/ppermute | solution.py:60
  316.3 27.8 %collective-permute-start.33 = (bf16[64,1024]{1,0:T(8,128)(2,1)S(1)}, bf16[64,1024]{1,0:T(8,128)(2,1)S(1)}, u32[]{:S(2)}, u32[]{:S(2)}) collective-permute-start(bf16[64,1024]{1,0:T(8,128)(2,1)S(1)} %bitcast.302), channel_id=1, source_target_pairs={{0,1},{1,0},{2,3},{3,2},{4,5},{5,4},{6,7},{7,6},{8,9},{9,8},{10,11... | collective-permute-start | bytes 393224 | tf_op jit(solution)/shard_map/ppermute | solution.py:205
  316.5 27.5 %collective-permute-start.34 = (bf16[64,1024]{1,0:T(8,128)(2,1)S(1)}, bf16[64,1024]{1,0:T(8,128)(2,1)S(1)}, u32[]{:S(2)}, u32[]{:S(2)}) collective-permute-start(bf16[64,1024]{1,0:T(8,128)(2,1)S(1)} %bitcast.301), channel_id=1, source_target_pairs={{0,2},{1,3},{2,0},{3,1},{4,6},{5,7},{6,4},{7,5},{8,10},{9,11},{10,... | collective-permute-start | bytes 393224 | tf_op jit(solution)/shard_map/ppermute | solution.py:205
  317.5 26.5 %collective-permute-start.35 = (bf16[64,1024]{1,0:T(8,128)(2,1)S(1)}, bf16[64,1024]{1,0:T(8,128)(2,1)S(1)}, u32[]{:S(2)}, u32[]{:S(2)}) collective-permute-start(bf16[64,1024]{1,0:T(8,128)(2,1)S(1)} %bitcast.300), channel_id=1, source_target_pairs={{0,3},{1,2},{2,1},{3,0},{4,7},{5,6},{6,5},{7,4},{8,11},{9,10},{10,... | collective-permute-start | bytes 393224 | tf_op jit(solution)/shard_map/ppermute | solution.py:205
  345.4 319.3 %reduce-scatter.5.cloned.1.call-start = ((), (), s32[]{:S(2)}) async-start(), calls=%async_computation.12 | async-start | bytes 7077888 | tf_op jit(solution)/shard_map/reduce_scatter | solution.py:1487
  399.4 25.6 %collective-permute-start.37 = (bf16[512,1024]{1,0:T(8,128)(2,1)S(1)}, bf16[512,1024]{1,0:T(8,128)(2,1)}, u32[]{:S(2)}, u32[]{:S(2)}) collective-permute-start(bf16[512,1024]{1,0:T(8,128)(2,1)S(1)} %fusion.9), channel_id=1, source_target_pairs={{0,2},{1,3},{2,0},{3,1},{4,6},{5,7},{6,4},{7,5},{8,10},{9,11},{10,... | collective-permute-start | bytes 3145736 | tf_op jit(solution)/shard_map/ppermute | solution.py:60
  434.6 25.4 %collective-permute-start.39 = (bf16[512,1024]{1,0:T(8,128)(2,1)S(1)}, bf16[512,1024]{1,0:T(8,128)(2,1)}, u32[]{:S(2)}, u32[]{:S(2)}) collective-permute-start(bf16[512,1024]{1,0:T(8,128)(2,1)S(1)} %convert_element_type.228.refs_0_), channel_id=1, source_target_pairs={{0,2},{1,3},{2,0},{3,1},{4,6},{5,7},{6,4},{7,5},{8,10},{9,11},{10,... | collective-permute-start | bytes 3145736 | tf_op jit(solution)/shard_map/ppermute | solution.py:60
  475.7 26.9 %collective-permute-start.42 = (bf16[64,1024]{1,0:T(8,128)(2,1)S(1)}, bf16[64,1024]{1,0:T(8,128)(2,1)S(1)}, u32[]{:S(2)}, u32[]{:S(2)}) collective-permute-start(bf16[64,1024]{1,0:T(8,128)(2,1)S(1)} %bitcast.299), channel_id=1, source_target_pairs={{0,1},{1,0},{2,3},{3,2},{4,5},{5,4},{6,7},{7,6},{8,9},{9,8},{10,11... | collective-permute-start | bytes 393224 | tf_op jit(solution)/shard_map/ppermute | solution.py:205
  475.8 26.8 %collective-permute-start.43 = (bf16[64,1024]{1,0:T(8,128)(2,1)S(1)}, bf16[64,1024]{1,0:T(8,128)(2,1)S(1)}, u32[]{:S(2)}, u32[]{:S(2)}) collective-permute-start(bf16[64,1024]{1,0:T(8,128)(2,1)S(1)} %bitcast.298), channel_id=1, source_target_pairs={{0,2},{1,3},{2,0},{3,1},{4,6},{5,7},{6,4},{7,5},{8,10},{9,11},{10,... | collective-permute-start | bytes 393224 | tf_op jit(solution)/shard_map/ppermute | solution.py:205
  476.9 25.8 %collective-permute-start.44 = (bf16[64,1024]{1,0:T(8,128)(2,1)S(1)}, bf16[64,1024]{1,0:T(8,128)(2,1)S(1)}, u32[]{:S(2)}, u32[]{:S(2)}) collective-permute-start(bf16[64,1024]{1,0:T(8,128)(2,1)S(1)} %bitcast.297), channel_id=1, source_target_pairs={{0,3},{1,2},{2,1},{3,0},{4,7},{5,6},{6,5},{7,4},{8,11},{9,10},{10,... | collective-permute-start | bytes 393224 | tf_op jit(solution)/shard_map/ppermute | solution.py:205
  508.7 31.3 %collective-permute-start.46 = (bf16[512,1024]{1,0:T(8,128)(2,1)S(1)}, bf16[512,1024]{1,0:T(8,128)(2,1)}, u32[]{:S(2)}, u32[]{:S(2)}) collective-permute-start(bf16[512,1024]{1,0:T(8,128)(2,1)S(1)} %fusion.7), channel_id=1, source_target_pairs={{0,2},{1,3},{2,0},{3,1},{4,6},{5,7},{6,4},{7,5},{8,10},{9,11},{10,... | collective-permute-start | bytes 3145736 | tf_op jit(solution)/shard_map/ppermute | solution.py:60
  540.0 44.2 %all-to-all-start.4 = ((bf16[32,32,512]{2,1,0:T(8,128)(2,1)}), bf16[32,32,512]{2,1,0:T(8,128)(2,1)S(1)}, u32[]{:S(2)}, u32[]{:S(2)}) async-start(bf16[32,32,512]{2,1,0:T(8,128)(2,1)} %bitcast.275), calls=%async_computation.5 | async-start | bytes 2097152 | tf_op jit(solution)/shard_map/all_to_all | solution.py:185
  544.4 22.8 %collective-permute-start.47 = (bf16[32,1024]{1,0:T(8,128)(2,1)}, bf16[32,1024]{1,0:T(8,128)(2,1)S(1)}, u32[]{:S(2)}, u32[]{:S(2)}) collective-permute-start(bf16[32,1024]{1,0:T(8,128)(2,1)} %get-tuple-element.681), channel_id=1, source_target_pairs={{0,1},{1,0},{2,3},{3,2},{4,5},{5,4},{6,7},{7,6},{8,9},{9,8},{10,11... | collective-permute-start | bytes 196616 | tf_op jit(solution)/shard_map/ppermute | solution.py:205
  544.6 22.7 %collective-permute-start.48 = (bf16[32,1024]{1,0:T(8,128)(2,1)}, bf16[32,1024]{1,0:T(8,128)(2,1)S(1)}, u32[]{:S(2)}, u32[]{:S(2)}) collective-permute-start(bf16[32,1024]{1,0:T(8,128)(2,1)} %get-tuple-element.682), channel_id=1, source_target_pairs={{0,2},{1,3},{2,0},{3,1},{4,6},{5,7},{6,4},{7,5},{8,10},{9,11},{10,... | collective-permute-start | bytes 196616 | tf_op jit(solution)/shard_map/ppermute | solution.py:205
  546.2 21.0 %collective-permute-start.49 = (bf16[32,1024]{1,0:T(8,128)(2,1)S(1)}, bf16[32,1024]{1,0:T(8,128)(2,1)S(1)}, u32[]{:S(2)}, u32[]{:S(2)}) collective-permute-start(bf16[32,1024]{1,0:T(8,128)(2,1)S(1)} %get-tuple-element.680), channel_id=1, source_target_pairs={{0,3},{1,2},{2,1},{3,0},{4,7},{5,6},{6,5},{7,4},{8,11},{9,10},{10,... | collective-permute-start | bytes 196616 | tf_op jit(solution)/shard_map/ppermute | solution.py:205
  598.2 32.5 %collective-permute-start.51 = (bf16[512,1024]{1,0:T(8,128)(2,1)}, bf16[512,1024]{1,0:T(8,128)(2,1)}, u32[]{:S(2)}, u32[]{:S(2)}) collective-permute-start(bf16[512,1024]{1,0:T(8,128)(2,1)} %fusion.6), channel_id=1, source_target_pairs={{0,2},{1,3},{2,0},{3,1},{4,6},{5,7},{6,4},{7,5},{8,10},{9,11},{10,... | collective-permute-start | bytes 3145736 | tf_op jit(solution)/shard_map/ppermute | solution.py:60
  600.8 31.4 %collective-permute-start.53 = (bf16[512,1024]{1,0:T(8,128)(2,1)}, bf16[512,1024]{1,0:T(8,128)(2,1)}, u32[]{:S(2)}, u32[]{:S(2)}) collective-permute-start(bf16[512,1024]{1,0:T(8,128)(2,1)} %dynamic-slice_bitcast_fusion), channel_id=1, source_target_pairs={{0,1},{1,0},{2,3},{3,2},{4,5},{5,4},{6,7},{7,6},{8,9},{9,8},{10,11... | collective-permute-start | bytes 3145736 | tf_op jit(solution)/shard_map/ppermute | solution.py:65
  604.6 53.5 %all-to-all-start.5 = ((bf16[32,32,512]{2,1,0:T(8,128)(2,1)}), bf16[32,32,512]{2,1,0:T(8,128)(2,1)}, u32[]{:S(2)}, u32[]{:S(2)}) async-start(bf16[32,32,512]{2,1,0:T(8,128)(2,1)} %bitcast.276), calls=%async_computation.6 | async-start | bytes 2097152 | tf_op jit(solution)/shard_map/all_to_all | solution.py:185
  669.3 10.1 %all-to-all-start.6 = ((f32[32,1,128]{2,1,0:T(1,128)}), f32[32,1,128]{2,1,0:T(1,128)S(1)}, u32[]{:S(2)}, u32[]{:S(2)}) async-start(f32[32,1,128]{2,1,0:T(1,128)} %broadcast_in_dim.42), calls=%async_computation.8 | async-start | bytes 32768 | tf_op jit(solution)/shard_map/all_to_all | solution.py:1550
  (103 other events, 909.9 us)
Sparse Core Ops, SparseCore 0:
  31.4 44.1 all-gather.2
  145.4 80.1 all-gather.4
  345.6 92.1 reduce-scatter.2
  504.2 155.7 reduce-scatter.4

commit v6 on v5

--- a/solution.py
+++ b/solution.py
@@ -1309,16 +1309,18 @@
                 [later_both[:, 3 * width :], later_shrink.astype(BF).reshape(-1, units)], -1
             )
             later_near = later_both[:, : 3 * width]
-    attended, logs, later_far, later_near, outputs, travel.pieces = far.hold(
-        attended, logs, later_far, later_near, outputs, travel.pieces
-    )
-    output, later_output = (settle_output(outputs[:, layer]) for layer in (0, 1))
+    attended, logs, later_far, later_near, travel.pieces = far.hold(
+        attended, logs, later_far, later_near, travel.pieces
+    )
     later_all = lax.all_gather(later_far, "dp", axis=0, tiled=True)
     while len(far.pieces) < outer:
         far.forward()
     while len(far.chains) < outer:
         far.cross()
-    attended, logs, later_near, grads = far.hold(attended, logs, later_near, travel.done())
+    attended, logs, later_near, grads, outputs = far.hold(
+        attended, logs, later_near, travel.done(), outputs
+    )
+    output, later_output = (settle_output(outputs[:, layer]) for layer in (0, 1))
     near = Gather(later_near)
     near.forward()
     near.cross()
@@ -1496,6 +1498,12 @@
             later_home = SeqSwap(later_first[:, :units].reshape(parts, rows_d, units))
         else:
             mixed, low = later_home.hold(mixed, low)
+        if half == halves - 1:
+            others = norm_grad(
+                hidden_low, expand_scaled, lows + [low], mixing_scaled, False
+            )
+            others, low = tie((others, low))
+            last_travel = SeqScatter(others)
         mixing_grad, gain_one_grad, shift_one_grad = weight_grad(
             normed,
             [low],
@@ -1518,17 +1526,16 @@
         mixing_grad = beside(mixing_grad, *pieces) if pieces else mixing_grad
         if half == 0:
             result, (mixing_grad,) = travel.done(result_own, (mixing_grad,))
+        if half == halves - 1:
+            (mixing_grad,) = last_travel.hold(mixing_grad)
         mixing_grad, lows, mixed, attended_grad, mixing_grads = tie(
             (mixing_grad, lows, mixed, attended_grad, mixing_grads)
         )
         mixing_grads.append(sum_exchange(mixing_grad))
     result = later_current + result + later_vectors[5] + later_vectors[7]
     result = result.reshape(stream.shape)
-    others = norm_grad(hidden_low, expand_scaled, lows, mixing_scaled, False)
-    travel = SeqScatter(others)
-    (lows,) = travel.hold(lows)
     own = norm_grad(hidden_low, expand_scaled, lows, mixing_scaled, True)
-    normed_grad = travel.done(own)[0]
+    normed_grad = last_travel.done(own)[0]
     gradient = norm_back(gradient, normed_grad, own_normed, scale)
     squares = sum_squares(later_first)
     mixing_grads[-1], gradient, result, squares = tie(

time: 712 us -> 699 us (0.982)
  starting transfers between devices: 85.1 us -> 71.3 us
    ppermute x9, starting transfers between devices: 25.5 us -> 10.5 us  [outer_ring(): lax.ppermute(value, 'dp', [(i, (i + inner) % size) for i in range(size)])]
    all_to_all x3, waiting for transfers between devices: 8.55 us -> 17.1 us  [seq_exchange(): return lax.all_to_all(value, 'seq', split_axis=0, concat_axis=0, tiled=True)]
  transfers between devices with their start and end apart: 68 -> 68, of which waited for: 29 -> 25; matrix products, arithmetic and copies ran while one was open for 12% -> 13% of each run, Pallas kernels for 46% -> 46%
where the time goes in v6:
time: 699 us; the launch traced here: 688 us
  Pallas kernels  351 us (50%)
  waiting for transfers between devices  135 us (19%)
  starting transfers between devices  71.3 us (10%)
  other arithmetic  57.3 us (8%)
  local copies, waits for them, and re-layouts  48.1 us (7%)
  between operations  21 us (3%)
    pallas_call x4, Pallas kernels, attend_back(): pl.pallas_call(attend_back_kernel, grid=(length // block,), in_specs=[pl....  80.4 us
    pallas_call x2, Pallas kernels, feed_back(): pl.pallas_call(partial(feed_back_kernel, joined, 9 + len(kept)), grid=(le...  49.6 us
    pallas_call x4, Pallas kernels, attend(): pl.pallas_call(attend_kernel, grid=(length // block,), in_specs=[pl.Block...  46.3 us
    pallas_call x3, Pallas kernels, feed(): pl.pallas_call(partial(feed_kernel, first is not None, last is not None,...  44.1 us
    ppermute x8, waiting for transfers between devices, chip_ring(): lax.ppermute(value, 'seq', [(i, (i + 2) % size) for i in range(size)])  38.8 us
    pallas_call x4, Pallas kernels, norm_grad(): pl.pallas_call(norm_grad_kernel, grid_spec=pltpu.PrefetchScalarGridSpec(n...  34.4 us
    ppermute x9, waiting for transfers between devices, outer_ring(): lax.ppermute(value, 'dp', [(i, (i + inner) % size) for i in range(size)])  25.5 us
    pallas_call x3, Pallas kernels, mix(): pl.pallas_call(partial(mix_kernel, count, len(pieces)), grid_spec=pltpu.P...  25.3 us
  transfers between devices with their start and end apart: 68, of which 25 were waited for; matrix products, arithmetic and copies ran while one was open for 13% of the time, Pallas kernels for 46%

profile of v6, /device:TPU:0, one launch (start us, length us, event | category | flops | bytes accessed | tf_op | source)
XLA Modules:
  0.0 688.4 jit_solution(12792171476975490498)
XLA Ops:
  10.8 4.2 all-to-all-start
  41.0 3.9 all-to-all-start.1
  48.3 4.4 all-to-all-done.1
  60.2 9.9 %collective-permute-done.6.refs_15_ = bf16[128,768]{1,0:T(8,128)(2,1)S(1)} collective-permute-done((bf16[128,768]{1,0:T(8,128)(2,1)}, bf16[128,768]{1,0:T(8,128)(2,1)S(1)}, u32[]{:S(2)}, u32[]{:S(2)}) %collective-permute-start.6) | collective-permute-done | bytes 196640 | tf_op jit(solution)/shard_map/ppermute | solution.py:47
  72.2 6.0 collective-permute-done.8.refs_14_
  84.8 11.1 %mix.3 = (bf16[2048,1024]{1,0:T(8,128)(2,1)}, bf16[2048,768]{1,0:T(8,128)(2,1)}, bf16[1024,768]{1,0:T(8,128)(2,1)}, bf16[1024,768]{1,0:T(8,128)(2,1)}, f32[8,768]{1,0:T(8,128)}) custom-call(s32[4]{0:T(128)} %pad_add_fusion.x_slots_ref.slots_ref, s32[8]{0:T(128)} %stack.201.slots_ref, bf16[512,1024]{1,0:T(8,128)(2,1)} %copy-done.15, ...), custom_call_target="tpu_custom_call" | custom-call | flops 1000 | bytes 1000 | tf_op jit(solution)/shard_map/mix/pallas_call | solution.py:336
  98.7 11.6 %attend.4 = (bf16[2048,128]{1,0:T(8,128)(2,1)}, f32[2,2048]{1,0:T(2,128)}) custom-call(bf16[2048,768]{1,0:T(8,128)(2,1)} %get-tuple-element.581.q_ref.k_ref.v_ref, bf16[2048,768]{1,0:T(8,128)(2,1)} %get-tuple-element.581.q_ref.k_ref.v_ref, bf16[2048,768]{1,0:T(8,128)(2,1)} %get-tuple-element.581.q_ref.k_ref.v_ref), custom_call_target="tpu_custom_call" | custom-call | flops 1000 | bytes 1000 | tf_op jit(solution)/shard_map/attend/pallas_call | solution.py:399
  110.3 3.8 all-to-all-start.2
  117.1 7.6 %all-to-all-done.2 = bf16[4,32,1792]{2,1,0:T(8,128)(2,1)S(1)} async-done(((bf16[4,32,1792]{2,1,0:T(8,128)(2,1)}), bf16[4,32,1792]{2,1,0:T(8,128)(2,1)S(1)}, u32[]{:S(2)}, u32[]{:S(2)}) %all-to-all-start.2) | async-done | bytes 458784 | tf_op jit(solution)/shard_map/all_to_all | solution.py:219
  127.7 11.6 %attend.5 = (bf16[2048,128]{1,0:T(8,128)(2,1)}, f32[2,2048]{1,0:T(2,128)}) custom-call(bf16[2048,768]{1,0:T(8,128)(2,1)} %get-tuple-element.581.q_ref.k_ref.v_ref, bf16[2048,768]{1,0:T(8,128)(2,1)} %get-tuple-element.581.q_ref.k_ref.v_ref, bf16[2048,768]{1,0:T(8,128)(2,1)} %get-tuple-element.581.q_ref.k_ref.v_ref), custom_call_target="tpu_custom_call" | custom-call | flops 1000 | bytes 1000 | tf_op jit(solution)/shard_map/attend/pallas_call | solution.py:399
  148.8 5.3 assemble.2
  154.2 6.0 all-to-all-done.3
  161.8 3.6 collective-permute-start.20
  167.6 16.3 %feed.3 = (bf16[2048,1024]{1,0:T(8,128)(2,1)}, bf16[2048,1024]{1,0:T(8,128)(2,1)}, bf16[1024,1024]{1,0:T(8,128)(2,1)}, f32[8,1024]{1,0:T(8,128)}, bf16[1024,1024...) custom-call(s32[1]{0:T(128)} %bitcast.41.y_ref, s32[8]{0:T(128)} %stack.201.slots_ref, ...), custom_call_target="tpu_custom_call" | custom-call | flops 1000 | bytes 1000 | tf_op jit(solution)/shard_map/feed/pallas_call | solution.py:699
  195.2 13.0 %feed.4 = (bf16[2048,1024]{1,0:T(8,128)(2,1)}, bf16[2048,1024]{1,0:T(8,128)(2,1)}, bf16[1024,1024]{1,0:T(8,128)(2,1)}) custom-call(s32[1]{0:T(128)} %bitcast.41.y_ref, s32[1]{0:T(128)} %constant.382.clone.1.slots_ref, bf16[2048,1024]{1,0:T(8,128)(2,1)} %get-tuple-element.379.x_ref.refs_4_, ...), custom_call_target="tpu_custom_call", output_to_operand_aliasing={{0}: (9, {}), {1}: (10, {})} | custom-call | flops 1000 | bytes 1000 | tf_op jit(solution)/shard_map/feed/pallas_call | solution.py:699
  208.8 12.4 %collective-permute-done.26.refs_13_ = bf16[128,768]{1,0:T(8,128)(2,1)S(1)} collective-permute-done((bf16[128,768]{1,0:T(8,128)(2,1)S(1)}, bf16[128,768]{1,0:T(8,128)(2,1)S(1)}, u32[]{:S(2)}, u32[]{:S(2)}) %collective-permute-start.26) | collective-permute-done | bytes 196640 | tf_op jit(solution)/shard_map/ppermute | solution.py:47
  236.4 7.8 %mix.4 = (bf16[2048,1024]{1,0:T(8,128)(2,1)}, bf16[2048,768]{1,0:T(8,128)(2,1)}, bf16[1024,768]{1,0:T(8,128)(2,1)}, bf16[1024,768]{1,0:T(8,128)(2,1)}, f32[8,768]{1,0:T(8,128)}) custom-call(s32[2]{0:T(128)} %pad_add_fusion.2.x_slots_ref, s32[8]{0:T(128)} %stack.201.slots_ref, bf16[512,1024]{1,0:T(8,128)(2,1)} %copy-done.16, ...), custom_call_target="tpu_custom_call" | custom-call | flops 1000 | bytes 1000 | tf_op jit(solution)/shard_map/mix/pallas_call | solution.py:336
  244.3 9.5 %collective-permute-done.31.refs_0_ = bf16[512,1024]{1,0:T(8,128)(2,1)} collective-permute-done((bf16[512,1024]{1,0:T(8,128)(2,1)S(1)}, bf16[512,1024]{1,0:T(8,128)(2,1)}, u32[]{:S(2)}, u32[]{:S(2)}) %collective-permute-start.31) | collective-permute-done | bytes 1048608 | tf_op jit(solution)/shard_map/ppermute | solution.py:60
  257.6 6.4 mix.5
  264.1 11.6 %attend.6 = (bf16[2048,128]{1,0:T(8,128)(2,1)}, f32[2,2048]{1,0:T(2,128)}) custom-call(bf16[2048,768]{1,0:T(8,128)(2,1)} %get-tuple-element.479.q_ref.k_ref.v_ref, bf16[2048,768]{1,0:T(8,128)(2,1)} %get-tuple-element.479.q_ref.k_ref.v_ref, bf16[2048,768]{1,0:T(8,128)(2,1)} %get-tuple-element.479.q_ref.k_ref.v_ref), custom_call_target="tpu_custom_call" | custom-call | flops 1000 | bytes 1000 | tf_op jit(solution)/shard_map/attend/pallas_call | solution.py:399
  275.6 11.6 %attend.7 = (bf16[2048,128]{1,0:T(8,128)(2,1)}, f32[2,2048]{1,0:T(2,128)}) custom-call(bf16[2048,768]{1,0:T(8,128)(2,1)} %get-tuple-element.479.q_ref.k_ref.v_ref, bf16[2048,768]{1,0:T(8,128)(2,1)} %get-tuple-element.479.q_ref.k_ref.v_ref, bf16[2048,768]{1,0:T(8,128)(2,1)} %get-tuple-element.479.q_ref.k_ref.v_ref), custom_call_target="tpu_custom_call" | custom-call | flops 1000 | bytes 1000 | tf_op jit(solution)/shard_map/attend/pallas_call | solution.py:399
  287.2 14.7 %feed.5 = (bf16[2048,1024]{1,0:T(8,128)(2,1)}, bf16[2048,1024]{1,0:T(8,128)(2,1)}, bf16[1024,1024]{1,0:T(8,128)(2,1)}, f32[8,1024]{1,0:T(8,128)}) custom-call(s32[1]{0:T(128)} %bitcast.41.y_ref, s32[1]{0:T(128)} %constant.382.clone.1.slots_ref, bf16[2048,1024]{1,0:T(8,128)(2,1)} %get-tuple-element.477.x_ref.refs_4_, f32[1,1024]{1,0:T(1,128)} %get-tuple-element.722, ...), custom_call_target="tpu_custom_call" | custom-call | flops 1000 | bytes 1000 | tf_op jit(solution)/shard_map/feed/pallas_call | solution.py:699
  302.0 4.1 product.2
  310.0 24.9 %feed_back.2 = (bf16[2048,1024]{1,0:T(8,128)(2,1)}, f32[1,1024]{1,0:T(1,128)}, bf16[2048,256]{1,0:T(8,128)(2,1)}, f32[1,1024]{1,0:T(1,128)}, f32[1,1024]{1,0:T(1,128)}, /*index=5*/bf16[1024,2304]{1,0:T(8,128)(2,1)}) custom-call(bf16[2048,1024]{1,0:T(8,128)(2,1)} %bitcast.253, ...), custom_call_target="tpu_custom_call" | custom-call | flops 1000 | bytes 1000 | tf_op jit(solution)/shard_map/feed_back/pallas_call | solution.py:950
  336.3 20.4 %attend_back.4 = (bf16[2048,384]{1,0:T(8,128)(2,1)}, f32[1,384]{1,0:T(1,128)}) custom-call(bf16[2048,768]{1,0:T(8,128)(2,1)} %get-tuple-element.479.q_ref.k_ref.v_ref, bf16[2048,768]{1,0:T(8,128)(2,1)} %get-tuple-element.479.q_ref.k_ref.v_ref, bf16[2048,768]{1,0:T(8,128)(2,1)} %get-tuple-element.479.q_ref.k_ref.v_ref, ...), custom_call_target="tpu_custom_call" | custom-call | flops 1000 | bytes 1000 | tf_op jit(solution)/shard_map/attend_back/pallas_call | solution.py:528
  356.7 20.0 %attend_back.5 = (bf16[2048,384]{1,0:T(8,128)(2,1)}, f32[1,384]{1,0:T(1,128)}) custom-call(bf16[2048,768]{1,0:T(8,128)(2,1)} %get-tuple-element.479.q_ref.k_ref.v_ref, bf16[2048,768]{1,0:T(8,128)(2,1)} %get-tuple-element.479.q_ref.k_ref.v_ref, bf16[2048,768]{1,0:T(8,128)(2,1)} %get-tuple-element.479.q_ref.k_ref.v_ref, ...), custom_call_target="tpu_custom_call" | custom-call | flops 1000 | bytes 1000 | tf_op jit(solution)/shard_map/attend_back/pallas_call | solution.py:528
  376.8 8.6 %norm_grad.4 = bf16[1024,1024]{1,0:T(8,128)(2,1)} custom-call(s32[1]{0:T(128)} %bitcast.41.y_ref, bf16[2048,1024]{1,0:T(8,128)(2,1)} %get-tuple-element.524.h_ref, bf16[1024,1024]{1,0:T(8,128)(2,1)} %get-tuple-element.522.wi_ref, bf16[1024,768]{1,0:T(8,128)(2,1)} %get-tuple-element.473.refs_4_.wm_ref, bf16[2048,384]{1,0:T(8,128)(2,1)} %get-tuple-element.533.refs_0_, ...), custom_call_target="tpu_custom_call" | custom-call | flops 1000 | bytes 1000 | tf_op jit(solution)/shard_map/norm_grad/pallas_call | solution.py:763
  390.7 7.1 %branch.2 = bf16[1024,1024]{1,0:T(8,128)(2,1)} custom-call(s32[1]{0:T(128)} %bitcast.41.y_ref, bf16[2048,1024]{1,0:T(8,128)(2,1)} %get-tuple-element.527.refs_3_.act_ref, bf16[1024,2048]{1,0:T(8,128)(2,1)} %all-gather.5.cloned.1.call-done.refs_3_.refs_1_.refs_6_.shrink_ref, bf16[256,1024]{1,0:T(8,128)(2,1)} %bitcast.261, ...), custom_call_target="tpu_custom_call" | custom-call | flops 1000 | bytes 1000 | tf_op jit(solution)/shard_map/branch/pallas_call | solution.py:726
  397.8 7.0 %branch.3 = bf16[1024,1024]{1,0:T(8,128)(2,1)} custom-call(s32[1]{0:T(128)} %bitcast.41.y_ref, bf16[2048,1024]{1,0:T(8,128)(2,1)} %get-tuple-element.527.refs_3_.act_ref, bf16[1024,2048]{1,0:T(8,128)(2,1)} %all-gather.5.cloned.1.call-done.refs_3_.refs_1_.refs_6_.shrink_ref, bf16[256,1024]{1,0:T(8,128)(2,1)} %bitcast.262, ...), custom_call_target="tpu_custom_call" | custom-call | flops 1000 | bytes 1000 | tf_op jit(solution)/shard_map/branch/pallas_call | solution.py:726
  404.8 8.7 %norm_grad.5 = bf16[1024,1024]{1,0:T(8,128)(2,1)} custom-call(s32[1]{0:T(128)} %bitcast.41.y_ref, bf16[2048,1024]{1,0:T(8,128)(2,1)} %get-tuple-element.524.h_ref, bf16[1024,1024]{1,0:T(8,128)(2,1)} %get-tuple-element.522.wi_ref, bf16[1024,768]{1,0:T(8,128)(2,1)} %get-tuple-element.473.refs_4_.wm_ref, bf16[2048,384]{1,0:T(8,128)(2,1)} %get-tuple-element.533.refs_0_, ...), custom_call_target="tpu_custom_call" | custom-call | flops 1000 | bytes 1000 | tf_op jit(solution)/shard_map/norm_grad/pallas_call | solution.py:763
  427.3 9.1 %weight_grad.3 = (bf16[1024,3072]{1,0:T(8,128)(2,1)}, f32[1,1024]{1,0:T(1,128)}, f32[1,1024]{1,0:T(1,128)}) custom-call(bf16[2048,1024]{1,0:T(8,128)(2,1)} %get-tuple-element.477.x_ref.refs_4_, bf16[1024,768]{1,0:T(8,128)(2,1)} %get-tuple-element.478.weight_ref, f32[1,1024]{1,0:T(1,128)} %get-tuple-element.724, f32[1,1024]{1,0:T(1,128)} %get-tuple-element.723, ...), custom_call_target="tpu_custom_call" | custom-call | flops 1000 | bytes 1000 | tf_op jit(solution)/shard_map/weight_grad/pallas_call | solution.py:824
  436.3 15.1 %collective-permute-done.39.refs_2_ = bf16[512,1024]{1,0:T(8,128)(2,1)} collective-permute-done((bf16[512,1024]{1,0:T(8,128)(2,1)S(1)}, bf16[512,1024]{1,0:T(8,128)(2,1)}, u32[]{:S(2)}, u32[]{:S(2)}) %collective-permute-start.39) | collective-permute-done | bytes 1048608 | tf_op jit(solution)/shard_map/ppermute | solution.py:60
  456.5 5.4 assemble.3
  461.9 4.1 product.3
  469.3 24.7 %feed_back.3 = (bf16[2048,1024]{1,0:T(8,128)(2,1)}, f32[1,1024]{1,0:T(1,128)}, bf16[2048,256]{1,0:T(8,128)(2,1)}, f32[1,1024]{1,0:T(1,128)}, f32[1,1024]{1,0:T(1,128)}, /*index=5*/bf16[1024,3072]{1,0:T(8,128)(2,1)}) custom-call(bf16[2048,1024]{1,0:T(8,128)(2,1)} %bitcast.251, ...), custom_call_target="tpu_custom_call", output_to_operand_aliasing={{5}: (9, {})} | custom-call | flops 1000 | bytes 1000 | tf_op jit(solution)/shard_map/feed_back/pallas_call | solution.py:950
  497.3 20.0 %attend_back.6 = (bf16[2048,384]{1,0:T(8,128)(2,1)}, f32[1,384]{1,0:T(1,128)}) custom-call(bf16[2048,768]{1,0:T(8,128)(2,1)} %get-tuple-element.581.q_ref.k_ref.v_ref, bf16[2048,768]{1,0:T(8,128)(2,1)} %get-tuple-element.581.q_ref.k_ref.v_ref, bf16[2048,768]{1,0:T(8,128)(2,1)} %get-tuple-element.581.q_ref.k_ref.v_ref, ...), custom_call_target="tpu_custom_call" | custom-call | flops 1000 | bytes 1000 | tf_op jit(solution)/shard_map/attend_back/pallas_call | solution.py:528
  524.6 6.9 %weight_grad.4 = (bf16[1024,384]{1,0:T(8,128)(2,1)}, f32[1,1024]{1,0:T(1,128)}, f32[1,1024]{1,0:T(1,128)}) custom-call(bf16[2048,1024]{1,0:T(8,128)(2,1)} %get-tuple-element.379.x_ref.refs_4_, bf16[1024,768]{1,0:T(8,128)(2,1)} %get-tuple-element.380.weight_ref, f32[1,1024]{1,0:T(1,128)} %get-tuple-element.730, f32[1,1024]{1,0:T(1,128)} %get-tuple-element.729, ...), custom_call_target="tpu_custom_call" | custom-call | flops 1000 | bytes 1000 | tf_op jit(solution)/shard_map/weight_grad/pallas_call | solution.py:824
  533.7 11.9 %collective-permute-done.46 = bf16[512,1024]{1,0:T(8,128)(2,1)} collective-permute-done((bf16[512,1024]{1,0:T(8,128)(2,1)S(1)}, bf16[512,1024]{1,0:T(8,128)(2,1)}, u32[]{:S(2)}, u32[]{:S(2)}) %collective-permute-start.46) | collective-permute-done | bytes 1048608 | tf_op jit(solution)/shard_map/ppermute | solution.py:60
  545.7 20.0 %attend_back.7 = (bf16[2048,384]{1,0:T(8,128)(2,1)}, f32[1,384]{1,0:T(1,128)}) custom-call(bf16[2048,768]{1,0:T(8,128)(2,1)} %get-tuple-element.581.q_ref.k_ref.v_ref, bf16[2048,768]{1,0:T(8,128)(2,1)} %get-tuple-element.581.q_ref.k_ref.v_ref, bf16[2048,768]{1,0:T(8,128)(2,1)} %get-tuple-element.581.q_ref.k_ref.v_ref, ...), custom_call_target="tpu_custom_call" | custom-call | flops 1000 | bytes 1000 | tf_op jit(solution)/shard_map/attend_back/pallas_call | solution.py:528
  569.2 8.6 %norm_grad.6 = bf16[1024,1024]{1,0:T(8,128)(2,1)} custom-call(s32[1]{0:T(128)} %bitcast.41.y_ref, bf16[2048,1024]{1,0:T(8,128)(2,1)} %get-tuple-element.585.h_ref, bf16[1024,1024]{1,0:T(8,128)(2,1)} %get-tuple-element.441.refs_0_.wi_ref, bf16[1024,768]{1,0:T(8,128)(2,1)} %get-tuple-element.586.wm_ref, bf16[2048,384]{1,0:T(8,128)(2,1)} %get-tuple-element.605.refs_0_, ...), custom_call_target="tpu_custom_call" | custom-call | flops 1000 | bytes 1000 | tf_op jit(solution)/shard_map/norm_grad/pallas_call | solution.py:763
  577.8 7.2 %weight_grad.5 = (bf16[1024,384]{1,0:T(8,128)(2,1)}, f32[1,1024]{1,0:T(1,128)}, f32[1,1024]{1,0:T(1,128)}) custom-call(bf16[2048,1024]{1,0:T(8,128)(2,1)} %get-tuple-element.379.x_ref.refs_4_, bf16[1024,768]{1,0:T(8,128)(2,1)} %get-tuple-element.380.weight_ref, f32[1,1024]{1,0:T(1,128)} %get-tuple-element.730, f32[1,1024]{1,0:T(1,128)} %get-tuple-element.729, ...), custom_call_target="tpu_custom_call" | custom-call | flops 1000 | bytes 1000 | tf_op jit(solution)/shard_map/weight_grad/pallas_call | solution.py:824
  601.5 10.4 %all-to-all-done.4 = bf16[32,32,512]{2,1,0:T(8,128)(2,1)S(1)} async-done(((bf16[32,32,512]{2,1,0:T(8,128)(2,1)}), bf16[32,32,512]{2,1,0:T(8,128)(2,1)S(1)}, u32[]{:S(2)}, u32[]{:S(2)}) %all-to-all-start.4) | async-done | bytes 1048608 | tf_op jit(solution)/shard_map/all_to_all | solution.py:185
  611.9 4.1 all-to-all-start.5
  616.0 8.6 %norm_grad.7 = bf16[1024,1024]{1,0:T(8,128)(2,1)} custom-call(s32[1]{0:T(128)} %bitcast.41.y_ref, bf16[2048,1024]{1,0:T(8,128)(2,1)} %get-tuple-element.585.h_ref, bf16[1024,1024]{1,0:T(8,128)(2,1)} %get-tuple-element.441.refs_0_.wi_ref, bf16[1024,768]{1,0:T(8,128)(2,1)} %get-tuple-element.586.wm_ref, bf16[2048,384]{1,0:T(8,128)(2,1)} %get-tuple-element.605.refs_0_, ...), custom_call_target="tpu_custom_call" | custom-call | flops 1000 | bytes 1000 | tf_op jit(solution)/shard_map/norm_grad/pallas_call | solution.py:763
  626.5 3.8 fusion.4
  637.7 5.7 all-to-all-done.5
  654.6 3.7 all-to-all-start.6
  669.8 10.5 %update.1 = (f32[2,32,3072]{2,1,0:T(8,128)}, f32[2,32,3072]{2,1,0:T(8,128)}, f32[2,32,3072]{2,1,0:T(8,128)}, f32[2,32,3072]{2,1,0:T(8,128)}, f32[2,32,1024]{2,1,...) custom-call(f32[1]{0:T(128)} %bitcast.140.clip_ref, ...), custom_call_target="tpu_custom_call" | custom-call | flops 1000 | bytes 1000 | tf_op jit(solution)/shard_map/update/pallas_call | solution.py:1041
  (470 shorter events, 194.6 us)
Async XLA Ops:
  10.8 14.2 %all-to-all-start = ((bf16[4,32,1824]{2,1,0:T(8,128)(2,1)}), bf16[4,32,1824]{2,1,0:T(8,128)(2,1)}, u32[]{:S(2)}, u32[]{:S(2)}) async-start(bf16[4,32,1824]{2,1,0:T(8,128)(2,1)} %pack.2), calls=%async_computation | async-start | bytes 983040 | tf_op jit(solution)/shard_map/all_to_all | solution.py:219
  15.0 80.9 %all-gather.3.cloned.1.call-start = ((), (), s32[]{:S(2)}) async-start(), calls=%async_computation.9 | async-start | bytes 1179648 | tf_op jit(solution)/shard_map/all_gather | solution.py:1234
  15.9 40.1 %collective-permute-start.3 = (bf16[512,1024]{1,0:T(8,128)(2,1)S(1)}, bf16[512,1024]{1,0:T(8,128)(2,1)}, u32[]{:S(2)}, u32[]{:S(2)}) collective-permute-start(bf16[512,1024]{1,0:T(8,128)(2,1)S(1)} %fusion.15.refs_0_), channel_id=1, source_target_pairs={{0,2},{1,3},{2,0},{3,1},{4,6},{5,7},{6,4},{7,5},{8,10},{9,11},{10,... | collective-permute-start | bytes 3145736 | tf_op jit(solution)/shard_map/ppermute | solution.py:60
  41.0 11.6 %all-to-all-start.1 = ((bf16[32,2,416]{2,1,0:T(2,128)(2,1)}), bf16[32,2,416]{2,1,0:T(2,128)(2,1)S(1)}, u32[]{:S(2)}, u32[]{:S(2)}) async-start(bf16[32,2,416]{2,1,0:T(2,128)(2,1)} %reshape.488), calls=%async_computation.1 | async-start | bytes 131072 | tf_op jit(solution)/shard_map/all_to_all | solution.py:1249
  44.9 11.0 %collective-permute-start.1 = (bf16[128,768]{1,0:T(8,128)(2,1)}, bf16[128,768]{1,0:T(8,128)(2,1)}, u32[]{:S(2)}, u32[]{:S(2)}) collective-permute-start(bf16[128,768]{1,0:T(8,128)(2,1)} %collective-permute-done.refs_11_), channel_id=1, source_target_pairs={{0,8},{4,12},{8,16},{12,20},{16,24},{20,28},{24,0},{28,4},{1,9},{5... | collective-permute-start | bytes 589832 | tf_op jit(solution)/shard_map/ppermute | solution.py:47
  57.0 13.1 %collective-permute-start.4 = (bf16[512,1024]{1,0:T(8,128)(2,1)S(1)}, bf16[512,1024]{1,0:T(8,128)(2,1)S(1)}, u32[]{:S(2)}, u32[]{:S(2)}) collective-permute-start(bf16[512,1024]{1,0:T(8,128)(2,1)S(1)} %fusion.15.refs_0_), channel_id=1, source_target_pairs={{0,1},{1,0},{2,3},{3,2},{4,5},{5,4},{6,7},{7,6},{8,9},{9,8},{10,11... | collective-permute-start | bytes 3145736 | tf_op jit(solution)/shard_map/ppermute | solution.py:65
  57.0 13.1 %collective-permute-start.5 = (bf16[512,1024]{1,0:T(8,128)(2,1)}, bf16[512,1024]{1,0:T(8,128)(2,1)S(1)}, u32[]{:S(2)}, u32[]{:S(2)}) collective-permute-start(bf16[512,1024]{1,0:T(8,128)(2,1)} %collective-permute-done.3.refs_2_), channel_id=1, source_target_pairs={{0,1},{1,0},{2,3},{3,2},{4,5},{5,4},{6,7},{7,6},{8,9},{9,8},{10,11... | collective-permute-start | bytes 3145736 | tf_op jit(solution)/shard_map/ppermute | solution.py:65
  57.5 12.6 %collective-permute-start.6 = (bf16[128,768]{1,0:T(8,128)(2,1)}, bf16[128,768]{1,0:T(8,128)(2,1)S(1)}, u32[]{:S(2)}, u32[]{:S(2)}) collective-permute-start(bf16[128,768]{1,0:T(8,128)(2,1)} %collective-permute-done.1.refs_13_), channel_id=1, source_target_pairs={{0,8},{4,12},{8,16},{12,20},{16,24},{20,28},{24,0},{28,4},{1,9},{5... | collective-permute-start | bytes 589832 | tf_op jit(solution)/shard_map/ppermute | solution.py:47
  57.5 12.6 %collective-permute-start.7 = (bf16[128,768]{1,0:T(8,128)(2,1)}, bf16[128,768]{1,0:T(8,128)(2,1)S(1)}, u32[]{:S(2)}, u32[]{:S(2)}) collective-permute-start(bf16[128,768]{1,0:T(8,128)(2,1)} %collective-permute-done.refs_11_), channel_id=1, source_target_pairs={{0,4},{4,0},{8,12},{12,8},{16,20},{20,16},{24,28},{28,24},{1,5},{5... | collective-permute-start | bytes 589832 | tf_op jit(solution)/shard_map/ppermute | solution.py:55
  81.1 14.8 %collective-permute-start.10 = (bf16[128,2048]{1,0:T(8,128)(2,1)S(1)}, bf16[128,2048]{1,0:T(8,128)(2,1)}, u32[]{:S(2)}, u32[]{:S(2)}) collective-permute-start(bf16[128,2048]{1,0:T(8,128)(2,1)S(1)} %pad_maximum_fusion.3.refs_3_), channel_id=1, source_target_pairs={{0,8},{4,12},{8,16},{12,20},{16,24},{20,28},{24,0},{28,4},{1,9},{5... | collective-permute-start | bytes 1572872 | tf_op jit(solution)/shard_map/ppermute | solution.py:47
  81.2 14.8 %collective-permute-start.11 = (bf16[128,2048]{1,0:T(8,128)(2,1)S(1)}, bf16[128,2048]{1,0:T(8,128)(2,1)S(1)}, u32[]{:S(2)}, u32[]{:S(2)}) collective-permute-start(bf16[128,2048]{1,0:T(8,128)(2,1)S(1)} %pad_maximum_fusion.3.refs_3_), channel_id=1, source_target_pairs={{0,4},{4,0},{8,12},{12,8},{16,20},{20,16},{24,28},{28,24},{1,5},{5... | collective-permute-start | bytes 1572872 | tf_op jit(solution)/shard_map/ppermute | solution.py:55
  95.9 28.8 %collective-permute-start.12 = (bf16[128,2048]{1,0:T(8,128)(2,1)}, bf16[128,2048]{1,0:T(8,128)(2,1)}, u32[]{:S(2)}, u32[]{:S(2)}) collective-permute-start(bf16[128,2048]{1,0:T(8,128)(2,1)} %collective-permute-done.10.refs_5_), channel_id=1, source_target_pairs={{0,8},{4,12},{8,16},{12,20},{16,24},{20,28},{24,0},{28,4},{1,9},{5... | collective-permute-start | bytes 1572872 | tf_op jit(solution)/shard_map/ppermute | solution.py:47
  96.5 28.2 %collective-permute-start.13 = (bf16[128,2048]{1,0:T(8,128)(2,1)}, bf16[128,2048]{1,0:T(8,128)(2,1)}, u32[]{:S(2)}, u32[]{:S(2)}) collective-permute-start(bf16[128,2048]{1,0:T(8,128)(2,1)} %collective-permute-done.10.refs_5_), channel_id=1, source_target_pairs={{0,4},{4,0},{8,12},{12,8},{16,20},{20,16},{24,28},{28,24},{1,5},{5... | collective-permute-start | bytes 1572872 | tf_op jit(solution)/shard_map/ppermute | solution.py:55
  97.2 43.6 %collective-permute-start.14 = (bf16[512,1024]{1,0:T(8,128)(2,1)S(1)}, bf16[512,1024]{1,0:T(8,128)(2,1)}, u32[]{:S(2)}, u32[]{:S(2)}) collective-permute-start(bf16[512,1024]{1,0:T(8,128)(2,1)S(1)} %get-tuple-element.414.refs_0_), channel_id=1, source_target_pairs={{0,2},{1,3},{2,0},{3,1},{4,6},{5,7},{6,4},{7,5},{8,10},{9,11},{10,... | collective-permute-start | bytes 3145736 | tf_op jit(solution)/shard_map/ppermute | solution.py:60
  110.3 14.4 %all-to-all-start.2 = ((bf16[4,32,1792]{2,1,0:T(8,128)(2,1)}), bf16[4,32,1792]{2,1,0:T(8,128)(2,1)S(1)}, u32[]{:S(2)}, u32[]{:S(2)}) async-start(bf16[4,32,1792]{2,1,0:T(8,128)(2,1)} %pack.3), calls=%async_computation.2 | async-start | bytes 917504 | tf_op jit(solution)/shard_map/all_to_all | solution.py:219
  124.7 16.1 %collective-permute-start.15 = (bf16[128,2048]{1,0:T(8,128)(2,1)}, bf16[128,2048]{1,0:T(8,128)(2,1)S(1)}, u32[]{:S(2)}, u32[]{:S(2)}) collective-permute-start(bf16[128,2048]{1,0:T(8,128)(2,1)} %collective-permute-done.12.refs_7_), channel_id=1, source_target_pairs={{0,8},{4,12},{8,16},{12,20},{16,24},{20,28},{24,0},{28,4},{1,9},{5... | collective-permute-start | bytes 1572872 | tf_op jit(solution)/shard_map/ppermute | solution.py:47
  127.0 13.8 %collective-permute-start.16 = (bf16[128,2048]{1,0:T(8,128)(2,1)}, bf16[128,2048]{1,0:T(8,128)(2,1)S(1)}, u32[]{:S(2)}, u32[]{:S(2)}) collective-permute-start(bf16[128,2048]{1,0:T(8,128)(2,1)} %collective-permute-done.12.refs_7_), channel_id=1, source_target_pairs={{0,4},{4,0},{8,12},{12,8},{16,20},{20,16},{24,28},{28,24},{1,5},{5... | collective-permute-start | bytes 1572872 | tf_op jit(solution)/shard_map/ppermute | solution.py:55
  142.2 18.0 %all-to-all-start.3 = ((bf16[4,2,64,1024]{3,2,1,0:T(8,128)(2,1)}), bf16[4,2,64,1024]{3,2,1,0:T(8,128)(2,1)S(1)}, u32[]{:S(2)}, u32[]{:S(2)}) async-start(bf16[4,2,64,1024]{3,2,1,0:T(8,128)(2,1)} %pad_maximum_fusion), calls=%async_computation.3 | async-start | bytes 2097152 | tf_op jit(solution)/shard_map/all_to_all | solution.py:219
  145.7 141.5 %all-gather.5.cloned.1.call-start = ((), (), s32[]{:S(2)}) async-start(), calls=%async_computation.10 | async-start | bytes 4718592 | tf_op jit(solution)/shard_map/all_gather | solution.py:1315
  145.8 16.0 %collective-permute-start.19 = (bf16[128,2048]{1,0:T(8,128)(2,1)}, bf16[128,2048]{1,0:T(8,128)(2,1)}, u32[]{:S(2)}, u32[]{:S(2)}) collective-permute-start(bf16[128,2048]{1,0:T(8,128)(2,1)} %copy-done.32), channel_id=1, source_target_pairs={{0,4},{4,0},{8,12},{12,8},{16,20},{20,16},{24,28},{28,24},{1,5},{5... | collective-permute-start | bytes 1572872 | tf_op jit(solution)/shard_map/ppermute | solution.py:55
  147.8 373.3 %reduce-scatter.3.cloned.1.call-start = ((), (), s32[]{:S(2)}) async-start(), calls=%async_computation.11 | async-start | bytes 5308416 | tf_op jit(solution)/shard_map/reduce_scatter | solution.py:1441
  161.8 22.1 %collective-permute-start.20 = (bf16[128,768]{1,0:T(8,128)(2,1)S(1)}, bf16[128,768]{1,0:T(8,128)(2,1)S(1)}, u32[]{:S(2)}, u32[]{:S(2)}) collective-permute-start(bf16[128,768]{1,0:T(8,128)(2,1)S(1)} %copy-done.29), channel_id=1, source_target_pairs={{0,8},{4,12},{8,16},{12,20},{16,24},{20,28},{24,0},{28,4},{1,9},{5... | collective-permute-start | bytes 589832 | tf_op jit(solution)/shard_map/ppermute | solution.py:47
  165.4 18.6 %collective-permute-start.21 = (bf16[128,768]{1,0:T(8,128)(2,1)S(1)}, bf16[128,768]{1,0:T(8,128)(2,1)S(1)}, u32[]{:S(2)}, u32[]{:S(2)}) collective-permute-start(bf16[128,768]{1,0:T(8,128)(2,1)S(1)} %copy-done.29), channel_id=1, source_target_pairs={{0,4},{4,0},{8,12},{12,8},{16,20},{20,16},{24,28},{28,24},{1,5},{5... | collective-permute-start | bytes 589832 | tf_op jit(solution)/shard_map/ppermute | solution.py:55
  191.4 29.8 %collective-permute-start.23 = (bf16[512,1024]{1,0:T(8,128)(2,1)}, bf16[512,1024]{1,0:T(8,128)(2,1)S(1)}, u32[]{:S(2)}, u32[]{:S(2)}) collective-permute-start(bf16[512,1024]{1,0:T(8,128)(2,1)} %fusion.14), channel_id=1, source_target_pairs={{0,2},{1,3},{2,0},{3,1},{4,6},{5,7},{6,4},{7,5},{8,10},{9,11},{10,... | collective-permute-start | bytes 3145736 | tf_op jit(solution)/shard_map/ppermute | solution.py:60
  193.5 14.7 %collective-permute-start.24 = (bf16[128,768]{1,0:T(8,128)(2,1)S(1)}, bf16[128,768]{1,0:T(8,128)(2,1)S(1)}, u32[]{:S(2)}, u32[]{:S(2)}) collective-permute-start(bf16[128,768]{1,0:T(8,128)(2,1)S(1)} %collective-permute-done.20.refs_9_), channel_id=1, source_target_pairs={{0,8},{4,12},{8,16},{12,20},{16,24},{20,28},{24,0},{28,4},{1,9},{5... | collective-permute-start | bytes 589832 | tf_op jit(solution)/shard_map/ppermute | solution.py:47
  193.6 14.7 %collective-permute-start.25 = (bf16[128,768]{1,0:T(8,128)(2,1)S(1)}, bf16[128,768]{1,0:T(8,128)(2,1)S(1)}, u32[]{:S(2)}, u32[]{:S(2)}) collective-permute-start(bf16[128,768]{1,0:T(8,128)(2,1)S(1)} %collective-permute-done.20.refs_9_), channel_id=1, source_target_pairs={{0,4},{4,0},{8,12},{12,8},{16,20},{20,16},{24,28},{28,24},{1,5},{5... | collective-permute-start | bytes 589832 | tf_op jit(solution)/shard_map/ppermute | solution.py:55
  208.3 13.0 %collective-permute-start.26 = (bf16[128,768]{1,0:T(8,128)(2,1)S(1)}, bf16[128,768]{1,0:T(8,128)(2,1)S(1)}, u32[]{:S(2)}, u32[]{:S(2)}) collective-permute-start(bf16[128,768]{1,0:T(8,128)(2,1)S(1)} %collective-permute-done.24.refs_11_), channel_id=1, source_target_pairs={{0,8},{4,12},{8,16},{12,20},{16,24},{20,28},{24,0},{28,4},{1,9},{5... | collective-permute-start | bytes 589832 | tf_op jit(solution)/shard_map/ppermute | solution.py:47
  208.3 12.9 %collective-permute-start.27 = (bf16[128,768]{1,0:T(8,128)(2,1)S(1)}, bf16[128,768]{1,0:T(8,128)(2,1)S(1)}, u32[]{:S(2)}, u32[]{:S(2)}) collective-permute-start(bf16[128,768]{1,0:T(8,128)(2,1)S(1)} %collective-permute-done.24.refs_11_), channel_id=1, source_target_pairs={{0,4},{4,0},{8,12},{12,8},{16,20},{20,16},{24,28},{28,24},{1,5},{5... | collective-permute-start | bytes 589832 | tf_op jit(solution)/shard_map/ppermute | solution.py:55
  228.3 25.5 %collective-permute-start.31 = (bf16[512,1024]{1,0:T(8,128)(2,1)S(1)}, bf16[512,1024]{1,0:T(8,128)(2,1)}, u32[]{:S(2)}, u32[]{:S(2)}) collective-permute-start(bf16[512,1024]{1,0:T(8,128)(2,1)S(1)} %fusion.16.refs_0_), channel_id=1, source_target_pairs={{0,2},{1,3},{2,0},{3,1},{4,6},{5,7},{6,4},{7,5},{8,10},{9,11},{10,... | collective-permute-start | bytes 3145736 | tf_op jit(solution)/shard_map/ppermute | solution.py:60
  307.2 27.7 %collective-permute-start.33 = (bf16[64,1024]{1,0:T(8,128)(2,1)S(1)}, bf16[64,1024]{1,0:T(8,128)(2,1)S(1)}, u32[]{:S(2)}, u32[]{:S(2)}) collective-permute-start(bf16[64,1024]{1,0:T(8,128)(2,1)S(1)} %bitcast.302), channel_id=1, source_target_pairs={{0,1},{1,0},{2,3},{3,2},{4,5},{5,4},{6,7},{7,6},{8,9},{9,8},{10,11... | collective-permute-start | bytes 393224 | tf_op jit(solution)/shard_map/ppermute | solution.py:205
  307.5 27.4 %collective-permute-start.34 = (bf16[64,1024]{1,0:T(8,128)(2,1)S(1)}, bf16[64,1024]{1,0:T(8,128)(2,1)S(1)}, u32[]{:S(2)}, u32[]{:S(2)}) collective-permute-start(bf16[64,1024]{1,0:T(8,128)(2,1)S(1)} %bitcast.301), channel_id=1, source_target_pairs={{0,2},{1,3},{2,0},{3,1},{4,6},{5,7},{6,4},{7,5},{8,10},{9,11},{10,... | collective-permute-start | bytes 393224 | tf_op jit(solution)/shard_map/ppermute | solution.py:205
  308.0 26.9 %collective-permute-start.35 = (bf16[64,1024]{1,0:T(8,128)(2,1)S(1)}, bf16[64,1024]{1,0:T(8,128)(2,1)S(1)}, u32[]{:S(2)}, u32[]{:S(2)}) collective-permute-start(bf16[64,1024]{1,0:T(8,128)(2,1)S(1)} %bitcast.300), channel_id=1, source_target_pairs={{0,3},{1,2},{2,1},{3,0},{4,7},{5,6},{6,5},{7,4},{8,11},{9,10},{10,... | collective-permute-start | bytes 393224 | tf_op jit(solution)/shard_map/ppermute | solution.py:205
  336.3 313.7 %reduce-scatter.5.cloned.1.call-start = ((), (), s32[]{:S(2)}) async-start(), calls=%async_computation.12 | async-start | bytes 7077888 | tf_op jit(solution)/shard_map/reduce_scatter | solution.py:1489
  390.1 25.6 %collective-permute-start.37 = (bf16[512,1024]{1,0:T(8,128)(2,1)S(1)}, bf16[512,1024]{1,0:T(8,128)(2,1)}, u32[]{:S(2)}, u32[]{:S(2)}) collective-permute-start(bf16[512,1024]{1,0:T(8,128)(2,1)S(1)} %fusion.9), channel_id=1, source_target_pairs={{0,2},{1,3},{2,0},{3,1},{4,6},{5,7},{6,4},{7,5},{8,10},{9,11},{10,... | collective-permute-start | bytes 3145736 | tf_op jit(solution)/shard_map/ppermute | solution.py:60
  426.0 25.4 %collective-permute-start.39 = (bf16[512,1024]{1,0:T(8,128)(2,1)S(1)}, bf16[512,1024]{1,0:T(8,128)(2,1)}, u32[]{:S(2)}, u32[]{:S(2)}) collective-permute-start(bf16[512,1024]{1,0:T(8,128)(2,1)S(1)} %convert_element_type.228.refs_0_), channel_id=1, source_target_pairs={{0,2},{1,3},{2,0},{3,1},{4,6},{5,7},{6,4},{7,5},{8,10},{9,11},{10,... | collective-permute-start | bytes 3145736 | tf_op jit(solution)/shard_map/ppermute | solution.py:60
  467.1 26.9 %collective-permute-start.42 = (bf16[64,1024]{1,0:T(8,128)(2,1)S(1)}, bf16[64,1024]{1,0:T(8,128)(2,1)S(1)}, u32[]{:S(2)}, u32[]{:S(2)}) collective-permute-start(bf16[64,1024]{1,0:T(8,128)(2,1)S(1)} %bitcast.299), channel_id=1, source_target_pairs={{0,1},{1,0},{2,3},{3,2},{4,5},{5,4},{6,7},{7,6},{8,9},{9,8},{10,11... | collective-permute-start | bytes 393224 | tf_op jit(solution)/shard_map/ppermute | solution.py:205
  467.2 26.8 %collective-permute-start.43 = (bf16[64,1024]{1,0:T(8,128)(2,1)S(1)}, bf16[64,1024]{1,0:T(8,128)(2,1)S(1)}, u32[]{:S(2)}, u32[]{:S(2)}) collective-permute-start(bf16[64,1024]{1,0:T(8,128)(2,1)S(1)} %bitcast.298), channel_id=1, source_target_pairs={{0,2},{1,3},{2,0},{3,1},{4,6},{5,7},{6,4},{7,5},{8,10},{9,11},{10,... | collective-permute-start | bytes 393224 | tf_op jit(solution)/shard_map/ppermute | solution.py:205
  467.9 26.1 %collective-permute-start.44 = (bf16[64,1024]{1,0:T(8,128)(2,1)S(1)}, bf16[64,1024]{1,0:T(8,128)(2,1)S(1)}, u32[]{:S(2)}, u32[]{:S(2)}) collective-permute-start(bf16[64,1024]{1,0:T(8,128)(2,1)S(1)} %bitcast.297), channel_id=1, source_target_pairs={{0,3},{1,2},{2,1},{3,0},{4,7},{5,6},{6,5},{7,4},{8,11},{9,10},{10,... | collective-permute-start | bytes 393224 | tf_op jit(solution)/shard_map/ppermute | solution.py:205
  496.9 20.6 %collective-permute-start.45 = (bf16[512,1024]{1,0:T(8,128)(2,1)S(1)}, bf16[512,1024]{1,0:T(8,128)(2,1)}, u32[]{:S(2)}, u32[]{:S(2)}) collective-permute-start(bf16[512,1024]{1,0:T(8,128)(2,1)S(1)} %dynamic-slice_bitcast_fusion.3), channel_id=1, source_target_pairs={{0,1},{1,0},{2,3},{3,2},{4,5},{5,4},{6,7},{7,6},{8,9},{9,8},{10,11... | collective-permute-start | bytes 3145736 | tf_op jit(solution)/shard_map/ppermute | solution.py:65
  519.5 26.2 %collective-permute-start.46 = (bf16[512,1024]{1,0:T(8,128)(2,1)S(1)}, bf16[512,1024]{1,0:T(8,128)(2,1)}, u32[]{:S(2)}, u32[]{:S(2)}) collective-permute-start(bf16[512,1024]{1,0:T(8,128)(2,1)S(1)} %fusion.7), channel_id=1, source_target_pairs={{0,2},{1,3},{2,0},{3,1},{4,6},{5,7},{6,4},{7,5},{8,10},{9,11},{10,... | collective-permute-start | bytes 3145736 | tf_op jit(solution)/shard_map/ppermute | solution.py:60
  522.8 46.4 %collective-permute-start.47 = (bf16[32,1024]{1,0:T(8,128)(2,1)}, bf16[32,1024]{1,0:T(8,128)(2,1)}, u32[]{:S(2)}, u32[]{:S(2)}) collective-permute-start(bf16[32,1024]{1,0:T(8,128)(2,1)} %get-tuple-element.683), channel_id=1, source_target_pairs={{0,1},{1,0},{2,3},{3,2},{4,5},{5,4},{6,7},{7,6},{8,9},{9,8},{10,11... | collective-permute-start | bytes 196616 | tf_op jit(solution)/shard_map/ppermute | solution.py:205
  522.8 46.4 %collective-permute-start.48 = (bf16[32,1024]{1,0:T(8,128)(2,1)}, bf16[32,1024]{1,0:T(8,128)(2,1)}, u32[]{:S(2)}, u32[]{:S(2)}) collective-permute-start(bf16[32,1024]{1,0:T(8,128)(2,1)} %get-tuple-element.684), channel_id=1, source_target_pairs={{0,2},{1,3},{2,0},{3,1},{4,6},{5,7},{6,4},{7,5},{8,10},{9,11},{10,... | collective-permute-start | bytes 196616 | tf_op jit(solution)/shard_map/ppermute | solution.py:205
  524.2 45.0 %collective-permute-start.49 = (bf16[32,1024]{1,0:T(8,128)(2,1)}, bf16[32,1024]{1,0:T(8,128)(2,1)}, u32[]{:S(2)}, u32[]{:S(2)}) collective-permute-start(bf16[32,1024]{1,0:T(8,128)(2,1)} %get-tuple-element.682), channel_id=1, source_target_pairs={{0,3},{1,2},{2,1},{3,0},{4,7},{5,6},{6,5},{7,4},{8,11},{9,10},{10,... | collective-permute-start | bytes 196616 | tf_op jit(solution)/shard_map/ppermute | solution.py:205
  566.5 45.4 %all-to-all-start.4 = ((bf16[32,32,512]{2,1,0:T(8,128)(2,1)}), bf16[32,32,512]{2,1,0:T(8,128)(2,1)S(1)}, u32[]{:S(2)}, u32[]{:S(2)}) async-start(bf16[32,32,512]{2,1,0:T(8,128)(2,1)} %bitcast.275), calls=%async_computation.5 | async-start | bytes 2097152 | tf_op jit(solution)/shard_map/all_to_all | solution.py:185
  594.0 30.6 %collective-permute-start.51 = (bf16[512,1024]{1,0:T(8,128)(2,1)}, bf16[512,1024]{1,0:T(8,128)(2,1)}, u32[]{:S(2)}, u32[]{:S(2)}) collective-permute-start(bf16[512,1024]{1,0:T(8,128)(2,1)} %fusion.6), channel_id=1, source_target_pairs={{0,2},{1,3},{2,0},{3,1},{4,6},{5,7},{6,4},{7,5},{8,10},{9,11},{10,... | collective-permute-start | bytes 3145736 | tf_op jit(solution)/shard_map/ppermute | solution.py:60
  596.8 29.7 %collective-permute-start.53 = (bf16[512,1024]{1,0:T(8,128)(2,1)}, bf16[512,1024]{1,0:T(8,128)(2,1)}, u32[]{:S(2)}, u32[]{:S(2)}) collective-permute-start(bf16[512,1024]{1,0:T(8,128)(2,1)} %dynamic-slice_bitcast_fusion), channel_id=1, source_target_pairs={{0,1},{1,0},{2,3},{3,2},{4,5},{5,4},{6,7},{7,6},{8,9},{9,8},{10,11... | collective-permute-start | bytes 3145736 | tf_op jit(solution)/shard_map/ppermute | solution.py:65
  611.9 31.5 %all-to-all-start.5 = ((bf16[32,32,512]{2,1,0:T(8,128)(2,1)}), bf16[32,32,512]{2,1,0:T(8,128)(2,1)}, u32[]{:S(2)}, u32[]{:S(2)}) async-start(bf16[32,32,512]{2,1,0:T(8,128)(2,1)} %bitcast.276), calls=%async_computation.6 | async-start | bytes 2097152 | tf_op jit(solution)/shard_map/all_to_all | solution.py:185
  654.6 10.7 %all-to-all-start.6 = ((f32[32,1,128]{2,1,0:T(1,128)}), f32[32,1,128]{2,1,0:T(1,128)S(1)}, u32[]{:S(2)}, u32[]{:S(2)}) async-start(f32[32,1,128]{2,1,0:T(1,128)} %broadcast_in_dim.42), calls=%async_computation.8 | async-start | bytes 32768 | tf_op jit(solution)/shard_map/all_to_all | solution.py:1557
  (101 other events, 1079.7 us)
Sparse Core Ops, SparseCore 0:
  31.4 44.1 all-gather.2
  148.7 84.2 all-gather.4
  336.4 93.3 reduce-scatter.2
  495.6 127.6 reduce-scatter.4

commit v7 on v6

--- a/solution.py
+++ b/solution.py
@@ -31,7 +31,7 @@
 QUERY_SCALE = 1.0 / math.sqrt(HD)
 BF = jnp.bfloat16
 F32 = jnp.float32
-VMEM_LIMIT = 60 * 1024 * 1024
+VMEM_LIMIT = 62 * 1024 * 1024
 LIGHT = pl.CostEstimate(flops=1000, bytes_accessed=1000, transcendentals=0)
 
 

time: 699 us -> 697 us (level)
  transfers between devices with their start and end apart: 68 -> 68, of which waited for: 25 -> 25; matrix products, arithmetic and copies ran while one was open for 13% -> 12% of each run, Pallas kernels for 46% -> 47%
where the time goes in v7:
time: 697 us; the launch traced here: 686 us
  Pallas kernels  351 us (50%)
  waiting for transfers between devices  136 us (20%)
  starting transfers between devices  70.3 us (10%)
  other arithmetic  57.1 us (8%)
  local copies, waits for them, and re-layouts  44.8 us (6%)
  between operations  21.1 us (3%)
    pallas_call x4, Pallas kernels, attend_back(): pl.pallas_call(attend_back_kernel, grid=(length // block,), in_specs=[pl....  80.5 us
    pallas_call x2, Pallas kernels, feed_back(): pl.pallas_call(partial(feed_back_kernel, joined, 9 + len(kept)), grid=(le...  49.8 us
    pallas_call x4, Pallas kernels, attend(): pl.pallas_call(attend_kernel, grid=(length // block,), in_specs=[pl.Block...  46.3 us
    pallas_call x3, Pallas kernels, feed(): pl.pallas_call(partial(feed_kernel, first is not None, last is not None,...  44.1 us
    ppermute x8, waiting for transfers between devices, chip_ring(): lax.ppermute(value, 'seq', [(i, (i + 2) % size) for i in range(size)])  40.2 us
    pallas_call x4, Pallas kernels, norm_grad(): pl.pallas_call(norm_grad_kernel, grid_spec=pltpu.PrefetchScalarGridSpec(n...  34.5 us
    pallas_call x3, Pallas kernels, mix(): pl.pallas_call(partial(mix_kernel, count, len(pieces)), grid_spec=pltpu.P...  25.3 us
    ppermute x9, waiting for transfers between devices, outer_ring(): lax.ppermute(value, 'dp', [(i, (i + inner) % size) for i in range(size)])  25.1 us
  transfers between devices with their start and end apart: 68, of which 25 were waited for; matrix products, arithmetic and copies ran while one was open for 12% of the time, Pallas kernels for 47%

profile of v7, /device:TPU:0, one launch (start us, length us, event | category | flops | bytes accessed | tf_op | source)
XLA Modules:
  0.0 685.9 jit_solution(2664777344717322195)
XLA Ops:
  10.6 4.4 all-to-all-start
  36.9 3.9 all-to-all-start.1
  44.1 4.4 all-to-all-done.1
  55.9 9.8 %collective-permute-done.6.refs_15_ = bf16[128,768]{1,0:T(8,128)(2,1)S(1)} collective-permute-done((bf16[128,768]{1,0:T(8,128)(2,1)S(1)}, bf16[128,768]{1,0:T(8,128)(2,1)S(1)}, u32[]{:S(2)}, u32[]{:S(2)}) %collective-permute-start.6) | collective-permute-done | bytes 196640 | tf_op jit(solution)/shard_map/ppermute | solution.py:47
  68.0 5.7 collective-permute-done.8.refs_14_
  80.2 11.1 %mix.3 = (bf16[2048,1024]{1,0:T(8,128)(2,1)}, bf16[2048,768]{1,0:T(8,128)(2,1)}, bf16[1024,768]{1,0:T(8,128)(2,1)}, bf16[1024,768]{1,0:T(8,128)(2,1)}, f32[8,768]{1,0:T(8,128)}) custom-call(s32[4]{0:T(128)} %pad_add_fusion.x_slots_ref.slots_ref, s32[8]{0:T(128)} %stack.201.slots_ref, bf16[512,1024]{1,0:T(8,128)(2,1)} %fusion.15.refs_0_, ...), custom_call_target="tpu_custom_call" | custom-call | flops 1000 | bytes 1000 | tf_op jit(solution)/shard_map/mix/pallas_call | solution.py:336
  93.9 11.6 %attend.4 = (bf16[2048,128]{1,0:T(8,128)(2,1)}, f32[2,2048]{1,0:T(2,128)}) custom-call(bf16[2048,768]{1,0:T(8,128)(2,1)} %get-tuple-element.581.q_ref.k_ref.v_ref, bf16[2048,768]{1,0:T(8,128)(2,1)} %get-tuple-element.581.q_ref.k_ref.v_ref, bf16[2048,768]{1,0:T(8,128)(2,1)} %get-tuple-element.581.q_ref.k_ref.v_ref), custom_call_target="tpu_custom_call" | custom-call | flops 1000 | bytes 1000 | tf_op jit(solution)/shard_map/attend/pallas_call | solution.py:399
  105.4 3.8 all-to-all-start.2
  112.2 8.1 %all-to-all-done.2 = bf16[4,32,1792]{2,1,0:T(8,128)(2,1)S(1)} async-done(((bf16[4,32,1792]{2,1,0:T(8,128)(2,1)}), bf16[4,32,1792]{2,1,0:T(8,128)(2,1)S(1)}, u32[]{:S(2)}, u32[]{:S(2)}) %all-to-all-start.2) | async-done | bytes 458784 | tf_op jit(solution)/shard_map/all_to_all | solution.py:219
  123.4 11.6 %attend.5 = (bf16[2048,128]{1,0:T(8,128)(2,1)}, f32[2,2048]{1,0:T(2,128)}) custom-call(bf16[2048,768]{1,0:T(8,128)(2,1)} %get-tuple-element.581.q_ref.k_ref.v_ref, bf16[2048,768]{1,0:T(8,128)(2,1)} %get-tuple-element.581.q_ref.k_ref.v_ref, bf16[2048,768]{1,0:T(8,128)(2,1)} %get-tuple-element.581.q_ref.k_ref.v_ref), custom_call_target="tpu_custom_call" | custom-call | flops 1000 | bytes 1000 | tf_op jit(solution)/shard_map/attend/pallas_call | solution.py:399
  137.1 4.3 all-to-all-start.3
  145.3 5.3 assemble.2
  150.6 5.3 all-to-all-done.3
  162.6 16.3 %feed.3 = (bf16[2048,1024]{1,0:T(8,128)(2,1)}, bf16[2048,1024]{1,0:T(8,128)(2,1)}, bf16[1024,1024]{1,0:T(8,128)(2,1)}, f32[8,1024]{1,0:T(8,128)}, bf16[1024,1024...) custom-call(s32[1]{0:T(128)} %bitcast.41.y_ref, s32[8]{0:T(128)} %stack.201.slots_ref, ...), custom_call_target="tpu_custom_call" | custom-call | flops 1000 | bytes 1000 | tf_op jit(solution)/shard_map/feed/pallas_call | solution.py:699
  190.6 13.0 %feed.4 = (bf16[2048,1024]{1,0:T(8,128)(2,1)}, bf16[2048,1024]{1,0:T(8,128)(2,1)}, bf16[1024,1024]{1,0:T(8,128)(2,1)}) custom-call(s32[1]{0:T(128)} %bitcast.41.y_ref, s32[1]{0:T(128)} %constant.382.clone.1.slots_ref, bf16[2048,1024]{1,0:T(8,128)(2,1)} %get-tuple-element.379.x_ref.refs_4_, ...), custom_call_target="tpu_custom_call", output_to_operand_aliasing={{0}: (9, {}), {1}: (10, {})} | custom-call | flops 1000 | bytes 1000 | tf_op jit(solution)/shard_map/feed/pallas_call | solution.py:699
  205.2 12.2 %collective-permute-done.26.refs_13_ = bf16[128,768]{1,0:T(8,128)(2,1)S(1)} collective-permute-done((bf16[128,768]{1,0:T(8,128)(2,1)S(1)}, bf16[128,768]{1,0:T(8,128)(2,1)S(1)}, u32[]{:S(2)}, u32[]{:S(2)}) %collective-permute-start.26) | collective-permute-done | bytes 196640 | tf_op jit(solution)/shard_map/ppermute | solution.py:47
  228.5 4.3 collective-permute-done.30.refs_14_
  233.8 7.8 %mix.4 = (bf16[2048,1024]{1,0:T(8,128)(2,1)}, bf16[2048,768]{1,0:T(8,128)(2,1)}, bf16[1024,768]{1,0:T(8,128)(2,1)}, bf16[1024,768]{1,0:T(8,128)(2,1)}, f32[8,768]{1,0:T(8,128)}) custom-call(s32[2]{0:T(128)} %pad_add_fusion.2.x_slots_ref, s32[8]{0:T(128)} %stack.201.slots_ref, bf16[512,1024]{1,0:T(8,128)(2,1)} %copy-done.18, bf16[512,1024]{1,0:T(8,128)(2,1)} %copy-done.26, ...), custom_call_target="tpu_custom_call" | custom-call | flops 1000 | bytes 1000 | tf_op jit(solution)/shard_map/mix/pallas_call | solution.py:336
  241.7 9.5 %collective-permute-done.31.refs_0_ = bf16[512,1024]{1,0:T(8,128)(2,1)} collective-permute-done((bf16[512,1024]{1,0:T(8,128)(2,1)S(1)}, bf16[512,1024]{1,0:T(8,128)(2,1)}, u32[]{:S(2)}, u32[]{:S(2)}) %collective-permute-start.31) | collective-permute-done | bytes 1048608 | tf_op jit(solution)/shard_map/ppermute | solution.py:60
  255.0 6.4 mix.5
  261.4 11.6 %attend.6 = (bf16[2048,128]{1,0:T(8,128)(2,1)}, f32[2,2048]{1,0:T(2,128)}) custom-call(bf16[2048,768]{1,0:T(8,128)(2,1)} %get-tuple-element.479.q_ref.k_ref.v_ref, bf16[2048,768]{1,0:T(8,128)(2,1)} %get-tuple-element.479.q_ref.k_ref.v_ref, bf16[2048,768]{1,0:T(8,128)(2,1)} %get-tuple-element.479.q_ref.k_ref.v_ref), custom_call_target="tpu_custom_call" | custom-call | flops 1000 | bytes 1000 | tf_op jit(solution)/shard_map/attend/pallas_call | solution.py:399
  273.0 11.6 %attend.7 = (bf16[2048,128]{1,0:T(8,128)(2,1)}, f32[2,2048]{1,0:T(2,128)}) custom-call(bf16[2048,768]{1,0:T(8,128)(2,1)} %get-tuple-element.479.q_ref.k_ref.v_ref, bf16[2048,768]{1,0:T(8,128)(2,1)} %get-tuple-element.479.q_ref.k_ref.v_ref, bf16[2048,768]{1,0:T(8,128)(2,1)} %get-tuple-element.479.q_ref.k_ref.v_ref), custom_call_target="tpu_custom_call" | custom-call | flops 1000 | bytes 1000 | tf_op jit(solution)/shard_map/attend/pallas_call | solution.py:399
  284.6 14.8 %feed.5 = (bf16[2048,1024]{1,0:T(8,128)(2,1)}, bf16[2048,1024]{1,0:T(8,128)(2,1)}, bf16[1024,1024]{1,0:T(8,128)(2,1)}, f32[8,1024]{1,0:T(8,128)}) custom-call(s32[1]{0:T(128)} %bitcast.41.y_ref, s32[1]{0:T(128)} %constant.382.clone.1.slots_ref, bf16[2048,1024]{1,0:T(8,128)(2,1)} %get-tuple-element.477.x_ref.refs_4_, f32[1,1024]{1,0:T(1,128)} %get-tuple-element.722, ...), custom_call_target="tpu_custom_call" | custom-call | flops 1000 | bytes 1000 | tf_op jit(solution)/shard_map/feed/pallas_call | solution.py:699
  299.3 4.0 product.2
  307.2 25.0 %feed_back.2 = (bf16[2048,1024]{1,0:T(8,128)(2,1)}, f32[1,1024]{1,0:T(1,128)}, bf16[2048,256]{1,0:T(8,128)(2,1)}, f32[1,1024]{1,0:T(1,128)}, f32[1,1024]{1,0:T(1,128)}, /*index=5*/bf16[1024,2304]{1,0:T(8,128)(2,1)}) custom-call(bf16[2048,1024]{1,0:T(8,128)(2,1)} %bitcast.253, ...), custom_call_target="tpu_custom_call" | custom-call | flops 1000 | bytes 1000 | tf_op jit(solution)/shard_map/feed_back/pallas_call | solution.py:950
  333.7 20.4 %attend_back.4 = (bf16[2048,384]{1,0:T(8,128)(2,1)}, f32[1,384]{1,0:T(1,128)}) custom-call(bf16[2048,768]{1,0:T(8,128)(2,1)} %get-tuple-element.479.q_ref.k_ref.v_ref, bf16[2048,768]{1,0:T(8,128)(2,1)} %get-tuple-element.479.q_ref.k_ref.v_ref, bf16[2048,768]{1,0:T(8,128)(2,1)} %get-tuple-element.479.q_ref.k_ref.v_ref, ...), custom_call_target="tpu_custom_call" | custom-call | flops 1000 | bytes 1000 | tf_op jit(solution)/shard_map/attend_back/pallas_call | solution.py:528
  354.2 20.0 %attend_back.5 = (bf16[2048,384]{1,0:T(8,128)(2,1)}, f32[1,384]{1,0:T(1,128)}) custom-call(bf16[2048,768]{1,0:T(8,128)(2,1)} %get-tuple-element.479.q_ref.k_ref.v_ref, bf16[2048,768]{1,0:T(8,128)(2,1)} %get-tuple-element.479.q_ref.k_ref.v_ref, bf16[2048,768]{1,0:T(8,128)(2,1)} %get-tuple-element.479.q_ref.k_ref.v_ref, ...), custom_call_target="tpu_custom_call" | custom-call | flops 1000 | bytes 1000 | tf_op jit(solution)/shard_map/attend_back/pallas_call | solution.py:528
  374.2 8.6 %norm_grad.4 = bf16[1024,1024]{1,0:T(8,128)(2,1)} custom-call(s32[1]{0:T(128)} %bitcast.41.y_ref, bf16[2048,1024]{1,0:T(8,128)(2,1)} %get-tuple-element.524.h_ref, bf16[1024,1024]{1,0:T(8,128)(2,1)} %get-tuple-element.522.wi_ref, bf16[1024,768]{1,0:T(8,128)(2,1)} %get-tuple-element.473.refs_4_.wm_ref, bf16[2048,384]{1,0:T(8,128)(2,1)} %get-tuple-element.533.refs_0_, ...), custom_call_target="tpu_custom_call" | custom-call | flops 1000 | bytes 1000 | tf_op jit(solution)/shard_map/norm_grad/pallas_call | solution.py:763
  387.8 7.1 %branch.2 = bf16[1024,1024]{1,0:T(8,128)(2,1)} custom-call(s32[1]{0:T(128)} %bitcast.41.y_ref, bf16[2048,1024]{1,0:T(8,128)(2,1)} %get-tuple-element.527.refs_3_.act_ref, bf16[1024,2048]{1,0:T(8,128)(2,1)} %all-gather.5.cloned.1.call-done.refs_3_.refs_1_.refs_6_.shrink_ref, bf16[256,1024]{1,0:T(8,128)(2,1)} %bitcast.261, ...), custom_call_target="tpu_custom_call" | custom-call | flops 1000 | bytes 1000 | tf_op jit(solution)/shard_map/branch/pallas_call | solution.py:726
  394.9 7.0 %branch.3 = bf16[1024,1024]{1,0:T(8,128)(2,1)} custom-call(s32[1]{0:T(128)} %bitcast.41.y_ref, bf16[2048,1024]{1,0:T(8,128)(2,1)} %get-tuple-element.527.refs_3_.act_ref, bf16[1024,2048]{1,0:T(8,128)(2,1)} %all-gather.5.cloned.1.call-done.refs_3_.refs_1_.refs_6_.shrink_ref, bf16[256,1024]{1,0:T(8,128)(2,1)} %bitcast.262, ...), custom_call_target="tpu_custom_call" | custom-call | flops 1000 | bytes 1000 | tf_op jit(solution)/shard_map/branch/pallas_call | solution.py:726
  401.9 8.7 %norm_grad.5 = bf16[1024,1024]{1,0:T(8,128)(2,1)} custom-call(s32[1]{0:T(128)} %bitcast.41.y_ref, bf16[2048,1024]{1,0:T(8,128)(2,1)} %get-tuple-element.524.h_ref, bf16[1024,1024]{1,0:T(8,128)(2,1)} %get-tuple-element.522.wi_ref, bf16[1024,768]{1,0:T(8,128)(2,1)} %get-tuple-element.473.refs_4_.wm_ref, bf16[2048,384]{1,0:T(8,128)(2,1)} %get-tuple-element.533.refs_0_, ...), custom_call_target="tpu_custom_call" | custom-call | flops 1000 | bytes 1000 | tf_op jit(solution)/shard_map/norm_grad/pallas_call | solution.py:763
  423.7 9.1 %weight_grad.3 = (bf16[1024,3072]{1,0:T(8,128)(2,1)}, f32[1,1024]{1,0:T(1,128)}, f32[1,1024]{1,0:T(1,128)}) custom-call(bf16[2048,1024]{1,0:T(8,128)(2,1)} %get-tuple-element.477.x_ref.refs_4_, bf16[1024,768]{1,0:T(8,128)(2,1)} %get-tuple-element.478.weight_ref, f32[1,1024]{1,0:T(1,128)} %get-tuple-element.724, f32[1,1024]{1,0:T(1,128)} %get-tuple-element.723, ...), custom_call_target="tpu_custom_call" | custom-call | flops 1000 | bytes 1000 | tf_op jit(solution)/shard_map/weight_grad/pallas_call | solution.py:824
  432.8 15.3 %collective-permute-done.39.refs_2_ = bf16[512,1024]{1,0:T(8,128)(2,1)} collective-permute-done((bf16[512,1024]{1,0:T(8,128)(2,1)S(1)}, bf16[512,1024]{1,0:T(8,128)(2,1)}, u32[]{:S(2)}, u32[]{:S(2)}) %collective-permute-start.39) | collective-permute-done | bytes 1048608 | tf_op jit(solution)/shard_map/ppermute | solution.py:60
  453.2 5.4 assemble.3
  458.7 4.0 product.3
  466.0 24.8 %feed_back.3 = (bf16[2048,1024]{1,0:T(8,128)(2,1)}, f32[1,1024]{1,0:T(1,128)}, bf16[2048,256]{1,0:T(8,128)(2,1)}, f32[1,1024]{1,0:T(1,128)}, f32[1,1024]{1,0:T(1,128)}, /*index=5*/bf16[1024,3072]{1,0:T(8,128)(2,1)}) custom-call(bf16[2048,1024]{1,0:T(8,128)(2,1)} %bitcast.251, ...), custom_call_target="tpu_custom_call", output_to_operand_aliasing={{5}: (9, {})} | custom-call | flops 1000 | bytes 1000 | tf_op jit(solution)/shard_map/feed_back/pallas_call | solution.py:950
  494.3 20.0 %attend_back.6 = (bf16[2048,384]{1,0:T(8,128)(2,1)}, f32[1,384]{1,0:T(1,128)}) custom-call(bf16[2048,768]{1,0:T(8,128)(2,1)} %get-tuple-element.581.q_ref.k_ref.v_ref, bf16[2048,768]{1,0:T(8,128)(2,1)} %get-tuple-element.581.q_ref.k_ref.v_ref, bf16[2048,768]{1,0:T(8,128)(2,1)} %get-tuple-element.581.q_ref.k_ref.v_ref, ...), custom_call_target="tpu_custom_call" | custom-call | flops 1000 | bytes 1000 | tf_op jit(solution)/shard_map/attend_back/pallas_call | solution.py:528
  520.7 7.0 %weight_grad.4 = (bf16[1024,384]{1,0:T(8,128)(2,1)}, f32[1,1024]{1,0:T(1,128)}, f32[1,1024]{1,0:T(1,128)}) custom-call(bf16[2048,1024]{1,0:T(8,128)(2,1)} %get-tuple-element.379.x_ref.refs_4_, bf16[1024,768]{1,0:T(8,128)(2,1)} %get-tuple-element.380.weight_ref, f32[1,1024]{1,0:T(1,128)} %get-tuple-element.730, f32[1,1024]{1,0:T(1,128)} %get-tuple-element.729, ...), custom_call_target="tpu_custom_call" | custom-call | flops 1000 | bytes 1000 | tf_op jit(solution)/shard_map/weight_grad/pallas_call | solution.py:824
  529.9 12.8 %collective-permute-done.46 = bf16[512,1024]{1,0:T(8,128)(2,1)} collective-permute-done((bf16[512,1024]{1,0:T(8,128)(2,1)S(1)}, bf16[512,1024]{1,0:T(8,128)(2,1)}, u32[]{:S(2)}, u32[]{:S(2)}) %collective-permute-start.46) | collective-permute-done | bytes 1048608 | tf_op jit(solution)/shard_map/ppermute | solution.py:60
  542.7 20.0 %attend_back.7 = (bf16[2048,384]{1,0:T(8,128)(2,1)}, f32[1,384]{1,0:T(1,128)}) custom-call(bf16[2048,768]{1,0:T(8,128)(2,1)} %get-tuple-element.581.q_ref.k_ref.v_ref, bf16[2048,768]{1,0:T(8,128)(2,1)} %get-tuple-element.581.q_ref.k_ref.v_ref, bf16[2048,768]{1,0:T(8,128)(2,1)} %get-tuple-element.581.q_ref.k_ref.v_ref, ...), custom_call_target="tpu_custom_call" | custom-call | flops 1000 | bytes 1000 | tf_op jit(solution)/shard_map/attend_back/pallas_call | solution.py:528
  566.6 8.6 %norm_grad.6 = bf16[1024,1024]{1,0:T(8,128)(2,1)} custom-call(s32[1]{0:T(128)} %bitcast.41.y_ref, bf16[2048,1024]{1,0:T(8,128)(2,1)} %get-tuple-element.585.h_ref, bf16[1024,1024]{1,0:T(8,128)(2,1)} %get-tuple-element.441.refs_0_.wi_ref, bf16[1024,768]{1,0:T(8,128)(2,1)} %get-tuple-element.586.wm_ref, bf16[2048,384]{1,0:T(8,128)(2,1)} %get-tuple-element.605.refs_0_, ...), custom_call_target="tpu_custom_call" | custom-call | flops 1000 | bytes 1000 | tf_op jit(solution)/shard_map/norm_grad/pallas_call | solution.py:763
  575.2 7.3 %weight_grad.5 = (bf16[1024,384]{1,0:T(8,128)(2,1)}, f32[1,1024]{1,0:T(1,128)}, f32[1,1024]{1,0:T(1,128)}) custom-call(bf16[2048,1024]{1,0:T(8,128)(2,1)} %get-tuple-element.379.x_ref.refs_4_, bf16[1024,768]{1,0:T(8,128)(2,1)} %get-tuple-element.380.weight_ref, f32[1,1024]{1,0:T(1,128)} %get-tuple-element.730, f32[1,1024]{1,0:T(1,128)} %get-tuple-element.729, ...), custom_call_target="tpu_custom_call" | custom-call | flops 1000 | bytes 1000 | tf_op jit(solution)/shard_map/weight_grad/pallas_call | solution.py:824
  596.2 13.3 %all-to-all-done.4 = bf16[32,32,512]{2,1,0:T(8,128)(2,1)S(1)} async-done(((bf16[32,32,512]{2,1,0:T(8,128)(2,1)}), bf16[32,32,512]{2,1,0:T(8,128)(2,1)S(1)}, u32[]{:S(2)}, u32[]{:S(2)}) %all-to-all-start.4) | async-done | bytes 1048608 | tf_op jit(solution)/shard_map/all_to_all | solution.py:185
  613.1 8.6 %norm_grad.7 = bf16[1024,1024]{1,0:T(8,128)(2,1)} custom-call(s32[1]{0:T(128)} %bitcast.41.y_ref, bf16[2048,1024]{1,0:T(8,128)(2,1)} %get-tuple-element.585.h_ref, bf16[1024,1024]{1,0:T(8,128)(2,1)} %get-tuple-element.441.refs_0_.wi_ref, bf16[1024,768]{1,0:T(8,128)(2,1)} %get-tuple-element.586.wm_ref, bf16[2048,384]{1,0:T(8,128)(2,1)} %get-tuple-element.605.refs_0_, ...), custom_call_target="tpu_custom_call" | custom-call | flops 1000 | bytes 1000 | tf_op jit(solution)/shard_map/norm_grad/pallas_call | solution.py:763
  623.6 4.1 fusion.4
  635.1 5.6 all-to-all-done.5
  651.9 3.9 all-to-all-start.6
  667.4 10.5 %update.1 = (f32[2,32,3072]{2,1,0:T(8,128)}, f32[2,32,3072]{2,1,0:T(8,128)}, f32[2,32,3072]{2,1,0:T(8,128)}, f32[2,32,3072]{2,1,0:T(8,128)}, f32[2,32,1024]{2,1,...) custom-call(f32[1]{0:T(128)} %bitcast.140.clip_ref, ...), custom_call_target="tpu_custom_call" | custom-call | flops 1000 | bytes 1000 | tf_op jit(solution)/shard_map/update/pallas_call | solution.py:1041
  (478 shorter events, 186.9 us)
Async XLA Ops:
  10.6 13.5 %all-to-all-start = ((bf16[4,32,1824]{2,1,0:T(8,128)(2,1)}), bf16[4,32,1824]{2,1,0:T(8,128)(2,1)S(1)}, u32[]{:S(2)}, u32[]{:S(2)}) async-start(bf16[4,32,1824]{2,1,0:T(8,128)(2,1)} %pack.2), calls=%async_computation | async-start | bytes 983040 | tf_op jit(solution)/shard_map/all_to_all | solution.py:219
  15.0 76.3 %all-gather.3.cloned.1.call-start = ((), (), s32[]{:S(2)}) async-start(), calls=%async_computation.9 | async-start | bytes 1179648 | tf_op jit(solution)/shard_map/all_gather | solution.py:1234
  18.4 33.3 %collective-permute-start.3 = (bf16[512,1024]{1,0:T(8,128)(2,1)}, bf16[512,1024]{1,0:T(8,128)(2,1)}, u32[]{:S(2)}, u32[]{:S(2)}) collective-permute-start(bf16[512,1024]{1,0:T(8,128)(2,1)} %fusion.15.refs_0_), channel_id=1, source_target_pairs={{0,2},{1,3},{2,0},{3,1},{4,6},{5,7},{6,4},{7,5},{8,10},{9,11},{10,... | collective-permute-start | bytes 3145736 | tf_op jit(solution)/shard_map/ppermute | solution.py:60
  36.9 11.6 %all-to-all-start.1 = ((bf16[32,2,416]{2,1,0:T(2,128)(2,1)}), bf16[32,2,416]{2,1,0:T(2,128)(2,1)S(1)}, u32[]{:S(2)}, u32[]{:S(2)}) async-start(bf16[32,2,416]{2,1,0:T(2,128)(2,1)} %reshape.488), calls=%async_computation.1 | async-start | bytes 131072 | tf_op jit(solution)/shard_map/all_to_all | solution.py:1249
  40.8 10.9 %collective-permute-start.1 = (bf16[128,768]{1,0:T(8,128)(2,1)}, bf16[128,768]{1,0:T(8,128)(2,1)S(1)}, u32[]{:S(2)}, u32[]{:S(2)}) collective-permute-start(bf16[128,768]{1,0:T(8,128)(2,1)} %collective-permute-done.refs_11_), channel_id=1, source_target_pairs={{0,8},{4,12},{8,16},{12,20},{16,24},{20,28},{24,0},{28,4},{1,9},{5... | collective-permute-start | bytes 589832 | tf_op jit(solution)/shard_map/ppermute | solution.py:47
  52.7 13.1 %collective-permute-start.4 = (bf16[512,1024]{1,0:T(8,128)(2,1)}, bf16[512,1024]{1,0:T(8,128)(2,1)S(1)}, u32[]{:S(2)}, u32[]{:S(2)}) collective-permute-start(bf16[512,1024]{1,0:T(8,128)(2,1)} %fusion.15.refs_0_), channel_id=1, source_target_pairs={{0,1},{1,0},{2,3},{3,2},{4,5},{5,4},{6,7},{7,6},{8,9},{9,8},{10,11... | collective-permute-start | bytes 3145736 | tf_op jit(solution)/shard_map/ppermute | solution.py:65
  52.7 13.1 %collective-permute-start.5 = (bf16[512,1024]{1,0:T(8,128)(2,1)}, bf16[512,1024]{1,0:T(8,128)(2,1)S(1)}, u32[]{:S(2)}, u32[]{:S(2)}) collective-permute-start(bf16[512,1024]{1,0:T(8,128)(2,1)} %collective-permute-done.3.refs_2_), channel_id=1, source_target_pairs={{0,1},{1,0},{2,3},{3,2},{4,5},{5,4},{6,7},{7,6},{8,9},{9,8},{10,11... | collective-permute-start | bytes 3145736 | tf_op jit(solution)/shard_map/ppermute | solution.py:65
  53.2 12.5 %collective-permute-start.6 = (bf16[128,768]{1,0:T(8,128)(2,1)S(1)}, bf16[128,768]{1,0:T(8,128)(2,1)S(1)}, u32[]{:S(2)}, u32[]{:S(2)}) collective-permute-start(bf16[128,768]{1,0:T(8,128)(2,1)S(1)} %collective-permute-done.1.refs_13_), channel_id=1, source_target_pairs={{0,8},{4,12},{8,16},{12,20},{16,24},{20,28},{24,0},{28,4},{1,9},{5... | collective-permute-start | bytes 589832 | tf_op jit(solution)/shard_map/ppermute | solution.py:47
  53.2 12.5 %collective-permute-start.7 = (bf16[128,768]{1,0:T(8,128)(2,1)}, bf16[128,768]{1,0:T(8,128)(2,1)S(1)}, u32[]{:S(2)}, u32[]{:S(2)}) collective-permute-start(bf16[128,768]{1,0:T(8,128)(2,1)} %collective-permute-done.refs_11_), channel_id=1, source_target_pairs={{0,4},{4,0},{8,12},{12,8},{16,20},{20,16},{24,28},{28,24},{1,5},{5... | collective-permute-start | bytes 589832 | tf_op jit(solution)/shard_map/ppermute | solution.py:55
  76.4 14.8 %collective-permute-start.10 = (bf16[128,2048]{1,0:T(8,128)(2,1)S(1)}, bf16[128,2048]{1,0:T(8,128)(2,1)}, u32[]{:S(2)}, u32[]{:S(2)}) collective-permute-start(bf16[128,2048]{1,0:T(8,128)(2,1)S(1)} %pad_maximum_fusion.3.refs_3_), channel_id=1, source_target_pairs={{0,8},{4,12},{8,16},{12,20},{16,24},{20,28},{24,0},{28,4},{1,9},{5... | collective-permute-start | bytes 1572872 | tf_op jit(solution)/shard_map/ppermute | solution.py:47
  76.5 14.8 %collective-permute-start.11 = (bf16[128,2048]{1,0:T(8,128)(2,1)S(1)}, bf16[128,2048]{1,0:T(8,128)(2,1)}, u32[]{:S(2)}, u32[]{:S(2)}) collective-permute-start(bf16[128,2048]{1,0:T(8,128)(2,1)S(1)} %pad_maximum_fusion.3.refs_3_), channel_id=1, source_target_pairs={{0,4},{4,0},{8,12},{12,8},{16,20},{20,16},{24,28},{28,24},{1,5},{5... | collective-permute-start | bytes 1572872 | tf_op jit(solution)/shard_map/ppermute | solution.py:55
  91.3 29.1 %collective-permute-start.12 = (bf16[128,2048]{1,0:T(8,128)(2,1)}, bf16[128,2048]{1,0:T(8,128)(2,1)}, u32[]{:S(2)}, u32[]{:S(2)}) collective-permute-start(bf16[128,2048]{1,0:T(8,128)(2,1)} %collective-permute-done.10.refs_5_), channel_id=1, source_target_pairs={{0,8},{4,12},{8,16},{12,20},{16,24},{20,28},{24,0},{28,4},{1,9},{5... | collective-permute-start | bytes 1572872 | tf_op jit(solution)/shard_map/ppermute | solution.py:47
  92.3 28.1 %collective-permute-start.13 = (bf16[128,2048]{1,0:T(8,128)(2,1)}, bf16[128,2048]{1,0:T(8,128)(2,1)}, u32[]{:S(2)}, u32[]{:S(2)}) collective-permute-start(bf16[128,2048]{1,0:T(8,128)(2,1)} %collective-permute-done.10.refs_5_), channel_id=1, source_target_pairs={{0,4},{4,0},{8,12},{12,8},{16,20},{20,16},{24,28},{28,24},{1,5},{5... | collective-permute-start | bytes 1572872 | tf_op jit(solution)/shard_map/ppermute | solution.py:55
  92.6 43.9 %collective-permute-start.14 = (bf16[512,1024]{1,0:T(8,128)(2,1)S(1)}, bf16[512,1024]{1,0:T(8,128)(2,1)}, u32[]{:S(2)}, u32[]{:S(2)}) collective-permute-start(bf16[512,1024]{1,0:T(8,128)(2,1)S(1)} %get-tuple-element.414.refs_0_), channel_id=1, source_target_pairs={{0,2},{1,3},{2,0},{3,1},{4,6},{5,7},{6,4},{7,5},{8,10},{9,11},{10,... | collective-permute-start | bytes 3145736 | tf_op jit(solution)/shard_map/ppermute | solution.py:60
  105.4 14.9 %all-to-all-start.2 = ((bf16[4,32,1792]{2,1,0:T(8,128)(2,1)}), bf16[4,32,1792]{2,1,0:T(8,128)(2,1)S(1)}, u32[]{:S(2)}, u32[]{:S(2)}) async-start(bf16[4,32,1792]{2,1,0:T(8,128)(2,1)} %pack.3), calls=%async_computation.2 | async-start | bytes 917504 | tf_op jit(solution)/shard_map/all_to_all | solution.py:219
  120.4 16.1 %collective-permute-start.15 = (bf16[128,2048]{1,0:T(8,128)(2,1)}, bf16[128,2048]{1,0:T(8,128)(2,1)}, u32[]{:S(2)}, u32[]{:S(2)}) collective-permute-start(bf16[128,2048]{1,0:T(8,128)(2,1)} %collective-permute-done.12.refs_7_), channel_id=1, source_target_pairs={{0,8},{4,12},{8,16},{12,20},{16,24},{20,28},{24,0},{28,4},{1,9},{5... | collective-permute-start | bytes 1572872 | tf_op jit(solution)/shard_map/ppermute | solution.py:47
  122.8 13.7 %collective-permute-start.16 = (bf16[128,2048]{1,0:T(8,128)(2,1)}, bf16[128,2048]{1,0:T(8,128)(2,1)}, u32[]{:S(2)}, u32[]{:S(2)}) collective-permute-start(bf16[128,2048]{1,0:T(8,128)(2,1)} %collective-permute-done.12.refs_7_), channel_id=1, source_target_pairs={{0,4},{4,0},{8,12},{12,8},{16,20},{20,16},{24,28},{28,24},{1,5},{5... | collective-permute-start | bytes 1572872 | tf_op jit(solution)/shard_map/ppermute | solution.py:55
  137.1 18.8 %all-to-all-start.3 = ((bf16[4,2,64,1024]{3,2,1,0:T(8,128)(2,1)}), bf16[4,2,64,1024]{3,2,1,0:T(8,128)(2,1)}, u32[]{:S(2)}, u32[]{:S(2)}) async-start(bf16[4,2,64,1024]{3,2,1,0:T(8,128)(2,1)} %pad_maximum_fusion), calls=%async_computation.3 | async-start | bytes 2097152 | tf_op jit(solution)/shard_map/all_to_all | solution.py:219
  141.3 143.2 %all-gather.5.cloned.1.call-start = ((), (), s32[]{:S(2)}) async-start(), calls=%async_computation.10 | async-start | bytes 4718592 | tf_op jit(solution)/shard_map/all_gather | solution.py:1315
  141.4 15.4 %collective-permute-start.19 = (bf16[128,2048]{1,0:T(8,128)(2,1)}, bf16[128,2048]{1,0:T(8,128)(2,1)S(1)}, u32[]{:S(2)}, u32[]{:S(2)}) collective-permute-start(bf16[128,2048]{1,0:T(8,128)(2,1)} %collective-permute-done.15.refs_9_), channel_id=1, source_target_pairs={{0,4},{4,0},{8,12},{12,8},{16,20},{20,16},{24,28},{28,24},{1,5},{5... | collective-permute-start | bytes 1572872 | tf_op jit(solution)/shard_map/ppermute | solution.py:55
  144.2 373.0 %reduce-scatter.3.cloned.1.call-start = ((), (), s32[]{:S(2)}) async-start(), calls=%async_computation.11 | async-start | bytes 5308416 | tf_op jit(solution)/shard_map/reduce_scatter | solution.py:1441
  156.8 22.2 %collective-permute-start.20 = (bf16[128,768]{1,0:T(8,128)(2,1)S(1)}, bf16[128,768]{1,0:T(8,128)(2,1)S(1)}, u32[]{:S(2)}, u32[]{:S(2)}) collective-permute-start(bf16[128,768]{1,0:T(8,128)(2,1)S(1)} %copy-done.31), channel_id=1, source_target_pairs={{0,8},{4,12},{8,16},{12,20},{16,24},{20,28},{24,0},{28,4},{1,9},{5... | collective-permute-start | bytes 589832 | tf_op jit(solution)/shard_map/ppermute | solution.py:47
  159.1 19.9 %collective-permute-start.21 = (bf16[128,768]{1,0:T(8,128)(2,1)S(1)}, bf16[128,768]{1,0:T(8,128)(2,1)S(1)}, u32[]{:S(2)}, u32[]{:S(2)}) collective-permute-start(bf16[128,768]{1,0:T(8,128)(2,1)S(1)} %copy-done.31), channel_id=1, source_target_pairs={{0,4},{4,0},{8,12},{12,8},{16,20},{20,16},{24,28},{28,24},{1,5},{5... | collective-permute-start | bytes 589832 | tf_op jit(solution)/shard_map/ppermute | solution.py:55
  187.0 30.4 %collective-permute-start.23 = (bf16[512,1024]{1,0:T(8,128)(2,1)}, bf16[512,1024]{1,0:T(8,128)(2,1)S(1)}, u32[]{:S(2)}, u32[]{:S(2)}) collective-permute-start(bf16[512,1024]{1,0:T(8,128)(2,1)} %fusion.14), channel_id=1, source_target_pairs={{0,2},{1,3},{2,0},{3,1},{4,6},{5,7},{6,4},{7,5},{8,10},{9,11},{10,... | collective-permute-start | bytes 3145736 | tf_op jit(solution)/shard_map/ppermute | solution.py:60
  189.2 14.5 %collective-permute-start.24 = (bf16[128,768]{1,0:T(8,128)(2,1)S(1)}, bf16[128,768]{1,0:T(8,128)(2,1)S(1)}, u32[]{:S(2)}, u32[]{:S(2)}) collective-permute-start(bf16[128,768]{1,0:T(8,128)(2,1)S(1)} %collective-permute-done.20.refs_9_), channel_id=1, source_target_pairs={{0,8},{4,12},{8,16},{12,20},{16,24},{20,28},{24,0},{28,4},{1,9},{5... | collective-permute-start | bytes 589832 | tf_op jit(solution)/shard_map/ppermute | solution.py:47
  189.9 13.7 %collective-permute-start.25 = (bf16[128,768]{1,0:T(8,128)(2,1)S(1)}, bf16[128,768]{1,0:T(8,128)(2,1)}, u32[]{:S(2)}, u32[]{:S(2)}) collective-permute-start(bf16[128,768]{1,0:T(8,128)(2,1)S(1)} %collective-permute-done.20.refs_9_), channel_id=1, source_target_pairs={{0,4},{4,0},{8,12},{12,8},{16,20},{20,16},{24,28},{28,24},{1,5},{5... | collective-permute-start | bytes 589832 | tf_op jit(solution)/shard_map/ppermute | solution.py:55
  203.7 13.7 %collective-permute-start.26 = (bf16[128,768]{1,0:T(8,128)(2,1)S(1)}, bf16[128,768]{1,0:T(8,128)(2,1)S(1)}, u32[]{:S(2)}, u32[]{:S(2)}) collective-permute-start(bf16[128,768]{1,0:T(8,128)(2,1)S(1)} %collective-permute-done.24.refs_11_), channel_id=1, source_target_pairs={{0,8},{4,12},{8,16},{12,20},{16,24},{20,28},{24,0},{28,4},{1,9},{5... | collective-permute-start | bytes 589832 | tf_op jit(solution)/shard_map/ppermute | solution.py:47
  203.7 13.7 %collective-permute-start.27 = (bf16[128,768]{1,0:T(8,128)(2,1)S(1)}, bf16[128,768]{1,0:T(8,128)(2,1)S(1)}, u32[]{:S(2)}, u32[]{:S(2)}) collective-permute-start(bf16[128,768]{1,0:T(8,128)(2,1)S(1)} %collective-permute-done.24.refs_11_), channel_id=1, source_target_pairs={{0,4},{4,0},{8,12},{12,8},{16,20},{20,16},{24,28},{28,24},{1,5},{5... | collective-permute-start | bytes 589832 | tf_op jit(solution)/shard_map/ppermute | solution.py:55
  225.6 25.6 %collective-permute-start.31 = (bf16[512,1024]{1,0:T(8,128)(2,1)S(1)}, bf16[512,1024]{1,0:T(8,128)(2,1)}, u32[]{:S(2)}, u32[]{:S(2)}) collective-permute-start(bf16[512,1024]{1,0:T(8,128)(2,1)S(1)} %fusion.16.refs_0_), channel_id=1, source_target_pairs={{0,2},{1,3},{2,0},{3,1},{4,6},{5,7},{6,4},{7,5},{8,10},{9,11},{10,... | collective-permute-start | bytes 3145736 | tf_op jit(solution)/shard_map/ppermute | solution.py:60
  304.5 27.8 %collective-permute-start.33 = (bf16[64,1024]{1,0:T(8,128)(2,1)S(1)}, bf16[64,1024]{1,0:T(8,128)(2,1)S(1)}, u32[]{:S(2)}, u32[]{:S(2)}) collective-permute-start(bf16[64,1024]{1,0:T(8,128)(2,1)S(1)} %bitcast.303), channel_id=1, source_target_pairs={{0,1},{1,0},{2,3},{3,2},{4,5},{5,4},{6,7},{7,6},{8,9},{9,8},{10,11... | collective-permute-start | bytes 393224 | tf_op jit(solution)/shard_map/ppermute | solution.py:205
  304.7 27.5 %collective-permute-start.34 = (bf16[64,1024]{1,0:T(8,128)(2,1)S(1)}, bf16[64,1024]{1,0:T(8,128)(2,1)S(1)}, u32[]{:S(2)}, u32[]{:S(2)}) collective-permute-start(bf16[64,1024]{1,0:T(8,128)(2,1)S(1)} %bitcast.302), channel_id=1, source_target_pairs={{0,2},{1,3},{2,0},{3,1},{4,6},{5,7},{6,4},{7,5},{8,10},{9,11},{10,... | collective-permute-start | bytes 393224 | tf_op jit(solution)/shard_map/ppermute | solution.py:205
  305.0 27.3 %collective-permute-start.35 = (bf16[64,1024]{1,0:T(8,128)(2,1)S(1)}, bf16[64,1024]{1,0:T(8,128)(2,1)S(1)}, u32[]{:S(2)}, u32[]{:S(2)}) collective-permute-start(bf16[64,1024]{1,0:T(8,128)(2,1)S(1)} %bitcast.301), channel_id=1, source_target_pairs={{0,3},{1,2},{2,1},{3,0},{4,7},{5,6},{6,5},{7,4},{8,11},{9,10},{10,... | collective-permute-start | bytes 393224 | tf_op jit(solution)/shard_map/ppermute | solution.py:205
  333.7 313.6 %reduce-scatter.5.cloned.1.call-start = ((), (), s32[]{:S(2)}) async-start(), calls=%async_computation.12 | async-start | bytes 7077888 | tf_op jit(solution)/shard_map/reduce_scatter | solution.py:1489
  387.5 25.6 %collective-permute-start.37 = (bf16[512,1024]{1,0:T(8,128)(2,1)S(1)}, bf16[512,1024]{1,0:T(8,128)(2,1)}, u32[]{:S(2)}, u32[]{:S(2)}) collective-permute-start(bf16[512,1024]{1,0:T(8,128)(2,1)S(1)} %fusion.9), channel_id=1, source_target_pairs={{0,2},{1,3},{2,0},{3,1},{4,6},{5,7},{6,4},{7,5},{8,10},{9,11},{10,... | collective-permute-start | bytes 3145736 | tf_op jit(solution)/shard_map/ppermute | solution.py:60
  422.8 25.4 %collective-permute-start.39 = (bf16[512,1024]{1,0:T(8,128)(2,1)S(1)}, bf16[512,1024]{1,0:T(8,128)(2,1)}, u32[]{:S(2)}, u32[]{:S(2)}) collective-permute-start(bf16[512,1024]{1,0:T(8,128)(2,1)S(1)} %convert_element_type.228.refs_0_), channel_id=1, source_target_pairs={{0,2},{1,3},{2,0},{3,1},{4,6},{5,7},{6,4},{7,5},{8,10},{9,11},{10,... | collective-permute-start | bytes 3145736 | tf_op jit(solution)/shard_map/ppermute | solution.py:60
  463.9 27.0 %collective-permute-start.42 = (bf16[64,1024]{1,0:T(8,128)(2,1)S(1)}, bf16[64,1024]{1,0:T(8,128)(2,1)S(1)}, u32[]{:S(2)}, u32[]{:S(2)}) collective-permute-start(bf16[64,1024]{1,0:T(8,128)(2,1)S(1)} %bitcast.300), channel_id=1, source_target_pairs={{0,1},{1,0},{2,3},{3,2},{4,5},{5,4},{6,7},{7,6},{8,9},{9,8},{10,11... | collective-permute-start | bytes 393224 | tf_op jit(solution)/shard_map/ppermute | solution.py:205
  464.0 26.8 %collective-permute-start.43 = (bf16[64,1024]{1,0:T(8,128)(2,1)S(1)}, bf16[64,1024]{1,0:T(8,128)(2,1)S(1)}, u32[]{:S(2)}, u32[]{:S(2)}) collective-permute-start(bf16[64,1024]{1,0:T(8,128)(2,1)S(1)} %bitcast.299), channel_id=1, source_target_pairs={{0,2},{1,3},{2,0},{3,1},{4,6},{5,7},{6,4},{7,5},{8,10},{9,11},{10,... | collective-permute-start | bytes 393224 | tf_op jit(solution)/shard_map/ppermute | solution.py:205
  464.3 26.5 %collective-permute-start.44 = (bf16[64,1024]{1,0:T(8,128)(2,1)S(1)}, bf16[64,1024]{1,0:T(8,128)(2,1)S(1)}, u32[]{:S(2)}, u32[]{:S(2)}) collective-permute-start(bf16[64,1024]{1,0:T(8,128)(2,1)S(1)} %bitcast.298), channel_id=1, source_target_pairs={{0,3},{1,2},{2,1},{3,0},{4,7},{5,6},{6,5},{7,4},{8,11},{9,10},{10,... | collective-permute-start | bytes 393224 | tf_op jit(solution)/shard_map/ppermute | solution.py:205
  493.9 20.6 %collective-permute-start.45 = (bf16[512,1024]{1,0:T(8,128)(2,1)S(1)}, bf16[512,1024]{1,0:T(8,128)(2,1)}, u32[]{:S(2)}, u32[]{:S(2)}) collective-permute-start(bf16[512,1024]{1,0:T(8,128)(2,1)S(1)} %dynamic-slice_bitcast_fusion.3), channel_id=1, source_target_pairs={{0,1},{1,0},{2,3},{3,2},{4,5},{5,4},{6,7},{7,6},{8,9},{9,8},{10,11... | collective-permute-start | bytes 3145736 | tf_op jit(solution)/shard_map/ppermute | solution.py:65
  516.6 26.2 %collective-permute-start.46 = (bf16[512,1024]{1,0:T(8,128)(2,1)S(1)}, bf16[512,1024]{1,0:T(8,128)(2,1)}, u32[]{:S(2)}, u32[]{:S(2)}) collective-permute-start(bf16[512,1024]{1,0:T(8,128)(2,1)S(1)} %fusion.7), channel_id=1, source_target_pairs={{0,2},{1,3},{2,0},{3,1},{4,6},{5,7},{6,4},{7,5},{8,10},{9,11},{10,... | collective-permute-start | bytes 3145736 | tf_op jit(solution)/shard_map/ppermute | solution.py:60
  518.9 47.6 %collective-permute-start.47 = (bf16[32,1024]{1,0:T(8,128)(2,1)}, bf16[32,1024]{1,0:T(8,128)(2,1)S(1)}, u32[]{:S(2)}, u32[]{:S(2)}) collective-permute-start(bf16[32,1024]{1,0:T(8,128)(2,1)} %get-tuple-element.683), channel_id=1, source_target_pairs={{0,1},{1,0},{2,3},{3,2},{4,5},{5,4},{6,7},{7,6},{8,9},{9,8},{10,11... | collective-permute-start | bytes 196616 | tf_op jit(solution)/shard_map/ppermute | solution.py:205
  518.9 47.6 %collective-permute-start.48 = (bf16[32,1024]{1,0:T(8,128)(2,1)}, bf16[32,1024]{1,0:T(8,128)(2,1)S(1)}, u32[]{:S(2)}, u32[]{:S(2)}) collective-permute-start(bf16[32,1024]{1,0:T(8,128)(2,1)} %get-tuple-element.684), channel_id=1, source_target_pairs={{0,2},{1,3},{2,0},{3,1},{4,6},{5,7},{6,4},{7,5},{8,10},{9,11},{10,... | collective-permute-start | bytes 196616 | tf_op jit(solution)/shard_map/ppermute | solution.py:205
  520.6 45.9 %collective-permute-start.49 = (bf16[32,1024]{1,0:T(8,128)(2,1)S(1)}, bf16[32,1024]{1,0:T(8,128)(2,1)S(1)}, u32[]{:S(2)}, u32[]{:S(2)}) collective-permute-start(bf16[32,1024]{1,0:T(8,128)(2,1)S(1)} %get-tuple-element.682), channel_id=1, source_target_pairs={{0,3},{1,2},{2,1},{3,0},{4,7},{5,6},{6,5},{7,4},{8,11},{9,10},{10,... | collective-permute-start | bytes 196616 | tf_op jit(solution)/shard_map/ppermute | solution.py:205
  563.6 45.9 %all-to-all-start.4 = ((bf16[32,32,512]{2,1,0:T(8,128)(2,1)}), bf16[32,32,512]{2,1,0:T(8,128)(2,1)S(1)}, u32[]{:S(2)}, u32[]{:S(2)}) async-start(bf16[32,32,512]{2,1,0:T(8,128)(2,1)} %bitcast.275), calls=%async_computation.5 | async-start | bytes 2097152 | tf_op jit(solution)/shard_map/all_to_all | solution.py:185
  591.3 30.4 %collective-permute-start.51 = (bf16[512,1024]{1,0:T(8,128)(2,1)}, bf16[512,1024]{1,0:T(8,128)(2,1)}, u32[]{:S(2)}, u32[]{:S(2)}) collective-permute-start(bf16[512,1024]{1,0:T(8,128)(2,1)} %fusion.6), channel_id=1, source_target_pairs={{0,2},{1,3},{2,0},{3,1},{4,6},{5,7},{6,4},{7,5},{8,10},{9,11},{10,... | collective-permute-start | bytes 3145736 | tf_op jit(solution)/shard_map/ppermute | solution.py:60
  594.0 29.4 %collective-permute-start.53 = (bf16[512,1024]{1,0:T(8,128)(2,1)}, bf16[512,1024]{1,0:T(8,128)(2,1)}, u32[]{:S(2)}, u32[]{:S(2)}) collective-permute-start(bf16[512,1024]{1,0:T(8,128)(2,1)} %dynamic-slice_bitcast_fusion), channel_id=1, source_target_pairs={{0,1},{1,0},{2,3},{3,2},{4,5},{5,4},{6,7},{7,6},{8,9},{9,8},{10,11... | collective-permute-start | bytes 3145736 | tf_op jit(solution)/shard_map/ppermute | solution.py:65
  609.5 31.3 %all-to-all-start.5 = ((bf16[32,32,512]{2,1,0:T(8,128)(2,1)}), bf16[32,32,512]{2,1,0:T(8,128)(2,1)}, u32[]{:S(2)}, u32[]{:S(2)}) async-start(bf16[32,32,512]{2,1,0:T(8,128)(2,1)} %bitcast.126), calls=%async_computation.6 | async-start | bytes 2097152 | tf_op jit(solution)/shard_map/all_to_all | solution.py:185
  651.9 11.0 %all-to-all-start.6 = ((f32[32,1,128]{2,1,0:T(1,128)}), f32[32,1,128]{2,1,0:T(1,128)S(1)}, u32[]{:S(2)}, u32[]{:S(2)}) async-start(f32[32,1,128]{2,1,0:T(1,128)} %broadcast_in_dim.42), calls=%async_computation.8 | async-start | bytes 32768 | tf_op jit(solution)/shard_map/all_to_all | solution.py:1557
  (105 other events, 950.7 us)
Sparse Core Ops, SparseCore 0:
  27.3 44.1 all-gather.2
  144.9 84.7 all-gather.4
  333.8 93.5 reduce-scatter.2
  492.4 129.6 reduce-scatter.4
